TPU v7x, 32 devices: a whole 2x2x4 slice. The times are simulated.
32 devices in a mesh: cases: 2 (over x), bus: 16 (over z, y, core).
Axes of the slice: x: 2, y: 2, z: 4, core: 2. Of those that a mesh axis runs over, the one named last changes fastest.
Arguments:
- ptdf: bfloat16 [20480, 10240], P('bus'), may hold values from -0.078125 to 0.078125
- line_limit: float32 [20480], P('bus'), may hold values from 1 to 8
- gen_cost: float32 [12288], P('bus'), may hold values from 0.1 to 2
- gen_max: float32 [12288], P('bus'), may hold values from 0.5 to 4
- gen_owner: int32 [12288, 1], P('bus'), may hold values from 0 to 15; in each aligned block of 768 rows (0 to 767, 768 to 1535, ...) at most 144 rows name the same one
- gen_local: int32 [12288], P('bus'), may hold values from 0 to 639
- availability: float32 [24576, 128], P(('cases', 'bus')), parts along dimension 0, may hold values from 0 to 1
- demand: float32 [20480, 128], P(('cases', 'bus')), parts along dimension 0, may hold values from 0.5 to 2.5
- dispatch: float32 [24576, 128], P(('cases', 'bus')), parts along dimension 0, may hold values from 0 to 2
- balance_price: float32 [256], P('cases'), parts along dimension 0, may hold values from -6 to 6
- line_price: float32 [40960, 128], P(('cases', 'bus')), parts along dimension 0, may hold values from -4 to 4
Outputs:
- dispatch_out: float32 [24576, 128], P(('cases', 'bus')), parts along dimension 0
- balance_out: float32 [256], P('cases'), parts along dimension 0
- line_out: float32 [40960, 128], P(('cases', 'bus')), parts along dimension 0
There are 2 independent parts, one for each index of `cases`. A program takes and returns all parts, laid end to end along the dimension named above; an argument that names none is the same for every part. Nothing has to cross between parts.
Inputs may be any that keep to these rules, and one draw needn't show every extreme that they name: `gen_owner`: among the 768 generators of one device (aligned blocks of rows), no owner is named more than 144 times, a bound that some block reaches.
All inputs are finite; a program needn't handle non-finite values.
Results may differ from a plain program's by a relative error of at most 0.0036.
Values may be sent and summed in bfloat16 or wider, within the bound.
No kernel may reach another device: no remote copies, remote signals or barrier semaphores. Data moves between devices by JAX's collectives and lax.ppermute only.
A program may use at most 128 MiB of HBM per device.

v0:
```python
import jax
import jax.numpy as jnp
from jax import lax
from jax.sharding import PartitionSpec as P

ITERS = 2


tau_step = 0.2
sigma_step = 0.15


def local(
    ptdf,
    line_limit,
    gen_cost,
    gen_max,
    gen_owner,
    gen_local,
    availability,
    demand,
    dispatch,
    balance_price,
    line_price,
):
    devices = lax.axis_size("bus")
    position = lax.axis_index("bus")
    bus_rows = demand.shape[0]
    all_buses = bus_rows * devices
    gen_rows = dispatch.shape[0]
    hour_count = dispatch.shape[1]
    capacity = max(2, 3 * gen_rows // devices)
    owner = gen_owner[:, 0]
    global_bus = owner * bus_rows + gen_local
    every_bus = lax.all_gather(global_bus, "bus", axis=0, tiled=True)
    owner_hits = (owner[:, None] == jnp.arange(devices, dtype=jnp.int32)[None, :]).astype(jnp.int32)
    owner_rank = jnp.sum((jnp.cumsum(owner_hits, axis=0) - owner_hits) * owner_hits, axis=1)
    slot_index = owner * capacity + owner_rank
    source_bus = every_bus.reshape(devices, gen_rows)
    mine = (source_bus // bus_rows == position).astype(jnp.int32)
    mine_rank = jnp.cumsum(mine, axis=1) - mine
    rank_ids = jnp.arange(capacity, dtype=jnp.int32)
    rank_match = mine[:, :, None] * (mine_rank[:, :, None] == rank_ids[None, None, :]).astype(
        jnp.int32
    )
    local_bus = source_bus - position * bus_rows
    arrived_buses = (
        jnp.sum(rank_match * local_bus[:, :, None], axis=1)
        + (1 - jnp.sum(rank_match, axis=1)) * bus_rows
    )
    flat_buses = arrived_buses.reshape(-1)
    pick_rows = jnp.minimum(flat_buses, bus_rows - 1)
    upper = gen_max[:, None] * availability
    limit = line_limit[:, None]
    for iteration in range(ITERS):
        line_half = line_price.astype(jnp.bfloat16)
        shadow = lax.psum_scatter(
            lax.dot_general(
                ptdf, line_half, (((0,), (0,)), ((), ())), preferred_element_type=jnp.float32
            ),
            "bus",
            scatter_dimension=0,
            tiled=True,
        )
        outgoing = jnp.take(shadow, pick_rows, axis=0).reshape(devices, capacity, hour_count)
        returned = lax.all_to_all(outgoing, "bus", split_axis=0, concat_axis=0, tiled=True)
        bus_price = jnp.take(returned.reshape(devices * capacity, hour_count), slot_index, axis=0)
        price = bus_price + balance_price[None, :]
        updated = jnp.clip(dispatch - tau_step * (gen_cost[:, None] + price), 0.0, upper)
        extra = 2.0 * updated - dispatch
        full_sums = jax.ops.segment_sum(extra, global_bus, num_segments=all_buses)
        injection = lax.psum_scatter(full_sums, "bus", scatter_dimension=0, tiled=True) - demand
        balance = lax.psum(jnp.sum(injection, axis=0), "bus")
        balance_price = balance_price + sigma_step * balance / all_buses
        flow = jnp.dot(
            ptdf,
            lax.all_gather(injection.astype(jnp.bfloat16), "bus", axis=0, tiled=True),
            preferred_element_type=jnp.float32,
        )
        shifted = line_price + sigma_step * flow
        line_price = shifted - sigma_step * jnp.clip(shifted / sigma_step, -limit, limit)
        dispatch = updated
    return (dispatch, balance_price, line_price)


def solution(mesh):
    return jax.shard_map(
        local,
        mesh=mesh,
        in_specs=(
            P("bus", None),
            P("bus"),
            P("bus"),
            P("bus"),
            P("bus", None),
            P("bus"),
            P(("cases", "bus"), None),
            P(("cases", "bus"), None),
            P(("cases", "bus"), None),
            P("cases"),
            P(("cases", "bus"), None),
        ),
        out_specs=(P(("cases", "bus"), None), P("cases"), P(("cases", "bus"), None)),
        check_vma=False,
    )
```

profile of v0, /device:TPU:0, one launch (start us, length us, event | category | flops | bytes accessed | tf_op | source)
XLA Modules:
  0.0 593.1 jit_solution(11332282485617281092)
XLA Ops:
  7.2 13.8 %fusion.24 = f32[10240,128]{1,0:T(8,128)} fusion(bf16[1280,10240]{1,0:T(8,128)(2,1)} %param.15, f32[1280,128]{1,0:T(8,128)} %param.25), kind=kOutput, calls=%fused_computation.42 | convolution fusion | flops 3355607040 | bytes 32112640 | tf_op jit(solution)/shard_map/dot_general | solution.py:58
  21.1 0.7 copy-done.11
  21.8 23.2 %all-gather = s32[16,1,768]{2,1,0:T(1,128)S(1)} all-gather(s32[1,1,768]{2,1,0:T(1,128)S(1)} %reshape.201), channel_id=1, replica_groups=mesh['cases'=2,'bus'=16] {'bus'}, dimensions={0}, use_global_device_ids=true | all-gather | bytes 52224 | tf_op jit(solution)/shard_map/all_gather | solution.py:35
  45.2 1.7 reduce-window.14
  47.3 1.6 select_reduce_fusion
  49.0 53.3 %reduce-scatter.5.cloned.1.call-done = f32[640,128]{1,0:T(8,128)} async-done(((f32[10240,128]{1,0:T(8,128)}), f32[640,128]{1,0:T(8,128)}) %reduce-scatter.5.cloned.1.call-update) | async-done | bytes 327696 | tf_op jit(solution)/shard_map/reduce_scatter | solution.py:57
  102.3 4.9 gather_fusion
  107.3 2.0 broadcast_select_fusion.1
  109.3 3.7 all-to-all-start
  113.1 1.7 reduce-window.16
  115.2 22.9 %all-to-all-done = f32[16,144,128]{2,1,0:T(8,128)S(1)} async-done(((f32[16,144,128]{2,1,0:T(8,128)}), f32[16,144,128]{2,1,0:T(8,128)S(1)}, u32[]{:S(2)}, u32[]{:S(2)}) %all-to-all-start) | async-done | bytes 1179680 | tf_op jit(solution)/shard_map/all_to_all | solution.py:66
  138.1 1.6 gather_fusion.1
  140.1 8.7 %scatter_custom_fusion = f32[10240,128]{1,0:T(8,128)} fusion(s32[768]{0:T(1024)S(1)} %multiply_add_fusion, f32[]{:T(128)} %constant.29.clone.1, f32[768,128]{1,0:T(8,128)S(1)} %copy-done.1, f32[768,128]{1,0:T(8,128)S(1)} %fusion.18, f32[]{:T(128)} %constant.66.clone.1), kind=kCustom, calls=%fused_computation.13 | custom fusion | flops 294912 | bytes 6029320 | tf_op jit(solution)/shard_map/scatter-add | solution.py:71
  148.9 81.3 %reduce-scatter.7.cloned.1.call-done = f32[640,128]{1,0:T(8,128)} async-done(((f32[10240,128]{1,0:T(8,128)}), f32[640,128]{1,0:T(8,128)}) %reduce-scatter.7.cloned.1.call-update) | async-done | bytes 327696 | tf_op jit(solution)/shard_map/reduce_scatter | solution.py:72
  230.3 1.7 subtract_reduce_fusion.1
  232.5 42.8 %all-gather.4.cloned.1.call-done = bf16[10240,128]{1,0:T(8,128)(2,1)} async-done(((bf16[640,128]{1,0:T(8,128)(2,1)}), bf16[10240,128]{1,0:T(8,128)(2,1)}) %all-gather.4.cloned.1.call-update) | async-done | bytes 2621456 | tf_op jit(solution)/shard_map/all_gather | solution.py:77
  275.2 13.8 %multiply_subtract_fusion.1 = f32[1280,128]{0,1:T(8,128)S(1)} fusion(f32[1280,128]{0,1:T(8,128)S(1)} %copy.52, bf16[10240,128]{1,0:T(8,128)(2,1)} %all-gather.4.cloned.1.call-done, bf16[1280,10240]{1,0:T(8,128)(2,1)} %param.15, f32[1280]{0:T(1024)S(1)} %neg.5, f32[1280]{0:T(1024)S(1)} %copy-done.7), kind=kOutput, calls=%fused_computation.22 | convolution fusion | flops 3356590080 | bytes 30156800 | tf_op jit(solution)/shard_map/dot_general | solution.py:75
  289.0 14.3 %convolution_bitcast_fusion = f32[10240,128]{0,1:T(8,128)} fusion(bf16[1280,10240]{1,0:T(8,128)(2,1)} %param.15, f32[1280,128]{0,1:T(8,128)S(1)} %multiply_subtract_fusion.1), kind=kOutput, calls=%fused_computation.6 | convolution fusion | flops 3355607040 | bytes 32112640 | tf_op jit(solution)/shard_map/dot_general | solution.py:58
  303.4 77.3 %reduce-scatter.9.cloned.1.call-done = f32[640,128]{0,1:T(8,128)} async-done(((f32[10240,128]{0,1:T(8,128)}), f32[640,128]{0,1:T(8,128)}) %reduce-scatter.9.cloned.1.call-update) | async-done | bytes 327696 | tf_op jit(solution)/shard_map/reduce_scatter | solution.py:57
  380.7 1.1 copy.53
  381.9 3.9 gather_fusion.2
  385.8 2.0 broadcast_select_fusion
  387.8 3.8 all-to-all-start.1
  391.7 47.2 %psum.14 = f32[128]{0:T(128)S(1)} all-reduce(f32[128]{0:T(128)S(1)} %get-tuple-element.28), channel_id=1, replica_groups=mesh['cases'=2,'bus'=16] {'bus'}, use_global_device_ids=true, to_apply=%region_12.15 | all-reduce | flops 128 | bytes 1024 | tf_op jit(solution)/shard_map/psum | solution.py:73
  439.0 1.6 gather_fusion.3
  440.9 8.7 %scatter_custom_fusion.1 = f32[10240,128]{1,0:T(8,128)} fusion(s32[768]{0:T(1024)S(1)} %multiply_add_fusion, f32[]{:T(128)} %constant.29.clone.1, f32[768,128]{1,0:T(8,128)S(1)} %fusion.18, f32[768,128]{1,0:T(8,128)S(1)} %fusion.13, f32[]{:T(128)} %constant.66.clone.1), kind=kCustom, calls=%fused_computation.11 | custom fusion | flops 294912 | bytes 6029320 | tf_op jit(solution)/shard_map/scatter-add | solution.py:71
  449.8 76.7 %reduce-scatter.11.cloned.1.call-done = f32[640,128]{1,0:T(8,128)} async-done(((f32[10240,128]{1,0:T(8,128)}), f32[640,128]{1,0:T(8,128)}) %reduce-scatter.11.cloned.1.call-update) | async-done | bytes 327696 | tf_op jit(solution)/shard_map/reduce_scatter | solution.py:72
  526.4 1.7 subtract_convert_fusion
  528.1 30.9 %psum.15 = f32[128]{0:T(128)S(1)} all-reduce(f32[128]{0:T(128)S(1)} %get-tuple-element.27), channel_id=1, replica_groups=mesh['cases'=2,'bus'=16] {'bus'}, use_global_device_ids=true, to_apply=%region_16.19 | all-reduce | flops 128 | bytes 1024 | tf_op jit(solution)/shard_map/psum | solution.py:73
  559.5 11.9 %all-gather.6.cloned.1.call-done = bf16[10240,128]{1,0:T(8,128)(2,1)} async-done(((bf16[640,128]{1,0:T(8,128)(2,1)}), bf16[10240,128]{1,0:T(8,128)(2,1)}) %all-gather.6.cloned.1.call-update) | async-done | bytes 2621456 | tf_op jit(solution)/shard_map/all_gather | solution.py:77
  571.4 13.8 %multiply_subtract_fusion = f32[1280,128]{0,1:T(8,128)S(1)} fusion(f32[1280,128]{0,1:T(8,128)S(1)} %multiply_subtract_fusion.1, bf16[10240,128]{1,0:T(8,128)(2,1)} %all-gather.6.cloned.1.call-done, bf16[1280,10240]{1,0:T(8,128)(2,1)} %param.15, f32[1280]{0:T(1024)S(1)} %neg.5, f32[1280]{0:T(1024)S(1)} %copy-done.7), kind=kOutput, calls=%fused_computation.21 | convolution fusion | flops 3356590080 | bytes 30156800 | tf_op jit(solution)/shard_map/dot_general | solution.py:75
  585.2 1.1 copy.54
  (68 shorter events, 3.1 us)
Async XLA Ops:
  7.2 95.2 %reduce-scatter.5.cloned.1.call-start = ((), (), s32[]{:S(2)}) async-start(), calls=%async_computation.6 | async-start | bytes 5570560 | tf_op jit(solution)/shard_map/reduce_scatter | solution.py:57
  21.0 0.7 copy-start.11
  21.0 0.7 copy-start.10
  107.2 32.5 %copy-start.1 = (f32[768,128]{1,0:T(8,128)S(1)}, f32[768,128]{1,0:T(8,128)}, u32[]{:S(2)}) copy-start(f32[768,128]{1,0:T(8,128)} %param.23) | copy-start | bytes 1179652
  107.2 32.5 %copy-start.3 = (f32[768,128]{1,0:T(8,128)S(1)}, f32[768,128]{1,0:T(8,128)}, u32[]{:S(2)}) copy-start(f32[768,128]{1,0:T(8,128)} %param.21) | copy-start | bytes 1179652
  107.2 32.5 %copy-start.8 = (f32[768]{0:T(1024)S(1)}, f32[768]{0:T(1024)}, u32[]{:S(2)}) copy-start(f32[768]{0:T(1024)} %param.17) | copy-start | bytes 9220
  107.2 32.5 %copy-start.9 = (f32[768]{0:T(1024)S(1)}, f32[768]{0:T(1024)}, u32[]{:S(2)}) copy-start(f32[768]{0:T(1024)} %param.18) | copy-start | bytes 9220
  107.3 32.5 %copy-start.12 = (f32[128]{0:T(128)S(1)}, f32[128]{0:T(128)}, u32[]{:S(2)}) copy-start(f32[128]{0:T(128)} %param.24) | copy-start | bytes 1540
  109.3 28.8 %all-to-all-start = ((f32[16,144,128]{2,1,0:T(8,128)}), f32[16,144,128]{2,1,0:T(8,128)S(1)}, u32[]{:S(2)}, u32[]{:S(2)}) async-start(f32[16,144,128]{2,1,0:T(8,128)} %bitcast.3), calls=%async_computation.1 | async-start | bytes 2359296 | tf_op jit(solution)/shard_map/all_to_all | solution.py:66
  113.0 117.3 %reduce-scatter.7.cloned.1.call-start = ((), (), s32[]{:S(2)}) async-start(), calls=%async_computation.7 | async-start | bytes 5570560 | tf_op jit(solution)/shard_map/reduce_scatter | solution.py:72
  140.1 90.2 %copy-start.5 = (f32[640,128]{1,0:T(8,128)S(1)}, f32[640,128]{1,0:T(8,128)}, u32[]{:S(2)}) copy-start(f32[640,128]{1,0:T(8,128)} %param.22) | copy-start | bytes 983044
  140.1 92.1 %copy-start = (f32[1280,128]{1,0:T(8,128)S(1)}, f32[1280,128]{1,0:T(8,128)}, u32[]{:S(2)}) copy-start(f32[1280,128]{1,0:T(8,128)} %param.25) | copy-start | bytes 1966084
  148.9 83.6 %copy-start.7 = (f32[1280]{0:T(1024)S(1)}, f32[1280]{0:T(1024)}, u32[]{:S(2)}) copy-start(f32[1280]{0:T(1024)} %param.16) | copy-start | bytes 15364
  148.9 126.4 %all-gather.4.cloned.1.call-start = ((), (), s32[]{:S(2)}) async-start(), calls=%async_computation.8 | async-start | bytes 2785280 | tf_op jit(solution)/shard_map/all_gather | solution.py:77
  232.0 148.8 %reduce-scatter.9.cloned.1.call-start = ((), (), s32[]{:S(2)}) async-start(), calls=%async_computation.9 | async-start | bytes 5570560 | tf_op jit(solution)/shard_map/reduce_scatter | solution.py:57
  387.8 52.7 %copy-start.4 = (f32[768,128]{1,0:T(8,128)S(1)}, f32[768,128]{1,0:T(8,128)}, u32[]{:S(2)}) copy-start(f32[768,128]{1,0:T(8,128)} %param.21) | copy-start | bytes 1179652
  387.8 51.1 %all-to-all-start.1 = ((f32[16,144,128]{2,1,0:T(8,128)}), f32[16,144,128]{2,1,0:T(8,128)S(1)}, u32[]{:S(2)}, u32[]{:S(2)}) async-start(f32[16,144,128]{2,1,0:T(8,128)} %bitcast.7), calls=%async_computation.4 | async-start | bytes 2359296 | tf_op jit(solution)/shard_map/all_to_all | solution.py:66
  391.7 134.8 %reduce-scatter.11.cloned.1.call-start = ((), (), s32[]{:S(2)}) async-start(), calls=%async_computation.10 | async-start | bytes 5570560 | tf_op jit(solution)/shard_map/reduce_scatter | solution.py:72
  440.9 8.8 %copy-start.2 = (f32[768,128]{1,0:T(8,128)}, f32[768,128]{1,0:T(8,128)S(1)}, u32[]{:S(2)}) copy-start(f32[768,128]{1,0:T(8,128)S(1)} %fusion.13) | copy-start | bytes 1179652
  440.9 85.5 %copy-start.6 = (f32[640,128]{1,0:T(8,128)S(1)}, f32[640,128]{1,0:T(8,128)}, u32[]{:S(2)}) copy-start(f32[640,128]{1,0:T(8,128)} %param.22) | copy-start | bytes 983044
  449.7 121.7 %all-gather.6.cloned.1.call-start = ((), (), s32[]{:S(2)}) async-start(), calls=%async_computation.11 | async-start | bytes 2785280 | tf_op jit(solution)/shard_map/all_gather | solution.py:77
Sparse Core Ops, SparseCore 0:
  21.2 81.1 reduce-scatter.4
  149.0 81.2 reduce-scatter.6
  233.1 42.0 all-gather.3
  303.5 77.1 reduce-scatter.8
  449.8 76.5 reduce-scatter.10
  529.2 42.1 all-gather.5
where the time goes:
time: 594 us; the launch traced here: 593 us
  waiting for transfers between devices  366 us (62%)
  blocking collectives  101 us (17%)
  matrix products  55.7 us (9%)
  other arithmetic  31.6 us (5%)
  local copies, waits for them, and re-layouts  15.7 us (3%)
  between operations  14.5 us (2%)
  starting transfers between devices  7.96 us (1%)
    reduce_scatter x2, waiting for transfers between devices, local(): lax.psum_scatter(full_sums, 'bus', scatter_dimension=0, tiled=True) - demand  158 us
    reduce_scatter x2, waiting for transfers between devices, local(): lax.psum_scatter(lax.dot_general(ptdf, line_half, (((0,), (0,)), ((), ())...  131 us
    psum x2, blocking collectives, local(): balance = lax.psum(jnp.sum(injection, axis=0), 'bus')  78.1 us
    all_gather x2, waiting for transfers between devices, local(): lax.all_gather(injection.astype(jnp.bfloat16), 'bus', axis=0, tiled=True)  54.6 us
    dot_general x2, matrix products, local(): lax.dot_general(ptdf, line_half, (((0,), (0,)), ((), ())), preferred_elem...  28.2 us
    dot_general x2, matrix products, local(): jnp.dot(ptdf, lax.all_gather(injection.astype(jnp.bfloat16), 'bus', axis=...  27.6 us
    all_gather x1, blocking collectives, local(): every_bus = lax.all_gather(global_bus, 'bus', axis=0, tiled=True)  23.2 us
    all_to_all x2, waiting for transfers between devices, local(): lax.all_to_all(outgoing, 'bus', split_axis=0, concat_axis=0, tiled=True)  22.9 us
  transfers between devices with their start and end apart: 8, of which 7 were waited for; matrix products, arithmetic and copies ran while one was open for 1% of the time, Pallas kernels for 0%

commit v1 on v0

v1 whole, which is shorter than its diff:
```python
import functools

import jax
import jax.numpy as jnp
from jax import lax
from jax.experimental import pallas as pl
from jax.experimental.pallas import tpu as pltpu
from jax.sharding import PartitionSpec as P

ITERS = 2

tau_step = 0.2
sigma_step = 0.15

META = 16
F32 = jnp.float32
BF16 = jnp.bfloat16
NT = (((1,), (1,)), ((), ()))
NN = (((1,), (0,)), ((), ()))


def dot(a, b, dims=NN):
    return lax.dot_general(a, b, dims, preferred_element_type=F32)


def halves(x):
    hi = x.astype(BF16)
    lo = (x - hi.astype(F32)).astype(BF16)
    return hi, lo


def thirds(x):
    hi = x.astype(BF16)
    rest = x - hi.astype(F32)
    mid = rest.astype(BF16)
    low = (rest - mid.astype(F32)).astype(BF16)
    return hi, mid, low


def pack_kernel(cap, owner_ref, local_ref, cost_ref, dispatch_ref, max_ref, avail_ref, out_ref, rank_ref, pay_ref, meta_ref):
    step = pl.program_id(0)
    gens = dispatch_ref.shape[0]
    hours = dispatch_ref.shape[1]

    @pl.when(step == 0)
    def _():
        owner = owner_ref[...]
        out_hits = lax.broadcasted_iota(jnp.int32, (rank_ref.shape[0], gens), 0)
        hits = (out_hits == owner).astype(F32)
        before = (
            lax.broadcasted_iota(jnp.int32, (gens, gens), 0) < lax.broadcasted_iota(jnp.int32, (gens, gens), 1)
        ).astype(F32)
        count = dot(hits.astype(BF16), before.astype(BF16))
        rank = jnp.sum(count * hits, axis=0, keepdims=True).astype(jnp.int32)
        rank_ref[...] = jnp.broadcast_to(owner * cap + rank, rank_ref.shape)
        pay_ref[:, :hours] = dispatch_ref[...].astype(BF16)
        pay_ref[:, hours:] = (max_ref[...] * avail_ref[...]).astype(BF16)
        local = local_ref[...]
        cost = cost_ref[...]
        hi, mid, low = thirds(cost)
        row = lax.broadcasted_iota(jnp.int32, (META, gens), 0)
        parts = [
            (local // 128 + 1).astype(F32),
            (local % 128).astype(F32),
            hi.astype(F32),
            mid.astype(F32),
            low.astype(F32),
        ]
        meta = jnp.zeros((META, gens), F32)
        for i, part in enumerate(parts):
            meta = jnp.where(row == i, part, meta)
        meta_ref[...] = meta.astype(BF16)

    slot = rank_ref[0:1, :] - step * cap
    pick = (lax.broadcasted_iota(jnp.int32, (cap, gens), 0) == slot).astype(F32).astype(BF16)
    out_ref[0, :cap, :] = dot(pick, pay_ref[...]).astype(BF16)
    out_ref[0, cap:, :] = jnp.zeros((META, 2 * hours), BF16)
    out_ref[0, cap:, :cap] = dot(meta_ref[...], pick, NT).astype(BF16)


def pack(devices, cap, owner, local_bus, cost, dispatch, gen_max, availability):
    gens, hours = dispatch.shape
    full = lambda *shape: pl.BlockSpec(shape, lambda i: (0,) * len(shape))
    return pl.pallas_call(
        functools.partial(pack_kernel, cap),
        grid=(devices,),
        out_shape=jax.ShapeDtypeStruct((devices, cap + META, 2 * hours), BF16),
        in_specs=[
            full(1, gens),
            full(1, gens),
            full(1, gens),
            full(gens, hours),
            full(gens, 1),
            full(gens, hours),
        ],
        out_specs=pl.BlockSpec((1, cap + META, 2 * hours), lambda i: (i, 0, 0)),
        scratch_shapes=[
            pltpu.VMEM((devices, gens), jnp.int32),
            pltpu.VMEM((gens, 2 * hours), BF16),
            pltpu.VMEM((META, gens), BF16),
        ],
        compiler_params=pltpu.CompilerParams(vmem_limit_bytes=48 << 20),
        cost_estimate=pl.CostEstimate(flops=4 * devices * cap * gens * hours, bytes_accessed=3 << 20, transcendentals=0),
        name="pack_generators",
    )(owner, local_bus, cost, dispatch, gen_max, availability)


def unpack_kernel(devices, cap, block, owner_ref, back_ref, dispatch_ref, max_ref, avail_ref, out_ref):
    gens = owner_ref.shape[0]
    owner = owner_ref[...]
    hits = (lax.broadcasted_iota(jnp.int32, (gens, devices), 1) == owner).astype(F32)
    before = (
        lax.broadcasted_iota(jnp.int32, (gens, gens), 1) < lax.broadcasted_iota(jnp.int32, (gens, gens), 0)
    ).astype(F32)
    count = dot(before.astype(BF16), hits.astype(BF16))
    rank = jnp.sum(count * hits, axis=1, keepdims=True).astype(jnp.int32)
    slot = owner * cap + rank
    out_ref[...] = jnp.zeros(out_ref.shape, F32)

    def body(step, carry):
        start = pl.multiple_of(step * block, block)
        pick = (lax.broadcasted_iota(jnp.int32, (gens, block), 1) == slot - start).astype(F32).astype(BF16)
        out_ref[...] += dot(pick, back_ref[pl.ds(start, block), :])
        return carry

    lax.fori_loop(0, back_ref.shape[0] // block, body, 0)
    change = out_ref[...]
    dispatch = dispatch_ref[...]
    upper = max_ref[...] * avail_ref[...]
    sent = dispatch.astype(BF16).astype(F32)
    to_upper = (upper.astype(BF16).astype(F32) - sent).astype(BF16).astype(F32)
    moved = jnp.minimum(jnp.maximum(dispatch + change, 0.0), upper)
    moved = jnp.where(change == to_upper, upper, moved)
    out_ref[...] = jnp.where(change == -sent, 0.0, moved)


def unpack(devices, cap, owner_column, back, dispatch, gen_max, availability):
    gens = owner_column.shape[0]
    hours = back.shape[2]
    slots = devices * cap
    block = 256 if slots % 256 == 0 else 128 if slots % 128 == 0 else 16
    return pl.pallas_call(
        functools.partial(unpack_kernel, devices, cap, block),
        out_shape=jax.ShapeDtypeStruct((gens, hours), F32),
        compiler_params=pltpu.CompilerParams(vmem_limit_bytes=48 << 20),
        cost_estimate=pl.CostEstimate(flops=2 * slots * gens * hours, bytes_accessed=1 << 20, transcendentals=0),
        name="unpack_dispatch",
    )(owner_column, back.reshape(slots, hours), dispatch, gen_max, availability)


def update_kernel(cap, first, last, parts, *refs):
    price_refs = refs[:parts]
    balance_ref, demand_ref, recv_ref, prev_ref, upd_ref, inj_ref, shadow_ref, acc_ref, extra_ref = refs[parts:]
    step = pl.program_id(0)
    buses, hours = demand_ref.shape

    @pl.when(step == 0)
    def _():
        shadow = price_refs[0][...].astype(F32)
        for ref in price_refs[1:]:
            shadow = shadow + ref[...].astype(F32)
        hi, lo = halves(shadow)
        shadow_ref[:hours, :] = hi
        shadow_ref[hours:, :] = lo
        acc_ref[...] = jnp.zeros(acc_ref.shape, F32)
        extra_ref[...] = jnp.zeros(extra_ref.shape, BF16)

    meta = recv_ref[0, cap:, :]
    meta32 = meta[:, : extra_ref.shape[0]].astype(F32)
    bus_row = ((meta32[0:1] - 1.0) * 128.0 + meta32[1:2]).astype(jnp.int32)
    eye = (
        lax.broadcasted_iota(jnp.int32, (cap, 2 * hours), 0) == lax.broadcasted_iota(jnp.int32, (cap, 2 * hours), 1)
    ).astype(F32)
    columns = dot(eye.astype(BF16), meta, NT)
    bus_column = ((columns[:, 0:1] - 1.0) * 128.0 + columns[:, 1:2]).astype(jnp.int32)
    cost = (columns[:, 2:3] + columns[:, 3:4]) + columns[:, 4:5]
    at_bus = (lax.broadcasted_iota(jnp.int32, (cap, buses), 1) == bus_column).astype(F32).astype(BF16)
    both = dot(at_bus, shadow_ref[...], NT)
    price = both[:, :hours] + both[:, hours:] + balance_ref[...]
    if first:
        dispatch = recv_ref[0, :cap, :hours].astype(F32)
    else:
        dispatch = prev_ref[0]
    upper = recv_ref[0, :cap, hours:].astype(F32)
    updated = jnp.minimum(jnp.maximum(dispatch - tau_step * (cost + price), 0.0), upper)
    if last:
        upd_ref[0] = (updated - recv_ref[0, :cap, :hours].astype(F32)).astype(BF16)
    else:
        upd_ref[0] = updated
    extra = 2.0 * updated - dispatch
    hi, lo = halves(extra)
    extra_ref[:cap, :hours] = hi
    extra_ref[:cap, hours:] = lo
    at_row = lax.broadcasted_iota(jnp.int32, (buses, extra_ref.shape[0]), 0)
    to_bus = (at_row == bus_row).astype(F32).astype(BF16)
    acc_ref[...] += dot(to_bus, extra_ref[...])

    @pl.when(step == pl.num_programs(0) - 1)
    def _():
        injection = acc_ref[:, :hours] + acc_ref[:, hours:] - demand_ref[...]
        inj_ref[:buses, :] = injection.astype(BF16)
        hi, mid, low = thirds(jnp.sum(injection, axis=0, keepdims=True))
        row = lax.broadcasted_iota(jnp.int32, (META, hours), 0)
        tail = jnp.where(row == 0, hi.astype(F32), 0.0)
        tail = jnp.where(row == 1, mid.astype(F32), tail)
        tail = jnp.where(row == 2, low.astype(F32), tail)
        inj_ref[buses:, :] = tail.astype(BF16)


def update(cap, first, last, prices, balance_price, demand, recv, previous):
    devices = recv.shape[0]
    buses, hours = demand.shape
    full = lambda *shape: pl.BlockSpec(shape, lambda i: (0,) * len(shape))
    slots = lambda width: pl.BlockSpec((1, cap, width), lambda i: (i, 0, 0))
    if first:
        previous, prev_spec = balance_price, full(1, hours)
    else:
        prev_spec = slots(hours)
    return pl.pallas_call(
        functools.partial(update_kernel, cap, first, last, len(prices)),
        grid=(devices,),
        out_shape=(
            jax.ShapeDtypeStruct((devices, cap, hours), BF16 if last else F32),
            jax.ShapeDtypeStruct((buses + META, hours), BF16),
        ),
        in_specs=[full(hours, buses)] * len(prices)
        + [
            full(1, hours),
            full(buses, hours),
            pl.BlockSpec((1, cap + META, 2 * hours), lambda i: (i, 0, 0)),
            prev_spec,
        ],
        out_specs=(slots(hours), full(buses + META, hours)),
        scratch_shapes=[
            pltpu.VMEM((2 * hours, buses), BF16),
            pltpu.VMEM((buses, 2 * hours), F32),
            pltpu.VMEM((-(-cap // 128) * 128, 2 * hours), BF16),
        ],
        compiler_params=pltpu.CompilerParams(vmem_limit_bytes=48 << 20),
        cost_estimate=pl.CostEstimate(flops=8 * devices * cap * buses * hours, bytes_accessed=4 << 20, transcendentals=0),
        name="update_generators",
    )(*prices, balance_price, demand, recv, previous)


def shadow_kernel(place_ref, line_ref, ptdf_ref, keep_ref, send_ref):
    step = pl.program_id(0)
    part = dot(line_ref[...], ptdf_ref[...])

    @pl.when(step == 0)
    def _():
        send_ref[1] = part.astype(BF16)

    @pl.when(step == 1)
    def _():
        keep_ref[1] = part

    @pl.when(step == 2)
    def _():
        send_ref[0] = part.astype(BF16)

    @pl.when(step == 3)
    def _():
        keep_ref[0] = part


def shadow_chunk(chunk, place, line_t, ptdf, buses):
    hours, lines = line_t.shape
    return pl.pallas_call(
        shadow_kernel,
        grid_spec=pltpu.PrefetchScalarGridSpec(
            num_scalar_prefetch=1,
            grid=(4,),
            in_specs=[
                pl.BlockSpec((hours, lines), lambda i, place: (0, 0)),
                pl.BlockSpec((lines, buses), lambda i, place: (0, place[0] ^ (4 * chunk + 3 - i))),
            ],
            out_specs=(
                pl.BlockSpec((2, hours, buses), lambda i, place: (0, 0, 0)),
                pl.BlockSpec((2, hours, buses), lambda i, place: (0, 0, 0)),
            ),
        ),
        out_shape=(
            jax.ShapeDtypeStruct((2, hours, buses), F32),
            jax.ShapeDtypeStruct((2, hours, buses), BF16),
        ),
        compiler_params=pltpu.CompilerParams(vmem_limit_bytes=48 << 20),
        cost_estimate=pl.CostEstimate(
            flops=8 * hours * lines * buses, bytes_accessed=8 * lines * buses, transcendentals=0
        ),
        name="shadow_chunk",
    )(place, line_t, ptdf)


def flow_kernel(start, end, place_ref, ptdf_ref, b0, b1, b2, b3, acc_ref, sum_ref, *rest):
    step = pl.program_id(0)
    if end:
        limit_ref, line_ref, out_ref, half_ref, sum_out, inj_ref = rest
    else:
        out_ref, sum_out, inj_ref = rest
    buses = inj_ref.shape[0] // 4

    @pl.when(step == 0)
    def _():
        total = jnp.zeros(sum_ref.shape, F32) if start else sum_ref[...]
        for rel, ref in enumerate((b0, b1, b2, b3)):
            offset = pl.multiple_of(((place_ref[0] ^ rel) & 3) * buses, META)
            inj_ref[pl.ds(offset, buses), :] = ref[:buses, :]
            tail = ref[buses:, :].astype(F32)
            total = total + jnp.sum(tail, axis=0, keepdims=True)
        sum_out[...] = total

    flow = dot(ptdf_ref[...], inj_ref[...])
    if not start:
        flow = flow + acc_ref[...]
    if end:
        shifted = line_ref[...] + sigma_step * flow
        limit = limit_ref[...]
        line = shifted - sigma_step * jnp.minimum(jnp.maximum(shifted / sigma_step, -limit), limit)
        out_ref[...] = line
        half_ref[...] = line.astype(BF16)
    else:
        out_ref[...] = flow


def flow_chunk(chunk, place, ptdf, blocks, acc, total, limit=None, line=None):
    lines = ptdf.shape[0]
    rows, hours = blocks[0].shape
    buses = rows - META
    start, end = acc is None, limit is not None
    tile = lines // 4
    tiled = lambda width: pl.BlockSpec((tile, width), lambda i, place: (i, 0))
    full = lambda *shape: pl.BlockSpec(shape, lambda i, place: (0,) * len(shape))
    if start:
        acc, acc_spec = total, full(1, hours)
    else:
        acc_spec = tiled(hours)
    operands = [ptdf, *blocks, acc, total]
    in_specs = [pl.BlockSpec((tile, 4 * buses), lambda i, place: (i, (place[0] >> 2) ^ chunk))]
    in_specs += [full(rows, hours)] * 4 + [acc_spec, full(1, hours)]
    out_shape = [jax.ShapeDtypeStruct((lines, hours), F32)]
    out_specs = [tiled(hours)]
    if end:
        operands += [limit, line]
        in_specs += [tiled(1), tiled(hours)]
        out_shape += [jax.ShapeDtypeStruct((lines, hours), BF16)]
        out_specs += [tiled(hours)]
    out_shape += [jax.ShapeDtypeStruct((1, hours), F32)]
    out_specs += [full(1, hours)]
    return pl.pallas_call(
        functools.partial(flow_kernel, start, end),
        grid_spec=pltpu.PrefetchScalarGridSpec(
            num_scalar_prefetch=1,
            grid=(4,),
            in_specs=in_specs,
            out_specs=tuple(out_specs),
            scratch_shapes=[pltpu.VMEM((4 * buses, hours), BF16)],
        ),
        out_shape=tuple(out_shape),
        compiler_params=pltpu.CompilerParams(vmem_limit_bytes=48 << 20),
        cost_estimate=pl.CostEstimate(
            flops=8 * hours * lines * buses, bytes_accessed=8 * lines * buses, transcendentals=0
        ),
        name="flow_chunk",
    )(place, *operands)


def swap(x, devices, mask):
    return lax.ppermute(x, "bus", [(i, i ^ mask) for i in range(devices)])


def local(
    ptdf,
    line_limit,
    gen_cost,
    gen_max,
    gen_owner,
    gen_local,
    availability,
    demand,
    dispatch,
    balance_price,
    line_price,
):
    devices = lax.axis_size("bus")
    place = lax.axis_index("bus").astype(jnp.int32).reshape(1)
    buses = demand.shape[0]
    all_buses = buses * devices
    gens, hours = dispatch.shape
    cap = -(-max(2, 3 * gens // devices) // 16) * 16
    staged = devices == 16 and buses % 128 == 0

    outgoing = pack(
        devices,
        cap,
        gen_owner.reshape(1, gens),
        gen_local.reshape(1, gens),
        gen_cost.reshape(1, gens),
        dispatch,
        gen_max.reshape(gens, 1),
        availability,
    )
    recv = lax.all_to_all(outgoing, "bus", split_axis=0, concat_axis=0, tiled=True)
    limit = line_limit.reshape(-1, 1)
    balance_row = balance_price.reshape(1, hours)
    line_half = line_price.astype(BF16)
    held = None
    for iteration in range(ITERS):
        last = iteration == ITERS - 1
        if staged:
            line_t = line_half.T
            prices = []
            for chunk in (3, 2, 1, 0):
                keep, send = shadow_chunk(chunk, place, line_t, ptdf, buses)
                got = swap(send, devices, 1)
                across = (keep[1] + got[1].astype(F32)).astype(BF16)
                crossed = swap(across, devices, 2)
                part = keep[0] + got[0].astype(F32) + crossed.astype(F32)
                if chunk:
                    part = swap(part.astype(BF16), devices, 4 * chunk)
                prices.append(part)
        else:
            shadow = lax.dot_general(ptdf, line_half, (((0,), (0,)), ((), ())), preferred_element_type=F32)
            prices = [lax.psum_scatter(shadow, "bus", scatter_dimension=0, tiled=True).T]
        held, block = update(cap, iteration == 0, last, prices, balance_row, demand, recv, held)
        if last:
            back = lax.all_to_all(held, "bus", split_axis=0, concat_axis=0, tiled=True)
        if staged:
            acc, total = None, balance_row
            for chunk in range(4):
                near = swap(block, devices, 4 * chunk) if chunk else block
                far = swap(near, devices, 2)
                blocks = [near, swap(near, devices, 1), far, swap(far, devices, 1)]
                if chunk < 3:
                    acc, total = flow_chunk(chunk, place, ptdf, blocks, acc, total)
                else:
                    line_price, line_half, total = flow_chunk(
                        chunk, place, ptdf, blocks, acc, total, limit, line_price
                    )
            balance = total
        else:
            every = lax.all_gather(block, "bus", axis=0, tiled=False)
            balance = jnp.sum(every[:, buses:].astype(F32), axis=(0, 1)).reshape(1, hours)
            flow = jnp.dot(ptdf, every[:, :buses].reshape(all_buses, hours), preferred_element_type=F32)
            shifted = line_price + sigma_step * flow
            line_price = shifted - sigma_step * jnp.clip(shifted / sigma_step, -limit, limit)
            line_half = line_price.astype(BF16)
        balance_row = balance_row + sigma_step * balance / all_buses
    dispatch = unpack(devices, cap, gen_owner, back, dispatch, gen_max.reshape(gens, 1), availability)
    return (dispatch, balance_row.reshape(hours), line_price)


def solution(mesh):
    return jax.shard_map(
        local,
        mesh=mesh,
        in_specs=(
            P("bus", None),
            P("bus"),
            P("bus"),
            P("bus"),
            P("bus", None),
            P("bus"),
            P(("cases", "bus"), None),
            P(("cases", "bus"), None),
            P(("cases", "bus"), None),
            P("cases"),
            P(("cases", "bus"), None),
        ),
        out_specs=(P(("cases", "bus"), None), P("cases"), P(("cases", "bus"), None)),
        check_vma=False,
    )
```

time: 594 us -> 270 us (0.45)
  waiting for transfers between devices: 366 us -> 77.9 us
  Pallas kernels: 0 us -> 115 us
  blocking collectives: 101 us -> 0 us
  matrix products: 55.7 us -> 0 us
  starting transfers between devices: 7.96 us -> 59.3 us
  other arithmetic: 31.6 us -> 1.26 us
  between operations: 14.5 us -> 1.22 us
    reduce_scatter x4 -> x0, waiting for transfers between devices: 289 us -> none  [the longest x2 158 us: local(): lax.psum_scatter(full_sums, 'bus', scatter_dimension=0, tiled=True) - demand]
    pallas_call x0 -> x20, Pallas kernels: none -> 115 us  [the longest x8 40 us: flow_chunk(): pl.pallas_call(functools.partial(flow_kernel, start, end), grid_spec=pltp...]
    psum x2 -> x0, blocking collectives: 78.1 us -> none  [local(): balance = lax.psum(jnp.sum(injection, axis=0), 'bus')]
    ppermute x0 -> x52, waiting for transfers between devices: none -> 77.9 us  [swap(): return lax.ppermute(x, 'bus', [(i, i ^ mask) for i in range(devices)])]
    dot_general x4 -> x0, matrix products: 55.7 us -> none  [the longest x2 28.2 us: local(): lax.dot_general(ptdf, line_half, (((0,), (0,)), ((), ())), preferred_elem...]
    all_gather x2 -> x0, waiting for transfers between devices: 54.6 us -> none  [local(): lax.all_gather(injection.astype(jnp.bfloat16), 'bus', axis=0, tiled=True)]
    ppermute x0 -> x52, starting transfers between devices: none -> 45.6 us  [swap(): return lax.ppermute(x, 'bus', [(i, i ^ mask) for i in range(devices)])]
    all_gather x1 -> x0, blocking collectives: 23.2 us -> none  [local(): every_bus = lax.all_gather(global_bus, 'bus', axis=0, tiled=True)]
  transfers between devices with their start and end apart: 8 -> 54, of which waited for: 7 -> 15; matrix products, arithmetic and copies ran while one was open for 1% -> 1% of each run, Pallas kernels for 0% -> 23%
where the time goes in v1:
time: 270 us; the launch traced here: 269 us
  Pallas kernels  115 us (43%)
  waiting for transfers between devices  77.9 us (29%)
  starting transfers between devices  59.3 us (22%)
  local copies, waits for them, and re-layouts  14.9 us (6%)
    ppermute x52, waiting for transfers between devices, swap(): return lax.ppermute(x, 'bus', [(i, i ^ mask) for i in range(devices)])  77.9 us
    ppermute x52, starting transfers between devices, swap(): return lax.ppermute(x, 'bus', [(i, i ^ mask) for i in range(devices)])  45.6 us
    pallas_call x8, Pallas kernels, flow_chunk(): pl.pallas_call(functools.partial(flow_kernel, start, end), grid_spec=pltp...  40 us
    pallas_call x8, Pallas kernels, shadow_chunk(): pl.pallas_call(shadow_kernel, grid_spec=pltpu.PrefetchScalarGridSpec(num_...  35.5 us
    pallas_call x2, Pallas kernels, update(): pl.pallas_call(functools.partial(update_kernel, cap, first, last, len(pri...  29.8 us
    unnamed x54, local copies, waits for them, and re-layouts  12.3 us
    all_to_all x1, starting transfers between devices, local(): lax.all_to_all(outgoing, 'bus', split_axis=0, concat_axis=0, tiled=True)  7.52 us
    all_to_all x1, starting transfers between devices, local(): back = lax.all_to_all(held, 'bus', split_axis=0, concat_axis=0, tiled=True)  6.17 us
  transfers between devices with their start and end apart: 54, of which 15 were waited for; matrix products, arithmetic and copies ran while one was open for 1% of the time, Pallas kernels for 23%

profile of v1, /device:TPU:0, one launch (start us, length us, event | category | flops | bytes accessed | tf_op | source)
XLA Modules:
  0.0 269.3 jit_solution(9358314457921546740)
XLA Ops:
  5.5 4.8 %pack_generators.1 = bf16[16,160,256]{2,1,0:T(8,128)(2,1)S(1)} custom-call(s32[1,768]{1,0:T(1,128)S(1)} %bitcast.64, s32[1,768]{1,0:T(1,128)S(1)} %reshape.77.local_ref, f32[1,768]{1,0:T(1,128)S(1)} %reshape.78.cost_ref, f32[768,128]{1,0:T(8,128)S(1)} %copy-done.4, f32[768,1]{1,0:T(8,128)S(1)} %reshape.83.max_ref, f32[768,128]{1,0:T(8,128)S(1)} %copy-done.6), custom_call_target="tpu_custom_call" | custom-call | flops 905969664 | bytes 3145728 | tf_op jit(solution)/shard_map/pack_generators/pallas_call | solution.py:84
  11.4 7.5 %all-to-all-start = ((bf16[16,160,256]{2,1,0:T(8,128)(2,1)}), bf16[16,160,256]{2,1,0:T(8,128)(2,1)S(1)}, u32[]{:S(2)}, u32[]{:S(2)}) async-start(bf16[16,160,256]{2,1,0:T(8,128)(2,1)} %copy-done.1), calls=%async_computation | async-start | bytes 2621440 | tf_op jit(solution)/shard_map/all_to_all | solution.py:402
  19.1 4.5 %shadow_chunk.10 = (f32[2,128,640]{2,1,0:T(8,128)S(1)}, bf16[2,128,640]{2,1,0:T(8,128)(2,1)S(1)}) custom-call(s32[1]{0:T(128)} %bitcast.place_ref, bf16[128,1280]{1,0:T(8,128)(2,1)S(1)} %bitcast.59, bf16[1280,10240]{1,0:T(8,128)(2,1)} %ptdf_ref.31), custom_call_target="tpu_custom_call" | custom-call | flops 838860800 | bytes 6553600 | tf_op jit(solution)/shard_map/shadow_chunk/pallas_call | solution.py:268
  24.1 4.4 %shadow_chunk.11 = (f32[2,128,640]{2,1,0:T(8,128)S(1)}, bf16[2,128,640]{2,1,0:T(8,128)(2,1)S(1)}) custom-call(s32[1]{0:T(128)} %bitcast.place_ref, bf16[128,1280]{1,0:T(8,128)(2,1)S(1)} %bitcast.60, bf16[1280,10240]{1,0:T(8,128)(2,1)} %ptdf_ref.31), custom_call_target="tpu_custom_call" | custom-call | flops 838860800 | bytes 6553600 | tf_op jit(solution)/shard_map/shadow_chunk/pallas_call | solution.py:268
  28.7 4.4 %shadow_chunk.9 = (f32[2,128,640]{2,1,0:T(8,128)S(1)}, bf16[2,128,640]{2,1,0:T(8,128)(2,1)S(1)}) custom-call(s32[1]{0:T(128)} %bitcast.place_ref, bf16[128,1280]{1,0:T(8,128)(2,1)S(1)} %bitcast.61, bf16[1280,10240]{1,0:T(8,128)(2,1)} %ptdf_ref.31), custom_call_target="tpu_custom_call" | custom-call | flops 838860800 | bytes 6553600 | tf_op jit(solution)/shard_map/shadow_chunk/pallas_call | solution.py:268
  33.6 4.4 %shadow_chunk.8 = (f32[2,128,640]{2,1,0:T(8,128)S(1)}, bf16[2,128,640]{2,1,0:T(8,128)(2,1)S(1)}) custom-call(s32[1]{0:T(128)} %bitcast.place_ref, bf16[128,1280]{1,0:T(8,128)(2,1)S(1)} %bitcast.62, bf16[1280,10240]{1,0:T(8,128)(2,1)} %ptdf_ref.31), custom_call_target="tpu_custom_call" | custom-call | flops 838860800 | bytes 6553600 | tf_op jit(solution)/shard_map/shadow_chunk/pallas_call | solution.py:268
  42.7 6.2 %collective-permute-done.7 = bf16[128,640]{1,0:T(8,128)(2,1)S(1)} collective-permute-done((bf16[128,640]{1,0:T(8,128)(2,1)S(1)}, bf16[128,640]{1,0:T(8,128)(2,1)S(1)}, u32[]{:S(2)}, u32[]{:S(2)}) %collective-permute-start.7) | collective-permute-done | bytes 163872 | tf_op jit(solution)/shard_map/ppermute | solution.py:368
  49.0 6.9 %collective-permute-done.4 = bf16[128,640]{1,0:T(8,128)(2,1)S(1)} collective-permute-done((bf16[128,640]{1,0:T(8,128)(2,1)S(1)}, bf16[128,640]{1,0:T(8,128)(2,1)S(1)}, u32[]{:S(2)}, u32[]{:S(2)}) %collective-permute-start.4) | collective-permute-done | bytes 163872 | tf_op jit(solution)/shard_map/ppermute | solution.py:368
  60.8 9.6 %collective-permute-done.5.refs_1_ = bf16[128,640]{1,0:T(8,128)(2,1)S(1)} collective-permute-done((bf16[128,640]{1,0:T(8,128)(2,1)S(1)}, bf16[128,640]{1,0:T(8,128)(2,1)S(1)}, u32[]{:S(2)}, u32[]{:S(2)}) %collective-permute-start.5) | collective-permute-done | bytes 163872 | tf_op jit(solution)/shard_map/ppermute | solution.py:368
  70.4 14.5 %update_generators.2 = (f32[16,144,128]{2,1,0:T(8,128)S(1)}, bf16[656,128]{1,0:T(8,128)(2,1)S(1)}) custom-call(bf16[128,640]{1,0:T(8,128)(2,1)S(1)} %collective-permute-done.2.refs_0_, bf16[128,640]{1,0:T(8,128)(2,1)S(1)} %collective-permute-done.5.refs_1_, bf16[128,640]{1,0:T(8,128)(2,1)S(1)} %collective-permute-done.8.refs_2_, ...), custom_call_target="tpu_custom_call" | custom-call | flops 1509949440 | bytes 4194304 | tf_op jit(solution)/shard_map/update_generators/pallas_call | solution.py:219
  93.4 3.7 %collective-permute-start.21 = (bf16[656,128]{1,0:T(8,128)(2,1)S(1)}, bf16[656,128]{1,0:T(8,128)(2,1)S(1)}, u32[]{:S(2)}, u32[]{:S(2)}) collective-permute-start(bf16[656,128]{1,0:T(8,128)(2,1)S(1)} %collective-permute-done.19.b0), channel_id=1, source_target_pairs={{0,2},{1,3},{2,0},{3,1},{4,6},{5,7},{6,4},{7,5},{8,10},{9,11},{10,... | collective-permute-start | bytes 503816 | tf_op jit(solution)/shard_map/ppermute | solution.py:368
  97.1 7.7 %collective-permute-done.15.b0 = bf16[656,128]{1,0:T(8,128)(2,1)S(1)} collective-permute-done((bf16[656,128]{1,0:T(8,128)(2,1)S(1)}, bf16[656,128]{1,0:T(8,128)(2,1)S(1)}, u32[]{:S(2)}, u32[]{:S(2)}) %collective-permute-start.15) | collective-permute-done | bytes 167968 | tf_op jit(solution)/shard_map/ppermute | solution.py:368
  107.5 4.4 %collective-permute-done.17.b2 = bf16[656,128]{1,0:T(8,128)(2,1)S(1)} collective-permute-done((bf16[656,128]{1,0:T(8,128)(2,1)S(1)}, bf16[656,128]{1,0:T(8,128)(2,1)S(1)}, u32[]{:S(2)}, u32[]{:S(2)}) %collective-permute-start.17) | collective-permute-done | bytes 167968 | tf_op jit(solution)/shard_map/ppermute | solution.py:368
  113.6 4.8 %flow_chunk.8 = (f32[1280,128]{1,0:T(8,128)S(1)}, f32[1,128]{1,0:T(1,128)S(1)}) custom-call(s32[1]{0:T(128)} %bitcast.place_ref, bf16[1280,10240]{1,0:T(8,128)(2,1)} %ptdf_ref.31, bf16[656,128]{1,0:T(8,128)(2,1)S(1)} %get-tuple-element.48.b0, bf16[656,128]{1,0:T(8,128)(2,1)S(1)} %collective-permute-done.23.b1, ...), custom_call_target="tpu_custom_call" | custom-call | flops 838860800 | bytes 6553600 | tf_op jit(solution)/shard_map/flow_chunk/pallas_call | solution.py:349
  118.5 4.9 %flow_chunk.9 = (f32[1280,128]{1,0:T(8,128)S(1)}, f32[1,128]{1,0:T(1,128)S(1)}) custom-call(s32[1]{0:T(128)} %bitcast.place_ref, bf16[1280,10240]{1,0:T(8,128)(2,1)} %ptdf_ref.31, bf16[656,128]{1,0:T(8,128)(2,1)S(1)} %collective-permute-done.19.b0, bf16[656,128]{1,0:T(8,128)(2,1)S(1)} %collective-permute-done.20.b1, ...), custom_call_target="tpu_custom_call" | custom-call | flops 838860800 | bytes 6553600 | tf_op jit(solution)/shard_map/flow_chunk/pallas_call | solution.py:349
  123.4 4.9 %flow_chunk.10 = (f32[1280,128]{1,0:T(8,128)S(1)}, f32[1,128]{1,0:T(1,128)S(1)}) custom-call(s32[1]{0:T(128)} %bitcast.place_ref, bf16[1280,10240]{1,0:T(8,128)(2,1)} %ptdf_ref.31, bf16[656,128]{1,0:T(8,128)(2,1)S(1)} %collective-permute-done.15.b0, bf16[656,128]{1,0:T(8,128)(2,1)S(1)} %collective-permute-done.16.b1, ...), custom_call_target="tpu_custom_call" | custom-call | flops 838860800 | bytes 6553600 | tf_op jit(solution)/shard_map/flow_chunk/pallas_call | solution.py:349
  128.3 4.9 %flow_chunk.11 = (f32[1280,128]{1,0:T(8,128)S(1)}, bf16[1280,128]{1,0:T(8,128)(2,1)S(1)}, f32[1,128]{1,0:T(1,128)S(1)}) custom-call(s32[1]{0:T(128)} %bitcast.place_ref, bf16[1280,10240]{1,0:T(8,128)(2,1)} %ptdf_ref.31, bf16[656,128]{1,0:T(8,128)(2,1)S(1)} %collective-permute-done.11.b0, bf16[656,128]{1,0:T(8,128)(2,1)S(1)} %collective-permute-done.12.b1, ...), custom_call_target="tpu_custom_call" | custom-call | flops 838860800 | bytes 6553600 | tf_op jit(solution)/shard_map/flow_chunk/pallas_call | solution.py:349
  134.2 4.4 %shadow_chunk.15 = (f32[2,128,640]{2,1,0:T(8,128)S(1)}, bf16[2,128,640]{2,1,0:T(8,128)(2,1)S(1)}) custom-call(s32[1]{0:T(128)} %bitcast.place_ref, bf16[128,1280]{1,0:T(8,128)(2,1)S(1)} %bitcast.55, bf16[1280,10240]{1,0:T(8,128)(2,1)} %ptdf_ref.31), custom_call_target="tpu_custom_call" | custom-call | flops 838860800 | bytes 6553600 | tf_op jit(solution)/shard_map/shadow_chunk/pallas_call | solution.py:268
  138.7 4.4 %shadow_chunk.14 = (f32[2,128,640]{2,1,0:T(8,128)S(1)}, bf16[2,128,640]{2,1,0:T(8,128)(2,1)S(1)}) custom-call(s32[1]{0:T(128)} %bitcast.place_ref, bf16[128,1280]{1,0:T(8,128)(2,1)S(1)} %bitcast.56, bf16[1280,10240]{1,0:T(8,128)(2,1)} %ptdf_ref.31), custom_call_target="tpu_custom_call" | custom-call | flops 838860800 | bytes 6553600 | tf_op jit(solution)/shard_map/shadow_chunk/pallas_call | solution.py:268
  143.7 4.4 %shadow_chunk.13 = (f32[2,128,640]{2,1,0:T(8,128)S(1)}, bf16[2,128,640]{2,1,0:T(8,128)(2,1)S(1)}) custom-call(s32[1]{0:T(128)} %bitcast.place_ref, bf16[128,1280]{1,0:T(8,128)(2,1)S(1)} %bitcast.57, bf16[1280,10240]{1,0:T(8,128)(2,1)} %ptdf_ref.31), custom_call_target="tpu_custom_call" | custom-call | flops 838860800 | bytes 6553600 | tf_op jit(solution)/shard_map/shadow_chunk/pallas_call | solution.py:268
  148.7 4.4 %shadow_chunk.12 = (f32[2,128,640]{2,1,0:T(8,128)S(1)}, bf16[2,128,640]{2,1,0:T(8,128)(2,1)S(1)}) custom-call(s32[1]{0:T(128)} %bitcast.place_ref, bf16[128,1280]{1,0:T(8,128)(2,1)S(1)} %bitcast.58, bf16[1280,10240]{1,0:T(8,128)(2,1)} %ptdf_ref.31), custom_call_target="tpu_custom_call" | custom-call | flops 838860800 | bytes 6553600 | tf_op jit(solution)/shard_map/shadow_chunk/pallas_call | solution.py:268
  157.8 6.1 %collective-permute-done.33 = bf16[128,640]{1,0:T(8,128)(2,1)S(1)} collective-permute-done((bf16[128,640]{1,0:T(8,128)(2,1)S(1)}, bf16[128,640]{1,0:T(8,128)(2,1)S(1)}, u32[]{:S(2)}, u32[]{:S(2)}) %collective-permute-start.33) | collective-permute-done | bytes 163872 | tf_op jit(solution)/shard_map/ppermute | solution.py:368
  173.6 7.9 %collective-permute-done.31.refs_1_ = bf16[128,640]{1,0:T(8,128)(2,1)S(1)} collective-permute-done((bf16[128,640]{1,0:T(8,128)(2,1)S(1)}, bf16[128,640]{1,0:T(8,128)(2,1)S(1)}, u32[]{:S(2)}, u32[]{:S(2)}) %collective-permute-start.31) | collective-permute-done | bytes 163872 | tf_op jit(solution)/shard_map/ppermute | solution.py:368
  181.6 15.3 %update_generators.3 = (bf16[16,144,128]{2,1,0:T(8,128)(2,1)}, bf16[656,128]{1,0:T(8,128)(2,1)S(1)}) custom-call(bf16[128,640]{1,0:T(8,128)(2,1)S(1)} %collective-permute-done.28.refs_0_, bf16[128,640]{1,0:T(8,128)(2,1)S(1)} %collective-permute-done.31.refs_1_, bf16[128,640]{1,0:T(8,128)(2,1)S(1)} %collective-permute-done.34.refs_2_, ...), custom_call_target="tpu_custom_call" | custom-call | flops 1509949440 | bytes 4194304 | tf_op jit(solution)/shard_map/update_generators/pallas_call | solution.py:219
  196.9 6.2 %all-to-all-start.1 = ((bf16[16,144,128]{2,1,0:T(8,128)(2,1)}), bf16[16,144,128]{2,1,0:T(8,128)(2,1)S(1)}, u32[]{:S(2)}, u32[]{:S(2)}) async-start(bf16[16,144,128]{2,1,0:T(8,128)(2,1)} %get-tuple-element.66), calls=%async_computation.1 | async-start | bytes 1179648 | tf_op jit(solution)/shard_map/all_to_all | solution.py:426
  209.4 9.8 %collective-permute-done.45.b0 = bf16[656,128]{1,0:T(8,128)(2,1)S(1)} collective-permute-done((bf16[656,128]{1,0:T(8,128)(2,1)S(1)}, bf16[656,128]{1,0:T(8,128)(2,1)S(1)}, u32[]{:S(2)}, u32[]{:S(2)}) %collective-permute-start.45) | collective-permute-done | bytes 167968 | tf_op jit(solution)/shard_map/ppermute | solution.py:368
  221.4 9.6 %collective-permute-done.41.b0 = bf16[656,128]{1,0:T(8,128)(2,1)S(1)} collective-permute-done((bf16[656,128]{1,0:T(8,128)(2,1)S(1)}, bf16[656,128]{1,0:T(8,128)(2,1)S(1)}, u32[]{:S(2)}, u32[]{:S(2)}) %collective-permute-start.41) | collective-permute-done | bytes 167968 | tf_op jit(solution)/shard_map/ppermute | solution.py:368
  243.6 4.8 %flow_chunk.12 = (f32[1280,128]{1,0:T(8,128)S(1)}, f32[1,128]{1,0:T(1,128)S(1)}) custom-call(s32[1]{0:T(128)} %bitcast.place_ref, bf16[1280,10240]{1,0:T(8,128)(2,1)} %ptdf_ref.31, bf16[656,128]{1,0:T(8,128)(2,1)S(1)} %copy-done.11, bf16[656,128]{1,0:T(8,128)(2,1)S(1)} %copy-done.15, bf16[656,128]{1,0:T(8,128)(2,1)S(1)} %copy-done.13, ...), custom_call_target="tpu_custom_call" | custom-call | flops 838860800 | bytes 6553600 | tf_op jit(solution)/shard_map/flow_chunk/pallas_call | solution.py:349
  248.5 4.9 %flow_chunk.13 = (f32[1280,128]{1,0:T(8,128)S(1)}, f32[1,128]{1,0:T(1,128)S(1)}) custom-call(s32[1]{0:T(128)} %bitcast.place_ref, bf16[1280,10240]{1,0:T(8,128)(2,1)} %ptdf_ref.31, bf16[656,128]{1,0:T(8,128)(2,1)S(1)} %collective-permute-done.45.b0, bf16[656,128]{1,0:T(8,128)(2,1)S(1)} %copy-done.9, bf16[656,128]{1,0:T(8,128)(2,1)S(1)} %collective-permute-done.47.b2, ...), custom_call_target="tpu_custom_call" | custom-call | flops 838860800 | bytes 6553600 | tf_op jit(solution)/shard_map/flow_chunk/pallas_call | solution.py:349
  253.4 5.0 %flow_chunk.14 = (f32[1280,128]{1,0:T(8,128)S(1)}, f32[1,128]{1,0:T(1,128)S(1)}) custom-call(s32[1]{0:T(128)} %bitcast.place_ref, bf16[1280,10240]{1,0:T(8,128)(2,1)} %ptdf_ref.31, bf16[656,128]{1,0:T(8,128)(2,1)S(1)} %collective-permute-done.41.b0, bf16[656,128]{1,0:T(8,128)(2,1)} %collective-permute-done.42.b1, ...), custom_call_target="tpu_custom_call" | custom-call | flops 838860800 | bytes 6553600 | tf_op jit(solution)/shard_map/flow_chunk/pallas_call | solution.py:349
  258.5 5.8 %flow_chunk.15 = (f32[1280,128]{1,0:T(8,128)}, bf16[1280,128]{1,0:T(8,128)(2,1)}, f32[1,128]{1,0:T(1,128)S(1)}) custom-call(s32[1]{0:T(128)} %bitcast.place_ref, bf16[1280,10240]{1,0:T(8,128)(2,1)} %ptdf_ref.31, bf16[656,128]{1,0:T(8,128)(2,1)S(1)} %collective-permute-done.37.b0, bf16[656,128]{1,0:T(8,128)(2,1)S(1)} %collective-permute-done.38.b1, ...), custom_call_target="tpu_custom_call" | custom-call | flops 838860800 | bytes 6553600 | tf_op jit(solution)/shard_map/flow_chunk/pallas_call | solution.py:349
  264.8 4.5 %unpack_dispatch.1 = f32[768,128]{1,0:T(8,128)} custom-call(s32[768,1]{1,0:T(8,128)S(1)} %copy.21.owner_ref, bf16[2304,128]{1,0:T(8,128)(2,1)S(1)} %bitcast.63, f32[768,128]{1,0:T(8,128)S(1)} %copy-done.5, f32[768,1]{1,0:T(8,128)S(1)} %reshape.83.max_ref, f32[768,128]{1,0:T(8,128)S(1)} %copy-done.7), custom_call_target="tpu_custom_call" | custom-call | flops 452984832 | bytes 1048576 | tf_op jit(solution)/shard_map/unpack_dispatch/pallas_call | solution.py:142
  (173 shorter events, 67.9 us)
Async XLA Ops:
  11.4 58.9 %all-to-all-start = ((bf16[16,160,256]{2,1,0:T(8,128)(2,1)}), bf16[16,160,256]{2,1,0:T(8,128)(2,1)S(1)}, u32[]{:S(2)}, u32[]{:S(2)}) async-start(bf16[16,160,256]{2,1,0:T(8,128)(2,1)} %copy-done.1), calls=%async_computation | async-start | bytes 2621440 | tf_op jit(solution)/shard_map/all_to_all | solution.py:402
  23.6 14.6 %collective-permute-start.6 = (bf16[2,128,640]{2,1,0:T(8,128)(2,1)S(1)}, bf16[2,128,640]{2,1,0:T(8,128)(2,1)S(1)}, u32[]{:S(2)}, u32[]{:S(2)}) collective-permute-start(bf16[2,128,640]{2,1,0:T(8,128)(2,1)S(1)} %get-tuple-element.45), channel_id=1, source_target_pairs={{0,1},{1,0},{2,3},{3,2},{4,5},{5,4},{6,7},{7,6},{8,9},{9,8},{10,11... | collective-permute-start | bytes 983048 | tf_op jit(solution)/shard_map/ppermute | solution.py:368
  28.5 11.7 %collective-permute-start.9 = (bf16[2,128,640]{2,1,0:T(8,128)(2,1)S(1)}, bf16[2,128,640]{2,1,0:T(8,128)(2,1)S(1)}, u32[]{:S(2)}, u32[]{:S(2)}) collective-permute-start(bf16[2,128,640]{2,1,0:T(8,128)(2,1)S(1)} %get-tuple-element.47), channel_id=1, source_target_pairs={{0,1},{1,0},{2,3},{3,2},{4,5},{5,4},{6,7},{7,6},{8,9},{9,8},{10,11... | collective-permute-start | bytes 983048 | tf_op jit(solution)/shard_map/ppermute | solution.py:368
  40.3 20.4 %collective-permute-start.10 = (bf16[128,640]{1,0:T(8,128)(2,1)S(1)}, bf16[128,640]{1,0:T(8,128)(2,1)S(1)}, u32[]{:S(2)}, u32[]{:S(2)}) collective-permute-start(bf16[128,640]{1,0:T(8,128)(2,1)S(1)} %fusion.9), channel_id=1, source_target_pairs={{0,2},{1,3},{2,0},{3,1},{4,6},{5,7},{6,4},{7,5},{8,10},{9,11},{10,... | collective-permute-start | bytes 491528 | tf_op jit(solution)/shard_map/ppermute | solution.py:368
  40.5 15.4 %collective-permute-start.4 = (bf16[128,640]{1,0:T(8,128)(2,1)S(1)}, bf16[128,640]{1,0:T(8,128)(2,1)S(1)}, u32[]{:S(2)}, u32[]{:S(2)}) collective-permute-start(bf16[128,640]{1,0:T(8,128)(2,1)S(1)} %fusion.7), channel_id=1, source_target_pairs={{0,2},{1,3},{2,0},{3,1},{4,6},{5,7},{6,4},{7,5},{8,10},{9,11},{10,... | collective-permute-start | bytes 491528 | tf_op jit(solution)/shard_map/ppermute | solution.py:368
  42.5 16.4 %collective-permute-start.1 = (bf16[128,640]{1,0:T(8,128)(2,1)S(1)}, bf16[128,640]{1,0:T(8,128)(2,1)S(1)}, u32[]{:S(2)}, u32[]{:S(2)}) collective-permute-start(bf16[128,640]{1,0:T(8,128)(2,1)S(1)} %fusion.6), channel_id=1, source_target_pairs={{0,2},{1,3},{2,0},{3,1},{4,6},{5,7},{6,4},{7,5},{8,10},{9,11},{10,... | collective-permute-start | bytes 491528 | tf_op jit(solution)/shard_map/ppermute | solution.py:368
  48.9 11.9 %collective-permute-start.8 = (bf16[128,640]{1,0:T(8,128)(2,1)S(1)}, bf16[128,640]{1,0:T(8,128)(2,1)S(1)}, u32[]{:S(2)}, u32[]{:S(2)}) collective-permute-start(bf16[128,640]{1,0:T(8,128)(2,1)S(1)} %fusion.3), channel_id=1, source_target_pairs={{0,4},{1,5},{2,6},{3,7},{4,0},{5,1},{6,2},{7,3},{8,12},{9,13},{10,... | collective-permute-start | bytes 491528 | tf_op jit(solution)/shard_map/ppermute | solution.py:368
  55.9 14.4 %collective-permute-start.5 = (bf16[128,640]{1,0:T(8,128)(2,1)S(1)}, bf16[128,640]{1,0:T(8,128)(2,1)S(1)}, u32[]{:S(2)}, u32[]{:S(2)}) collective-permute-start(bf16[128,640]{1,0:T(8,128)(2,1)S(1)} %fusion.4), channel_id=1, source_target_pairs={{0,8},{1,9},{2,10},{3,11},{4,12},{5,13},{6,14},{7,15},{8,0},{9,1},... | collective-permute-start | bytes 491528 | tf_op jit(solution)/shard_map/ppermute | solution.py:368
  90.1 14.7 %collective-permute-start.15 = (bf16[656,128]{1,0:T(8,128)(2,1)S(1)}, bf16[656,128]{1,0:T(8,128)(2,1)S(1)}, u32[]{:S(2)}, u32[]{:S(2)}) collective-permute-start(bf16[656,128]{1,0:T(8,128)(2,1)S(1)} %get-tuple-element.48.b0), channel_id=1, source_target_pairs={{0,8},{1,9},{2,10},{3,11},{4,12},{5,13},{6,14},{7,15},{8,0},{9,1},... | collective-permute-start | bytes 503816 | tf_op jit(solution)/shard_map/ppermute | solution.py:368
  91.9 13.2 %collective-permute-start.23 = (bf16[656,128]{1,0:T(8,128)(2,1)S(1)}, bf16[656,128]{1,0:T(8,128)(2,1)S(1)}, u32[]{:S(2)}, u32[]{:S(2)}) collective-permute-start(bf16[656,128]{1,0:T(8,128)(2,1)S(1)} %get-tuple-element.48.b0), channel_id=1, source_target_pairs={{0,1},{1,0},{2,3},{3,2},{4,5},{5,4},{6,7},{7,6},{8,9},{9,8},{10,11... | collective-permute-start | bytes 503816 | tf_op jit(solution)/shard_map/ppermute | solution.py:368
  91.9 13.2 %collective-permute-start.11 = (bf16[656,128]{1,0:T(8,128)(2,1)S(1)}, bf16[656,128]{1,0:T(8,128)(2,1)S(1)}, u32[]{:S(2)}, u32[]{:S(2)}) collective-permute-start(bf16[656,128]{1,0:T(8,128)(2,1)S(1)} %get-tuple-element.48.b0), channel_id=1, source_target_pairs={{0,12},{1,13},{2,14},{3,15},{4,8},{5,9},{6,10},{7,11},{8,4},{9,5},... | collective-permute-start | bytes 503816 | tf_op jit(solution)/shard_map/ppermute | solution.py:368
  93.4 13.6 %collective-permute-start.21 = (bf16[656,128]{1,0:T(8,128)(2,1)S(1)}, bf16[656,128]{1,0:T(8,128)(2,1)S(1)}, u32[]{:S(2)}, u32[]{:S(2)}) collective-permute-start(bf16[656,128]{1,0:T(8,128)(2,1)S(1)} %collective-permute-done.19.b0), channel_id=1, source_target_pairs={{0,2},{1,3},{2,0},{3,1},{4,6},{5,7},{6,4},{7,5},{8,10},{9,11},{10,... | collective-permute-start | bytes 503816 | tf_op jit(solution)/shard_map/ppermute | solution.py:368
  107.1 16.3 %collective-permute-start.16 = (bf16[656,128]{1,0:T(8,128)(2,1)S(1)}, bf16[656,128]{1,0:T(8,128)(2,1)S(1)}, u32[]{:S(2)}, u32[]{:S(2)}) collective-permute-start(bf16[656,128]{1,0:T(8,128)(2,1)S(1)} %collective-permute-done.15.b0), channel_id=1, source_target_pairs={{0,1},{1,0},{2,3},{3,2},{4,5},{5,4},{6,7},{7,6},{8,9},{9,8},{10,11... | collective-permute-start | bytes 503816 | tf_op jit(solution)/shard_map/ppermute | solution.py:368
  112.1 16.2 %collective-permute-start.12 = (bf16[656,128]{1,0:T(8,128)(2,1)S(1)}, bf16[656,128]{1,0:T(8,128)(2,1)S(1)}, u32[]{:S(2)}, u32[]{:S(2)}) collective-permute-start(bf16[656,128]{1,0:T(8,128)(2,1)S(1)} %collective-permute-done.11.b0), channel_id=1, source_target_pairs={{0,1},{1,0},{2,3},{3,2},{4,5},{5,4},{6,7},{7,6},{8,9},{9,8},{10,11... | collective-permute-start | bytes 503816 | tf_op jit(solution)/shard_map/ppermute | solution.py:368
  113.6 14.6 %collective-permute-start.14 = (bf16[656,128]{1,0:T(8,128)(2,1)S(1)}, bf16[656,128]{1,0:T(8,128)(2,1)S(1)}, u32[]{:S(2)}, u32[]{:S(2)}) collective-permute-start(bf16[656,128]{1,0:T(8,128)(2,1)S(1)} %collective-permute-done.13.b2), channel_id=1, source_target_pairs={{0,1},{1,0},{2,3},{3,2},{4,5},{5,4},{6,7},{7,6},{8,9},{9,8},{10,11... | collective-permute-start | bytes 503816 | tf_op jit(solution)/shard_map/ppermute | solution.py:368
  153.4 20.2 %collective-permute-start.36 = (bf16[128,640]{1,0:T(8,128)(2,1)S(1)}, bf16[128,640]{1,0:T(8,128)(2,1)S(1)}, u32[]{:S(2)}, u32[]{:S(2)}) collective-permute-start(bf16[128,640]{1,0:T(8,128)(2,1)S(1)} %fusion.13), channel_id=1, source_target_pairs={{0,2},{1,3},{2,0},{3,1},{4,6},{5,7},{6,4},{7,5},{8,10},{9,11},{10,... | collective-permute-start | bytes 491528 | tf_op jit(solution)/shard_map/ppermute | solution.py:368
  155.6 11.8 %collective-permute-start.30 = (bf16[128,640]{1,0:T(8,128)(2,1)S(1)}, bf16[128,640]{1,0:T(8,128)(2,1)S(1)}, u32[]{:S(2)}, u32[]{:S(2)}) collective-permute-start(bf16[128,640]{1,0:T(8,128)(2,1)S(1)} %fusion.11), channel_id=1, source_target_pairs={{0,2},{1,3},{2,0},{3,1},{4,6},{5,7},{6,4},{7,5},{8,10},{9,11},{10,... | collective-permute-start | bytes 491528 | tf_op jit(solution)/shard_map/ppermute | solution.py:368
  156.2 14.4 %collective-permute-start.27 = (bf16[128,640]{1,0:T(8,128)(2,1)S(1)}, bf16[128,640]{1,0:T(8,128)(2,1)S(1)}, u32[]{:S(2)}, u32[]{:S(2)}) collective-permute-start(bf16[128,640]{1,0:T(8,128)(2,1)S(1)} %fusion.10), channel_id=1, source_target_pairs={{0,2},{1,3},{2,0},{3,1},{4,6},{5,7},{6,4},{7,5},{8,10},{9,11},{10,... | collective-permute-start | bytes 491528 | tf_op jit(solution)/shard_map/ppermute | solution.py:368
  167.5 14.0 %collective-permute-start.31 = (bf16[128,640]{1,0:T(8,128)(2,1)S(1)}, bf16[128,640]{1,0:T(8,128)(2,1)S(1)}, u32[]{:S(2)}, u32[]{:S(2)}) collective-permute-start(bf16[128,640]{1,0:T(8,128)(2,1)S(1)} %fusion.1), channel_id=1, source_target_pairs={{0,8},{1,9},{2,10},{3,11},{4,12},{5,13},{6,14},{7,15},{8,0},{9,1},... | collective-permute-start | bytes 491528 | tf_op jit(solution)/shard_map/ppermute | solution.py:368
  196.9 67.9 %all-to-all-start.1 = ((bf16[16,144,128]{2,1,0:T(8,128)(2,1)}), bf16[16,144,128]{2,1,0:T(8,128)(2,1)S(1)}, u32[]{:S(2)}, u32[]{:S(2)}) async-start(bf16[16,144,128]{2,1,0:T(8,128)(2,1)} %get-tuple-element.66), calls=%async_computation.1 | async-start | bytes 1179648 | tf_op jit(solution)/shard_map/all_to_all | solution.py:426
  203.0 16.2 %collective-permute-start.45 = (bf16[656,128]{1,0:T(8,128)(2,1)S(1)}, bf16[656,128]{1,0:T(8,128)(2,1)S(1)}, u32[]{:S(2)}, u32[]{:S(2)}) collective-permute-start(bf16[656,128]{1,0:T(8,128)(2,1)S(1)} %get-tuple-element.67.b0), channel_id=1, source_target_pairs={{0,4},{1,5},{2,6},{3,7},{4,0},{5,1},{6,2},{7,3},{8,12},{9,13},{10,... | collective-permute-start | bytes 503816 | tf_op jit(solution)/shard_map/ppermute | solution.py:368
  205.0 15.7 %collective-permute-start.50 = (bf16[656,128]{1,0:T(8,128)(2,1)S(1)}, bf16[656,128]{1,0:T(8,128)(2,1)S(1)}, u32[]{:S(2)}, u32[]{:S(2)}) collective-permute-start(bf16[656,128]{1,0:T(8,128)(2,1)S(1)} %get-tuple-element.67.b0), channel_id=1, source_target_pairs={{0,2},{1,3},{2,0},{3,1},{4,6},{5,7},{6,4},{7,5},{8,10},{9,11},{10,... | collective-permute-start | bytes 503816 | tf_op jit(solution)/shard_map/ppermute | solution.py:368
  206.5 24.5 %collective-permute-start.41 = (bf16[656,128]{1,0:T(8,128)(2,1)S(1)}, bf16[656,128]{1,0:T(8,128)(2,1)S(1)}, u32[]{:S(2)}, u32[]{:S(2)}) collective-permute-start(bf16[656,128]{1,0:T(8,128)(2,1)S(1)} %get-tuple-element.67.b0), channel_id=1, source_target_pairs={{0,8},{1,9},{2,10},{3,11},{4,12},{5,13},{6,14},{7,15},{8,0},{9,1},... | collective-permute-start | bytes 503816 | tf_op jit(solution)/shard_map/ppermute | solution.py:368
  208.8 23.7 %collective-permute-start.49 = (bf16[656,128]{1,0:T(8,128)(2,1)S(1)}, bf16[656,128]{1,0:T(8,128)(2,1)S(1)}, u32[]{:S(2)}, u32[]{:S(2)}) collective-permute-start(bf16[656,128]{1,0:T(8,128)(2,1)S(1)} %get-tuple-element.67.b0), channel_id=1, source_target_pairs={{0,1},{1,0},{2,3},{3,2},{4,5},{5,4},{6,7},{7,6},{8,9},{9,8},{10,11... | collective-permute-start | bytes 503816 | tf_op jit(solution)/shard_map/ppermute | solution.py:368
  208.8 24.4 %collective-permute-start.37 = (bf16[656,128]{1,0:T(8,128)(2,1)S(1)}, bf16[656,128]{1,0:T(8,128)(2,1)S(1)}, u32[]{:S(2)}, u32[]{:S(2)}) collective-permute-start(bf16[656,128]{1,0:T(8,128)(2,1)S(1)} %get-tuple-element.67.b0), channel_id=1, source_target_pairs={{0,12},{1,13},{2,14},{3,15},{4,8},{5,9},{6,10},{7,11},{8,4},{9,5},... | collective-permute-start | bytes 503816 | tf_op jit(solution)/shard_map/ppermute | solution.py:368
  219.2 14.6 %collective-permute-start.47 = (bf16[656,128]{1,0:T(8,128)(2,1)S(1)}, bf16[656,128]{1,0:T(8,128)(2,1)S(1)}, u32[]{:S(2)}, u32[]{:S(2)}) collective-permute-start(bf16[656,128]{1,0:T(8,128)(2,1)S(1)} %collective-permute-done.45.b0), channel_id=1, source_target_pairs={{0,2},{1,3},{2,0},{3,1},{4,6},{5,7},{6,4},{7,5},{8,10},{9,11},{10,... | collective-permute-start | bytes 503816 | tf_op jit(solution)/shard_map/ppermute | solution.py:368
  220.7 13.3 %collective-permute-start.51 = (bf16[656,128]{1,0:T(8,128)(2,1)S(1)}, bf16[656,128]{1,0:T(8,128)(2,1)S(1)}, u32[]{:S(2)}, u32[]{:S(2)}) collective-permute-start(bf16[656,128]{1,0:T(8,128)(2,1)S(1)} %collective-permute-done.50.b2), channel_id=1, source_target_pairs={{0,1},{1,0},{2,3},{3,2},{4,5},{5,4},{6,7},{7,6},{8,9},{9,8},{10,11... | collective-permute-start | bytes 503816 | tf_op jit(solution)/shard_map/ppermute | solution.py:368
  233.8 14.7 %collective-permute-start.48 = (bf16[656,128]{1,0:T(8,128)(2,1)S(1)}, bf16[656,128]{1,0:T(8,128)(2,1)}, u32[]{:S(2)}, u32[]{:S(2)}) collective-permute-start(bf16[656,128]{1,0:T(8,128)(2,1)S(1)} %collective-permute-done.47.b2), channel_id=1, source_target_pairs={{0,1},{1,0},{2,3},{3,2},{4,5},{5,4},{6,7},{7,6},{8,9},{9,8},{10,11... | collective-permute-start | bytes 503816 | tf_op jit(solution)/shard_map/ppermute | solution.py:368
  234.6 18.8 %collective-permute-start.42 = (bf16[656,128]{1,0:T(8,128)(2,1)S(1)}, bf16[656,128]{1,0:T(8,128)(2,1)}, u32[]{:S(2)}, u32[]{:S(2)}) collective-permute-start(bf16[656,128]{1,0:T(8,128)(2,1)S(1)} %collective-permute-done.41.b0), channel_id=1, source_target_pairs={{0,1},{1,0},{2,3},{3,2},{4,5},{5,4},{6,7},{7,6},{8,9},{9,8},{10,11... | collective-permute-start | bytes 503816 | tf_op jit(solution)/shard_map/ppermute | solution.py:368
  236.5 16.9 %collective-permute-start.44 = (bf16[656,128]{1,0:T(8,128)(2,1)S(1)}, bf16[656,128]{1,0:T(8,128)(2,1)}, u32[]{:S(2)}, u32[]{:S(2)}) collective-permute-start(bf16[656,128]{1,0:T(8,128)(2,1)S(1)} %collective-permute-done.43.b2), channel_id=1, source_target_pairs={{0,1},{1,0},{2,3},{3,2},{4,5},{5,4},{6,7},{7,6},{8,9},{9,8},{10,11... | collective-permute-start | bytes 503816 | tf_op jit(solution)/shard_map/ppermute | solution.py:368
  237.4 21.1 %collective-permute-start.38 = (bf16[656,128]{1,0:T(8,128)(2,1)S(1)}, bf16[656,128]{1,0:T(8,128)(2,1)S(1)}, u32[]{:S(2)}, u32[]{:S(2)}) collective-permute-start(bf16[656,128]{1,0:T(8,128)(2,1)S(1)} %collective-permute-done.37.b0), channel_id=1, source_target_pairs={{0,1},{1,0},{2,3},{3,2},{4,5},{5,4},{6,7},{7,6},{8,9},{9,8},{10,11... | collective-permute-start | bytes 503816 | tf_op jit(solution)/shard_map/ppermute | solution.py:368
  240.0 18.5 %collective-permute-start.40 = (bf16[656,128]{1,0:T(8,128)(2,1)S(1)}, bf16[656,128]{1,0:T(8,128)(2,1)S(1)}, u32[]{:S(2)}, u32[]{:S(2)}) collective-permute-start(bf16[656,128]{1,0:T(8,128)(2,1)S(1)} %collective-permute-done.39.b2), channel_id=1, source_target_pairs={{0,1},{1,0},{2,3},{3,2},{4,5},{5,4},{6,7},{7,6},{8,9},{9,8},{10,11... | collective-permute-start | bytes 503816 | tf_op jit(solution)/shard_map/ppermute | solution.py:368
  (48 other events, 436.1 us)

commit v2 on v1

--- a/solution.py
+++ b/solution.py
@@ -12,6 +12,9 @@
 tau_step = 0.2
 sigma_step = 0.15
 
+GROUP = 4
+LIMIT = 48 << 20
+COST = 3
 META = 16
 F32 = jnp.float32
 BF16 = jnp.bfloat16
@@ -37,31 +40,40 @@
     return hi, mid, low
 
 
-def pack_kernel(cap, owner_ref, local_ref, cost_ref, dispatch_ref, max_ref, avail_ref, out_ref, rank_ref, pay_ref, meta_ref):
+def as_row(ref):
+    return jnp.concatenate([ref[i : i + 1, :] for i in range(ref.shape[0])], axis=1)
+
+
+def pack_kernel(cap, owner_ref, local_ref, cost_ref, dispatch_ref, max_ref, avail_ref, out_ref, slot_ref, pay_ref, meta_ref):
     step = pl.program_id(0)
-    gens = dispatch_ref.shape[0]
-    hours = dispatch_ref.shape[1]
+    gens, hours = dispatch_ref.shape
+    group = out_ref.shape[0]
 
     @pl.when(step == 0)
     def _():
-        owner = owner_ref[...]
-        out_hits = lax.broadcasted_iota(jnp.int32, (rank_ref.shape[0], gens), 0)
-        hits = (out_hits == owner).astype(F32)
+        owner = as_row(owner_ref)
+        hits = (lax.broadcasted_iota(jnp.int32, (slot_ref.shape[0], gens), 0) == owner).astype(F32)
         before = (
             lax.broadcasted_iota(jnp.int32, (gens, gens), 0) < lax.broadcasted_iota(jnp.int32, (gens, gens), 1)
         ).astype(F32)
         count = dot(hits.astype(BF16), before.astype(BF16))
         rank = jnp.sum(count * hits, axis=0, keepdims=True).astype(jnp.int32)
-        rank_ref[...] = jnp.broadcast_to(owner * cap + rank, rank_ref.shape)
+        slot_ref[...] = jnp.broadcast_to(owner * cap + rank, slot_ref.shape)
         pay_ref[:, :hours] = dispatch_ref[...].astype(BF16)
-        pay_ref[:, hours:] = (max_ref[...] * avail_ref[...]).astype(BF16)
-        local = local_ref[...]
-        cost = cost_ref[...]
-        hi, mid, low = thirds(cost)
+        lanes = max_ref.shape[1]
+        eye = (
+            lax.broadcasted_iota(jnp.int32, (lanes, lanes), 0) == lax.broadcasted_iota(jnp.int32, (lanes, lanes), 1)
+        ).astype(F32)
+        for i in range(gens // lanes):
+            rows = slice(i * lanes, (i + 1) * lanes)
+            most = jnp.sum(eye * max_ref[i : i + 1, :], axis=1, keepdims=True)
+            pay_ref[rows, hours:] = (most * avail_ref[rows, :]).astype(BF16)
+        local = as_row(local_ref)
+        hi, mid, low = thirds(as_row(cost_ref))
         row = lax.broadcasted_iota(jnp.int32, (META, gens), 0)
         parts = [
-            (local // 128 + 1).astype(F32),
-            (local % 128).astype(F32),
+            (lax.shift_right_logical(local, 7) + 1).astype(F32),
+            (local & 127).astype(F32),
             hi.astype(F32),
             mid.astype(F32),
             low.astype(F32),
@@ -71,38 +83,49 @@
             meta = jnp.where(row == i, part, meta)
         meta_ref[...] = meta.astype(BF16)
 
-    slot = rank_ref[0:1, :] - step * cap
-    pick = (lax.broadcasted_iota(jnp.int32, (cap, gens), 0) == slot).astype(F32).astype(BF16)
-    out_ref[0, :cap, :] = dot(pick, pay_ref[...]).astype(BF16)
-    out_ref[0, cap:, :] = jnp.zeros((META, 2 * hours), BF16)
-    out_ref[0, cap:, :cap] = dot(meta_ref[...], pick, NT).astype(BF16)
+    slot = slot_ref[0:1, :] - step * (group * cap)
+    place = lax.broadcasted_iota(jnp.int32, (cap, gens), 0)
+    picks = [(place == slot - i * cap).astype(F32).astype(BF16) for i in range(group)]
+    moved = dot(jnp.concatenate(picks, axis=0), pay_ref[...]).astype(BF16)
+    for i in range(group):
+        out_ref[i, :cap, :] = moved[i * cap : (i + 1) * cap]
+        out_ref[i, cap:, :] = jnp.zeros((META, 2 * hours), BF16)
+        out_ref[i, cap:, :cap] = dot(meta_ref[...], picks[i], NT).astype(BF16)
 
 
 def pack(devices, cap, owner, local_bus, cost, dispatch, gen_max, availability):
     gens, hours = dispatch.shape
     full = lambda *shape: pl.BlockSpec(shape, lambda i: (0,) * len(shape))
+    folded = (gens // 128, 128)
     return pl.pallas_call(
         functools.partial(pack_kernel, cap),
-        grid=(devices,),
+        grid=(devices // GROUP,),
         out_shape=jax.ShapeDtypeStruct((devices, cap + META, 2 * hours), BF16),
         in_specs=[
-            full(1, gens),
-            full(1, gens),
-            full(1, gens),
+            full(*folded),
+            full(*folded),
+            full(*folded),
             full(gens, hours),
-            full(gens, 1),
+            full(*folded),
             full(gens, hours),
         ],
-        out_specs=pl.BlockSpec((1, cap + META, 2 * hours), lambda i: (i, 0, 0)),
+        out_specs=pl.BlockSpec((GROUP, cap + META, 2 * hours), lambda i: (i, 0, 0)),
         scratch_shapes=[
             pltpu.VMEM((devices, gens), jnp.int32),
             pltpu.VMEM((gens, 2 * hours), BF16),
             pltpu.VMEM((META, gens), BF16),
         ],
-        compiler_params=pltpu.CompilerParams(vmem_limit_bytes=48 << 20),
+        compiler_params=pltpu.CompilerParams(vmem_limit_bytes=LIMIT),
         cost_estimate=pl.CostEstimate(flops=4 * devices * cap * gens * hours, bytes_accessed=3 << 20, transcendentals=0),
         name="pack_generators",
-    )(owner, local_bus, cost, dispatch, gen_max, availability)
+    )(
+        owner.reshape(folded),
+        local_bus.reshape(folded),
+        cost.reshape(folded),
+        dispatch,
+        gen_max.reshape(folded),
+        availability,
+    )
 
 
 def unpack_kernel(devices, cap, block, owner_ref, back_ref, dispatch_ref, max_ref, avail_ref, out_ref):
@@ -142,7 +165,7 @@
     return pl.pallas_call(
         functools.partial(unpack_kernel, devices, cap, block),
         out_shape=jax.ShapeDtypeStruct((gens, hours), F32),
-        compiler_params=pltpu.CompilerParams(vmem_limit_bytes=48 << 20),
+        compiler_params=pltpu.CompilerParams(vmem_limit_bytes=LIMIT),
         cost_estimate=pl.CostEstimate(flops=2 * slots * gens * hours, bytes_accessed=1 << 20, transcendentals=0),
         name="unpack_dispatch",
     )(owner_column, back.reshape(slots, hours), dispatch, gen_max, availability)
@@ -165,35 +188,44 @@
         acc_ref[...] = jnp.zeros(acc_ref.shape, F32)
         extra_ref[...] = jnp.zeros(extra_ref.shape, BF16)
 
-    meta = recv_ref[0, cap:, :]
-    meta32 = meta[:, : extra_ref.shape[0]].astype(F32)
-    bus_row = ((meta32[0:1] - 1.0) * 128.0 + meta32[1:2]).astype(jnp.int32)
+    group = recv_ref.shape[0]
+    pad = extra_ref.shape[0] // group
+    wide = 2 * hours
+    meta = recv_ref[:, cap:, :].reshape(group * META, wide)
     eye = (
-        lax.broadcasted_iota(jnp.int32, (cap, 2 * hours), 0) == lax.broadcasted_iota(jnp.int32, (cap, 2 * hours), 1)
+        lax.broadcasted_iota(jnp.int32, (cap, wide), 0) == lax.broadcasted_iota(jnp.int32, (cap, wide), 1)
     ).astype(F32)
     columns = dot(eye.astype(BF16), meta, NT)
-    bus_column = ((columns[:, 0:1] - 1.0) * 128.0 + columns[:, 1:2]).astype(jnp.int32)
-    cost = (columns[:, 2:3] + columns[:, 3:4]) + columns[:, 4:5]
-    at_bus = (lax.broadcasted_iota(jnp.int32, (cap, buses), 1) == bus_column).astype(F32).astype(BF16)
-    both = dot(at_bus, shadow_ref[...], NT)
-    price = both[:, :hours] + both[:, hours:] + balance_ref[...]
-    if first:
-        dispatch = recv_ref[0, :cap, :hours].astype(F32)
-    else:
-        dispatch = prev_ref[0]
-    upper = recv_ref[0, :cap, hours:].astype(F32)
-    updated = jnp.minimum(jnp.maximum(dispatch - tau_step * (cost + price), 0.0), upper)
-    if last:
-        upd_ref[0] = (updated - recv_ref[0, :cap, :hours].astype(F32)).astype(BF16)
-    else:
-        upd_ref[0] = updated
-    extra = 2.0 * updated - dispatch
-    hi, lo = halves(extra)
-    extra_ref[:cap, :hours] = hi
-    extra_ref[:cap, hours:] = lo
-    at_row = lax.broadcasted_iota(jnp.int32, (buses, extra_ref.shape[0]), 0)
-    to_bus = (at_row == bus_row).astype(F32).astype(BF16)
-    acc_ref[...] += dot(to_bus, extra_ref[...])
+    buses_at = lax.broadcasted_iota(jnp.int32, (cap, buses), 1)
+    picks = []
+    for i in range(group):
+        at = i * META
+        bus_column = ((columns[:, at : at + 1] - 1.0) * 128.0 + columns[:, at + 1 : at + 2]).astype(jnp.int32)
+        picks.append((buses_at == bus_column).astype(F32).astype(BF16))
+    both = dot(jnp.concatenate(picks, axis=0), shadow_ref[...], NT)
+    for i in range(group):
+        at = i * META
+        cost = (columns[:, at + 2 : at + 3] + columns[:, at + 3 : at + 4]) + columns[:, at + 4 : at + 5]
+        rows = slice(i * cap, (i + 1) * cap)
+        price = both[rows, :hours] + both[rows, hours:] + balance_ref[...]
+        sent = recv_ref[i, :cap, :hours].astype(F32)
+        dispatch = sent if first else prev_ref[i]
+        upper = recv_ref[i, :cap, hours:].astype(F32)
+        updated = jnp.minimum(jnp.maximum(dispatch - tau_step * (cost + price), 0.0), upper)
+        if last:
+            upd_ref[i] = (updated - sent).astype(BF16)
+        else:
+            upd_ref[i] = updated
+        hi, lo = halves(2.0 * updated - dispatch)
+        extra_ref[i * pad : i * pad + cap, :hours] = hi
+        extra_ref[i * pad : i * pad + cap, hours:] = lo
+    at_row = lax.broadcasted_iota(jnp.int32, (buses, pad), 0)
+    picks = []
+    for i in range(group):
+        row = recv_ref[i, cap:, :pad].astype(F32)
+        bus_row = ((row[0:1] - 1.0) * 128.0 + row[1:2]).astype(jnp.int32)
+        picks.append((at_row == bus_row).astype(F32).astype(BF16))
+    acc_ref[...] += dot(jnp.concatenate(picks, axis=1), extra_ref[...])
 
     @pl.when(step == pl.num_programs(0) - 1)
     def _():
@@ -211,14 +243,14 @@
     devices = recv.shape[0]
     buses, hours = demand.shape
     full = lambda *shape: pl.BlockSpec(shape, lambda i: (0,) * len(shape))
-    slots = lambda width: pl.BlockSpec((1, cap, width), lambda i: (i, 0, 0))
+    slots = lambda width: pl.BlockSpec((GROUP, cap, width), lambda i: (i, 0, 0))
     if first:
         previous, prev_spec = balance_price, full(1, hours)
     else:
         prev_spec = slots(hours)
     return pl.pallas_call(
         functools.partial(update_kernel, cap, first, last, len(prices)),
-        grid=(devices,),
+        grid=(devices // GROUP,),
         out_shape=(
             jax.ShapeDtypeStruct((devices, cap, hours), BF16 if last else F32),
             jax.ShapeDtypeStruct((buses + META, hours), BF16),
@@ -227,16 +259,16 @@
         + [
             full(1, hours),
             full(buses, hours),
-            pl.BlockSpec((1, cap + META, 2 * hours), lambda i: (i, 0, 0)),
+            pl.BlockSpec((GROUP, cap + META, 2 * hours), lambda i: (i, 0, 0)),
             prev_spec,
         ],
         out_specs=(slots(hours), full(buses + META, hours)),
         scratch_shapes=[
             pltpu.VMEM((2 * hours, buses), BF16),
             pltpu.VMEM((buses, 2 * hours), F32),
-            pltpu.VMEM((-(-cap // 128) * 128, 2 * hours), BF16),
+            pltpu.VMEM((GROUP * (-(-cap // 128) * 128), 2 * hours), BF16),
         ],
-        compiler_params=pltpu.CompilerParams(vmem_limit_bytes=48 << 20),
+        compiler_params=pltpu.CompilerParams(vmem_limit_bytes=LIMIT),
         cost_estimate=pl.CostEstimate(flops=8 * devices * cap * buses * hours, bytes_accessed=4 << 20, transcendentals=0),
         name="update_generators",
     )(*prices, balance_price, demand, recv, previous)
@@ -283,9 +315,9 @@
             jax.ShapeDtypeStruct((2, hours, buses), F32),
             jax.ShapeDtypeStruct((2, hours, buses), BF16),
         ),
-        compiler_params=pltpu.CompilerParams(vmem_limit_bytes=48 << 20),
+        compiler_params=pltpu.CompilerParams(vmem_limit_bytes=LIMIT),
         cost_estimate=pl.CostEstimate(
-            flops=8 * hours * lines * buses, bytes_accessed=8 * lines * buses, transcendentals=0
+            flops=COST * 8 * hours * lines * buses, bytes_accessed=8 * lines * buses, transcendentals=0
         ),
         name="shadow_chunk",
     )(place, line_t, ptdf)
@@ -309,17 +341,27 @@
             total = total + jnp.sum(tail, axis=0, keepdims=True)
         sum_out[...] = total
 
-    flow = dot(ptdf_ref[...], inj_ref[...])
-    if not start:
-        flow = flow + acc_ref[...]
+    depth = ptdf_ref.shape[1]
+    rows = pl.ds(pl.multiple_of(step * depth, depth), depth)
+    part = dot(ptdf_ref[...], inj_ref[rows, :])
+
+    @pl.when(step == 0)
+    def _():
+        out_ref[...] = part if start else acc_ref[...] + part
+
+    @pl.when(step > 0)
+    def _():
+        out_ref[...] += part
+
     if end:
-        shifted = line_ref[...] + sigma_step * flow
-        limit = limit_ref[...]
-        line = shifted - sigma_step * jnp.minimum(jnp.maximum(shifted / sigma_step, -limit), limit)
-        out_ref[...] = line
-        half_ref[...] = line.astype(BF16)
-    else:
-        out_ref[...] = flow
+
+        @pl.when(step == pl.num_programs(0) - 1)
+        def _():
+            shifted = line_ref[...] + sigma_step * out_ref[...]
+            limit = limit_ref[...]
+            line = shifted - sigma_step * jnp.minimum(jnp.maximum(shifted / sigma_step, -limit), limit)
+            out_ref[...] = line
+            half_ref[...] = line.astype(BF16)
 
 
 def flow_chunk(chunk, place, ptdf, blocks, acc, total, limit=None, line=None):
@@ -327,38 +369,38 @@
     rows, hours = blocks[0].shape
     buses = rows - META
     start, end = acc is None, limit is not None
-    tile = lines // 4
-    tiled = lambda width: pl.BlockSpec((tile, width), lambda i, place: (i, 0))
+    steps = 5
+    depth = 4 * buses // steps
     full = lambda *shape: pl.BlockSpec(shape, lambda i, place: (0,) * len(shape))
     if start:
         acc, acc_spec = total, full(1, hours)
     else:
-        acc_spec = tiled(hours)
+        acc_spec = full(lines, hours)
     operands = [ptdf, *blocks, acc, total]
-    in_specs = [pl.BlockSpec((tile, 4 * buses), lambda i, place: (i, (place[0] >> 2) ^ chunk))]
+    in_specs = [pl.BlockSpec((lines, depth), lambda i, place: (0, ((place[0] >> 2) ^ chunk) * steps + i))]
     in_specs += [full(rows, hours)] * 4 + [acc_spec, full(1, hours)]
     out_shape = [jax.ShapeDtypeStruct((lines, hours), F32)]
-    out_specs = [tiled(hours)]
+    out_specs = [full(lines, hours)]
     if end:
         operands += [limit, line]
-        in_specs += [tiled(1), tiled(hours)]
+        in_specs += [full(lines, 1), full(lines, hours)]
         out_shape += [jax.ShapeDtypeStruct((lines, hours), BF16)]
-        out_specs += [tiled(hours)]
+        out_specs += [full(lines, hours)]
     out_shape += [jax.ShapeDtypeStruct((1, hours), F32)]
     out_specs += [full(1, hours)]
     return pl.pallas_call(
         functools.partial(flow_kernel, start, end),
         grid_spec=pltpu.PrefetchScalarGridSpec(
             num_scalar_prefetch=1,
-            grid=(4,),
+            grid=(steps,),
             in_specs=in_specs,
             out_specs=tuple(out_specs),
             scratch_shapes=[pltpu.VMEM((4 * buses, hours), BF16)],
         ),
         out_shape=tuple(out_shape),
-        compiler_params=pltpu.CompilerParams(vmem_limit_bytes=48 << 20),
+        compiler_params=pltpu.CompilerParams(vmem_limit_bytes=LIMIT),
         cost_estimate=pl.CostEstimate(
-            flops=8 * hours * lines * buses, bytes_accessed=8 * lines * buses, transcendentals=0
+            flops=COST * 8 * hours * lines * buses, bytes_accessed=8 * lines * buses, transcendentals=0
         ),
         name="flow_chunk",
     )(place, *operands)
@@ -392,52 +434,101 @@
     outgoing = pack(
         devices,
         cap,
-        gen_owner.reshape(1, gens),
-        gen_local.reshape(1, gens),
-        gen_cost.reshape(1, gens),
+        gen_owner,
+        gen_local,
+        gen_cost,
         dispatch,
-        gen_max.reshape(gens, 1),
+        gen_max,
         availability,
     )
-    recv = lax.all_to_all(outgoing, "bus", split_axis=0, concat_axis=0, tiled=True)
     limit = line_limit.reshape(-1, 1)
     balance_row = balance_price.reshape(1, hours)
     line_half = line_price.astype(BF16)
+    if staged:
+        line_half, outgoing = lax.optimization_barrier((line_half, outgoing))
+    recv = lax.all_to_all(outgoing, "bus", split_axis=0, concat_axis=0, tiled=True)
     held = None
     for iteration in range(ITERS):
         last = iteration == ITERS - 1
         if staged:
             line_t = line_half.T
-            prices = []
-            for chunk in (3, 2, 1, 0):
-                keep, send = shadow_chunk(chunk, place, line_t, ptdf, buses)
-                got = swap(send, devices, 1)
-                across = (keep[1] + got[1].astype(F32)).astype(BF16)
-                crossed = swap(across, devices, 2)
-                part = keep[0] + got[0].astype(F32) + crossed.astype(F32)
+            keeps, gots, crossed, parts = {}, {}, {}, {}
+
+            def across(chunk):
+                both = (keeps[chunk][1] + gots[chunk][1].astype(F32)).astype(BF16)
+                crossed[chunk] = swap(both, devices, 2)
+                return both
+
+            def settle(chunk):
+                part = keeps[chunk][0] + gots[chunk][0].astype(F32) + crossed[chunk].astype(F32)
+                if chunk == 2:
+                    part = part + parts[3].astype(F32)
                 if chunk:
-                    part = swap(part.astype(BF16), devices, 4 * chunk)
-                prices.append(part)
+                    part = part.astype(BF16)
+                    parts[chunk] = swap(part, devices, 8 if chunk == 2 else 4)
+                else:
+                    parts[chunk] = part
+                return part
+
+            def product(chunk, line_t):
+                keeps[chunk], send = shadow_chunk(chunk, place, line_t, ptdf, buses)
+                gots[chunk] = swap(send, devices, 1)
+
+            product(3, line_t)
+            product(2, line_t)
+            line_t, _ = lax.optimization_barrier((line_t, across(3)))
+            product(1, line_t)
+            line_t, _, _ = lax.optimization_barrier((line_t, across(2), settle(3)))
+            product(0, line_t)
+            across(1)
+            settle(2)
+            across(0)
+            settle(1)
+            settle(0)
+            prices = [parts[0], parts[1], parts[2]]
         else:
             shadow = lax.dot_general(ptdf, line_half, (((0,), (0,)), ((), ())), preferred_element_type=F32)
             prices = [lax.psum_scatter(shadow, "bus", scatter_dimension=0, tiled=True).T]
         held, block = update(cap, iteration == 0, last, prices, balance_row, demand, recv, held)
-        if last:
-            back = lax.all_to_all(held, "bus", split_axis=0, concat_axis=0, tiled=True)
         if staged:
-            acc, total = None, balance_row
-            for chunk in range(4):
-                near = swap(block, devices, 4 * chunk) if chunk else block
-                far = swap(near, devices, 2)
-                blocks = [near, swap(near, devices, 1), far, swap(far, devices, 1)]
-                if chunk < 3:
-                    acc, total = flow_chunk(chunk, place, ptdf, blocks, acc, total)
-                else:
-                    line_price, line_half, total = flow_chunk(
-                        chunk, place, ptdf, blocks, acc, total, limit, line_price
-                    )
+            near, far, cross, far_cross = {0: block}, {}, {}, {}
+
+            def spread(chunk):
+                far[chunk] = swap(near[chunk], devices, 2)
+                cross[chunk] = swap(near[chunk], devices, 1)
+
+            def settle_far(chunk):
+                far_cross[chunk] = swap(far[chunk], devices, 1)
+
+            def blocks(chunk):
+                return [near[chunk], cross[chunk], far[chunk], far_cross[chunk]]
+
+            near[2] = swap(block, devices, 8)
+            near[1] = swap(block, devices, 4)
+            spread(0)
+            near[3] = swap(near[2], devices, 4)
+            spread(1)
+            spread(2)
+            settle_far(0)
+            near[1], near[2], row = lax.optimization_barrier((near[1], near[2], balance_row))
+            acc, total = flow_chunk(0, place, ptdf, blocks(0), None, row)
+            near[3], acc = lax.optimization_barrier((near[3], acc))
+            spread(3)
+            if last:
+                held, _ = lax.optimization_barrier((held, near[3]))
+                back = lax.all_to_all(held, "bus", split_axis=0, concat_axis=0, tiled=True)
+            settle_far(1)
+            acc, total = flow_chunk(1, place, ptdf, blocks(1), acc, total)
+            settle_far(2)
+            acc, total = flow_chunk(2, place, ptdf, blocks(2), acc, total)
+            settle_far(3)
+            line_price, line_half, total = flow_chunk(
+                3, place, ptdf, blocks(3), acc, total, limit, line_price
+            )
             balance = total
         else:
+            if last:
+                back = lax.all_to_all(held, "bus", split_axis=0, concat_axis=0, tiled=True)
             every = lax.all_gather(block, "bus", axis=0, tiled=False)
             balance = jnp.sum(every[:, buses:].astype(F32), axis=(0, 1)).reshape(1, hours)
             flow = jnp.dot(ptdf, every[:, :buses].reshape(all_buses, hours), preferred_element_type=F32)

time: 270 us -> 221 us (0.82)
  waiting for transfers between devices: 77.9 us -> 55.5 us
  Pallas kernels: 115 us -> 104 us
  starting transfers between devices: 59.3 us -> 48.7 us
  local copies, waits for them, and re-layouts: 14.9 us -> 7.94 us
    ppermute x52, waiting for transfers between devices: 77.9 us -> 55.5 us  [swap(): return lax.ppermute(x, 'bus', [(i, i ^ mask) for i in range(devices)])]
    pallas_call x2, Pallas kernels: 29.8 us -> 12.7 us  [update(): pl.pallas_call(functools.partial(update_kernel, cap, first, last, len(pri...]
    pallas_call x8, Pallas kernels: 40 us -> 48.2 us  [flow_chunk(): pl.pallas_call(functools.partial(flow_kernel, start, end), grid_spec=pltp...]
    ppermute x52, starting transfers between devices: 45.6 us -> 38 us  [swap(): return lax.ppermute(x, 'bus', [(i, i ^ mask) for i in range(devices)])]
    unnamed x54 -> x42, local copies, waits for them, and re-layouts: 12.3 us -> 7.38 us
  transfers between devices with their start and end apart: 54 -> 54, of which waited for: 15 -> 18; matrix products, arithmetic and copies ran while one was open for 1% -> 1% of each run, Pallas kernels for 23% -> 31%
where the time goes in v2:
time: 221 us; the launch traced here: 220 us
  Pallas kernels  104 us (47%)
  waiting for transfers between devices  55.5 us (25%)
  starting transfers between devices  48.7 us (22%)
  local copies, waits for them, and re-layouts  7.94 us (4%)
    ppermute x52, waiting for transfers between devices, swap(): return lax.ppermute(x, 'bus', [(i, i ^ mask) for i in range(devices)])  55.5 us
    pallas_call x8, Pallas kernels, flow_chunk(): pl.pallas_call(functools.partial(flow_kernel, start, end), grid_spec=pltp...  48.2 us
    ppermute x52, starting transfers between devices, swap(): return lax.ppermute(x, 'bus', [(i, i ^ mask) for i in range(devices)])  38 us
    pallas_call x8, Pallas kernels, shadow_chunk(): pl.pallas_call(shadow_kernel, grid_spec=pltpu.PrefetchScalarGridSpec(num_...  35.5 us
    pallas_call x2, Pallas kernels, update(): pl.pallas_call(functools.partial(update_kernel, cap, first, last, len(pri...  12.7 us
    unnamed x42, local copies, waits for them, and re-layouts  7.38 us
    all_to_all x1, starting transfers between devices, local(): lax.all_to_all(outgoing, 'bus', split_axis=0, concat_axis=0, tiled=True)  7.06 us
    pallas_call x1, Pallas kernels, unpack(): pl.pallas_call(functools.partial(unpack_kernel, devices, cap, block), out...  4.49 us
  transfers between devices with their start and end apart: 54, of which 18 were waited for; matrix products, arithmetic and copies ran while one was open for 1% of the time, Pallas kernels for 31%

profile of v2, /device:TPU:0, one launch (start us, length us, event | category | flops | bytes accessed | tf_op | source)
XLA Modules:
  0.0 219.8 jit_solution(5323269782912700598)
XLA Ops:
  6.7 3.6 %pack_generators.1 = bf16[16,160,256]{2,1,0:T(8,128)(2,1)} custom-call(s32[6,128]{1,0:T(8,128)S(1)} %bitcast.70, s32[6,128]{1,0:T(8,128)S(1)} %bitcast.75, f32[6,128]{1,0:T(8,128)S(1)} %bitcast.76, f32[768,128]{1,0:T(8,128)S(1)} %copy-done.4, f32[6,128]{1,0:T(8,128)S(1)} %bitcast.69, f32[768,128]{1,0:T(8,128)S(1)} %copy-done.6), custom_call_target="tpu_custom_call" | custom-call | flops 905969664 | bytes 3145728 | tf_op jit(solution)/shard_map/pack_generators/pallas_call | solution.py:100
  10.2 4.4 %shadow_chunk.8 = (f32[2,128,640]{2,1,0:T(8,128)S(1)}, bf16[2,128,640]{2,1,0:T(8,128)(2,1)S(1)}) custom-call(s32[1]{0:T(128)} %bitcast.place_ref, bf16[128,1280]{1,0:T(8,128)(2,1)S(1)} %bitcast.64, bf16[1280,10240]{1,0:T(8,128)(2,1)} %ptdf_ref.31), custom_call_target="tpu_custom_call" | custom-call | flops 2516582400 | bytes 6553600 | tf_op jit(solution)/shard_map/shadow_chunk/pallas_call | solution.py:300
  15.2 7.1 %all-to-all-start = ((bf16[16,160,256]{2,1,0:T(8,128)(2,1)}), bf16[16,160,256]{2,1,0:T(8,128)(2,1)S(1)}, u32[]{:S(2)}, u32[]{:S(2)}) async-start(bf16[16,160,256]{2,1,0:T(8,128)(2,1)} %pack_generators.1), calls=%async_computation | async-start | bytes 2621440 | tf_op jit(solution)/shard_map/all_to_all | solution.py:449
  22.2 4.4 %shadow_chunk.9 = (f32[2,128,640]{2,1,0:T(8,128)S(1)}, bf16[2,128,640]{2,1,0:T(8,128)(2,1)S(1)}) custom-call(s32[1]{0:T(128)} %bitcast.place_ref, bf16[128,1280]{1,0:T(8,128)(2,1)S(1)} %bitcast.65, bf16[1280,10240]{1,0:T(8,128)(2,1)} %ptdf_ref.31), custom_call_target="tpu_custom_call" | custom-call | flops 2516582400 | bytes 6553600 | tf_op jit(solution)/shard_map/shadow_chunk/pallas_call | solution.py:300
  28.9 4.4 %shadow_chunk.11 = (f32[2,128,640]{2,1,0:T(8,128)S(1)}, bf16[2,128,640]{2,1,0:T(8,128)(2,1)S(1)}) custom-call(s32[1]{0:T(128)} %bitcast.place_ref, bf16[128,1280]{1,0:T(8,128)(2,1)S(1)} %bitcast.66, bf16[1280,10240]{1,0:T(8,128)(2,1)} %ptdf_ref.31), custom_call_target="tpu_custom_call" | custom-call | flops 2516582400 | bytes 6553600 | tf_op jit(solution)/shard_map/shadow_chunk/pallas_call | solution.py:300
  33.9 5.8 %collective-permute-done.2 = bf16[128,640]{1,0:T(8,128)(2,1)S(1)} collective-permute-done((bf16[128,640]{1,0:T(8,128)(2,1)S(1)}, bf16[128,640]{1,0:T(8,128)(2,1)S(1)}, u32[]{:S(2)}, u32[]{:S(2)}) %collective-permute-start.2) | collective-permute-done | bytes 163872 | tf_op jit(solution)/shard_map/ppermute | solution.py:410
  39.9 4.4 %shadow_chunk.10 = (f32[2,128,640]{2,1,0:T(8,128)S(1)}, bf16[2,128,640]{2,1,0:T(8,128)(2,1)S(1)}) custom-call(s32[1]{0:T(128)} %bitcast.place_ref, bf16[128,1280]{1,0:T(8,128)(2,1)S(1)} %bitcast.67, bf16[1280,10240]{1,0:T(8,128)(2,1)} %ptdf_ref.31), custom_call_target="tpu_custom_call" | custom-call | flops 2516582400 | bytes 6553600 | tf_op jit(solution)/shard_map/shadow_chunk/pallas_call | solution.py:300
  44.8 3.3 %collective-permute-done.9 = bf16[128,640]{1,0:T(8,128)(2,1)S(1)} collective-permute-done((bf16[128,640]{1,0:T(8,128)(2,1)S(1)}, bf16[128,640]{1,0:T(8,128)(2,1)S(1)}, u32[]{:S(2)}, u32[]{:S(2)}) %collective-permute-start.9) | collective-permute-done | bytes 163872 | tf_op jit(solution)/shard_map/ppermute | solution.py:410
  48.2 4.4 %collective-permute-start.10 = (bf16[128,640]{1,0:T(8,128)(2,1)S(1)}, bf16[128,640]{1,0:T(8,128)(2,1)S(1)}, u32[]{:S(2)}, u32[]{:S(2)}) collective-permute-start(bf16[128,640]{1,0:T(8,128)(2,1)S(1)} %fusion.5), channel_id=1, source_target_pairs={{0,8},{1,9},{2,10},{3,11},{4,12},{5,13},{6,14},{7,15},{8,0},{9,1},... | collective-permute-start | bytes 491528 | tf_op jit(solution)/shard_map/ppermute | solution.py:410
  58.2 3.3 %collective-permute-done.10.refs_2_ = bf16[128,640]{1,0:T(8,128)(2,1)S(1)} collective-permute-done((bf16[128,640]{1,0:T(8,128)(2,1)S(1)}, bf16[128,640]{1,0:T(8,128)(2,1)S(1)}, u32[]{:S(2)}, u32[]{:S(2)}) %collective-permute-start.10) | collective-permute-done | bytes 163872 | tf_op jit(solution)/shard_map/ppermute | solution.py:410
  63.8 6.3 %update_generators.2 = (f32[16,144,128]{2,1,0:T(8,128)S(1)}, bf16[656,128]{1,0:T(8,128)(2,1)S(1)}) custom-call(f32[128,640]{1,0:T(8,128)S(1)} %bitcast_add_fusion.6.refs_0_, bf16[128,640]{1,0:T(8,128)(2,1)S(1)} %collective-permute-done.7.refs_1_, bf16[128,640]{1,0:T(8,128)(2,1)S(1)} %collective-permute-done.10.refs_2_, f32[1,128]{1,0:T(1,128)S(1)} %bitcast.71, ...), custom_call_target="tpu_custom_call" | custom-call | flops 1509949440 | bytes 4194304 | tf_op jit(solution)/shard_map/update_generators/pallas_call | solution.py:251
  76.6 3.9 %collective-permute-done.11.b0 = bf16[656,128]{1,0:T(8,128)(2,1)S(1)} collective-permute-done((bf16[656,128]{1,0:T(8,128)(2,1)S(1)}, bf16[656,128]{1,0:T(8,128)(2,1)S(1)}, u32[]{:S(2)}, u32[]{:S(2)}) %collective-permute-start.11) | collective-permute-done | bytes 167968 | tf_op jit(solution)/shard_map/ppermute | solution.py:410
  82.7 5.7 %flow_chunk.8 = (f32[1280,128]{1,0:T(8,128)S(1)}, f32[1,128]{1,0:T(1,128)S(1)}) custom-call(s32[1]{0:T(128)} %bitcast.place_ref, bf16[1280,10240]{1,0:T(8,128)(2,1)} %ptdf_ref.31, bf16[656,128]{1,0:T(8,128)(2,1)S(1)} %get-tuple-element.69.b0, bf16[656,128]{1,0:T(8,128)(2,1)S(1)} %collective-permute-done.13.b1, ...), custom_call_target="tpu_custom_call" | custom-call | flops 2516582400 | bytes 6553600 | tf_op jit(solution)/shard_map/flow_chunk/pallas_call | solution.py:391
  91.3 3.6 %collective-permute-done.18.b2 = bf16[656,128]{1,0:T(8,128)(2,1)S(1)} collective-permute-done((bf16[656,128]{1,0:T(8,128)(2,1)S(1)}, bf16[656,128]{1,0:T(8,128)(2,1)S(1)}, u32[]{:S(2)}, u32[]{:S(2)}) %collective-permute-start.18) | collective-permute-done | bytes 167968 | tf_op jit(solution)/shard_map/ppermute | solution.py:410
  94.9 5.8 %flow_chunk.9 = (f32[1280,128]{1,0:T(8,128)S(1)}, f32[1,128]{1,0:T(1,128)S(1)}) custom-call(s32[1]{0:T(128)} %bitcast.place_ref, bf16[1280,10240]{1,0:T(8,128)(2,1)} %ptdf_ref.31, bf16[656,128]{1,0:T(8,128)(2,1)S(1)} %collective-permute-done.16.b0, bf16[656,128]{1,0:T(8,128)(2,1)S(1)} %collective-permute-done.23.b1, ...), custom_call_target="tpu_custom_call" | custom-call | flops 2516582400 | bytes 6553600 | tf_op jit(solution)/shard_map/flow_chunk/pallas_call | solution.py:391
  100.7 5.8 %flow_chunk.10 = (f32[1280,128]{1,0:T(8,128)S(1)}, f32[1,128]{1,0:T(1,128)S(1)}) custom-call(s32[1]{0:T(128)} %bitcast.place_ref, bf16[1280,10240]{1,0:T(8,128)(2,1)} %ptdf_ref.31, bf16[656,128]{1,0:T(8,128)(2,1)S(1)} %collective-permute-done.11.b0, bf16[656,128]{1,0:T(8,128)(2,1)S(1)} %collective-permute-done.20.b1, ...), custom_call_target="tpu_custom_call" | custom-call | flops 2516582400 | bytes 6553600 | tf_op jit(solution)/shard_map/flow_chunk/pallas_call | solution.py:391
  106.6 6.2 %flow_chunk.11 = (f32[1280,128]{1,0:T(8,128)S(1)}, bf16[1280,128]{1,0:T(8,128)(2,1)S(1)}, f32[1,128]{1,0:T(1,128)S(1)}) custom-call(s32[1]{0:T(128)} %bitcast.place_ref, bf16[1280,10240]{1,0:T(8,128)(2,1)} %ptdf_ref.31, bf16[656,128]{1,0:T(8,128)(2,1)S(1)} %collective-permute-done.12.b0, bf16[656,128]{1,0:T(8,128)(2,1)S(1)} %collective-permute-done.17.b1, ...), custom_call_target="tpu_custom_call" | custom-call | flops 2516582400 | bytes 6553600 | tf_op jit(solution)/shard_map/flow_chunk/pallas_call | solution.py:391
  113.8 4.4 %shadow_chunk.12 = (f32[2,128,640]{2,1,0:T(8,128)S(1)}, bf16[2,128,640]{2,1,0:T(8,128)(2,1)S(1)}) custom-call(s32[1]{0:T(128)} %bitcast.place_ref, bf16[128,1280]{1,0:T(8,128)(2,1)S(1)} %bitcast.60, bf16[1280,10240]{1,0:T(8,128)(2,1)} %ptdf_ref.31), custom_call_target="tpu_custom_call" | custom-call | flops 2516582400 | bytes 6553600 | tf_op jit(solution)/shard_map/shadow_chunk/pallas_call | solution.py:300
  118.8 4.4 %shadow_chunk.13 = (f32[2,128,640]{2,1,0:T(8,128)S(1)}, bf16[2,128,640]{2,1,0:T(8,128)(2,1)S(1)}) custom-call(s32[1]{0:T(128)} %bitcast.place_ref, bf16[128,1280]{1,0:T(8,128)(2,1)S(1)} %bitcast.61, bf16[1280,10240]{1,0:T(8,128)(2,1)} %ptdf_ref.31), custom_call_target="tpu_custom_call" | custom-call | flops 2516582400 | bytes 6553600 | tf_op jit(solution)/shard_map/shadow_chunk/pallas_call | solution.py:300
  126.5 4.4 %shadow_chunk.15 = (f32[2,128,640]{2,1,0:T(8,128)S(1)}, bf16[2,128,640]{2,1,0:T(8,128)(2,1)S(1)}) custom-call(s32[1]{0:T(128)} %bitcast.place_ref, bf16[128,1280]{1,0:T(8,128)(2,1)S(1)} %bitcast.62, bf16[1280,10240]{1,0:T(8,128)(2,1)} %ptdf_ref.31), custom_call_target="tpu_custom_call" | custom-call | flops 2516582400 | bytes 6553600 | tf_op jit(solution)/shard_map/shadow_chunk/pallas_call | solution.py:300
  132.9 4.4 %shadow_chunk.14 = (f32[2,128,640]{2,1,0:T(8,128)S(1)}, bf16[2,128,640]{2,1,0:T(8,128)(2,1)S(1)}) custom-call(s32[1]{0:T(128)} %bitcast.place_ref, bf16[128,1280]{1,0:T(8,128)(2,1)S(1)} %bitcast.63, bf16[1280,10240]{1,0:T(8,128)(2,1)} %ptdf_ref.31), custom_call_target="tpu_custom_call" | custom-call | flops 2516582400 | bytes 6553600 | tf_op jit(solution)/shard_map/shadow_chunk/pallas_call | solution.py:300
  142.5 5.0 %collective-permute-done.32 = bf16[128,640]{1,0:T(8,128)(2,1)S(1)} collective-permute-done((bf16[128,640]{1,0:T(8,128)(2,1)S(1)}, bf16[128,640]{1,0:T(8,128)(2,1)S(1)}, u32[]{:S(2)}, u32[]{:S(2)}) %collective-permute-start.32) | collective-permute-done | bytes 163872 | tf_op jit(solution)/shard_map/ppermute | solution.py:410
  149.5 3.5 %collective-permute-done.33.refs_1_ = bf16[128,640]{1,0:T(8,128)(2,1)S(1)} collective-permute-done((bf16[128,640]{1,0:T(8,128)(2,1)S(1)}, bf16[128,640]{1,0:T(8,128)(2,1)S(1)}, u32[]{:S(2)}, u32[]{:S(2)}) %collective-permute-start.33) | collective-permute-done | bytes 163872 | tf_op jit(solution)/shard_map/ppermute | solution.py:410
  153.0 6.4 %update_generators.3 = (bf16[16,144,128]{2,1,0:T(8,128)(2,1)S(1)}, bf16[656,128]{1,0:T(8,128)(2,1)S(1)}) custom-call(f32[128,640]{1,0:T(8,128)S(1)} %bitcast_add_fusion.2.refs_0_, bf16[128,640]{1,0:T(8,128)(2,1)S(1)} %collective-permute-done.33.refs_1_, bf16[128,640]{1,0:T(8,128)(2,1)S(1)} %collective-permute-done.36.refs_2_, ...), custom_call_target="tpu_custom_call" | custom-call | flops 1509949440 | bytes 4194304 | tf_op jit(solution)/shard_map/update_generators/pallas_call | solution.py:251
  169.7 5.7 %flow_chunk.12 = (f32[1280,128]{1,0:T(8,128)S(1)}, f32[1,128]{1,0:T(1,128)S(1)}) custom-call(s32[1]{0:T(128)} %bitcast.place_ref, bf16[1280,10240]{1,0:T(8,128)(2,1)} %ptdf_ref.31, bf16[656,128]{1,0:T(8,128)(2,1)S(1)} %get-tuple-element.95.b0, bf16[656,128]{1,0:T(8,128)(2,1)S(1)} %collective-permute-done.39.b1, ...), custom_call_target="tpu_custom_call" | custom-call | flops 2516582400 | bytes 6553600 | tf_op jit(solution)/shard_map/flow_chunk/pallas_call | solution.py:391
  175.4 3.6 %all-to-all-start.1 = ((bf16[16,144,128]{2,1,0:T(8,128)(2,1)}), bf16[16,144,128]{2,1,0:T(8,128)(2,1)S(1)}, u32[]{:S(2)}, u32[]{:S(2)}) async-start(bf16[16,144,128]{2,1,0:T(8,128)(2,1)} %copy-done.3), calls=%async_computation.1 | async-start | bytes 1179648 | tf_op jit(solution)/shard_map/all_to_all | solution.py:519
  182.5 8.6 %collective-permute-done.47.b2 = bf16[656,128]{1,0:T(8,128)(2,1)} collective-permute-done((bf16[656,128]{1,0:T(8,128)(2,1)S(1)}, bf16[656,128]{1,0:T(8,128)(2,1)}, u32[]{:S(2)}, u32[]{:S(2)}) %collective-permute-start.47) | collective-permute-done | bytes 167968 | tf_op jit(solution)/shard_map/ppermute | solution.py:410
  191.0 4.6 %collective-permute-done.44.b2 = bf16[656,128]{1,0:T(8,128)(2,1)S(1)} collective-permute-done((bf16[656,128]{1,0:T(8,128)(2,1)S(1)}, bf16[656,128]{1,0:T(8,128)(2,1)S(1)}, u32[]{:S(2)}, u32[]{:S(2)}) %collective-permute-start.44) | collective-permute-done | bytes 167968 | tf_op jit(solution)/shard_map/ppermute | solution.py:410
  195.7 6.0 %flow_chunk.13 = (f32[1280,128]{1,0:T(8,128)S(1)}, f32[1,128]{1,0:T(1,128)S(1)}) custom-call(s32[1]{0:T(128)} %bitcast.place_ref, bf16[1280,10240]{1,0:T(8,128)(2,1)} %ptdf_ref.31, bf16[656,128]{1,0:T(8,128)(2,1)S(1)} %collective-permute-done.42.b0, bf16[656,128]{1,0:T(8,128)(2,1)} %collective-permute-done.49.b1, ...), custom_call_target="tpu_custom_call" | custom-call | flops 2516582400 | bytes 6553600 | tf_op jit(solution)/shard_map/flow_chunk/pallas_call | solution.py:391
  201.7 5.9 %flow_chunk.14 = (f32[1280,128]{1,0:T(8,128)S(1)}, f32[1,128]{1,0:T(1,128)S(1)}) custom-call(s32[1]{0:T(128)} %bitcast.place_ref, bf16[1280,10240]{1,0:T(8,128)(2,1)} %ptdf_ref.31, bf16[656,128]{1,0:T(8,128)(2,1)S(1)} %collective-permute-done.37.b0, bf16[656,128]{1,0:T(8,128)(2,1)S(1)} %collective-permute-done.46.b1, ...), custom_call_target="tpu_custom_call" | custom-call | flops 2516582400 | bytes 6553600 | tf_op jit(solution)/shard_map/flow_chunk/pallas_call | solution.py:391
  207.6 7.2 %flow_chunk.15 = (f32[1280,128]{1,0:T(8,128)}, bf16[1280,128]{1,0:T(8,128)(2,1)}, f32[1,128]{1,0:T(1,128)S(1)}) custom-call(s32[1]{0:T(128)} %bitcast.place_ref, bf16[1280,10240]{1,0:T(8,128)(2,1)} %ptdf_ref.31, bf16[656,128]{1,0:T(8,128)(2,1)S(1)} %collective-permute-done.38.b0, bf16[656,128]{1,0:T(8,128)(2,1)S(1)} %collective-permute-done.43.b1, ...), custom_call_target="tpu_custom_call" | custom-call | flops 2516582400 | bytes 6553600 | tf_op jit(solution)/shard_map/flow_chunk/pallas_call | solution.py:391
  215.3 4.5 %unpack_dispatch.1 = f32[768,128]{1,0:T(8,128)} custom-call(s32[768,1]{1,0:T(8,128)S(1)} %copy.20.owner_ref, bf16[2304,128]{1,0:T(8,128)(2,1)S(1)} %bitcast.68, f32[768,128]{1,0:T(8,128)S(1)} %copy-done.5, f32[768,1]{1,0:T(8,128)S(1)} %reshape.87.max_ref, f32[768,128]{1,0:T(8,128)S(1)} %copy-done.7), custom_call_target="tpu_custom_call" | custom-call | flops 452984832 | bytes 1048576 | tf_op jit(solution)/shard_map/unpack_dispatch/pallas_call | solution.py:165
  (160 shorter events, 57.4 us)
Async XLA Ops:
  14.6 12.5 %collective-permute-start = (bf16[2,128,640]{2,1,0:T(8,128)(2,1)S(1)}, bf16[2,128,640]{2,1,0:T(8,128)(2,1)S(1)}, u32[]{:S(2)}, u32[]{:S(2)}) collective-permute-start(bf16[2,128,640]{2,1,0:T(8,128)(2,1)S(1)} %get-tuple-element.59), channel_id=1, source_target_pairs={{0,1},{1,0},{2,3},{3,2},{4,5},{5,4},{6,7},{7,6},{8,9},{9,8},{10,11... | collective-permute-start | bytes 983048 | tf_op jit(solution)/shard_map/ppermute | solution.py:410
  15.2 48.7 %all-to-all-start = ((bf16[16,160,256]{2,1,0:T(8,128)(2,1)}), bf16[16,160,256]{2,1,0:T(8,128)(2,1)S(1)}, u32[]{:S(2)}, u32[]{:S(2)}) async-start(bf16[16,160,256]{2,1,0:T(8,128)(2,1)} %pack_generators.1), calls=%async_computation | async-start | bytes 2621440 | tf_op jit(solution)/shard_map/all_to_all | solution.py:449
  27.2 12.6 %collective-permute-start.2 = (bf16[128,640]{1,0:T(8,128)(2,1)S(1)}, bf16[128,640]{1,0:T(8,128)(2,1)S(1)}, u32[]{:S(2)}, u32[]{:S(2)}) collective-permute-start(bf16[128,640]{1,0:T(8,128)(2,1)S(1)} %fusion.8), channel_id=1, source_target_pairs={{0,2},{1,3},{2,0},{3,1},{4,6},{5,7},{6,4},{7,5},{8,10},{9,11},{10,... | collective-permute-start | bytes 491528 | tf_op jit(solution)/shard_map/ppermute | solution.py:410
  33.4 11.1 %collective-permute-start.5 = (bf16[2,128,640]{2,1,0:T(8,128)(2,1)S(1)}, bf16[2,128,640]{2,1,0:T(8,128)(2,1)S(1)}, u32[]{:S(2)}, u32[]{:S(2)}) collective-permute-start(bf16[2,128,640]{2,1,0:T(8,128)(2,1)S(1)} %get-tuple-element.67), channel_id=1, source_target_pairs={{0,1},{1,0},{2,3},{3,2},{4,5},{5,4},{6,7},{7,6},{8,9},{9,8},{10,11... | collective-permute-start | bytes 983048 | tf_op jit(solution)/shard_map/ppermute | solution.py:410
  33.5 11.3 %collective-permute-start.8 = (bf16[128,640]{1,0:T(8,128)(2,1)S(1)}, bf16[128,640]{1,0:T(8,128)(2,1)S(1)}, u32[]{:S(2)}, u32[]{:S(2)}) collective-permute-start(bf16[128,640]{1,0:T(8,128)(2,1)S(1)} %fusion.9), channel_id=1, source_target_pairs={{0,2},{1,3},{2,0},{3,1},{4,6},{5,7},{6,4},{7,5},{8,10},{9,11},{10,... | collective-permute-start | bytes 491528 | tf_op jit(solution)/shard_map/ppermute | solution.py:410
  39.8 8.3 %collective-permute-start.9 = (bf16[128,640]{1,0:T(8,128)(2,1)S(1)}, bf16[128,640]{1,0:T(8,128)(2,1)S(1)}, u32[]{:S(2)}, u32[]{:S(2)}) collective-permute-start(bf16[128,640]{1,0:T(8,128)(2,1)S(1)} %fusion.7), channel_id=1, source_target_pairs={{0,4},{1,5},{2,6},{3,7},{4,0},{5,1},{6,2},{7,3},{8,12},{9,13},{10,... | collective-permute-start | bytes 491528 | tf_op jit(solution)/shard_map/ppermute | solution.py:410
  44.4 8.3 %collective-permute-start.3 = (bf16[2,128,640]{2,1,0:T(8,128)(2,1)S(1)}, bf16[2,128,640]{2,1,0:T(8,128)(2,1)S(1)}, u32[]{:S(2)}, u32[]{:S(2)}) collective-permute-start(bf16[2,128,640]{2,1,0:T(8,128)(2,1)S(1)} %get-tuple-element.65), channel_id=1, source_target_pairs={{0,1},{1,0},{2,3},{3,2},{4,5},{5,4},{6,7},{7,6},{8,9},{9,8},{10,11... | collective-permute-start | bytes 983048 | tf_op jit(solution)/shard_map/ppermute | solution.py:410
  44.5 9.7 %collective-permute-start.6 = (bf16[128,640]{1,0:T(8,128)(2,1)S(1)}, bf16[128,640]{1,0:T(8,128)(2,1)S(1)}, u32[]{:S(2)}, u32[]{:S(2)}) collective-permute-start(bf16[128,640]{1,0:T(8,128)(2,1)S(1)} %fusion.11), channel_id=1, source_target_pairs={{0,2},{1,3},{2,0},{3,1},{4,6},{5,7},{6,4},{7,5},{8,10},{9,11},{10,... | collective-permute-start | bytes 491528 | tf_op jit(solution)/shard_map/ppermute | solution.py:410
  48.2 13.4 %collective-permute-start.10 = (bf16[128,640]{1,0:T(8,128)(2,1)S(1)}, bf16[128,640]{1,0:T(8,128)(2,1)S(1)}, u32[]{:S(2)}, u32[]{:S(2)}) collective-permute-start(bf16[128,640]{1,0:T(8,128)(2,1)S(1)} %fusion.5), channel_id=1, source_target_pairs={{0,8},{1,9},{2,10},{3,11},{4,12},{5,13},{6,14},{7,15},{8,0},{9,1},... | collective-permute-start | bytes 491528 | tf_op jit(solution)/shard_map/ppermute | solution.py:410
  54.3 9.5 %collective-permute-start.7 = (bf16[128,640]{1,0:T(8,128)(2,1)S(1)}, bf16[128,640]{1,0:T(8,128)(2,1)S(1)}, u32[]{:S(2)}, u32[]{:S(2)}) collective-permute-start(bf16[128,640]{1,0:T(8,128)(2,1)S(1)} %fusion.6), channel_id=1, source_target_pairs={{0,4},{1,5},{2,6},{3,7},{4,0},{5,1},{6,2},{7,3},{8,12},{9,13},{10,... | collective-permute-start | bytes 491528 | tf_op jit(solution)/shard_map/ppermute | solution.py:410
  71.2 9.3 %collective-permute-start.11 = (bf16[656,128]{1,0:T(8,128)(2,1)S(1)}, bf16[656,128]{1,0:T(8,128)(2,1)S(1)}, u32[]{:S(2)}, u32[]{:S(2)}) collective-permute-start(bf16[656,128]{1,0:T(8,128)(2,1)S(1)} %get-tuple-element.69.b0), channel_id=1, source_target_pairs={{0,8},{1,9},{2,10},{3,11},{4,12},{5,13},{6,14},{7,15},{8,0},{9,1},... | collective-permute-start | bytes 503816 | tf_op jit(solution)/shard_map/ppermute | solution.py:410
  71.5 9.1 %collective-permute-start.16 = (bf16[656,128]{1,0:T(8,128)(2,1)S(1)}, bf16[656,128]{1,0:T(8,128)(2,1)S(1)}, u32[]{:S(2)}, u32[]{:S(2)}) collective-permute-start(bf16[656,128]{1,0:T(8,128)(2,1)S(1)} %get-tuple-element.69.b0), channel_id=1, source_target_pairs={{0,4},{1,5},{2,6},{3,7},{4,0},{5,1},{6,2},{7,3},{8,12},{9,13},{10,... | collective-permute-start | bytes 503816 | tf_op jit(solution)/shard_map/ppermute | solution.py:410
  80.7 9.3 %collective-permute-start.24 = (bf16[656,128]{1,0:T(8,128)(2,1)S(1)}, bf16[656,128]{1,0:T(8,128)(2,1)S(1)}, u32[]{:S(2)}, u32[]{:S(2)}) collective-permute-start(bf16[656,128]{1,0:T(8,128)(2,1)S(1)} %collective-permute-done.16.b0), channel_id=1, source_target_pairs={{0,2},{1,3},{2,0},{3,1},{4,6},{5,7},{6,4},{7,5},{8,10},{9,11},{10,... | collective-permute-start | bytes 503816 | tf_op jit(solution)/shard_map/ppermute | solution.py:410
  82.1 8.6 %collective-permute-start.23 = (bf16[656,128]{1,0:T(8,128)(2,1)S(1)}, bf16[656,128]{1,0:T(8,128)(2,1)S(1)}, u32[]{:S(2)}, u32[]{:S(2)}) collective-permute-start(bf16[656,128]{1,0:T(8,128)(2,1)S(1)} %collective-permute-done.16.b0), channel_id=1, source_target_pairs={{0,1},{1,0},{2,3},{3,2},{4,5},{5,4},{6,7},{7,6},{8,9},{9,8},{10,11... | collective-permute-start | bytes 503816 | tf_op jit(solution)/shard_map/ppermute | solution.py:410
  82.1 8.7 %collective-permute-start.21 = (bf16[656,128]{1,0:T(8,128)(2,1)S(1)}, bf16[656,128]{1,0:T(8,128)(2,1)S(1)}, u32[]{:S(2)}, u32[]{:S(2)}) collective-permute-start(bf16[656,128]{1,0:T(8,128)(2,1)S(1)} %collective-permute-done.11.b0), channel_id=1, source_target_pairs={{0,2},{1,3},{2,0},{3,1},{4,6},{5,7},{6,4},{7,5},{8,10},{9,11},{10,... | collective-permute-start | bytes 503816 | tf_op jit(solution)/shard_map/ppermute | solution.py:410
  90.2 10.5 %collective-permute-start.20 = (bf16[656,128]{1,0:T(8,128)(2,1)S(1)}, bf16[656,128]{1,0:T(8,128)(2,1)S(1)}, u32[]{:S(2)}, u32[]{:S(2)}) collective-permute-start(bf16[656,128]{1,0:T(8,128)(2,1)S(1)} %collective-permute-done.11.b0), channel_id=1, source_target_pairs={{0,1},{1,0},{2,3},{3,2},{4,5},{5,4},{6,7},{7,6},{8,9},{9,8},{10,11... | collective-permute-start | bytes 503816 | tf_op jit(solution)/shard_map/ppermute | solution.py:410
  90.8 15.8 %collective-permute-start.17 = (bf16[656,128]{1,0:T(8,128)(2,1)S(1)}, bf16[656,128]{1,0:T(8,128)(2,1)S(1)}, u32[]{:S(2)}, u32[]{:S(2)}) collective-permute-start(bf16[656,128]{1,0:T(8,128)(2,1)S(1)} %collective-permute-done.12.b0), channel_id=1, source_target_pairs={{0,1},{1,0},{2,3},{3,2},{4,5},{5,4},{6,7},{7,6},{8,9},{9,8},{10,11... | collective-permute-start | bytes 503816 | tf_op jit(solution)/shard_map/ppermute | solution.py:410
  90.9 9.9 %collective-permute-start.22 = (bf16[656,128]{1,0:T(8,128)(2,1)S(1)}, bf16[656,128]{1,0:T(8,128)(2,1)S(1)}, u32[]{:S(2)}, u32[]{:S(2)}) collective-permute-start(bf16[656,128]{1,0:T(8,128)(2,1)S(1)} %collective-permute-done.21.b2), channel_id=1, source_target_pairs={{0,1},{1,0},{2,3},{3,2},{4,5},{5,4},{6,7},{7,6},{8,9},{9,8},{10,11... | collective-permute-start | bytes 503816 | tf_op jit(solution)/shard_map/ppermute | solution.py:410
  94.9 11.7 %collective-permute-start.19 = (bf16[656,128]{1,0:T(8,128)(2,1)S(1)}, bf16[656,128]{1,0:T(8,128)(2,1)S(1)}, u32[]{:S(2)}, u32[]{:S(2)}) collective-permute-start(bf16[656,128]{1,0:T(8,128)(2,1)S(1)} %collective-permute-done.18.b2), channel_id=1, source_target_pairs={{0,1},{1,0},{2,3},{3,2},{4,5},{5,4},{6,7},{7,6},{8,9},{9,8},{10,11... | collective-permute-start | bytes 503816 | tf_op jit(solution)/shard_map/ppermute | solution.py:410
  125.0 12.6 %collective-permute-start.34 = (bf16[128,640]{1,0:T(8,128)(2,1)S(1)}, bf16[128,640]{1,0:T(8,128)(2,1)S(1)}, u32[]{:S(2)}, u32[]{:S(2)}) collective-permute-start(bf16[128,640]{1,0:T(8,128)(2,1)S(1)} %fusion.13), channel_id=1, source_target_pairs={{0,2},{1,3},{2,0},{3,1},{4,6},{5,7},{6,4},{7,5},{8,10},{9,11},{10,... | collective-permute-start | bytes 491528 | tf_op jit(solution)/shard_map/ppermute | solution.py:410
  131.0 9.3 %collective-permute-start.31 = (bf16[2,128,640]{2,1,0:T(8,128)(2,1)S(1)}, bf16[2,128,640]{2,1,0:T(8,128)(2,1)S(1)}, u32[]{:S(2)}, u32[]{:S(2)}) collective-permute-start(bf16[2,128,640]{2,1,0:T(8,128)(2,1)S(1)} %get-tuple-element.91), channel_id=1, source_target_pairs={{0,1},{1,0},{2,3},{3,2},{4,5},{5,4},{6,7},{7,6},{8,9},{9,8},{10,11... | collective-permute-start | bytes 983048 | tf_op jit(solution)/shard_map/ppermute | solution.py:410
  137.9 11.6 %collective-permute-start.36 = (bf16[128,640]{1,0:T(8,128)(2,1)S(1)}, bf16[128,640]{1,0:T(8,128)(2,1)S(1)}, u32[]{:S(2)}, u32[]{:S(2)}) collective-permute-start(bf16[128,640]{1,0:T(8,128)(2,1)S(1)} %fusion.1), channel_id=1, source_target_pairs={{0,8},{1,9},{2,10},{3,11},{4,12},{5,13},{6,14},{7,15},{8,0},{9,1},... | collective-permute-start | bytes 491528 | tf_op jit(solution)/shard_map/ppermute | solution.py:410
  141.0 8.4 %collective-permute-start.30 = (bf16[128,640]{1,0:T(8,128)(2,1)S(1)}, bf16[128,640]{1,0:T(8,128)(2,1)S(1)}, u32[]{:S(2)}, u32[]{:S(2)}) collective-permute-start(bf16[128,640]{1,0:T(8,128)(2,1)S(1)} %fusion.14), channel_id=1, source_target_pairs={{0,2},{1,3},{2,0},{3,1},{4,6},{5,7},{6,4},{7,5},{8,10},{9,11},{10,... | collective-permute-start | bytes 491528 | tf_op jit(solution)/shard_map/ppermute | solution.py:410
  168.0 13.4 %collective-permute-start.50 = (bf16[656,128]{1,0:T(8,128)(2,1)S(1)}, bf16[656,128]{1,0:T(8,128)(2,1)}, u32[]{:S(2)}, u32[]{:S(2)}) collective-permute-start(bf16[656,128]{1,0:T(8,128)(2,1)S(1)} %collective-permute-done.42.b0), channel_id=1, source_target_pairs={{0,2},{1,3},{2,0},{3,1},{4,6},{5,7},{6,4},{7,5},{8,10},{9,11},{10,... | collective-permute-start | bytes 503816 | tf_op jit(solution)/shard_map/ppermute | solution.py:410
  175.4 39.9 %all-to-all-start.1 = ((bf16[16,144,128]{2,1,0:T(8,128)(2,1)}), bf16[16,144,128]{2,1,0:T(8,128)(2,1)S(1)}, u32[]{:S(2)}, u32[]{:S(2)}) async-start(bf16[16,144,128]{2,1,0:T(8,128)(2,1)} %copy-done.3), calls=%async_computation.1 | async-start | bytes 1179648 | tf_op jit(solution)/shard_map/all_to_all | solution.py:519
  179.4 11.6 %collective-permute-start.47 = (bf16[656,128]{1,0:T(8,128)(2,1)S(1)}, bf16[656,128]{1,0:T(8,128)(2,1)}, u32[]{:S(2)}, u32[]{:S(2)}) collective-permute-start(bf16[656,128]{1,0:T(8,128)(2,1)S(1)} %collective-permute-done.37.b0), channel_id=1, source_target_pairs={{0,2},{1,3},{2,0},{3,1},{4,6},{5,7},{6,4},{7,5},{8,10},{9,11},{10,... | collective-permute-start | bytes 503816 | tf_op jit(solution)/shard_map/ppermute | solution.py:410
  181.1 14.6 %collective-permute-start.44 = (bf16[656,128]{1,0:T(8,128)(2,1)S(1)}, bf16[656,128]{1,0:T(8,128)(2,1)S(1)}, u32[]{:S(2)}, u32[]{:S(2)}) collective-permute-start(bf16[656,128]{1,0:T(8,128)(2,1)S(1)} %collective-permute-done.38.b0), channel_id=1, source_target_pairs={{0,2},{1,3},{2,0},{3,1},{4,6},{5,7},{6,4},{7,5},{8,10},{9,11},{10,... | collective-permute-start | bytes 503816 | tf_op jit(solution)/shard_map/ppermute | solution.py:410
  181.4 14.2 %collective-permute-start.51 = (bf16[656,128]{1,0:T(8,128)(2,1)}, bf16[656,128]{1,0:T(8,128)(2,1)}, u32[]{:S(2)}, u32[]{:S(2)}) collective-permute-start(bf16[656,128]{1,0:T(8,128)(2,1)} %collective-permute-done.50.b2), channel_id=1, source_target_pairs={{0,1},{1,0},{2,3},{3,2},{4,5},{5,4},{6,7},{7,6},{8,9},{9,8},{10,11... | collective-permute-start | bytes 503816 | tf_op jit(solution)/shard_map/ppermute | solution.py:410
  181.8 19.8 %collective-permute-start.46 = (bf16[656,128]{1,0:T(8,128)(2,1)S(1)}, bf16[656,128]{1,0:T(8,128)(2,1)S(1)}, u32[]{:S(2)}, u32[]{:S(2)}) collective-permute-start(bf16[656,128]{1,0:T(8,128)(2,1)S(1)} %collective-permute-done.37.b0), channel_id=1, source_target_pairs={{0,1},{1,0},{2,3},{3,2},{4,5},{5,4},{6,7},{7,6},{8,9},{9,8},{10,11... | collective-permute-start | bytes 503816 | tf_op jit(solution)/shard_map/ppermute | solution.py:410
  182.4 25.2 %collective-permute-start.43 = (bf16[656,128]{1,0:T(8,128)(2,1)S(1)}, bf16[656,128]{1,0:T(8,128)(2,1)S(1)}, u32[]{:S(2)}, u32[]{:S(2)}) collective-permute-start(bf16[656,128]{1,0:T(8,128)(2,1)S(1)} %collective-permute-done.38.b0), channel_id=1, source_target_pairs={{0,1},{1,0},{2,3},{3,2},{4,5},{5,4},{6,7},{7,6},{8,9},{9,8},{10,11... | collective-permute-start | bytes 503816 | tf_op jit(solution)/shard_map/ppermute | solution.py:410
  191.0 10.6 %collective-permute-start.48 = (bf16[656,128]{1,0:T(8,128)(2,1)}, bf16[656,128]{1,0:T(8,128)(2,1)S(1)}, u32[]{:S(2)}, u32[]{:S(2)}) collective-permute-start(bf16[656,128]{1,0:T(8,128)(2,1)} %collective-permute-done.47.b2), channel_id=1, source_target_pairs={{0,1},{1,0},{2,3},{3,2},{4,5},{5,4},{6,7},{7,6},{8,9},{9,8},{10,11... | collective-permute-start | bytes 503816 | tf_op jit(solution)/shard_map/ppermute | solution.py:410
  195.6 11.9 %collective-permute-start.45 = (bf16[656,128]{1,0:T(8,128)(2,1)S(1)}, bf16[656,128]{1,0:T(8,128)(2,1)S(1)}, u32[]{:S(2)}, u32[]{:S(2)}) collective-permute-start(bf16[656,128]{1,0:T(8,128)(2,1)S(1)} %collective-permute-done.44.b2), channel_id=1, source_target_pairs={{0,1},{1,0},{2,3},{3,2},{4,5},{5,4},{6,7},{7,6},{8,9},{9,8},{10,11... | collective-permute-start | bytes 503816 | tf_op jit(solution)/shard_map/ppermute | solution.py:410
  (42 other events, 283.9 us)

commit v3 on v2

--- a/solution.py
+++ b/solution.py
@@ -128,7 +128,7 @@
     )
 
 
-def unpack_kernel(devices, cap, block, owner_ref, back_ref, dispatch_ref, max_ref, avail_ref, out_ref):
+def slot_kernel(devices, cap, owner_ref, slot_ref):
     gens = owner_ref.shape[0]
     owner = owner_ref[...]
     hits = (lax.broadcasted_iota(jnp.int32, (gens, devices), 1) == owner).astype(F32)
@@ -137,17 +137,27 @@
     ).astype(F32)
     count = dot(before.astype(BF16), hits.astype(BF16))
     rank = jnp.sum(count * hits, axis=1, keepdims=True).astype(jnp.int32)
-    slot = owner * cap + rank
-    out_ref[...] = jnp.zeros(out_ref.shape, F32)
-
-    def body(step, carry):
-        start = pl.multiple_of(step * block, block)
-        pick = (lax.broadcasted_iota(jnp.int32, (gens, block), 1) == slot - start).astype(F32).astype(BF16)
-        out_ref[...] += dot(pick, back_ref[pl.ds(start, block), :])
-        return carry
-
-    lax.fori_loop(0, back_ref.shape[0] // block, body, 0)
-    change = out_ref[...]
+    slot_ref[...] = owner * cap + rank
+
+
+def slot_column(devices, cap, owner_column):
+    return pl.pallas_call(
+        functools.partial(slot_kernel, devices, cap),
+        out_shape=jax.ShapeDtypeStruct(owner_column.shape, jnp.int32),
+        compiler_params=pltpu.CompilerParams(vmem_limit_bytes=LIMIT),
+        name="slot_column",
+    )(owner_column)
+
+
+def unpack_kernel(block, slot_ref, back_ref, dispatch_ref, max_ref, avail_ref, out_ref):
+    gens = slot_ref.shape[0]
+    slot = slot_ref[...]
+    at = lax.broadcasted_iota(jnp.int32, (gens, block), 1)
+    change = None
+    for start in range(0, back_ref.shape[0], block):
+        pick = (at == slot - start).astype(F32).astype(BF16)
+        part = dot(pick, back_ref[start : start + block, :])
+        change = part if change is None else change + part
     dispatch = dispatch_ref[...]
     upper = max_ref[...] * avail_ref[...]
     sent = dispatch.astype(BF16).astype(F32)
@@ -157,18 +167,18 @@
     out_ref[...] = jnp.where(change == -sent, 0.0, moved)
 
 
-def unpack(devices, cap, owner_column, back, dispatch, gen_max, availability):
-    gens = owner_column.shape[0]
-    hours = back.shape[2]
+def unpack(slot, back, dispatch, gen_max, availability):
+    gens = slot.shape[0]
+    devices, cap, hours = back.shape
     slots = devices * cap
-    block = 256 if slots % 256 == 0 else 128 if slots % 128 == 0 else 16
+    block = next(size for size in (768, 256, 128, 16) if slots % size == 0)
     return pl.pallas_call(
-        functools.partial(unpack_kernel, devices, cap, block),
+        functools.partial(unpack_kernel, block),
         out_shape=jax.ShapeDtypeStruct((gens, hours), F32),
         compiler_params=pltpu.CompilerParams(vmem_limit_bytes=LIMIT),
         cost_estimate=pl.CostEstimate(flops=2 * slots * gens * hours, bytes_accessed=1 << 20, transcendentals=0),
         name="unpack_dispatch",
-    )(owner_column, back.reshape(slots, hours), dispatch, gen_max, availability)
+    )(slot, back.reshape(slots, hours), dispatch, gen_max, availability)
 
 
 def update_kernel(cap, first, last, parts, *refs):
@@ -274,9 +284,13 @@
     )(*prices, balance_price, demand, recv, previous)
 
 
-def shadow_kernel(place_ref, line_ref, ptdf_ref, keep_ref, send_ref):
+def shadow_kernel(place_ref, line_ref, *refs):
+    ptdf_refs, (keep_ref, send_ref) = refs[:-2], refs[-2:]
     step = pl.program_id(0)
-    part = dot(line_ref[...], ptdf_ref[...])
+    depth = ptdf_refs[0].shape[0]
+    part = dot(line_ref[:, :depth], ptdf_refs[0][...])
+    for i, ref in enumerate(ptdf_refs[1:], 1):
+        part = part + dot(line_ref[:, i * depth : (i + 1) * depth], ref[...])
 
     @pl.when(step == 0)
     def _():
@@ -297,6 +311,7 @@
 
 def shadow_chunk(chunk, place, line_t, ptdf, buses):
     hours, lines = line_t.shape
+    pieces = 5
     return pl.pallas_call(
         shadow_kernel,
         grid_spec=pltpu.PrefetchScalarGridSpec(
@@ -304,7 +319,10 @@
             grid=(4,),
             in_specs=[
                 pl.BlockSpec((hours, lines), lambda i, place: (0, 0)),
-                pl.BlockSpec((lines, buses), lambda i, place: (0, place[0] ^ (4 * chunk + 3 - i))),
+            ]
+            + [
+                pl.BlockSpec((lines // pieces, buses), lambda i, place, p=p: (p, place[0] ^ (4 * chunk + 3 - i)))
+                for p in range(pieces)
             ],
             out_specs=(
                 pl.BlockSpec((2, hours, buses), lambda i, place: (0, 0, 0)),
@@ -320,10 +338,12 @@
             flops=COST * 8 * hours * lines * buses, bytes_accessed=8 * lines * buses, transcendentals=0
         ),
         name="shadow_chunk",
-    )(place, line_t, ptdf)
-
-
-def flow_kernel(start, end, place_ref, ptdf_ref, b0, b1, b2, b3, acc_ref, sum_ref, *rest):
+    )(place, line_t, *[ptdf] * pieces)
+
+
+def flow_kernel(start, end, pieces, place_ref, *refs):
+    ptdf_refs = refs[:pieces]
+    b0, b1, b2, b3, acc_ref, sum_ref, *rest = refs[pieces:]
     step = pl.program_id(0)
     if end:
         limit_ref, line_ref, out_ref, half_ref, sum_out, inj_ref = rest
@@ -341,17 +361,20 @@
             total = total + jnp.sum(tail, axis=0, keepdims=True)
         sum_out[...] = total
 
-    depth = ptdf_ref.shape[1]
-    rows = pl.ds(pl.multiple_of(step * depth, depth), depth)
-    part = dot(ptdf_ref[...], inj_ref[rows, :])
+    tile, depth = ptdf_refs[0].shape
+    inj = inj_ref[pl.ds(pl.multiple_of(step * depth, depth), depth), :]
+    parts = [dot(ref[...], inj) for ref in ptdf_refs]
 
     @pl.when(step == 0)
     def _():
-        out_ref[...] = part if start else acc_ref[...] + part
+        for i, part in enumerate(parts):
+            rows = slice(i * tile, (i + 1) * tile)
+            out_ref[rows, :] = part if start else acc_ref[rows, :] + part
 
     @pl.when(step > 0)
     def _():
-        out_ref[...] += part
+        for i, part in enumerate(parts):
+            out_ref[i * tile : (i + 1) * tile, :] += part
 
     if end:
 
@@ -369,15 +392,18 @@
     rows, hours = blocks[0].shape
     buses = rows - META
     start, end = acc is None, limit is not None
-    steps = 5
+    steps, pieces = 5, 4
     depth = 4 * buses // steps
     full = lambda *shape: pl.BlockSpec(shape, lambda i, place: (0,) * len(shape))
     if start:
         acc, acc_spec = total, full(1, hours)
     else:
         acc_spec = full(lines, hours)
-    operands = [ptdf, *blocks, acc, total]
-    in_specs = [pl.BlockSpec((lines, depth), lambda i, place: (0, ((place[0] >> 2) ^ chunk) * steps + i))]
+    operands = [ptdf] * pieces + [*blocks, acc, total]
+    in_specs = [
+        pl.BlockSpec((lines // pieces, depth), lambda i, place, p=p: (p, ((place[0] >> 2) ^ chunk) * steps + i))
+        for p in range(pieces)
+    ]
     in_specs += [full(rows, hours)] * 4 + [acc_spec, full(1, hours)]
     out_shape = [jax.ShapeDtypeStruct((lines, hours), F32)]
     out_specs = [full(lines, hours)]
@@ -389,7 +415,7 @@
     out_shape += [jax.ShapeDtypeStruct((1, hours), F32)]
     out_specs += [full(1, hours)]
     return pl.pallas_call(
-        functools.partial(flow_kernel, start, end),
+        functools.partial(flow_kernel, start, end, pieces),
         grid_spec=pltpu.PrefetchScalarGridSpec(
             num_scalar_prefetch=1,
             grid=(steps,),
@@ -444,9 +470,8 @@
     limit = line_limit.reshape(-1, 1)
     balance_row = balance_price.reshape(1, hours)
     line_half = line_price.astype(BF16)
-    if staged:
-        line_half, outgoing = lax.optimization_barrier((line_half, outgoing))
     recv = lax.all_to_all(outgoing, "bus", split_axis=0, concat_axis=0, tiled=True)
+    slot = None if staged else slot_column(devices, cap, gen_owner)
     held = None
     for iteration in range(ITERS):
         last = iteration == ITERS - 1
@@ -475,6 +500,8 @@
                 gots[chunk] = swap(send, devices, 1)
 
             product(3, line_t)
+            if iteration == 0:
+                line_t, _ = lax.optimization_barrier((line_t, outgoing))
             product(2, line_t)
             line_t, _ = lax.optimization_barrier((line_t, across(3)))
             product(1, line_t)
@@ -512,6 +539,9 @@
             settle_far(0)
             near[1], near[2], row = lax.optimization_barrier((near[1], near[2], balance_row))
             acc, total = flow_chunk(0, place, ptdf, blocks(0), None, row)
+            if iteration == 0:
+                owner, acc = lax.optimization_barrier((gen_owner, acc))
+                slot = slot_column(devices, cap, owner)
             near[3], acc = lax.optimization_barrier((near[3], acc))
             spread(3)
             if last:
@@ -520,6 +550,7 @@
             settle_far(1)
             acc, total = flow_chunk(1, place, ptdf, blocks(1), acc, total)
             settle_far(2)
+            far[3], acc = lax.optimization_barrier((far[3], acc))
             acc, total = flow_chunk(2, place, ptdf, blocks(2), acc, total)
             settle_far(3)
             line_price, line_half, total = flow_chunk(
@@ -536,7 +567,7 @@
             line_price = shifted - sigma_step * jnp.clip(shifted / sigma_step, -limit, limit)
             line_half = line_price.astype(BF16)
         balance_row = balance_row + sigma_step * balance / all_buses
-    dispatch = unpack(devices, cap, gen_owner, back, dispatch, gen_max.reshape(gens, 1), availability)
+    dispatch = unpack(slot, back, dispatch, gen_max.reshape(gens, 1), availability)
     return (dispatch, balance_row.reshape(hours), line_price)
 
 

time: 221 us -> 206 us (0.932)
  waiting for transfers between devices: 55.5 us -> 48 us
  local copies, waits for them, and re-layouts: 7.94 us -> 3.1 us
    ppermute x52, waiting for transfers between devices: 55.5 us -> 48 us  [swap(): return lax.ppermute(x, 'bus', [(i, i ^ mask) for i in range(devices)])]
    unnamed x42 -> x41, local copies, waits for them, and re-layouts: 7.38 us -> 2.36 us
    ppermute x52, starting transfers between devices: 38 us -> 35.7 us  [swap(): return lax.ppermute(x, 'bus', [(i, i ^ mask) for i in range(devices)])]
    pallas_call x9 -> x10, Pallas kernels: 52.7 us -> 50.7 us  [the longest x8 48.1 us: flow_chunk(): pl.pallas_call(functools.partial(flow_kernel, start, end, pieces), grid_s...]
  transfers between devices with their start and end apart: 54 -> 54, of which waited for: 18 -> 18; matrix products, arithmetic and copies ran while one was open for 1% -> 2% of each run, Pallas kernels for 31% -> 35%
where the time goes in v3:
time: 206 us; the launch traced here: 205 us
  Pallas kernels  102 us (50%)
  waiting for transfers between devices  48 us (23%)
  starting transfers between devices  46.9 us (23%)
  other arithmetic  3.2 us (2%)
  local copies, waits for them, and re-layouts  3.1 us (2%)
    pallas_call x8, Pallas kernels, flow_chunk(): pl.pallas_call(functools.partial(flow_kernel, start, end, pieces), grid_s...  48.1 us
    ppermute x52, waiting for transfers between devices, swap(): return lax.ppermute(x, 'bus', [(i, i ^ mask) for i in range(devices)])  48 us
    ppermute x52, starting transfers between devices, swap(): return lax.ppermute(x, 'bus', [(i, i ^ mask) for i in range(devices)])  35.7 us
    pallas_call x8, Pallas kernels, shadow_chunk(): pl.pallas_call(shadow_kernel, grid_spec=pltpu.PrefetchScalarGridSpec(num_...  35.2 us
    pallas_call x2, Pallas kernels, update(): pl.pallas_call(functools.partial(update_kernel, cap, first, last, len(pri...  12.7 us
    all_to_all x1, starting transfers between devices, local(): lax.all_to_all(outgoing, 'bus', split_axis=0, concat_axis=0, tiled=True)  7.04 us
    all_to_all x1, starting transfers between devices, local(): back = lax.all_to_all(held, 'bus', split_axis=0, concat_axis=0, tiled=True)  4.2 us
  transfers between devices with their start and end apart: 54, of which 18 were waited for; matrix products, arithmetic and copies ran while one was open for 2% of the time, Pallas kernels for 35%

profile of v3, /device:TPU:0, one launch (start us, length us, event | category | flops | bytes accessed | tf_op | source)
XLA Modules:
  0.0 204.6 jit_solution(7635605503606009623)
XLA Ops:
  2.0 4.5 %shadow_chunk.8 = (f32[2,128,640]{2,1,0:T(8,128)S(1)}, bf16[2,128,640]{2,1,0:T(8,128)(2,1)S(1)}) custom-call(s32[1]{0:T(128)} %bitcast.place_ref, bf16[128,1280]{1,0:T(8,128)(2,1)S(1)} %bitcast.66, bf16[1280,10240]{1,0:T(8,128)(2,1)} %refs_3_.31, bf16[1280,10240]{1,0:T(8,128)(2,1)} %refs_3_.31, bf16[1280,10240]{1,0:T(8,128)(2,1)} %refs_3_.31, ...), custom_call_target="tpu_custom_call" | custom-call | flops 2516582400 | bytes 6553600 | tf_op jit(solution)/shard_map/shadow_chunk/pallas_call | solution.py:315
  7.0 3.6 %pack_generators.1 = bf16[16,160,256]{2,1,0:T(8,128)(2,1)} custom-call(s32[6,128]{1,0:T(8,128)S(1)} %bitcast.72, s32[6,128]{1,0:T(8,128)S(1)} %bitcast.77, f32[6,128]{1,0:T(8,128)S(1)} %bitcast.78, f32[768,128]{1,0:T(8,128)S(1)} %copy-done.4, f32[6,128]{1,0:T(8,128)S(1)} %bitcast.71, f32[768,128]{1,0:T(8,128)S(1)} %copy-done.6), custom_call_target="tpu_custom_call" | custom-call | flops 905969664 | bytes 3145728 | tf_op jit(solution)/shard_map/pack_generators/pallas_call | solution.py:100
  10.6 7.0 %all-to-all-start = ((bf16[16,160,256]{2,1,0:T(8,128)(2,1)}), bf16[16,160,256]{2,1,0:T(8,128)(2,1)S(1)}, u32[]{:S(2)}, u32[]{:S(2)}) async-start(bf16[16,160,256]{2,1,0:T(8,128)(2,1)} %pack_generators.1), calls=%async_computation | async-start | bytes 2621440 | tf_op jit(solution)/shard_map/all_to_all | solution.py:473
  17.6 4.4 %shadow_chunk.9 = (f32[2,128,640]{2,1,0:T(8,128)S(1)}, bf16[2,128,640]{2,1,0:T(8,128)(2,1)S(1)}) custom-call(s32[1]{0:T(128)} %bitcast.place_ref, bf16[128,1280]{1,0:T(8,128)(2,1)S(1)} %bitcast.67, bf16[1280,10240]{1,0:T(8,128)(2,1)} %refs_3_.31, bf16[1280,10240]{1,0:T(8,128)(2,1)} %refs_3_.31, bf16[1280,10240]{1,0:T(8,128)(2,1)} %refs_3_.31, ...), custom_call_target="tpu_custom_call" | custom-call | flops 2516582400 | bytes 6553600 | tf_op jit(solution)/shard_map/shadow_chunk/pallas_call | solution.py:315
  25.2 4.4 %shadow_chunk.11 = (f32[2,128,640]{2,1,0:T(8,128)S(1)}, bf16[2,128,640]{2,1,0:T(8,128)(2,1)S(1)}) custom-call(s32[1]{0:T(128)} %bitcast.place_ref, bf16[128,1280]{1,0:T(8,128)(2,1)S(1)} %bitcast.68, bf16[1280,10240]{1,0:T(8,128)(2,1)} %refs_3_.31, bf16[1280,10240]{1,0:T(8,128)(2,1)} %refs_3_.31, bf16[1280,10240]{1,0:T(8,128)(2,1)} %refs_3_.31, ...), custom_call_target="tpu_custom_call" | custom-call | flops 2516582400 | bytes 6553600 | tf_op jit(solution)/shard_map/shadow_chunk/pallas_call | solution.py:315
  30.2 5.0 %collective-permute-done.2 = bf16[128,640]{1,0:T(8,128)(2,1)S(1)} collective-permute-done((bf16[128,640]{1,0:T(8,128)(2,1)S(1)}, bf16[128,640]{1,0:T(8,128)(2,1)S(1)}, u32[]{:S(2)}, u32[]{:S(2)}) %collective-permute-start.2) | collective-permute-done | bytes 163872 | tf_op jit(solution)/shard_map/ppermute | solution.py:436
  36.2 4.4 %shadow_chunk.10 = (f32[2,128,640]{2,1,0:T(8,128)S(1)}, bf16[2,128,640]{2,1,0:T(8,128)(2,1)S(1)}) custom-call(s32[1]{0:T(128)} %bitcast.place_ref, bf16[128,1280]{1,0:T(8,128)(2,1)S(1)} %bitcast.69, bf16[1280,10240]{1,0:T(8,128)(2,1)} %refs_3_.31, bf16[1280,10240]{1,0:T(8,128)(2,1)} %refs_3_.31, bf16[1280,10240]{1,0:T(8,128)(2,1)} %refs_3_.31, ...), custom_call_target="tpu_custom_call" | custom-call | flops 2516582400 | bytes 6553600 | tf_op jit(solution)/shard_map/shadow_chunk/pallas_call | solution.py:315
  43.7 4.4 %collective-permute-start.10 = (bf16[128,640]{1,0:T(8,128)(2,1)S(1)}, bf16[128,640]{1,0:T(8,128)(2,1)S(1)}, u32[]{:S(2)}, u32[]{:S(2)}) collective-permute-start(bf16[128,640]{1,0:T(8,128)(2,1)S(1)} %fusion.5), channel_id=1, source_target_pairs={{0,8},{1,9},{2,10},{3,11},{4,12},{5,13},{6,14},{7,15},{8,0},{9,1},... | collective-permute-start | bytes 491528 | tf_op jit(solution)/shard_map/ppermute | solution.py:436
  49.7 2.1 %collective-permute-start.7 = (bf16[128,640]{1,0:T(8,128)(2,1)S(1)}, bf16[128,640]{1,0:T(8,128)(2,1)S(1)}, u32[]{:S(2)}, u32[]{:S(2)}) collective-permute-start(bf16[128,640]{1,0:T(8,128)(2,1)S(1)} %fusion.6), channel_id=1, source_target_pairs={{0,4},{1,5},{2,6},{3,7},{4,0},{5,1},{6,2},{7,3},{8,12},{9,13},{10,... | collective-permute-start | bytes 491528 | tf_op jit(solution)/shard_map/ppermute | solution.py:436
  53.7 3.3 %collective-permute-done.10.refs_2_ = bf16[128,640]{1,0:T(8,128)(2,1)S(1)} collective-permute-done((bf16[128,640]{1,0:T(8,128)(2,1)S(1)}, bf16[128,640]{1,0:T(8,128)(2,1)S(1)}, u32[]{:S(2)}, u32[]{:S(2)}) %collective-permute-start.10) | collective-permute-done | bytes 163872 | tf_op jit(solution)/shard_map/ppermute | solution.py:436
  58.9 6.3 %update_generators.2 = (f32[16,144,128]{2,1,0:T(8,128)S(1)}, bf16[656,128]{1,0:T(8,128)(2,1)S(1)}) custom-call(f32[128,640]{1,0:T(8,128)S(1)} %bitcast_add_fusion.6.refs_0_, bf16[128,640]{1,0:T(8,128)(2,1)S(1)} %collective-permute-done.7.refs_1_, bf16[128,640]{1,0:T(8,128)(2,1)S(1)} %collective-permute-done.10.refs_2_, f32[1,128]{1,0:T(1,128)S(1)} %bitcast.73, ...), custom_call_target="tpu_custom_call" | custom-call | flops 1509949440 | bytes 4194304 | tf_op jit(solution)/shard_map/update_generators/pallas_call | solution.py:261
  66.6 2.5 %collective-permute-start.15 = (bf16[656,128]{1,0:T(8,128)(2,1)S(1)}, bf16[656,128]{1,0:T(8,128)(2,1)S(1)}, u32[]{:S(2)}, u32[]{:S(2)}) collective-permute-start(bf16[656,128]{1,0:T(8,128)(2,1)S(1)} %get-tuple-element.73.refs_4_), channel_id=1, source_target_pairs={{0,8},{1,9},{2,10},{3,11},{4,12},{5,13},{6,14},{7,15},{8,0},{9,1},... | collective-permute-start | bytes 503816 | tf_op jit(solution)/shard_map/ppermute | solution.py:436
  69.1 2.5 %collective-permute-done.12.refs_6_ = bf16[656,128]{1,0:T(8,128)(2,1)S(1)} collective-permute-done((bf16[656,128]{1,0:T(8,128)(2,1)S(1)}, bf16[656,128]{1,0:T(8,128)(2,1)S(1)}, u32[]{:S(2)}, u32[]{:S(2)}) %collective-permute-start.12) | collective-permute-done | bytes 167968 | tf_op jit(solution)/shard_map/ppermute | solution.py:436
  71.6 3.0 %collective-permute-done.14.refs_4_ = bf16[656,128]{1,0:T(8,128)(2,1)S(1)} collective-permute-done((bf16[656,128]{1,0:T(8,128)(2,1)S(1)}, bf16[656,128]{1,0:T(8,128)(2,1)S(1)}, u32[]{:S(2)}, u32[]{:S(2)}) %collective-permute-start.14) | collective-permute-done | bytes 167968 | tf_op jit(solution)/shard_map/ppermute | solution.py:436
  80.0 5.6 %flow_chunk.8 = (f32[1280,128]{1,0:T(8,128)S(1)}, f32[1,128]{1,0:T(1,128)S(1)}) custom-call(s32[1]{0:T(128)} %bitcast.place_ref, bf16[1280,10240]{1,0:T(8,128)(2,1)} %refs_3_.31, bf16[1280,10240]{1,0:T(8,128)(2,1)} %refs_3_.31, bf16[1280,10240]{1,0:T(8,128)(2,1)} %refs_3_.31, bf16[1280,10240]{1,0:T(8,128)(2,1)} %refs_3_.31, ...), custom_call_target="tpu_custom_call" | custom-call | flops 2516582400 | bytes 6553600 | tf_op jit(solution)/shard_map/flow_chunk/pallas_call | solution.py:417
  88.1 5.7 %flow_chunk.9 = (f32[1280,128]{1,0:T(8,128)S(1)}, f32[1,128]{1,0:T(1,128)S(1)}) custom-call(s32[1]{0:T(128)} %bitcast.place_ref, bf16[1280,10240]{1,0:T(8,128)(2,1)} %refs_3_.31, bf16[1280,10240]{1,0:T(8,128)(2,1)} %refs_3_.31, bf16[1280,10240]{1,0:T(8,128)(2,1)} %refs_3_.31, bf16[1280,10240]{1,0:T(8,128)(2,1)} %refs_3_.31, ...), custom_call_target="tpu_custom_call" | custom-call | flops 2516582400 | bytes 6553600 | tf_op jit(solution)/shard_map/flow_chunk/pallas_call | solution.py:417
  94.2 5.8 %flow_chunk.10 = (f32[1280,128]{1,0:T(8,128)S(1)}, f32[1,128]{1,0:T(1,128)S(1)}) custom-call(s32[1]{0:T(128)} %bitcast.place_ref, bf16[1280,10240]{1,0:T(8,128)(2,1)} %refs_3_.31, bf16[1280,10240]{1,0:T(8,128)(2,1)} %refs_3_.31, bf16[1280,10240]{1,0:T(8,128)(2,1)} %refs_3_.31, bf16[1280,10240]{1,0:T(8,128)(2,1)} %refs_3_.31, ...), custom_call_target="tpu_custom_call" | custom-call | flops 2516582400 | bytes 6553600 | tf_op jit(solution)/shard_map/flow_chunk/pallas_call | solution.py:417
  100.0 6.1 %flow_chunk.11 = (f32[1280,128]{1,0:T(8,128)S(1)}, bf16[1280,128]{1,0:T(8,128)(2,1)S(1)}, f32[1,128]{1,0:T(1,128)S(1)}) custom-call(s32[1]{0:T(128)} %bitcast.place_ref, bf16[1280,10240]{1,0:T(8,128)(2,1)} %refs_3_.31, bf16[1280,10240]{1,0:T(8,128)(2,1)} %refs_3_.31, bf16[1280,10240]{1,0:T(8,128)(2,1)} %refs_3_.31, bf16[1280,10240]{1,0:T(8,128)(2,1)} %refs_3_.31, ...), custom_call_target="tpu_custom_call" | custom-call | flops 2516582400 | bytes 6553600 | tf_op jit(solution)/shard_map/flow_chunk/pallas_call | solution.py:417
  106.3 4.4 %shadow_chunk.12 = (f32[2,128,640]{2,1,0:T(8,128)S(1)}, bf16[2,128,640]{2,1,0:T(8,128)(2,1)S(1)}) custom-call(s32[1]{0:T(128)} %bitcast.place_ref, bf16[128,1280]{1,0:T(8,128)(2,1)S(1)} %bitcast.62, bf16[1280,10240]{1,0:T(8,128)(2,1)} %refs_3_.31, bf16[1280,10240]{1,0:T(8,128)(2,1)} %refs_3_.31, bf16[1280,10240]{1,0:T(8,128)(2,1)} %refs_3_.31, ...), custom_call_target="tpu_custom_call" | custom-call | flops 2516582400 | bytes 6553600 | tf_op jit(solution)/shard_map/shadow_chunk/pallas_call | solution.py:315
  111.1 4.4 %shadow_chunk.13 = (f32[2,128,640]{2,1,0:T(8,128)S(1)}, bf16[2,128,640]{2,1,0:T(8,128)(2,1)S(1)}) custom-call(s32[1]{0:T(128)} %bitcast.place_ref, bf16[128,1280]{1,0:T(8,128)(2,1)S(1)} %bitcast.63, bf16[1280,10240]{1,0:T(8,128)(2,1)} %refs_3_.31, bf16[1280,10240]{1,0:T(8,128)(2,1)} %refs_3_.31, bf16[1280,10240]{1,0:T(8,128)(2,1)} %refs_3_.31, ...), custom_call_target="tpu_custom_call" | custom-call | flops 2516582400 | bytes 6553600 | tf_op jit(solution)/shard_map/shadow_chunk/pallas_call | solution.py:315
  118.0 4.4 %shadow_chunk.15 = (f32[2,128,640]{2,1,0:T(8,128)S(1)}, bf16[2,128,640]{2,1,0:T(8,128)(2,1)S(1)}) custom-call(s32[1]{0:T(128)} %bitcast.place_ref, bf16[128,1280]{1,0:T(8,128)(2,1)S(1)} %bitcast.64, bf16[1280,10240]{1,0:T(8,128)(2,1)} %refs_3_.31, bf16[1280,10240]{1,0:T(8,128)(2,1)} %refs_3_.31, bf16[1280,10240]{1,0:T(8,128)(2,1)} %refs_3_.31, ...), custom_call_target="tpu_custom_call" | custom-call | flops 2516582400 | bytes 6553600 | tf_op jit(solution)/shard_map/shadow_chunk/pallas_call | solution.py:315
  123.0 4.4 %shadow_chunk.14 = (f32[2,128,640]{2,1,0:T(8,128)S(1)}, bf16[2,128,640]{2,1,0:T(8,128)(2,1)S(1)}) custom-call(s32[1]{0:T(128)} %bitcast.place_ref, bf16[128,1280]{1,0:T(8,128)(2,1)S(1)} %bitcast.65, bf16[1280,10240]{1,0:T(8,128)(2,1)} %refs_3_.31, bf16[1280,10240]{1,0:T(8,128)(2,1)} %refs_3_.31, bf16[1280,10240]{1,0:T(8,128)(2,1)} %refs_3_.31, ...), custom_call_target="tpu_custom_call" | custom-call | flops 2516582400 | bytes 6553600 | tf_op jit(solution)/shard_map/shadow_chunk/pallas_call | solution.py:315
  132.4 5.0 %collective-permute-done.32 = bf16[128,640]{1,0:T(8,128)(2,1)S(1)} collective-permute-done((bf16[128,640]{1,0:T(8,128)(2,1)S(1)}, bf16[128,640]{1,0:T(8,128)(2,1)S(1)}, u32[]{:S(2)}, u32[]{:S(2)}) %collective-permute-start.32) | collective-permute-done | bytes 163872 | tf_op jit(solution)/shard_map/ppermute | solution.py:436
  139.8 3.1 %collective-permute-done.33.refs_1_ = bf16[128,640]{1,0:T(8,128)(2,1)S(1)} collective-permute-done((bf16[128,640]{1,0:T(8,128)(2,1)S(1)}, bf16[128,640]{1,0:T(8,128)(2,1)S(1)}, u32[]{:S(2)}, u32[]{:S(2)}) %collective-permute-start.33) | collective-permute-done | bytes 163872 | tf_op jit(solution)/shard_map/ppermute | solution.py:436
  142.8 6.3 %update_generators.3 = (bf16[16,144,128]{2,1,0:T(8,128)(2,1)S(1)}, bf16[656,128]{1,0:T(8,128)(2,1)S(1)}) custom-call(f32[128,640]{1,0:T(8,128)S(1)} %bitcast_add_fusion.2.refs_0_, bf16[128,640]{1,0:T(8,128)(2,1)S(1)} %collective-permute-done.33.refs_1_, bf16[128,640]{1,0:T(8,128)(2,1)S(1)} %collective-permute-done.36.refs_2_, ...), custom_call_target="tpu_custom_call" | custom-call | flops 1509949440 | bytes 4194304 | tf_op jit(solution)/shard_map/update_generators/pallas_call | solution.py:261
  154.6 4.9 %collective-permute-done.37.refs_4_ = bf16[656,128]{1,0:T(8,128)(2,1)} collective-permute-done((bf16[656,128]{1,0:T(8,128)(2,1)S(1)}, bf16[656,128]{1,0:T(8,128)(2,1)}, u32[]{:S(2)}, u32[]{:S(2)}) %collective-permute-start.37) | collective-permute-done | bytes 167968 | tf_op jit(solution)/shard_map/ppermute | solution.py:436
  160.4 5.7 %flow_chunk.12 = (f32[1280,128]{1,0:T(8,128)S(1)}, f32[1,128]{1,0:T(1,128)S(1)}) custom-call(s32[1]{0:T(128)} %bitcast.place_ref, bf16[1280,10240]{1,0:T(8,128)(2,1)} %refs_3_.31, bf16[1280,10240]{1,0:T(8,128)(2,1)} %refs_3_.31, bf16[1280,10240]{1,0:T(8,128)(2,1)} %refs_3_.31, bf16[1280,10240]{1,0:T(8,128)(2,1)} %refs_3_.31, ...), custom_call_target="tpu_custom_call" | custom-call | flops 2516582400 | bytes 6553600 | tf_op jit(solution)/shard_map/flow_chunk/pallas_call | solution.py:417
  166.1 4.2 %all-to-all-start.1 = ((bf16[16,144,128]{2,1,0:T(8,128)(2,1)}), bf16[16,144,128]{2,1,0:T(8,128)(2,1)S(1)}, u32[]{:S(2)}, u32[]{:S(2)}) async-start(bf16[16,144,128]{2,1,0:T(8,128)(2,1)} %copy-done.3), calls=%async_computation.1 | async-start | bytes 1179648 | tf_op jit(solution)/shard_map/all_to_all | solution.py:549
  174.3 8.0 %collective-permute-done.50.refs_6_ = bf16[656,128]{1,0:T(8,128)(2,1)} collective-permute-done((bf16[656,128]{1,0:T(8,128)(2,1)}, bf16[656,128]{1,0:T(8,128)(2,1)}, u32[]{:S(2)}, u32[]{:S(2)}) %collective-permute-start.50) | collective-permute-done | bytes 167968 | tf_op jit(solution)/shard_map/ppermute | solution.py:436
  182.3 6.0 %flow_chunk.13 = (f32[1280,128]{1,0:T(8,128)S(1)}, f32[1,128]{1,0:T(1,128)S(1)}) custom-call(s32[1]{0:T(128)} %bitcast.place_ref, bf16[1280,10240]{1,0:T(8,128)(2,1)} %refs_3_.31, bf16[1280,10240]{1,0:T(8,128)(2,1)} %refs_3_.31, bf16[1280,10240]{1,0:T(8,128)(2,1)} %refs_3_.31, bf16[1280,10240]{1,0:T(8,128)(2,1)} %refs_3_.31, ...), custom_call_target="tpu_custom_call" | custom-call | flops 2516582400 | bytes 6553600 | tf_op jit(solution)/shard_map/flow_chunk/pallas_call | solution.py:417
  188.9 6.0 %flow_chunk.14 = (f32[1280,128]{1,0:T(8,128)S(1)}, f32[1,128]{1,0:T(1,128)S(1)}) custom-call(s32[1]{0:T(128)} %bitcast.place_ref, bf16[1280,10240]{1,0:T(8,128)(2,1)} %refs_3_.31, bf16[1280,10240]{1,0:T(8,128)(2,1)} %refs_3_.31, bf16[1280,10240]{1,0:T(8,128)(2,1)} %refs_3_.31, bf16[1280,10240]{1,0:T(8,128)(2,1)} %refs_3_.31, ...), custom_call_target="tpu_custom_call" | custom-call | flops 2516582400 | bytes 6553600 | tf_op jit(solution)/shard_map/flow_chunk/pallas_call | solution.py:417
  194.9 7.3 %flow_chunk.15 = (f32[1280,128]{1,0:T(8,128)}, bf16[1280,128]{1,0:T(8,128)(2,1)}, f32[1,128]{1,0:T(1,128)S(1)}) custom-call(s32[1]{0:T(128)} %bitcast.place_ref, bf16[1280,10240]{1,0:T(8,128)(2,1)} %refs_3_.31, bf16[1280,10240]{1,0:T(8,128)(2,1)} %refs_3_.31, bf16[1280,10240]{1,0:T(8,128)(2,1)} %refs_3_.31, bf16[1280,10240]{1,0:T(8,128)(2,1)} %refs_3_.31, ...), custom_call_target="tpu_custom_call" | custom-call | flops 2516582400 | bytes 6553600 | tf_op jit(solution)/shard_map/flow_chunk/pallas_call | solution.py:417
  (161 shorter events, 48.8 us)
Async XLA Ops:
  6.4 16.1 %collective-permute-start = (bf16[2,128,640]{2,1,0:T(8,128)(2,1)S(1)}, bf16[2,128,640]{2,1,0:T(8,128)(2,1)}, u32[]{:S(2)}, u32[]{:S(2)}) collective-permute-start(bf16[2,128,640]{2,1,0:T(8,128)(2,1)S(1)} %get-tuple-element.64), channel_id=1, source_target_pairs={{0,1},{1,0},{2,3},{3,2},{4,5},{5,4},{6,7},{7,6},{8,9},{9,8},{10,11... | collective-permute-start | bytes 983048 | tf_op jit(solution)/shard_map/ppermute | solution.py:436
  10.6 48.3 %all-to-all-start = ((bf16[16,160,256]{2,1,0:T(8,128)(2,1)}), bf16[16,160,256]{2,1,0:T(8,128)(2,1)S(1)}, u32[]{:S(2)}, u32[]{:S(2)}) async-start(bf16[16,160,256]{2,1,0:T(8,128)(2,1)} %pack_generators.1), calls=%async_computation | async-start | bytes 2621440 | tf_op jit(solution)/shard_map/all_to_all | solution.py:473
  22.1 7.7 %collective-permute-start.1 = (bf16[2,128,640]{2,1,0:T(8,128)(2,1)S(1)}, bf16[2,128,640]{2,1,0:T(8,128)(2,1)S(1)}, u32[]{:S(2)}, u32[]{:S(2)}) collective-permute-start(bf16[2,128,640]{2,1,0:T(8,128)(2,1)S(1)} %get-tuple-element.67), channel_id=1, source_target_pairs={{0,1},{1,0},{2,3},{3,2},{4,5},{5,4},{6,7},{7,6},{8,9},{9,8},{10,11... | collective-permute-start | bytes 983048 | tf_op jit(solution)/shard_map/ppermute | solution.py:436
  23.5 11.7 %collective-permute-start.2 = (bf16[128,640]{1,0:T(8,128)(2,1)S(1)}, bf16[128,640]{1,0:T(8,128)(2,1)S(1)}, u32[]{:S(2)}, u32[]{:S(2)}) collective-permute-start(bf16[128,640]{1,0:T(8,128)(2,1)S(1)} %fusion.8), channel_id=1, source_target_pairs={{0,2},{1,3},{2,0},{3,1},{4,6},{5,7},{6,4},{7,5},{8,10},{9,11},{10,... | collective-permute-start | bytes 491528 | tf_op jit(solution)/shard_map/ppermute | solution.py:436
  29.6 11.1 %collective-permute-start.5 = (bf16[2,128,640]{2,1,0:T(8,128)(2,1)S(1)}, bf16[2,128,640]{2,1,0:T(8,128)(2,1)S(1)}, u32[]{:S(2)}, u32[]{:S(2)}) collective-permute-start(bf16[2,128,640]{2,1,0:T(8,128)(2,1)S(1)} %get-tuple-element.72), channel_id=1, source_target_pairs={{0,1},{1,0},{2,3},{3,2},{4,5},{5,4},{6,7},{7,6},{8,9},{9,8},{10,11... | collective-permute-start | bytes 983048 | tf_op jit(solution)/shard_map/ppermute | solution.py:436
  29.8 11.7 %collective-permute-start.8 = (bf16[128,640]{1,0:T(8,128)(2,1)S(1)}, bf16[128,640]{1,0:T(8,128)(2,1)S(1)}, u32[]{:S(2)}, u32[]{:S(2)}) collective-permute-start(bf16[128,640]{1,0:T(8,128)(2,1)S(1)} %fusion.9), channel_id=1, source_target_pairs={{0,2},{1,3},{2,0},{3,1},{4,6},{5,7},{6,4},{7,5},{8,10},{9,11},{10,... | collective-permute-start | bytes 491528 | tf_op jit(solution)/shard_map/ppermute | solution.py:436
  40.8 8.9 %collective-permute-start.6 = (bf16[128,640]{1,0:T(8,128)(2,1)S(1)}, bf16[128,640]{1,0:T(8,128)(2,1)S(1)}, u32[]{:S(2)}, u32[]{:S(2)}) collective-permute-start(bf16[128,640]{1,0:T(8,128)(2,1)S(1)} %fusion.11), channel_id=1, source_target_pairs={{0,2},{1,3},{2,0},{3,1},{4,6},{5,7},{6,4},{7,5},{8,10},{9,11},{10,... | collective-permute-start | bytes 491528 | tf_op jit(solution)/shard_map/ppermute | solution.py:436
  43.7 13.3 %collective-permute-start.10 = (bf16[128,640]{1,0:T(8,128)(2,1)S(1)}, bf16[128,640]{1,0:T(8,128)(2,1)S(1)}, u32[]{:S(2)}, u32[]{:S(2)}) collective-permute-start(bf16[128,640]{1,0:T(8,128)(2,1)S(1)} %fusion.5), channel_id=1, source_target_pairs={{0,8},{1,9},{2,10},{3,11},{4,12},{5,13},{6,14},{7,15},{8,0},{9,1},... | collective-permute-start | bytes 491528 | tf_op jit(solution)/shard_map/ppermute | solution.py:436
  49.7 9.1 %collective-permute-start.7 = (bf16[128,640]{1,0:T(8,128)(2,1)S(1)}, bf16[128,640]{1,0:T(8,128)(2,1)S(1)}, u32[]{:S(2)}, u32[]{:S(2)}) collective-permute-start(bf16[128,640]{1,0:T(8,128)(2,1)S(1)} %fusion.6), channel_id=1, source_target_pairs={{0,4},{1,5},{2,6},{3,7},{4,0},{5,1},{6,2},{7,3},{8,12},{9,13},{10,... | collective-permute-start | bytes 491528 | tf_op jit(solution)/shard_map/ppermute | solution.py:436
  66.6 8.0 %collective-permute-start.14 = (bf16[656,128]{1,0:T(8,128)(2,1)S(1)}, bf16[656,128]{1,0:T(8,128)(2,1)S(1)}, u32[]{:S(2)}, u32[]{:S(2)}) collective-permute-start(bf16[656,128]{1,0:T(8,128)(2,1)S(1)} %get-tuple-element.73.refs_4_), channel_id=1, source_target_pairs={{0,4},{1,5},{2,6},{3,7},{4,0},{5,1},{6,2},{7,3},{8,12},{9,13},{10,... | collective-permute-start | bytes 503816 | tf_op jit(solution)/shard_map/ppermute | solution.py:436
  66.6 9.9 %collective-permute-start.15 = (bf16[656,128]{1,0:T(8,128)(2,1)S(1)}, bf16[656,128]{1,0:T(8,128)(2,1)S(1)}, u32[]{:S(2)}, u32[]{:S(2)}) collective-permute-start(bf16[656,128]{1,0:T(8,128)(2,1)S(1)} %get-tuple-element.73.refs_4_), channel_id=1, source_target_pairs={{0,8},{1,9},{2,10},{3,11},{4,12},{5,13},{6,14},{7,15},{8,0},{9,1},... | collective-permute-start | bytes 503816 | tf_op jit(solution)/shard_map/ppermute | solution.py:436
  69.1 7.6 %collective-permute-start.11 = (bf16[656,128]{1,0:T(8,128)(2,1)S(1)}, bf16[656,128]{1,0:T(8,128)(2,1)S(1)}, u32[]{:S(2)}, u32[]{:S(2)}) collective-permute-start(bf16[656,128]{1,0:T(8,128)(2,1)S(1)} %get-tuple-element.73.refs_4_), channel_id=1, source_target_pairs={{0,1},{1,0},{2,3},{3,2},{4,5},{5,4},{6,7},{7,6},{8,9},{9,8},{10,11... | collective-permute-start | bytes 503816 | tf_op jit(solution)/shard_map/ppermute | solution.py:436
  76.6 9.1 %collective-permute-start.16 = (bf16[656,128]{1,0:T(8,128)(2,1)S(1)}, bf16[656,128]{1,0:T(8,128)(2,1)S(1)}, u32[]{:S(2)}, u32[]{:S(2)}) collective-permute-start(bf16[656,128]{1,0:T(8,128)(2,1)S(1)} %collective-permute-done.15.refs_4_), channel_id=1, source_target_pairs={{0,4},{1,5},{2,6},{3,7},{4,0},{5,1},{6,2},{7,3},{8,12},{9,13},{10,... | collective-permute-start | bytes 503816 | tf_op jit(solution)/shard_map/ppermute | solution.py:436
  76.6 11.0 %collective-permute-start.19 = (bf16[656,128]{1,0:T(8,128)(2,1)S(1)}, bf16[656,128]{1,0:T(8,128)(2,1)S(1)}, u32[]{:S(2)}, u32[]{:S(2)}) collective-permute-start(bf16[656,128]{1,0:T(8,128)(2,1)S(1)} %collective-permute-done.14.refs_4_), channel_id=1, source_target_pairs={{0,1},{1,0},{2,3},{3,2},{4,5},{5,4},{6,7},{7,6},{8,9},{9,8},{10,11... | collective-permute-start | bytes 503816 | tf_op jit(solution)/shard_map/ppermute | solution.py:436
  76.7 11.1 %collective-permute-start.24 = (bf16[656,128]{1,0:T(8,128)(2,1)S(1)}, bf16[656,128]{1,0:T(8,128)(2,1)S(1)}, u32[]{:S(2)}, u32[]{:S(2)}) collective-permute-start(bf16[656,128]{1,0:T(8,128)(2,1)S(1)} %collective-permute-done.15.refs_4_), channel_id=1, source_target_pairs={{0,2},{1,3},{2,0},{3,1},{4,6},{5,7},{6,4},{7,5},{8,10},{9,11},{10,... | collective-permute-start | bytes 503816 | tf_op jit(solution)/shard_map/ppermute | solution.py:436
  78.3 15.9 %collective-permute-start.23 = (bf16[656,128]{1,0:T(8,128)(2,1)S(1)}, bf16[656,128]{1,0:T(8,128)(2,1)S(1)}, u32[]{:S(2)}, u32[]{:S(2)}) collective-permute-start(bf16[656,128]{1,0:T(8,128)(2,1)S(1)} %collective-permute-done.15.refs_4_), channel_id=1, source_target_pairs={{0,1},{1,0},{2,3},{3,2},{4,5},{5,4},{6,7},{7,6},{8,9},{9,8},{10,11... | collective-permute-start | bytes 503816 | tf_op jit(solution)/shard_map/ppermute | solution.py:436
  80.0 8.1 %collective-permute-start.21 = (bf16[656,128]{1,0:T(8,128)(2,1)S(1)}, bf16[656,128]{1,0:T(8,128)(2,1)S(1)}, u32[]{:S(2)}, u32[]{:S(2)}) collective-permute-start(bf16[656,128]{1,0:T(8,128)(2,1)S(1)} %collective-permute-done.20.refs_6_), channel_id=1, source_target_pairs={{0,1},{1,0},{2,3},{3,2},{4,5},{5,4},{6,7},{7,6},{8,9},{9,8},{10,11... | collective-permute-start | bytes 503816 | tf_op jit(solution)/shard_map/ppermute | solution.py:436
  85.7 8.2 %collective-permute-start.18 = (bf16[656,128]{1,0:T(8,128)(2,1)S(1)}, bf16[656,128]{1,0:T(8,128)(2,1)S(1)}, u32[]{:S(2)}, u32[]{:S(2)}) collective-permute-start(bf16[656,128]{1,0:T(8,128)(2,1)S(1)} %collective-permute-done.16.refs_4_), channel_id=1, source_target_pairs={{0,2},{1,3},{2,0},{3,1},{4,6},{5,7},{6,4},{7,5},{8,10},{9,11},{10,... | collective-permute-start | bytes 503816 | tf_op jit(solution)/shard_map/ppermute | solution.py:436
  87.6 12.3 %collective-permute-start.17 = (bf16[656,128]{1,0:T(8,128)(2,1)S(1)}, bf16[656,128]{1,0:T(8,128)(2,1)S(1)}, u32[]{:S(2)}, u32[]{:S(2)}) collective-permute-start(bf16[656,128]{1,0:T(8,128)(2,1)S(1)} %collective-permute-done.16.refs_4_), channel_id=1, source_target_pairs={{0,1},{1,0},{2,3},{3,2},{4,5},{5,4},{6,7},{7,6},{8,9},{9,8},{10,11... | collective-permute-start | bytes 503816 | tf_op jit(solution)/shard_map/ppermute | solution.py:436
  117.2 10.4 %collective-permute-start.34 = (bf16[128,640]{1,0:T(8,128)(2,1)S(1)}, bf16[128,640]{1,0:T(8,128)(2,1)S(1)}, u32[]{:S(2)}, u32[]{:S(2)}) collective-permute-start(bf16[128,640]{1,0:T(8,128)(2,1)S(1)} %fusion.13), channel_id=1, source_target_pairs={{0,2},{1,3},{2,0},{3,1},{4,6},{5,7},{6,4},{7,5},{8,10},{9,11},{10,... | collective-permute-start | bytes 491528 | tf_op jit(solution)/shard_map/ppermute | solution.py:436
  122.4 7.8 %collective-permute-start.31 = (bf16[2,128,640]{2,1,0:T(8,128)(2,1)S(1)}, bf16[2,128,640]{2,1,0:T(8,128)(2,1)S(1)}, u32[]{:S(2)}, u32[]{:S(2)}) collective-permute-start(bf16[2,128,640]{2,1,0:T(8,128)(2,1)S(1)} %get-tuple-element.99), channel_id=1, source_target_pairs={{0,1},{1,0},{2,3},{3,2},{4,5},{5,4},{6,7},{7,6},{8,9},{9,8},{10,11... | collective-permute-start | bytes 983048 | tf_op jit(solution)/shard_map/ppermute | solution.py:436
  129.3 10.5 %collective-permute-start.36 = (bf16[128,640]{1,0:T(8,128)(2,1)S(1)}, bf16[128,640]{1,0:T(8,128)(2,1)S(1)}, u32[]{:S(2)}, u32[]{:S(2)}) collective-permute-start(bf16[128,640]{1,0:T(8,128)(2,1)S(1)} %fusion.1), channel_id=1, source_target_pairs={{0,8},{1,9},{2,10},{3,11},{4,12},{5,13},{6,14},{7,15},{8,0},{9,1},... | collective-permute-start | bytes 491528 | tf_op jit(solution)/shard_map/ppermute | solution.py:436
  131.2 8.5 %collective-permute-start.30 = (bf16[128,640]{1,0:T(8,128)(2,1)S(1)}, bf16[128,640]{1,0:T(8,128)(2,1)S(1)}, u32[]{:S(2)}, u32[]{:S(2)}) collective-permute-start(bf16[128,640]{1,0:T(8,128)(2,1)S(1)} %fusion.14), channel_id=1, source_target_pairs={{0,2},{1,3},{2,0},{3,1},{4,6},{5,7},{6,4},{7,5},{8,10},{9,11},{10,... | collective-permute-start | bytes 491528 | tf_op jit(solution)/shard_map/ppermute | solution.py:436
  150.8 8.7 %collective-permute-start.37 = (bf16[656,128]{1,0:T(8,128)(2,1)S(1)}, bf16[656,128]{1,0:T(8,128)(2,1)}, u32[]{:S(2)}, u32[]{:S(2)}) collective-permute-start(bf16[656,128]{1,0:T(8,128)(2,1)S(1)} %get-tuple-element.103.refs_4_), channel_id=1, source_target_pairs={{0,8},{1,9},{2,10},{3,11},{4,12},{5,13},{6,14},{7,15},{8,0},{9,1},... | collective-permute-start | bytes 503816 | tf_op jit(solution)/shard_map/ppermute | solution.py:436
  153.0 7.4 %collective-permute-start.39 = (bf16[656,128]{1,0:T(8,128)(2,1)S(1)}, bf16[656,128]{1,0:T(8,128)(2,1)S(1)}, u32[]{:S(2)}, u32[]{:S(2)}) collective-permute-start(bf16[656,128]{1,0:T(8,128)(2,1)S(1)} %get-tuple-element.103.refs_4_), channel_id=1, source_target_pairs={{0,1},{1,0},{2,3},{3,2},{4,5},{5,4},{6,7},{7,6},{8,9},{9,8},{10,11... | collective-permute-start | bytes 503816 | tf_op jit(solution)/shard_map/ppermute | solution.py:436
  160.3 12.1 %collective-permute-start.46 = (bf16[656,128]{1,0:T(8,128)(2,1)S(1)}, bf16[656,128]{1,0:T(8,128)(2,1)}, u32[]{:S(2)}, u32[]{:S(2)}) collective-permute-start(bf16[656,128]{1,0:T(8,128)(2,1)S(1)} %collective-permute-done.42.refs_4_), channel_id=1, source_target_pairs={{0,2},{1,3},{2,0},{3,1},{4,6},{5,7},{6,4},{7,5},{8,10},{9,11},{10,... | collective-permute-start | bytes 503816 | tf_op jit(solution)/shard_map/ppermute | solution.py:436
  166.1 36.6 %all-to-all-start.1 = ((bf16[16,144,128]{2,1,0:T(8,128)(2,1)}), bf16[16,144,128]{2,1,0:T(8,128)(2,1)S(1)}, u32[]{:S(2)}, u32[]{:S(2)}) async-start(bf16[16,144,128]{2,1,0:T(8,128)(2,1)} %copy-done.3), calls=%async_computation.1 | async-start | bytes 1179648 | tf_op jit(solution)/shard_map/all_to_all | solution.py:549
  170.7 11.6 %collective-permute-start.50 = (bf16[656,128]{1,0:T(8,128)(2,1)}, bf16[656,128]{1,0:T(8,128)(2,1)}, u32[]{:S(2)}, u32[]{:S(2)}) collective-permute-start(bf16[656,128]{1,0:T(8,128)(2,1)} %collective-permute-done.37.refs_4_), channel_id=1, source_target_pairs={{0,2},{1,3},{2,0},{3,1},{4,6},{5,7},{6,4},{7,5},{8,10},{9,11},{10,... | collective-permute-start | bytes 503816 | tf_op jit(solution)/shard_map/ppermute | solution.py:436
  172.4 10.0 %collective-permute-start.47 = (bf16[656,128]{1,0:T(8,128)(2,1)}, bf16[656,128]{1,0:T(8,128)(2,1)}, u32[]{:S(2)}, u32[]{:S(2)}) collective-permute-start(bf16[656,128]{1,0:T(8,128)(2,1)} %collective-permute-done.46.refs_6_), channel_id=1, source_target_pairs={{0,1},{1,0},{2,3},{3,2},{4,5},{5,4},{6,7},{7,6},{8,9},{9,8},{10,11... | collective-permute-start | bytes 503816 | tf_op jit(solution)/shard_map/ppermute | solution.py:436
  173.5 15.4 %collective-permute-start.49 = (bf16[656,128]{1,0:T(8,128)(2,1)}, bf16[656,128]{1,0:T(8,128)(2,1)S(1)}, u32[]{:S(2)}, u32[]{:S(2)}) collective-permute-start(bf16[656,128]{1,0:T(8,128)(2,1)} %collective-permute-done.37.refs_4_), channel_id=1, source_target_pairs={{0,1},{1,0},{2,3},{3,2},{4,5},{5,4},{6,7},{7,6},{8,9},{9,8},{10,11... | collective-permute-start | bytes 503816 | tf_op jit(solution)/shard_map/ppermute | solution.py:436
  174.0 14.3 %collective-permute-start.44 = (bf16[656,128]{1,0:T(8,128)(2,1)}, bf16[656,128]{1,0:T(8,128)(2,1)S(1)}, u32[]{:S(2)}, u32[]{:S(2)}) collective-permute-start(bf16[656,128]{1,0:T(8,128)(2,1)} %collective-permute-done.38.refs_4_), channel_id=1, source_target_pairs={{0,2},{1,3},{2,0},{3,1},{4,6},{5,7},{6,4},{7,5},{8,10},{9,11},{10,... | collective-permute-start | bytes 503816 | tf_op jit(solution)/shard_map/ppermute | solution.py:436
  174.3 20.5 %collective-permute-start.43 = (bf16[656,128]{1,0:T(8,128)(2,1)}, bf16[656,128]{1,0:T(8,128)(2,1)S(1)}, u32[]{:S(2)}, u32[]{:S(2)}) collective-permute-start(bf16[656,128]{1,0:T(8,128)(2,1)} %collective-permute-done.38.refs_4_), channel_id=1, source_target_pairs={{0,1},{1,0},{2,3},{3,2},{4,5},{5,4},{6,7},{7,6},{8,9},{9,8},{10,11... | collective-permute-start | bytes 503816 | tf_op jit(solution)/shard_map/ppermute | solution.py:436
  (42 other events, 311.9 us)

commit v4 on v3

--- a/solution.py
+++ b/solution.py
@@ -13,7 +13,7 @@
 sigma_step = 0.15
 
 GROUP = 4
-LIMIT = 48 << 20
+LIMIT = 16 << 20
 COST = 3
 META = 16
 F32 = jnp.float32
@@ -284,152 +284,113 @@
     )(*prices, balance_price, demand, recv, previous)
 
 
-def shadow_kernel(place_ref, line_ref, *refs):
-    ptdf_refs, (keep_ref, send_ref) = refs[:-2], refs[-2:]
-    step = pl.program_id(0)
-    depth = ptdf_refs[0].shape[0]
-    part = dot(line_ref[:, :depth], ptdf_refs[0][...])
-    for i, ref in enumerate(ptdf_refs[1:], 1):
-        part = part + dot(line_ref[:, i * depth : (i + 1) * depth], ref[...])
-
-    @pl.when(step == 0)
-    def _():
-        send_ref[1] = part.astype(BF16)
-
-    @pl.when(step == 1)
-    def _():
-        keep_ref[1] = part
-
-    @pl.when(step == 2)
-    def _():
-        send_ref[0] = part.astype(BF16)
-
-    @pl.when(step == 3)
-    def _():
-        keep_ref[0] = part
-
-
-def shadow_chunk(chunk, place, line_t, ptdf, buses):
+def shadow_kernel(chunk, fetch, place_ref, line_ref, ptdf_ref, keep_ref, send_ref, *rest):
+    buses = keep_ref.shape[2]
+    columns = [slice(rel * buses, (rel + 1) * buses) for rel in range(4)]
+    if fetch:
+        held_ref, sems = rest
+        copies = []
+        for rel in range(4):
+            start = pl.multiple_of((place_ref[0] ^ (4 * chunk + rel)) * buses, 128)
+            copies.append(
+                pltpu.make_async_copy(
+                    ptdf_ref.at[:, pl.ds(start, buses)], held_ref.at[:, pl.ds(rel * buses, buses)], sems.at[rel]
+                )
+            )
+        for rel in (3, 2, 1, 0):
+            copies[rel].start()
+    else:
+        held_ref = ptdf_ref
+
+    def part(rel):
+        if fetch:
+            copies[rel].wait()
+        return dot(line_ref[...], held_ref[:, columns[rel]])
+
+    send_ref[1] = part(3).astype(BF16)
+    keep_ref[1] = part(2)
+    send_ref[0] = part(1).astype(BF16)
+    keep_ref[0] = part(0)
+
+
+def shadow_chunk(chunk, fetch, place, line_t, ptdf, buses):
     hours, lines = line_t.shape
-    pieces = 5
+    vmem = pl.BlockSpec(memory_space=pltpu.VMEM)
+    out_shape = [
+        jax.ShapeDtypeStruct((2, hours, buses), F32),
+        jax.ShapeDtypeStruct((2, hours, buses), BF16),
+    ]
+    if fetch:
+        out_shape.append(pltpu.VMEM((lines, 4 * buses), BF16))
     return pl.pallas_call(
-        shadow_kernel,
-        grid_spec=pltpu.PrefetchScalarGridSpec(
-            num_scalar_prefetch=1,
-            grid=(4,),
-            in_specs=[
-                pl.BlockSpec((hours, lines), lambda i, place: (0, 0)),
-            ]
-            + [
-                pl.BlockSpec((lines // pieces, buses), lambda i, place, p=p: (p, place[0] ^ (4 * chunk + 3 - i)))
-                for p in range(pieces)
-            ],
-            out_specs=(
-                pl.BlockSpec((2, hours, buses), lambda i, place: (0, 0, 0)),
-                pl.BlockSpec((2, hours, buses), lambda i, place: (0, 0, 0)),
-            ),
-        ),
-        out_shape=(
-            jax.ShapeDtypeStruct((2, hours, buses), F32),
-            jax.ShapeDtypeStruct((2, hours, buses), BF16),
-        ),
+        functools.partial(shadow_kernel, chunk, fetch),
+        in_specs=[pl.BlockSpec(memory_space=pltpu.SMEM), vmem, pl.BlockSpec(memory_space=pltpu.MemorySpace.HBM) if fetch else vmem],
+        out_specs=tuple([vmem] * len(out_shape)),
+        out_shape=tuple(out_shape),
+        scratch_shapes=[pltpu.SemaphoreType.DMA((4,))] if fetch else [],
         compiler_params=pltpu.CompilerParams(vmem_limit_bytes=LIMIT),
         cost_estimate=pl.CostEstimate(
             flops=COST * 8 * hours * lines * buses, bytes_accessed=8 * lines * buses, transcendentals=0
         ),
         name="shadow_chunk",
-    )(place, line_t, *[ptdf] * pieces)
-
-
-def flow_kernel(start, end, pieces, place_ref, *refs):
-    ptdf_refs = refs[:pieces]
-    b0, b1, b2, b3, acc_ref, sum_ref, *rest = refs[pieces:]
-    step = pl.program_id(0)
+    )(place, line_t, pltpu.with_memory_space_constraint(ptdf, pltpu.MemorySpace.HBM) if fetch else ptdf)
+
+
+def flow_kernel(start, end, ptdf_ref, b0, b1, b2, b3, acc_ref, sum_ref, *rest):
     if end:
         limit_ref, line_ref, out_ref, half_ref, sum_out, inj_ref = rest
     else:
         out_ref, sum_out, inj_ref = rest
     buses = inj_ref.shape[0] // 4
-
-    @pl.when(step == 0)
-    def _():
-        total = jnp.zeros(sum_ref.shape, F32) if start else sum_ref[...]
-        for rel, ref in enumerate((b0, b1, b2, b3)):
-            offset = pl.multiple_of(((place_ref[0] ^ rel) & 3) * buses, META)
-            inj_ref[pl.ds(offset, buses), :] = ref[:buses, :]
-            tail = ref[buses:, :].astype(F32)
-            total = total + jnp.sum(tail, axis=0, keepdims=True)
-        sum_out[...] = total
-
-    tile, depth = ptdf_refs[0].shape
-    inj = inj_ref[pl.ds(pl.multiple_of(step * depth, depth), depth), :]
-    parts = [dot(ref[...], inj) for ref in ptdf_refs]
-
-    @pl.when(step == 0)
-    def _():
-        for i, part in enumerate(parts):
-            rows = slice(i * tile, (i + 1) * tile)
-            out_ref[rows, :] = part if start else acc_ref[rows, :] + part
-
-    @pl.when(step > 0)
-    def _():
-        for i, part in enumerate(parts):
-            out_ref[i * tile : (i + 1) * tile, :] += part
-
-    if end:
-
-        @pl.when(step == pl.num_programs(0) - 1)
-        def _():
-            shifted = line_ref[...] + sigma_step * out_ref[...]
-            limit = limit_ref[...]
+    total = jnp.zeros(sum_ref.shape, F32) if start else sum_ref[...]
+    for rel, ref in enumerate((b0, b1, b2, b3)):
+        inj_ref[rel * buses : (rel + 1) * buses, :] = ref[:buses, :]
+        tail = ref[buses:, :].astype(F32)
+        total = total + jnp.sum(tail, axis=0, keepdims=True)
+    sum_out[...] = total
+    tile = ptdf_ref.shape[0] // 4
+
+    def body(i, carry):
+        rows = pl.ds(pl.multiple_of(i * tile, tile), tile)
+        flow = dot(ptdf_ref[rows, :], inj_ref[...])
+        if not start:
+            flow = flow + acc_ref[rows, :]
+        if end:
+            shifted = line_ref[rows, :] + sigma_step * flow
+            limit = limit_ref[rows, :]
             line = shifted - sigma_step * jnp.minimum(jnp.maximum(shifted / sigma_step, -limit), limit)
-            out_ref[...] = line
-            half_ref[...] = line.astype(BF16)
-
-
-def flow_chunk(chunk, place, ptdf, blocks, acc, total, limit=None, line=None):
+            out_ref[rows, :] = line
+            half_ref[rows, :] = line.astype(BF16)
+        else:
+            out_ref[rows, :] = flow
+        return carry
+
+    lax.fori_loop(0, 4, body, 0)
+
+
+def flow_chunk(ptdf, blocks, acc, total, limit=None, line=None):
     lines = ptdf.shape[0]
     rows, hours = blocks[0].shape
     buses = rows - META
     start, end = acc is None, limit is not None
-    steps, pieces = 5, 4
-    depth = 4 * buses // steps
-    full = lambda *shape: pl.BlockSpec(shape, lambda i, place: (0,) * len(shape))
-    if start:
-        acc, acc_spec = total, full(1, hours)
-    else:
-        acc_spec = full(lines, hours)
-    operands = [ptdf] * pieces + [*blocks, acc, total]
-    in_specs = [
-        pl.BlockSpec((lines // pieces, depth), lambda i, place, p=p: (p, ((place[0] >> 2) ^ chunk) * steps + i))
-        for p in range(pieces)
-    ]
-    in_specs += [full(rows, hours)] * 4 + [acc_spec, full(1, hours)]
+    operands = [ptdf, *blocks, total if start else acc, total]
     out_shape = [jax.ShapeDtypeStruct((lines, hours), F32)]
-    out_specs = [full(lines, hours)]
     if end:
         operands += [limit, line]
-        in_specs += [full(lines, 1), full(lines, hours)]
         out_shape += [jax.ShapeDtypeStruct((lines, hours), BF16)]
-        out_specs += [full(lines, hours)]
     out_shape += [jax.ShapeDtypeStruct((1, hours), F32)]
-    out_specs += [full(1, hours)]
+    in_specs = [pl.BlockSpec(memory_space=pltpu.VMEM)] * len(operands)
     return pl.pallas_call(
-        functools.partial(flow_kernel, start, end, pieces),
-        grid_spec=pltpu.PrefetchScalarGridSpec(
-            num_scalar_prefetch=1,
-            grid=(steps,),
-            in_specs=in_specs,
-            out_specs=tuple(out_specs),
-            scratch_shapes=[pltpu.VMEM((4 * buses, hours), BF16)],
-        ),
+        functools.partial(flow_kernel, start, end),
+        in_specs=in_specs,
         out_shape=tuple(out_shape),
+        scratch_shapes=[pltpu.VMEM((4 * buses, hours), BF16)],
         compiler_params=pltpu.CompilerParams(vmem_limit_bytes=LIMIT),
         cost_estimate=pl.CostEstimate(
             flops=COST * 8 * hours * lines * buses, bytes_accessed=8 * lines * buses, transcendentals=0
         ),
         name="flow_chunk",
-    )(place, *operands)
+    )(*operands)
 
 
 def swap(x, devices, mask):
@@ -472,7 +433,7 @@
     line_half = line_price.astype(BF16)
     recv = lax.all_to_all(outgoing, "bus", split_axis=0, concat_axis=0, tiled=True)
     slot = None if staged else slot_column(devices, cap, gen_owner)
-    held = None
+    held, resident = None, {}
     for iteration in range(ITERS):
         last = iteration == ITERS - 1
         if staged:
@@ -496,7 +457,10 @@
                 return part
 
             def product(chunk, line_t):
-                keeps[chunk], send = shadow_chunk(chunk, place, line_t, ptdf, buses)
+                if chunk in resident:
+                    keeps[chunk], send = shadow_chunk(chunk, False, place, line_t, resident[chunk], buses)
+                else:
+                    keeps[chunk], send, resident[chunk] = shadow_chunk(chunk, True, place, line_t, ptdf, buses)
                 gots[chunk] = swap(send, devices, 1)
 
             product(3, line_t)
@@ -538,7 +502,7 @@
             spread(2)
             settle_far(0)
             near[1], near[2], row = lax.optimization_barrier((near[1], near[2], balance_row))
-            acc, total = flow_chunk(0, place, ptdf, blocks(0), None, row)
+            acc, total = flow_chunk(resident[0], blocks(0), None, row)
             if iteration == 0:
                 owner, acc = lax.optimization_barrier((gen_owner, acc))
                 slot = slot_column(devices, cap, owner)
@@ -548,13 +512,13 @@
                 held, _ = lax.optimization_barrier((held, near[3]))
                 back = lax.all_to_all(held, "bus", split_axis=0, concat_axis=0, tiled=True)
             settle_far(1)
-            acc, total = flow_chunk(1, place, ptdf, blocks(1), acc, total)
+            acc, total = flow_chunk(resident[1], blocks(1), acc, total)
             settle_far(2)
             far[3], acc = lax.optimization_barrier((far[3], acc))
-            acc, total = flow_chunk(2, place, ptdf, blocks(2), acc, total)
+            acc, total = flow_chunk(resident[2], blocks(2), acc, total)
             settle_far(3)
             line_price, line_half, total = flow_chunk(
-                3, place, ptdf, blocks(3), acc, total, limit, line_price
+                resident[3], blocks(3), acc, total, limit, line_price
             )
             balance = total
         else:

time: 206 us -> 200 us (0.971)
  Pallas kernels: 102 us -> 61.2 us
  local copies, waits for them, and re-layouts: 3.1 us -> 40.6 us
  waiting for transfers between devices: 48 us -> 43.4 us
  starting transfers between devices: 46.9 us -> 49.5 us
    pallas_call x16, Pallas kernels: 83.3 us -> 41.7 us  [the longest x8 23.1 us: flow_chunk(): pl.pallas_call(functools.partial(flow_kernel, start, end), in_specs=in_sp...]
    unnamed x41 -> x79, local copies, waits for them, and re-layouts: 2.36 us -> 39.9 us
    ppermute x52, waiting for transfers between devices: 48 us -> 43.4 us  [swap(): return lax.ppermute(x, 'bus', [(i, i ^ mask) for i in range(devices)])]
    ppermute x52, starting transfers between devices: 35.7 us -> 38.9 us  [swap(): return lax.ppermute(x, 'bus', [(i, i ^ mask) for i in range(devices)])]
  transfers between devices with their start and end apart: 54 -> 54, of which waited for: 18 -> 18; matrix products, arithmetic and copies ran while one was open for 2% -> 2% of each run, Pallas kernels for 35% -> 19%
where the time goes in v4:
time: 200 us; the launch traced here: 199 us
  Pallas kernels  61.2 us (31%)
  starting transfers between devices  49.5 us (25%)
  waiting for transfers between devices  43.4 us (22%)
  local copies, waits for them, and re-layouts  40.6 us (20%)
  other arithmetic  3.18 us (2%)
    ppermute x52, waiting for transfers between devices, swap(): return lax.ppermute(x, 'bus', [(i, i ^ mask) for i in range(devices)])  43.4 us
    unnamed x79, local copies, waits for them, and re-layouts  39.9 us
    ppermute x52, starting transfers between devices, swap(): return lax.ppermute(x, 'bus', [(i, i ^ mask) for i in range(devices)])  38.9 us
    pallas_call x8, Pallas kernels, flow_chunk(): pl.pallas_call(functools.partial(flow_kernel, start, end), in_specs=in_sp...  23.1 us
    pallas_call x8, Pallas kernels, shadow_chunk(): pl.pallas_call(functools.partial(shadow_kernel, chunk, fetch), in_specs=[...  18.5 us
    pallas_call x2, Pallas kernels, update(): pl.pallas_call(functools.partial(update_kernel, cap, first, last, len(pri...  13.4 us
    all_to_all x1, starting transfers between devices, local(): lax.all_to_all(outgoing, 'bus', split_axis=0, concat_axis=0, tiled=True)  7.06 us
  transfers between devices with their start and end apart: 54, of which 18 were waited for; matrix products, arithmetic and copies ran while one was open for 2% of the time, Pallas kernels for 19%

profile of v4, /device:TPU:0, one launch (start us, length us, event | category | flops | bytes accessed | tf_op | source)
XLA Modules:
  0.0 199.3 jit_solution(12119745066111657069)
XLA Ops:
  2.0 3.5 %shadow_chunk.8 = (f32[2,128,640]{2,1,0:T(8,128)S(1)}, bf16[2,128,640]{2,1,0:T(8,128)(2,1)S(1)}, bf16[1280,2560]{1,0:T(8,128)(2,1)S(1)}) custom-call(s32[1]{0:T(128)} %bitcast.place_ref, bf16[128,1280]{1,0:T(8,128)(2,1)S(1)} %bitcast.62, bf16[1280,10240]{1,0:T(8,128)(2,1)} %ptdf_ref.7), custom_call_target="tpu_custom_call" | custom-call | flops 2516582400 | bytes 6553600 | tf_op jit(solution)/shard_map/shadow_chunk/pallas_call | solution.py:325
  5.5 2.7 %copy-done.4 = bf16[1280,2560]{1,0:T(8,128)(2,1)} copy-done((bf16[1280,2560]{1,0:T(8,128)(2,1)}, bf16[1280,2560]{1,0:T(8,128)(2,1)S(1)}, u32[]{:S(2)}) %copy-start.4) | copy-done | bytes 6553624
  8.7 3.6 %pack_generators.1 = bf16[16,160,256]{2,1,0:T(8,128)(2,1)} custom-call(s32[6,128]{1,0:T(8,128)S(1)} %bitcast.72, s32[6,128]{1,0:T(8,128)S(1)} %bitcast.81, f32[6,128]{1,0:T(8,128)S(1)} %bitcast.82, f32[768,128]{1,0:T(8,128)S(1)} %copy-done.1, f32[6,128]{1,0:T(8,128)S(1)} %bitcast.71, f32[768,128]{1,0:T(8,128)S(1)} %copy-done.2), custom_call_target="tpu_custom_call" | custom-call | flops 905969664 | bytes 3145728 | tf_op jit(solution)/shard_map/pack_generators/pallas_call | solution.py:100
  12.2 7.1 %all-to-all-start = ((bf16[16,160,256]{2,1,0:T(8,128)(2,1)}), bf16[16,160,256]{2,1,0:T(8,128)(2,1)S(1)}, u32[]{:S(2)}, u32[]{:S(2)}) async-start(bf16[16,160,256]{2,1,0:T(8,128)(2,1)} %pack_generators.1), calls=%async_computation | async-start | bytes 2621440 | tf_op jit(solution)/shard_map/all_to_all | solution.py:434
  19.3 3.4 %shadow_chunk.9 = (f32[2,128,640]{2,1,0:T(8,128)S(1)}, bf16[2,128,640]{2,1,0:T(8,128)(2,1)S(1)}, bf16[1280,2560]{1,0:T(8,128)(2,1)S(1)}) custom-call(s32[1]{0:T(128)} %bitcast.place_ref, bf16[128,1280]{1,0:T(8,128)(2,1)S(1)} %bitcast.63, bf16[1280,10240]{1,0:T(8,128)(2,1)} %ptdf_ref.7), custom_call_target="tpu_custom_call" | custom-call | flops 2516582400 | bytes 6553600 | tf_op jit(solution)/shard_map/shadow_chunk/pallas_call | solution.py:325
  22.8 2.8 %copy-done.6 = bf16[1280,2560]{1,0:T(8,128)(2,1)} copy-done((bf16[1280,2560]{1,0:T(8,128)(2,1)}, bf16[1280,2560]{1,0:T(8,128)(2,1)S(1)}, u32[]{:S(2)}) %copy-start.6) | copy-done | bytes 6553624
  28.6 3.4 %shadow_chunk.11 = (f32[2,128,640]{2,1,0:T(8,128)S(1)}, bf16[2,128,640]{2,1,0:T(8,128)(2,1)S(1)}, bf16[1280,2560]{1,0:T(8,128)(2,1)S(1)}) custom-call(s32[1]{0:T(128)} %bitcast.place_ref, bf16[128,1280]{1,0:T(8,128)(2,1)S(1)} %bitcast.64, bf16[1280,10240]{1,0:T(8,128)(2,1)} %ptdf_ref.7), custom_call_target="tpu_custom_call" | custom-call | flops 2516582400 | bytes 6553600 | tf_op jit(solution)/shard_map/shadow_chunk/pallas_call | solution.py:325
  39.0 3.4 %shadow_chunk.10 = (f32[2,128,640]{2,1,0:T(8,128)S(1)}, bf16[2,128,640]{2,1,0:T(8,128)(2,1)S(1)}, bf16[1280,2560]{1,0:T(8,128)(2,1)S(1)}) custom-call(s32[1]{0:T(128)} %bitcast.place_ref, bf16[128,1280]{1,0:T(8,128)(2,1)S(1)} %bitcast.65, bf16[1280,10240]{1,0:T(8,128)(2,1)} %ptdf_ref.7), custom_call_target="tpu_custom_call" | custom-call | flops 2516582400 | bytes 6553600 | tf_op jit(solution)/shard_map/shadow_chunk/pallas_call | solution.py:325
  42.5 2.8 %copy-done.13 = bf16[1280,2560]{1,0:T(8,128)(2,1)} copy-done((bf16[1280,2560]{1,0:T(8,128)(2,1)}, bf16[1280,2560]{1,0:T(8,128)(2,1)S(1)}, u32[]{:S(2)}) %copy-start.13) | copy-done | bytes 6553624
  46.2 3.7 %collective-permute-start.10 = (bf16[128,640]{1,0:T(8,128)(2,1)S(1)}, bf16[128,640]{1,0:T(8,128)(2,1)S(1)}, u32[]{:S(2)}, u32[]{:S(2)}) collective-permute-start(bf16[128,640]{1,0:T(8,128)(2,1)S(1)} %fusion.5), channel_id=1, source_target_pairs={{0,8},{1,9},{2,10},{3,11},{4,12},{5,13},{6,14},{7,15},{8,0},{9,1},... | collective-permute-start | bytes 491528 | tf_op jit(solution)/shard_map/ppermute | solution.py:397
  52.0 2.8 %collective-permute-start.7 = (bf16[128,640]{1,0:T(8,128)(2,1)S(1)}, bf16[128,640]{1,0:T(8,128)(2,1)S(1)}, u32[]{:S(2)}, u32[]{:S(2)}) collective-permute-start(bf16[128,640]{1,0:T(8,128)(2,1)S(1)} %fusion.6), channel_id=1, source_target_pairs={{0,4},{1,5},{2,6},{3,7},{4,0},{5,1},{6,2},{7,3},{8,12},{9,13},{10,... | collective-permute-start | bytes 491528 | tf_op jit(solution)/shard_map/ppermute | solution.py:397
  60.0 6.3 %update_generators.2 = (f32[16,144,128]{2,1,0:T(8,128)S(1)}, bf16[656,128]{1,0:T(8,128)(2,1)S(1)}) custom-call(f32[128,640]{1,0:T(8,128)S(1)} %bitcast_add_fusion.6.refs_0_, bf16[128,640]{1,0:T(8,128)(2,1)S(1)} %collective-permute-done.7.refs_1_, bf16[128,640]{1,0:T(8,128)(2,1)S(1)} %collective-permute-done.10.refs_2_, f32[1,128]{1,0:T(1,128)S(1)} %bitcast.83, ...), custom_call_target="tpu_custom_call" | custom-call | flops 1509949440 | bytes 4194304 | tf_op jit(solution)/shard_map/update_generators/pallas_call | solution.py:261
  67.4 3.1 %collective-permute-start.12 = (bf16[656,128]{1,0:T(8,128)(2,1)S(1)}, bf16[656,128]{1,0:T(8,128)(2,1)S(1)}, u32[]{:S(2)}, u32[]{:S(2)}) collective-permute-start(bf16[656,128]{1,0:T(8,128)(2,1)S(1)} %get-tuple-element.78.b0), channel_id=1, source_target_pairs={{0,2},{1,3},{2,0},{3,1},{4,6},{5,7},{6,4},{7,5},{8,10},{9,11},{10,... | collective-permute-start | bytes 503816 | tf_op jit(solution)/shard_map/ppermute | solution.py:397
  74.4 4.8 %collective-permute-done.14.b0 = bf16[656,128]{1,0:T(8,128)(2,1)S(1)} collective-permute-done((bf16[656,128]{1,0:T(8,128)(2,1)S(1)}, bf16[656,128]{1,0:T(8,128)(2,1)S(1)}, u32[]{:S(2)}, u32[]{:S(2)}) %collective-permute-start.14) | collective-permute-done | bytes 167968 | tf_op jit(solution)/shard_map/ppermute | solution.py:397
  84.8 3.0 %copy-done.14 = bf16[1280,2560]{1,0:T(8,128)(2,1)S(1)} copy-done((bf16[1280,2560]{1,0:T(8,128)(2,1)S(1)}, bf16[1280,2560]{1,0:T(8,128)(2,1)}, u32[]{:S(2)}) %copy-start.14) | copy-done | bytes 6553624
  91.0 3.0 %copy-done.10 = bf16[1280,2560]{1,0:T(8,128)(2,1)S(1)} copy-done((bf16[1280,2560]{1,0:T(8,128)(2,1)S(1)}, bf16[1280,2560]{1,0:T(8,128)(2,1)}, u32[]{:S(2)}) %copy-start.10) | copy-done | bytes 6553624
  99.6 2.7 %flow_chunk.11 = (f32[1280,128]{1,0:T(8,128)S(1)}, bf16[1280,128]{1,0:T(8,128)(2,1)S(1)}, f32[1,128]{1,0:T(1,128)S(1)}) custom-call(bf16[1280,2560]{1,0:T(8,128)(2,1)S(1)} %bitcast.74, bf16[656,128]{1,0:T(8,128)(2,1)S(1)} %collective-permute-done.16.b0, bf16[656,128]{1,0:T(8,128)(2,1)S(1)} %collective-permute-done.17.b1, ...), custom_call_target="tpu_custom_call" | custom-call | flops 2516582400 | bytes 6553600 | tf_op jit(solution)/shard_map/flow_chunk/pallas_call | solution.py:383
  103.4 2.9 %copy-done.5 = bf16[1280,2560]{1,0:T(8,128)(2,1)S(1)} copy-done((bf16[1280,2560]{1,0:T(8,128)(2,1)S(1)}, bf16[1280,2560]{1,0:T(8,128)(2,1)}, u32[]{:S(2)}) %copy-start.5) | copy-done | bytes 6553624
  108.0 2.9 %copy-done.7 = bf16[1280,2560]{1,0:T(8,128)(2,1)S(1)} copy-done((bf16[1280,2560]{1,0:T(8,128)(2,1)S(1)}, bf16[1280,2560]{1,0:T(8,128)(2,1)}, u32[]{:S(2)}) %copy-start.7) | copy-done | bytes 6553624
  115.2 2.9 %copy-done.11 = bf16[1280,2560]{1,0:T(8,128)(2,1)S(1)} copy-done((bf16[1280,2560]{1,0:T(8,128)(2,1)S(1)}, bf16[1280,2560]{1,0:T(8,128)(2,1)}, u32[]{:S(2)}) %copy-start.11) | copy-done | bytes 6553624
  119.9 2.9 %copy-done.15 = bf16[1280,2560]{1,0:T(8,128)(2,1)S(1)} copy-done((bf16[1280,2560]{1,0:T(8,128)(2,1)S(1)}, bf16[1280,2560]{1,0:T(8,128)(2,1)}, u32[]{:S(2)}) %copy-start.15) | copy-done | bytes 6553624
  129.8 5.0 %collective-permute-done.32 = bf16[128,640]{1,0:T(8,128)(2,1)S(1)} collective-permute-done((bf16[128,640]{1,0:T(8,128)(2,1)S(1)}, bf16[128,640]{1,0:T(8,128)(2,1)S(1)}, u32[]{:S(2)}, u32[]{:S(2)}) %collective-permute-start.32) | collective-permute-done | bytes 163872 | tf_op jit(solution)/shard_map/ppermute | solution.py:397
  136.8 3.5 %collective-permute-done.33.refs_1_ = bf16[128,640]{1,0:T(8,128)(2,1)S(1)} collective-permute-done((bf16[128,640]{1,0:T(8,128)(2,1)S(1)}, bf16[128,640]{1,0:T(8,128)(2,1)S(1)}, u32[]{:S(2)}, u32[]{:S(2)}) %collective-permute-start.33) | collective-permute-done | bytes 163872 | tf_op jit(solution)/shard_map/ppermute | solution.py:397
  140.2 7.0 %update_generators.3 = (bf16[16,144,128]{2,1,0:T(8,128)(2,1)}, bf16[656,128]{1,0:T(8,128)(2,1)S(1)}) custom-call(f32[128,640]{1,0:T(8,128)S(1)} %bitcast_add_fusion.2.refs_0_, bf16[128,640]{1,0:T(8,128)(2,1)S(1)} %collective-permute-done.33.refs_1_, bf16[128,640]{1,0:T(8,128)(2,1)S(1)} %collective-permute-done.36.refs_2_, ...), custom_call_target="tpu_custom_call" | custom-call | flops 1509949440 | bytes 4194304 | tf_op jit(solution)/shard_map/update_generators/pallas_call | solution.py:261
  152.6 3.4 %collective-permute-done.37.b0 = bf16[656,128]{1,0:T(8,128)(2,1)S(1)} collective-permute-done((bf16[656,128]{1,0:T(8,128)(2,1)S(1)}, bf16[656,128]{1,0:T(8,128)(2,1)S(1)}, u32[]{:S(2)}, u32[]{:S(2)}) %collective-permute-start.37) | collective-permute-done | bytes 167968 | tf_op jit(solution)/shard_map/ppermute | solution.py:397
  163.1 3.6 %all-to-all-start.1 = ((bf16[16,144,128]{2,1,0:T(8,128)(2,1)}), bf16[16,144,128]{2,1,0:T(8,128)(2,1)S(1)}, u32[]{:S(2)}, u32[]{:S(2)}) async-start(bf16[16,144,128]{2,1,0:T(8,128)(2,1)} %get-tuple-element.115), calls=%async_computation.1 | async-start | bytes 1179648 | tf_op jit(solution)/shard_map/all_to_all | solution.py:513
  170.6 8.0 %collective-permute-done.50.b2 = bf16[656,128]{1,0:T(8,128)(2,1)} collective-permute-done((bf16[656,128]{1,0:T(8,128)(2,1)S(1)}, bf16[656,128]{1,0:T(8,128)(2,1)}, u32[]{:S(2)}, u32[]{:S(2)}) %collective-permute-start.50) | collective-permute-done | bytes 167968 | tf_op jit(solution)/shard_map/ppermute | solution.py:397
  178.6 2.9 %copy-done.12 = bf16[1280,2560]{1,0:T(8,128)(2,1)S(1)} copy-done((bf16[1280,2560]{1,0:T(8,128)(2,1)S(1)}, bf16[1280,2560]{1,0:T(8,128)(2,1)}, u32[]{:S(2)}) %copy-start.12) | copy-done | bytes 6553624
  182.6 3.7 %flow_chunk.13 = (f32[1280,128]{1,0:T(8,128)S(1)}, f32[1,128]{1,0:T(1,128)S(1)}) custom-call(bf16[1280,2560]{1,0:T(8,128)(2,1)S(1)} %copy-done.12, bf16[656,128]{1,0:T(8,128)(2,1)} %collective-permute-done.42.b0, bf16[656,128]{1,0:T(8,128)(2,1)} %collective-permute-done.45.b1, bf16[656,128]{1,0:T(8,128)(2,1)} %collective-permute-done.46.b2, ...), custom_call_target="tpu_custom_call" | custom-call | flops 2516582400 | bytes 6553600 | tf_op jit(solution)/shard_map/flow_chunk/pallas_call | solution.py:383
  186.9 2.9 %copy-done.8 = bf16[1280,2560]{1,0:T(8,128)(2,1)S(1)} copy-done((bf16[1280,2560]{1,0:T(8,128)(2,1)S(1)}, bf16[1280,2560]{1,0:T(8,128)(2,1)}, u32[]{:S(2)}) %copy-start.8) | copy-done | bytes 6553624
  189.8 3.5 %flow_chunk.14 = (f32[1280,128]{1,0:T(8,128)S(1)}, f32[1,128]{1,0:T(1,128)S(1)}) custom-call(bf16[1280,2560]{1,0:T(8,128)(2,1)S(1)} %copy-done.8, bf16[656,128]{1,0:T(8,128)(2,1)S(1)} %collective-permute-done.37.b0, bf16[656,128]{1,0:T(8,128)(2,1)S(1)} %collective-permute-done.49.b1, bf16[656,128]{1,0:T(8,128)(2,1)} %collective-permute-done.50.b2, ...), custom_call_target="tpu_custom_call" | custom-call | flops 2516582400 | bytes 6553600 | tf_op jit(solution)/shard_map/flow_chunk/pallas_call | solution.py:383
  193.4 3.4 %flow_chunk.15 = (f32[1280,128]{1,0:T(8,128)}, bf16[1280,128]{1,0:T(8,128)(2,1)}, f32[1,128]{1,0:T(1,128)S(1)}) custom-call(bf16[1280,2560]{1,0:T(8,128)(2,1)S(1)} %bitcast.76, bf16[656,128]{1,0:T(8,128)(2,1)S(1)} %copy-done.19, bf16[656,128]{1,0:T(8,128)(2,1)S(1)} %collective-permute-done.43.b1, bf16[656,128]{1,0:T(8,128)(2,1)S(1)} %collective-permute-done.44.b2, ...), custom_call_target="tpu_custom_call" | custom-call | flops 2516582400 | bytes 6553600 | tf_op jit(solution)/shard_map/flow_chunk/pallas_call | solution.py:383
  (203 shorter events, 77.5 us)
Async XLA Ops:
  8.1 17.8 %collective-permute-start = (bf16[2,128,640]{2,1,0:T(8,128)(2,1)S(1)}, bf16[2,128,640]{2,1,0:T(8,128)(2,1)}, u32[]{:S(2)}, u32[]{:S(2)}) collective-permute-start(bf16[2,128,640]{2,1,0:T(8,128)(2,1)S(1)} %get-tuple-element.68), channel_id=1, source_target_pairs={{0,1},{1,0},{2,3},{3,2},{4,5},{5,4},{6,7},{7,6},{8,9},{9,8},{10,11... | collective-permute-start | bytes 983048 | tf_op jit(solution)/shard_map/ppermute | solution.py:397
  12.2 47.8 %all-to-all-start = ((bf16[16,160,256]{2,1,0:T(8,128)(2,1)}), bf16[16,160,256]{2,1,0:T(8,128)(2,1)S(1)}, u32[]{:S(2)}, u32[]{:S(2)}) async-start(bf16[16,160,256]{2,1,0:T(8,128)(2,1)} %pack_generators.1), calls=%async_computation | async-start | bytes 2621440 | tf_op jit(solution)/shard_map/all_to_all | solution.py:434
  25.5 9.3 %collective-permute-start.1 = (bf16[2,128,640]{2,1,0:T(8,128)(2,1)S(1)}, bf16[2,128,640]{2,1,0:T(8,128)(2,1)S(1)}, u32[]{:S(2)}, u32[]{:S(2)}) collective-permute-start(bf16[2,128,640]{2,1,0:T(8,128)(2,1)S(1)} %get-tuple-element.71), channel_id=1, source_target_pairs={{0,1},{1,0},{2,3},{3,2},{4,5},{5,4},{6,7},{7,6},{8,9},{9,8},{10,11... | collective-permute-start | bytes 983048 | tf_op jit(solution)/shard_map/ppermute | solution.py:397
  26.9 10.3 %collective-permute-start.2 = (bf16[128,640]{1,0:T(8,128)(2,1)S(1)}, bf16[128,640]{1,0:T(8,128)(2,1)S(1)}, u32[]{:S(2)}, u32[]{:S(2)}) collective-permute-start(bf16[128,640]{1,0:T(8,128)(2,1)S(1)} %fusion.8), channel_id=1, source_target_pairs={{0,2},{1,3},{2,0},{3,1},{4,6},{5,7},{6,4},{7,5},{8,10},{9,11},{10,... | collective-permute-start | bytes 491528 | tf_op jit(solution)/shard_map/ppermute | solution.py:397
  34.7 10.5 %collective-permute-start.5 = (bf16[2,128,640]{2,1,0:T(8,128)(2,1)S(1)}, bf16[2,128,640]{2,1,0:T(8,128)(2,1)S(1)}, u32[]{:S(2)}, u32[]{:S(2)}) collective-permute-start(bf16[2,128,640]{2,1,0:T(8,128)(2,1)S(1)} %get-tuple-element.77), channel_id=1, source_target_pairs={{0,1},{1,0},{2,3},{3,2},{4,5},{5,4},{6,7},{7,6},{8,9},{9,8},{10,11... | collective-permute-start | bytes 983048 | tf_op jit(solution)/shard_map/ppermute | solution.py:397
  34.9 11.3 %collective-permute-start.8 = (bf16[128,640]{1,0:T(8,128)(2,1)S(1)}, bf16[128,640]{1,0:T(8,128)(2,1)S(1)}, u32[]{:S(2)}, u32[]{:S(2)}) collective-permute-start(bf16[128,640]{1,0:T(8,128)(2,1)S(1)} %fusion.9), channel_id=1, source_target_pairs={{0,2},{1,3},{2,0},{3,1},{4,6},{5,7},{6,4},{7,5},{8,10},{9,11},{10,... | collective-permute-start | bytes 491528 | tf_op jit(solution)/shard_map/ppermute | solution.py:397
  38.2 8.0 %collective-permute-start.9 = (bf16[128,640]{1,0:T(8,128)(2,1)S(1)}, bf16[128,640]{1,0:T(8,128)(2,1)S(1)}, u32[]{:S(2)}, u32[]{:S(2)}) collective-permute-start(bf16[128,640]{1,0:T(8,128)(2,1)S(1)} %fusion.7), channel_id=1, source_target_pairs={{0,4},{1,5},{2,6},{3,7},{4,0},{5,1},{6,2},{7,3},{8,12},{9,13},{10,... | collective-permute-start | bytes 491528 | tf_op jit(solution)/shard_map/ppermute | solution.py:397
  46.2 12.4 %collective-permute-start.10 = (bf16[128,640]{1,0:T(8,128)(2,1)S(1)}, bf16[128,640]{1,0:T(8,128)(2,1)S(1)}, u32[]{:S(2)}, u32[]{:S(2)}) collective-permute-start(bf16[128,640]{1,0:T(8,128)(2,1)S(1)} %fusion.5), channel_id=1, source_target_pairs={{0,8},{1,9},{2,10},{3,11},{4,12},{5,13},{6,14},{7,15},{8,0},{9,1},... | collective-permute-start | bytes 491528 | tf_op jit(solution)/shard_map/ppermute | solution.py:397
  52.0 8.0 %collective-permute-start.7 = (bf16[128,640]{1,0:T(8,128)(2,1)S(1)}, bf16[128,640]{1,0:T(8,128)(2,1)S(1)}, u32[]{:S(2)}, u32[]{:S(2)}) collective-permute-start(bf16[128,640]{1,0:T(8,128)(2,1)S(1)} %fusion.6), channel_id=1, source_target_pairs={{0,4},{1,5},{2,6},{3,7},{4,0},{5,1},{6,2},{7,3},{8,12},{9,13},{10,... | collective-permute-start | bytes 491528 | tf_op jit(solution)/shard_map/ppermute | solution.py:397
  70.5 8.7 %collective-permute-start.14 = (bf16[656,128]{1,0:T(8,128)(2,1)S(1)}, bf16[656,128]{1,0:T(8,128)(2,1)S(1)}, u32[]{:S(2)}, u32[]{:S(2)}) collective-permute-start(bf16[656,128]{1,0:T(8,128)(2,1)S(1)} %get-tuple-element.78.b0), channel_id=1, source_target_pairs={{0,4},{1,5},{2,6},{3,7},{4,0},{5,1},{6,2},{7,3},{8,12},{9,13},{10,... | collective-permute-start | bytes 503816 | tf_op jit(solution)/shard_map/ppermute | solution.py:397
  70.5 10.4 %collective-permute-start.15 = (bf16[656,128]{1,0:T(8,128)(2,1)S(1)}, bf16[656,128]{1,0:T(8,128)(2,1)S(1)}, u32[]{:S(2)}, u32[]{:S(2)}) collective-permute-start(bf16[656,128]{1,0:T(8,128)(2,1)S(1)} %get-tuple-element.78.b0), channel_id=1, source_target_pairs={{0,8},{1,9},{2,10},{3,11},{4,12},{5,13},{6,14},{7,15},{8,0},{9,1},... | collective-permute-start | bytes 503816 | tf_op jit(solution)/shard_map/ppermute | solution.py:397
  73.0 8.2 %collective-permute-start.11 = (bf16[656,128]{1,0:T(8,128)(2,1)S(1)}, bf16[656,128]{1,0:T(8,128)(2,1)S(1)}, u32[]{:S(2)}, u32[]{:S(2)}) collective-permute-start(bf16[656,128]{1,0:T(8,128)(2,1)S(1)} %get-tuple-element.78.b0), channel_id=1, source_target_pairs={{0,1},{1,0},{2,3},{3,2},{4,5},{5,4},{6,7},{7,6},{8,9},{9,8},{10,11... | collective-permute-start | bytes 503816 | tf_op jit(solution)/shard_map/ppermute | solution.py:397
  74.4 8.6 %collective-permute-start.13 = (bf16[656,128]{1,0:T(8,128)(2,1)S(1)}, bf16[656,128]{1,0:T(8,128)(2,1)S(1)}, u32[]{:S(2)}, u32[]{:S(2)}) collective-permute-start(bf16[656,128]{1,0:T(8,128)(2,1)S(1)} %collective-permute-done.12.b2), channel_id=1, source_target_pairs={{0,1},{1,0},{2,3},{3,2},{4,5},{5,4},{6,7},{7,6},{8,9},{9,8},{10,11... | collective-permute-start | bytes 503816 | tf_op jit(solution)/shard_map/ppermute | solution.py:397
  80.9 9.4 %collective-permute-start.16 = (bf16[656,128]{1,0:T(8,128)(2,1)S(1)}, bf16[656,128]{1,0:T(8,128)(2,1)S(1)}, u32[]{:S(2)}, u32[]{:S(2)}) collective-permute-start(bf16[656,128]{1,0:T(8,128)(2,1)S(1)} %collective-permute-done.15.b0), channel_id=1, source_target_pairs={{0,4},{1,5},{2,6},{3,7},{4,0},{5,1},{6,2},{7,3},{8,12},{9,13},{10,... | collective-permute-start | bytes 503816 | tf_op jit(solution)/shard_map/ppermute | solution.py:397
  81.2 9.1 %collective-permute-start.19 = (bf16[656,128]{1,0:T(8,128)(2,1)S(1)}, bf16[656,128]{1,0:T(8,128)(2,1)S(1)}, u32[]{:S(2)}, u32[]{:S(2)}) collective-permute-start(bf16[656,128]{1,0:T(8,128)(2,1)S(1)} %collective-permute-done.14.b0), channel_id=1, source_target_pairs={{0,1},{1,0},{2,3},{3,2},{4,5},{5,4},{6,7},{7,6},{8,9},{9,8},{10,11... | collective-permute-start | bytes 503816 | tf_op jit(solution)/shard_map/ppermute | solution.py:397
  81.2 9.7 %collective-permute-start.24 = (bf16[656,128]{1,0:T(8,128)(2,1)S(1)}, bf16[656,128]{1,0:T(8,128)(2,1)S(1)}, u32[]{:S(2)}, u32[]{:S(2)}) collective-permute-start(bf16[656,128]{1,0:T(8,128)(2,1)S(1)} %collective-permute-done.15.b0), channel_id=1, source_target_pairs={{0,2},{1,3},{2,0},{3,1},{4,6},{5,7},{6,4},{7,5},{8,10},{9,11},{10,... | collective-permute-start | bytes 503816 | tf_op jit(solution)/shard_map/ppermute | solution.py:397
  83.0 14.1 %collective-permute-start.23 = (bf16[656,128]{1,0:T(8,128)(2,1)S(1)}, bf16[656,128]{1,0:T(8,128)(2,1)S(1)}, u32[]{:S(2)}, u32[]{:S(2)}) collective-permute-start(bf16[656,128]{1,0:T(8,128)(2,1)S(1)} %collective-permute-done.15.b0), channel_id=1, source_target_pairs={{0,1},{1,0},{2,3},{3,2},{4,5},{5,4},{6,7},{7,6},{8,9},{9,8},{10,11... | collective-permute-start | bytes 503816 | tf_op jit(solution)/shard_map/ppermute | solution.py:397
  90.4 9.2 %collective-permute-start.17 = (bf16[656,128]{1,0:T(8,128)(2,1)S(1)}, bf16[656,128]{1,0:T(8,128)(2,1)S(1)}, u32[]{:S(2)}, u32[]{:S(2)}) collective-permute-start(bf16[656,128]{1,0:T(8,128)(2,1)S(1)} %collective-permute-done.16.b0), channel_id=1, source_target_pairs={{0,1},{1,0},{2,3},{3,2},{4,5},{5,4},{6,7},{7,6},{8,9},{9,8},{10,11... | collective-permute-start | bytes 503816 | tf_op jit(solution)/shard_map/ppermute | solution.py:397
  113.9 10.3 %collective-permute-start.34 = (bf16[128,640]{1,0:T(8,128)(2,1)S(1)}, bf16[128,640]{1,0:T(8,128)(2,1)S(1)}, u32[]{:S(2)}, u32[]{:S(2)}) collective-permute-start(bf16[128,640]{1,0:T(8,128)(2,1)S(1)} %fusion.13), channel_id=1, source_target_pairs={{0,2},{1,3},{2,0},{3,1},{4,6},{5,7},{6,4},{7,5},{8,10},{9,11},{10,... | collective-permute-start | bytes 491528 | tf_op jit(solution)/shard_map/ppermute | solution.py:397
  119.3 8.2 %collective-permute-start.31 = (bf16[2,128,640]{2,1,0:T(8,128)(2,1)S(1)}, bf16[2,128,640]{2,1,0:T(8,128)(2,1)S(1)}, u32[]{:S(2)}, u32[]{:S(2)}) collective-permute-start(bf16[2,128,640]{2,1,0:T(8,128)(2,1)S(1)} %get-tuple-element.107), channel_id=1, source_target_pairs={{0,1},{1,0},{2,3},{3,2},{4,5},{5,4},{6,7},{7,6},{8,9},{9,8},{10,11... | collective-permute-start | bytes 983048 | tf_op jit(solution)/shard_map/ppermute | solution.py:397
  126.2 10.5 %collective-permute-start.36 = (bf16[128,640]{1,0:T(8,128)(2,1)S(1)}, bf16[128,640]{1,0:T(8,128)(2,1)S(1)}, u32[]{:S(2)}, u32[]{:S(2)}) collective-permute-start(bf16[128,640]{1,0:T(8,128)(2,1)S(1)} %fusion.1), channel_id=1, source_target_pairs={{0,8},{1,9},{2,10},{3,11},{4,12},{5,13},{6,14},{7,15},{8,0},{9,1},... | collective-permute-start | bytes 491528 | tf_op jit(solution)/shard_map/ppermute | solution.py:397
  128.3 8.4 %collective-permute-start.30 = (bf16[128,640]{1,0:T(8,128)(2,1)S(1)}, bf16[128,640]{1,0:T(8,128)(2,1)S(1)}, u32[]{:S(2)}, u32[]{:S(2)}) collective-permute-start(bf16[128,640]{1,0:T(8,128)(2,1)S(1)} %fusion.14), channel_id=1, source_target_pairs={{0,2},{1,3},{2,0},{3,1},{4,6},{5,7},{6,4},{7,5},{8,10},{9,11},{10,... | collective-permute-start | bytes 491528 | tf_op jit(solution)/shard_map/ppermute | solution.py:397
  147.8 8.2 %collective-permute-start.37 = (bf16[656,128]{1,0:T(8,128)(2,1)S(1)}, bf16[656,128]{1,0:T(8,128)(2,1)S(1)}, u32[]{:S(2)}, u32[]{:S(2)}) collective-permute-start(bf16[656,128]{1,0:T(8,128)(2,1)S(1)} %get-tuple-element.111.b0), channel_id=1, source_target_pairs={{0,8},{1,9},{2,10},{3,11},{4,12},{5,13},{6,14},{7,15},{8,0},{9,1},... | collective-permute-start | bytes 503816 | tf_op jit(solution)/shard_map/ppermute | solution.py:397
  150.0 9.1 %collective-permute-start.39 = (bf16[656,128]{1,0:T(8,128)(2,1)S(1)}, bf16[656,128]{1,0:T(8,128)(2,1)S(1)}, u32[]{:S(2)}, u32[]{:S(2)}) collective-permute-start(bf16[656,128]{1,0:T(8,128)(2,1)S(1)} %get-tuple-element.111.b0), channel_id=1, source_target_pairs={{0,1},{1,0},{2,3},{3,2},{4,5},{5,4},{6,7},{7,6},{8,9},{9,8},{10,11... | collective-permute-start | bytes 503816 | tf_op jit(solution)/shard_map/ppermute | solution.py:397
  156.9 11.7 %collective-permute-start.46 = (bf16[656,128]{1,0:T(8,128)(2,1)}, bf16[656,128]{1,0:T(8,128)(2,1)}, u32[]{:S(2)}, u32[]{:S(2)}) collective-permute-start(bf16[656,128]{1,0:T(8,128)(2,1)} %collective-permute-done.42.b0), channel_id=1, source_target_pairs={{0,2},{1,3},{2,0},{3,1},{4,6},{5,7},{6,4},{7,5},{8,10},{9,11},{10,... | collective-permute-start | bytes 503816 | tf_op jit(solution)/shard_map/ppermute | solution.py:397
  163.1 34.2 %all-to-all-start.1 = ((bf16[16,144,128]{2,1,0:T(8,128)(2,1)}), bf16[16,144,128]{2,1,0:T(8,128)(2,1)S(1)}, u32[]{:S(2)}, u32[]{:S(2)}) async-start(bf16[16,144,128]{2,1,0:T(8,128)(2,1)} %get-tuple-element.115), calls=%async_computation.1 | async-start | bytes 1179648 | tf_op jit(solution)/shard_map/all_to_all | solution.py:513
  167.0 11.6 %collective-permute-start.50 = (bf16[656,128]{1,0:T(8,128)(2,1)S(1)}, bf16[656,128]{1,0:T(8,128)(2,1)}, u32[]{:S(2)}, u32[]{:S(2)}) collective-permute-start(bf16[656,128]{1,0:T(8,128)(2,1)S(1)} %collective-permute-done.37.b0), channel_id=1, source_target_pairs={{0,2},{1,3},{2,0},{3,1},{4,6},{5,7},{6,4},{7,5},{8,10},{9,11},{10,... | collective-permute-start | bytes 503816 | tf_op jit(solution)/shard_map/ppermute | solution.py:397
  168.7 10.0 %collective-permute-start.47 = (bf16[656,128]{1,0:T(8,128)(2,1)}, bf16[656,128]{1,0:T(8,128)(2,1)}, u32[]{:S(2)}, u32[]{:S(2)}) collective-permute-start(bf16[656,128]{1,0:T(8,128)(2,1)} %collective-permute-done.46.b2), channel_id=1, source_target_pairs={{0,1},{1,0},{2,3},{3,2},{4,5},{5,4},{6,7},{7,6},{8,9},{9,8},{10,11... | collective-permute-start | bytes 503816 | tf_op jit(solution)/shard_map/ppermute | solution.py:397
  169.8 17.2 %collective-permute-start.49 = (bf16[656,128]{1,0:T(8,128)(2,1)S(1)}, bf16[656,128]{1,0:T(8,128)(2,1)S(1)}, u32[]{:S(2)}, u32[]{:S(2)}) collective-permute-start(bf16[656,128]{1,0:T(8,128)(2,1)S(1)} %collective-permute-done.37.b0), channel_id=1, source_target_pairs={{0,1},{1,0},{2,3},{3,2},{4,5},{5,4},{6,7},{7,6},{8,9},{9,8},{10,11... | collective-permute-start | bytes 503816 | tf_op jit(solution)/shard_map/ppermute | solution.py:397
  170.3 16.1 %collective-permute-start.44 = (bf16[656,128]{1,0:T(8,128)(2,1)}, bf16[656,128]{1,0:T(8,128)(2,1)S(1)}, u32[]{:S(2)}, u32[]{:S(2)}) collective-permute-start(bf16[656,128]{1,0:T(8,128)(2,1)} %copy-done.18), channel_id=1, source_target_pairs={{0,2},{1,3},{2,0},{3,1},{4,6},{5,7},{6,4},{7,5},{8,10},{9,11},{10,... | collective-permute-start | bytes 503816 | tf_op jit(solution)/shard_map/ppermute | solution.py:397
  170.6 22.7 %collective-permute-start.43 = (bf16[656,128]{1,0:T(8,128)(2,1)}, bf16[656,128]{1,0:T(8,128)(2,1)S(1)}, u32[]{:S(2)}, u32[]{:S(2)}) collective-permute-start(bf16[656,128]{1,0:T(8,128)(2,1)} %copy-done.18), channel_id=1, source_target_pairs={{0,1},{1,0},{2,3},{3,2},{4,5},{5,4},{6,7},{7,6},{8,9},{9,8},{10,11... | collective-permute-start | bytes 503816 | tf_op jit(solution)/shard_map/ppermute | solution.py:397
  178.6 8.3 %collective-permute-start.51 = (bf16[656,128]{1,0:T(8,128)(2,1)}, bf16[656,128]{1,0:T(8,128)(2,1)S(1)}, u32[]{:S(2)}, u32[]{:S(2)}) collective-permute-start(bf16[656,128]{1,0:T(8,128)(2,1)} %collective-permute-done.50.b2), channel_id=1, source_target_pairs={{0,1},{1,0},{2,3},{3,2},{4,5},{5,4},{6,7},{7,6},{8,9},{9,8},{10,11... | collective-permute-start | bytes 503816 | tf_op jit(solution)/shard_map/ppermute | solution.py:397
  (61 other events, 453.0 us)

commit v5 on v4

--- a/solution.py
+++ b/solution.py
@@ -13,7 +13,7 @@
 sigma_step = 0.15
 
 GROUP = 4
-LIMIT = 16 << 20
+LIMIT = 12 << 20
 COST = 3
 META = 16
 F32 = jnp.float32
@@ -44,21 +44,23 @@
     return jnp.concatenate([ref[i : i + 1, :] for i in range(ref.shape[0])], axis=1)
 
 
-def pack_kernel(cap, owner_ref, local_ref, cost_ref, dispatch_ref, max_ref, avail_ref, out_ref, slot_ref, pay_ref, meta_ref):
+def pack_kernel(
+    cap, devices, owner_ref, local_ref, cost_ref, dispatch_ref, max_ref, avail_ref, out_ref, slot_ref, pay_ref, meta_ref
+):
     step = pl.program_id(0)
     gens, hours = dispatch_ref.shape
     group = out_ref.shape[0]
 
     @pl.when(step == 0)
     def _():
-        owner = as_row(owner_ref)
-        hits = (lax.broadcasted_iota(jnp.int32, (slot_ref.shape[0], gens), 0) == owner).astype(F32)
+        owner = owner_ref[...]
+        hits = (lax.broadcasted_iota(jnp.int32, (devices, gens), 0) == owner).astype(F32)
         before = (
             lax.broadcasted_iota(jnp.int32, (gens, gens), 0) < lax.broadcasted_iota(jnp.int32, (gens, gens), 1)
         ).astype(F32)
         count = dot(hits.astype(BF16), before.astype(BF16))
         rank = jnp.sum(count * hits, axis=0, keepdims=True).astype(jnp.int32)
-        slot_ref[...] = jnp.broadcast_to(owner * cap + rank, slot_ref.shape)
+        slot_ref[...] = owner * cap + rank
         pay_ref[:, :hours] = dispatch_ref[...].astype(BF16)
         lanes = max_ref.shape[1]
         eye = (
@@ -83,7 +85,7 @@
             meta = jnp.where(row == i, part, meta)
         meta_ref[...] = meta.astype(BF16)
 
-    slot = slot_ref[0:1, :] - step * (group * cap)
+    slot = slot_ref[...] - step * (group * cap)
     place = lax.broadcasted_iota(jnp.int32, (cap, gens), 0)
     picks = [(place == slot - i * cap).astype(F32).astype(BF16) for i in range(group)]
     moved = dot(jnp.concatenate(picks, axis=0), pay_ref[...]).astype(BF16)
@@ -98,20 +100,22 @@
     full = lambda *shape: pl.BlockSpec(shape, lambda i: (0,) * len(shape))
     folded = (gens // 128, 128)
     return pl.pallas_call(
-        functools.partial(pack_kernel, cap),
+        functools.partial(pack_kernel, cap, devices),
         grid=(devices // GROUP,),
-        out_shape=jax.ShapeDtypeStruct((devices, cap + META, 2 * hours), BF16),
+        out_shape=(
+            jax.ShapeDtypeStruct((devices, cap + META, 2 * hours), BF16),
+            jax.ShapeDtypeStruct((1, gens), jnp.int32),
+        ),
         in_specs=[
-            full(*folded),
+            full(1, gens),
             full(*folded),
             full(*folded),
             full(gens, hours),
             full(*folded),
             full(gens, hours),
         ],
-        out_specs=pl.BlockSpec((GROUP, cap + META, 2 * hours), lambda i: (i, 0, 0)),
+        out_specs=(pl.BlockSpec((GROUP, cap + META, 2 * hours), lambda i: (i, 0, 0)), full(1, gens)),
         scratch_shapes=[
-            pltpu.VMEM((devices, gens), jnp.int32),
             pltpu.VMEM((gens, 2 * hours), BF16),
             pltpu.VMEM((META, gens), BF16),
         ],
@@ -119,7 +123,7 @@
         cost_estimate=pl.CostEstimate(flops=4 * devices * cap * gens * hours, bytes_accessed=3 << 20, transcendentals=0),
         name="pack_generators",
     )(
-        owner.reshape(folded),
+        owner.reshape(1, gens),
         local_bus.reshape(folded),
         cost.reshape(folded),
         dispatch,
@@ -128,30 +132,9 @@
     )
 
 
-def slot_kernel(devices, cap, owner_ref, slot_ref):
-    gens = owner_ref.shape[0]
-    owner = owner_ref[...]
-    hits = (lax.broadcasted_iota(jnp.int32, (gens, devices), 1) == owner).astype(F32)
-    before = (
-        lax.broadcasted_iota(jnp.int32, (gens, gens), 1) < lax.broadcasted_iota(jnp.int32, (gens, gens), 0)
-    ).astype(F32)
-    count = dot(before.astype(BF16), hits.astype(BF16))
-    rank = jnp.sum(count * hits, axis=1, keepdims=True).astype(jnp.int32)
-    slot_ref[...] = owner * cap + rank
-
-
-def slot_column(devices, cap, owner_column):
-    return pl.pallas_call(
-        functools.partial(slot_kernel, devices, cap),
-        out_shape=jax.ShapeDtypeStruct(owner_column.shape, jnp.int32),
-        compiler_params=pltpu.CompilerParams(vmem_limit_bytes=LIMIT),
-        name="slot_column",
-    )(owner_column)
-
-
 def unpack_kernel(block, slot_ref, back_ref, dispatch_ref, max_ref, avail_ref, out_ref):
-    gens = slot_ref.shape[0]
-    slot = slot_ref[...]
+    gens = slot_ref.shape[1]
+    slot = jnp.broadcast_to(slot_ref[...].astype(F32), (128, gens)).T[:, 0:1].astype(jnp.int32)
     at = lax.broadcasted_iota(jnp.int32, (gens, block), 1)
     change = None
     for start in range(0, back_ref.shape[0], block):
@@ -168,7 +151,7 @@
 
 
 def unpack(slot, back, dispatch, gen_max, availability):
-    gens = slot.shape[0]
+    gens = slot.shape[1]
     devices, cap, hours = back.shape
     slots = devices * cap
     block = next(size for size in (768, 256, 128, 16) if slots % size == 0)
@@ -284,9 +267,12 @@
     )(*prices, balance_price, demand, recv, previous)
 
 
-def shadow_kernel(chunk, fetch, place_ref, line_ref, ptdf_ref, keep_ref, send_ref, *rest):
+def shadow_kernel(chunk, fetch, turn, place_ref, line_ref, ptdf_ref, keep_ref, send_ref, *rest):
     buses = keep_ref.shape[2]
     columns = [slice(rel * buses, (rel + 1) * buses) for rel in range(4)]
+    if turn:
+        *rest, line_t_ref, sems = rest
+        rest = [*rest, sems]
     if fetch:
         held_ref, sems = rest
         copies = []
@@ -301,6 +287,9 @@
             copies[rel].start()
     else:
         held_ref = ptdf_ref
+    if turn:
+        line_t_ref[...] = line_ref[...].T.astype(BF16)
+        line_ref = line_t_ref
 
     def part(rel):
         if fetch:
@@ -313,8 +302,9 @@
     keep_ref[0] = part(0)
 
 
-def shadow_chunk(chunk, fetch, place, line_t, ptdf, buses):
-    hours, lines = line_t.shape
+def shadow_chunk(chunk, fetch, place, line, ptdf, buses):
+    turn = line.dtype == F32
+    lines, hours = line.shape if turn else line.shape[::-1]
     vmem = pl.BlockSpec(memory_space=pltpu.VMEM)
     out_shape = [
         jax.ShapeDtypeStruct((2, hours, buses), F32),
@@ -322,8 +312,10 @@
     ]
     if fetch:
         out_shape.append(pltpu.VMEM((lines, 4 * buses), BF16))
+    if turn:
+        out_shape.append(jax.ShapeDtypeStruct((hours, lines), BF16))
     return pl.pallas_call(
-        functools.partial(shadow_kernel, chunk, fetch),
+        functools.partial(shadow_kernel, chunk, fetch, turn),
         in_specs=[pl.BlockSpec(memory_space=pltpu.SMEM), vmem, pl.BlockSpec(memory_space=pltpu.MemorySpace.HBM) if fetch else vmem],
         out_specs=tuple([vmem] * len(out_shape)),
         out_shape=tuple(out_shape),
@@ -333,7 +325,7 @@
             flops=COST * 8 * hours * lines * buses, bytes_accessed=8 * lines * buses, transcendentals=0
         ),
         name="shadow_chunk",
-    )(place, line_t, pltpu.with_memory_space_constraint(ptdf, pltpu.MemorySpace.HBM) if fetch else ptdf)
+    )(place, line, pltpu.with_memory_space_constraint(ptdf, pltpu.MemorySpace.HBM) if fetch else ptdf)
 
 
 def flow_kernel(start, end, ptdf_ref, b0, b1, b2, b3, acc_ref, sum_ref, *rest):
@@ -360,12 +352,13 @@
             limit = limit_ref[rows, :]
             line = shifted - sigma_step * jnp.minimum(jnp.maximum(shifted / sigma_step, -limit), limit)
             out_ref[rows, :] = line
-            half_ref[rows, :] = line.astype(BF16)
         else:
             out_ref[rows, :] = flow
         return carry
 
     lax.fori_loop(0, 4, body, 0)
+    if end:
+        half_ref[...] = out_ref[...].T.astype(BF16)
 
 
 def flow_chunk(ptdf, blocks, acc, total, limit=None, line=None):
@@ -377,7 +370,7 @@
     out_shape = [jax.ShapeDtypeStruct((lines, hours), F32)]
     if end:
         operands += [limit, line]
-        out_shape += [jax.ShapeDtypeStruct((lines, hours), BF16)]
+        out_shape += [jax.ShapeDtypeStruct((hours, lines), BF16)]
     out_shape += [jax.ShapeDtypeStruct((1, hours), F32)]
     in_specs = [pl.BlockSpec(memory_space=pltpu.VMEM)] * len(operands)
     return pl.pallas_call(
@@ -418,7 +411,7 @@
     cap = -(-max(2, 3 * gens // devices) // 16) * 16
     staged = devices == 16 and buses % 128 == 0
 
-    outgoing = pack(
+    outgoing, slot = pack(
         devices,
         cap,
         gen_owner,
@@ -430,14 +423,13 @@
     )
     limit = line_limit.reshape(-1, 1)
     balance_row = balance_price.reshape(1, hours)
-    line_half = line_price.astype(BF16)
+    line_half = line_price if staged else line_price.astype(BF16)
     recv = lax.all_to_all(outgoing, "bus", split_axis=0, concat_axis=0, tiled=True)
-    slot = None if staged else slot_column(devices, cap, gen_owner)
     held, resident = None, {}
     for iteration in range(ITERS):
         last = iteration == ITERS - 1
         if staged:
-            line_t = line_half.T
+            line_t = line_half
             keeps, gots, crossed, parts = {}, {}, {}, {}
 
             def across(chunk):
@@ -460,10 +452,14 @@
                 if chunk in resident:
                     keeps[chunk], send = shadow_chunk(chunk, False, place, line_t, resident[chunk], buses)
                 else:
-                    keeps[chunk], send, resident[chunk] = shadow_chunk(chunk, True, place, line_t, ptdf, buses)
+                    keeps[chunk], send, resident[chunk], *turned = shadow_chunk(
+                        chunk, True, place, line_t, ptdf, buses
+                    )
+                    line_t = turned[0] if turned else line_t
                 gots[chunk] = swap(send, devices, 1)
-
-            product(3, line_t)
+                return line_t
+
+            line_t = product(3, line_t)
             if iteration == 0:
                 line_t, _ = lax.optimization_barrier((line_t, outgoing))
             product(2, line_t)
@@ -503,9 +499,6 @@
             settle_far(0)
             near[1], near[2], row = lax.optimization_barrier((near[1], near[2], balance_row))
             acc, total = flow_chunk(resident[0], blocks(0), None, row)
-            if iteration == 0:
-                owner, acc = lax.optimization_barrier((gen_owner, acc))
-                slot = slot_column(devices, cap, owner)
             near[3], acc = lax.optimization_barrier((near[3], acc))
             spread(3)
             if last:

time: 200 us -> 187 us (0.935)
  local copies, waits for them, and re-layouts: 40.6 us -> 26.9 us
  waiting for transfers between devices: 43.4 us -> 48.5 us
  Pallas kernels: 61.2 us -> 58.3 us
    unnamed x79 -> x66, local copies, waits for them, and re-layouts: 39.9 us -> 26.5 us
    ppermute x52, waiting for transfers between devices: 43.4 us -> 48.5 us  [swap(): return lax.ppermute(x, 'bus', [(i, i ^ mask) for i in range(devices)])]
    pallas_call x8, Pallas kernels: 23.1 us -> 20.7 us  [flow_chunk(): pl.pallas_call(functools.partial(flow_kernel, start, end), in_specs=in_sp...]
    pallas_call x10 -> x9, Pallas kernels: 22.8 us -> 22.1 us  [the longest x8 18.6 us: shadow_chunk(): pl.pallas_call(functools.partial(shadow_kernel, chunk, fetch, turn), in_s...]
  transfers between devices with their start and end apart: 54 -> 54, of which waited for: 18 -> 21; matrix products, arithmetic and copies ran while one was open for 2% -> 2% of each run, Pallas kernels for 19% -> 19%
where the time goes in v5:
time: 187 us
  Pallas kernels  58.3 us (31%)
  starting transfers between devices  48.7 us (26%)
  waiting for transfers between devices  48.5 us (26%)
  local copies, waits for them, and re-layouts  26.9 us (14%)
  other arithmetic  3.1 us (2%)
    ppermute x52, waiting for transfers between devices, swap(): return lax.ppermute(x, 'bus', [(i, i ^ mask) for i in range(devices)])  48.5 us
    ppermute x52, starting transfers between devices, swap(): return lax.ppermute(x, 'bus', [(i, i ^ mask) for i in range(devices)])  38 us
    unnamed x66, local copies, waits for them, and re-layouts  26.5 us
    pallas_call x8, Pallas kernels, flow_chunk(): pl.pallas_call(functools.partial(flow_kernel, start, end), in_specs=in_sp...  20.7 us
    pallas_call x8, Pallas kernels, shadow_chunk(): pl.pallas_call(functools.partial(shadow_kernel, chunk, fetch, turn), in_s...  18.6 us
    pallas_call x2, Pallas kernels, update(): pl.pallas_call(functools.partial(update_kernel, cap, first, last, len(pri...  13.4 us
    all_to_all x1, starting transfers between devices, local(): lax.all_to_all(outgoing, 'bus', split_axis=0, concat_axis=0, tiled=True)  7.06 us
  transfers between devices with their start and end apart: 54, of which 21 were waited for; matrix products, arithmetic and copies ran while one was open for 2% of the time, Pallas kernels for 19%

profile of v5, /device:TPU:0, one launch (start us, length us, event | category | flops | bytes accessed | tf_op | source)
XLA Modules:
  0.0 186.8 jit_solution(947366378607994146)
XLA Ops:
  1.8 3.5 %shadow_chunk.8 = (f32[2,128,640]{2,1,0:T(8,128)S(1)}, bf16[2,128,640]{2,1,0:T(8,128)(2,1)S(1)}, bf16[1280,2560]{1,0:T(8,128)(2,1)S(1)}, bf16[128,1280]{1,0:T(8,128)(2,1)S(1)}) custom-call(s32[1]{0:T(128)} %bitcast.4.place_ref, f32[1280,128]{1,0:T(8,128)S(1)} %copy-done, bf16[1280,10240]{1,0:T(8,128)(2,1)} %ptdf_ref.7), custom_call_target="tpu_custom_call" | custom-call | flops 2516582400 | bytes 6553600 | tf_op jit(solution)/shard_map/shadow_chunk/pallas_call | solution.py:317
  5.3 2.7 %copy-done.5 = bf16[1280,2560]{1,0:T(8,128)(2,1)} copy-done((bf16[1280,2560]{1,0:T(8,128)(2,1)}, bf16[1280,2560]{1,0:T(8,128)(2,1)S(1)}, u32[]{:S(2)}) %copy-start.5) | copy-done | bytes 6553624
  8.4 3.6 %pack_generators.1 = (bf16[16,160,256]{2,1,0:T(8,128)(2,1)}, s32[1,768]{1,0:T(1,128)S(1)}) custom-call(s32[1,768]{1,0:T(1,128)S(1)} %bitcast.72, s32[6,128]{1,0:T(8,128)S(1)} %bitcast.70, f32[6,128]{1,0:T(8,128)S(1)} %bitcast.71, f32[768,128]{1,0:T(8,128)S(1)} %copy-done.2, f32[6,128]{1,0:T(8,128)S(1)} %bitcast.59, f32[768,128]{1,0:T(8,128)S(1)} %copy-done.3), custom_call_target="tpu_custom_call" | custom-call | flops 905969664 | bytes 3145728 | tf_op jit(solution)/shard_map/pack_generators/pallas_call | solution.py:102
  12.0 7.1 %all-to-all-start = ((bf16[16,160,256]{2,1,0:T(8,128)(2,1)}), bf16[16,160,256]{2,1,0:T(8,128)(2,1)S(1)}, u32[]{:S(2)}, u32[]{:S(2)}) async-start(bf16[16,160,256]{2,1,0:T(8,128)(2,1)} %get-tuple-element.70), calls=%async_computation | async-start | bytes 2621440 | tf_op jit(solution)/shard_map/all_to_all | solution.py:427
  19.1 3.4 %shadow_chunk.9 = (f32[2,128,640]{2,1,0:T(8,128)S(1)}, bf16[2,128,640]{2,1,0:T(8,128)(2,1)S(1)}, bf16[1280,2560]{1,0:T(8,128)(2,1)S(1)}) custom-call(s32[1]{0:T(128)} %bitcast.4.place_ref, bf16[128,1280]{1,0:T(8,128)(2,1)S(1)} %get-tuple-element.77.line_ref, bf16[1280,10240]{1,0:T(8,128)(2,1)} %ptdf_ref.7), custom_call_target="tpu_custom_call" | custom-call | flops 2516582400 | bytes 6553600 | tf_op jit(solution)/shard_map/shadow_chunk/pallas_call | solution.py:317
  22.5 2.8 %copy-done.6 = bf16[1280,2560]{1,0:T(8,128)(2,1)} copy-done((bf16[1280,2560]{1,0:T(8,128)(2,1)}, bf16[1280,2560]{1,0:T(8,128)(2,1)S(1)}, u32[]{:S(2)}) %copy-start.6) | copy-done | bytes 6553624
  28.4 3.4 %shadow_chunk.11 = (f32[2,128,640]{2,1,0:T(8,128)S(1)}, bf16[2,128,640]{2,1,0:T(8,128)(2,1)S(1)}, bf16[1280,2560]{1,0:T(8,128)(2,1)S(1)}) custom-call(s32[1]{0:T(128)} %bitcast.4.place_ref, bf16[128,1280]{1,0:T(8,128)(2,1)S(1)} %get-tuple-element.77.line_ref, bf16[1280,10240]{1,0:T(8,128)(2,1)} %ptdf_ref.7), custom_call_target="tpu_custom_call" | custom-call | flops 2516582400 | bytes 6553600 | tf_op jit(solution)/shard_map/shadow_chunk/pallas_call | solution.py:317
  31.9 2.7 %copy-done.8 = bf16[1280,2560]{1,0:T(8,128)(2,1)} copy-done((bf16[1280,2560]{1,0:T(8,128)(2,1)}, bf16[1280,2560]{1,0:T(8,128)(2,1)S(1)}, u32[]{:S(2)}) %copy-start.8) | copy-done | bytes 6553624
  38.8 3.4 %shadow_chunk.10 = (f32[2,128,640]{2,1,0:T(8,128)S(1)}, bf16[2,128,640]{2,1,0:T(8,128)(2,1)S(1)}, bf16[1280,2560]{1,0:T(8,128)(2,1)S(1)}) custom-call(s32[1]{0:T(128)} %bitcast.4.place_ref, bf16[128,1280]{1,0:T(8,128)(2,1)S(1)} %get-tuple-element.77.line_ref, bf16[1280,10240]{1,0:T(8,128)(2,1)} %ptdf_ref.7), custom_call_target="tpu_custom_call" | custom-call | flops 2516582400 | bytes 6553600 | tf_op jit(solution)/shard_map/shadow_chunk/pallas_call | solution.py:317
  42.2 2.8 %copy-done.11 = bf16[1280,2560]{1,0:T(8,128)(2,1)} copy-done((bf16[1280,2560]{1,0:T(8,128)(2,1)}, bf16[1280,2560]{1,0:T(8,128)(2,1)S(1)}, u32[]{:S(2)}) %copy-start.11) | copy-done | bytes 6553624
  46.0 3.7 %collective-permute-start.10 = (bf16[128,640]{1,0:T(8,128)(2,1)S(1)}, bf16[128,640]{1,0:T(8,128)(2,1)S(1)}, u32[]{:S(2)}, u32[]{:S(2)}) collective-permute-start(bf16[128,640]{1,0:T(8,128)(2,1)S(1)} %fusion.5), channel_id=1, source_target_pairs={{0,8},{1,9},{2,10},{3,11},{4,12},{5,13},{6,14},{7,15},{8,0},{9,1},... | collective-permute-start | bytes 491528 | tf_op jit(solution)/shard_map/ppermute | solution.py:390
  51.8 2.8 %collective-permute-start.7 = (bf16[128,640]{1,0:T(8,128)(2,1)S(1)}, bf16[128,640]{1,0:T(8,128)(2,1)S(1)}, u32[]{:S(2)}, u32[]{:S(2)}) collective-permute-start(bf16[128,640]{1,0:T(8,128)(2,1)S(1)} %fusion.6), channel_id=1, source_target_pairs={{0,4},{1,5},{2,6},{3,7},{4,0},{5,1},{6,2},{7,3},{8,12},{9,13},{10,... | collective-permute-start | bytes 491528 | tf_op jit(solution)/shard_map/ppermute | solution.py:390
  55.9 2.5 %collective-permute-done.10.refs_2_ = bf16[128,640]{1,0:T(8,128)(2,1)S(1)} collective-permute-done((bf16[128,640]{1,0:T(8,128)(2,1)S(1)}, bf16[128,640]{1,0:T(8,128)(2,1)S(1)}, u32[]{:S(2)}, u32[]{:S(2)}) %collective-permute-start.10) | collective-permute-done | bytes 163872 | tf_op jit(solution)/shard_map/ppermute | solution.py:390
  59.8 6.3 %update_generators.2 = (f32[16,144,128]{2,1,0:T(8,128)S(1)}, bf16[656,128]{1,0:T(8,128)(2,1)S(1)}) custom-call(f32[128,640]{1,0:T(8,128)S(1)} %bitcast_add_fusion.6.refs_0_, bf16[128,640]{1,0:T(8,128)(2,1)S(1)} %collective-permute-done.7.refs_1_, bf16[128,640]{1,0:T(8,128)(2,1)S(1)} %collective-permute-done.10.refs_2_, f32[1,128]{1,0:T(1,128)S(1)} %bitcast.73, ...), custom_call_target="tpu_custom_call" | custom-call | flops 1509949440 | bytes 4194304 | tf_op jit(solution)/shard_map/update_generators/pallas_call | solution.py:244
  66.1 3.2 %collective-permute-start.14 = (bf16[656,128]{1,0:T(8,128)(2,1)S(1)}, bf16[656,128]{1,0:T(8,128)(2,1)S(1)}, u32[]{:S(2)}, u32[]{:S(2)}) collective-permute-start(bf16[656,128]{1,0:T(8,128)(2,1)S(1)} %get-tuple-element.82.b0), channel_id=1, source_target_pairs={{0,2},{1,3},{2,0},{3,1},{4,6},{5,7},{6,4},{7,5},{8,10},{9,11},{10,... | collective-permute-start | bytes 503816 | tf_op jit(solution)/shard_map/ppermute | solution.py:390
  69.3 2.6 %collective-permute-start.11 = (bf16[656,128]{1,0:T(8,128)(2,1)S(1)}, bf16[656,128]{1,0:T(8,128)(2,1)S(1)}, u32[]{:S(2)}, u32[]{:S(2)}) collective-permute-start(bf16[656,128]{1,0:T(8,128)(2,1)S(1)} %get-tuple-element.82.b0), channel_id=1, source_target_pairs={{0,8},{1,9},{2,10},{3,11},{4,12},{5,13},{6,14},{7,15},{8,0},{9,1},... | collective-permute-start | bytes 503816 | tf_op jit(solution)/shard_map/ppermute | solution.py:390
  73.2 4.8 %collective-permute-done.16.b0 = bf16[656,128]{1,0:T(8,128)(2,1)S(1)} collective-permute-done((bf16[656,128]{1,0:T(8,128)(2,1)S(1)}, bf16[656,128]{1,0:T(8,128)(2,1)S(1)}, u32[]{:S(2)}, u32[]{:S(2)}) %collective-permute-start.16) | collective-permute-done | bytes 167968 | tf_op jit(solution)/shard_map/ppermute | solution.py:390
  83.5 3.0 %copy-done.12 = bf16[1280,2560]{1,0:T(8,128)(2,1)S(1)} copy-done((bf16[1280,2560]{1,0:T(8,128)(2,1)S(1)}, bf16[1280,2560]{1,0:T(8,128)(2,1)}, u32[]{:S(2)}) %copy-start.12) | copy-done | bytes 6553624
  89.7 3.0 %copy-done.9 = bf16[1280,2560]{1,0:T(8,128)(2,1)S(1)} copy-done((bf16[1280,2560]{1,0:T(8,128)(2,1)S(1)}, bf16[1280,2560]{1,0:T(8,128)(2,1)}, u32[]{:S(2)}) %copy-start.9) | copy-done | bytes 6553624
  95.8 2.4 %flow_chunk.10 = (f32[1280,128]{1,0:T(8,128)S(1)}, f32[1,128]{1,0:T(1,128)S(1)}) custom-call(bf16[1280,2560]{1,0:T(8,128)(2,1)S(1)} %bitcast.65, bf16[656,128]{1,0:T(8,128)(2,1)S(1)} %collective-permute-done.11.b0, bf16[656,128]{1,0:T(8,128)(2,1)S(1)} %collective-permute-done.23.b1, bf16[656,128]{1,0:T(8,128)(2,1)S(1)} %collective-permute-done.24.b2, ...), custom_call_target="tpu_custom_call" | custom-call | flops 2516582400 | bytes 6553600 | tf_op jit(solution)/shard_map/flow_chunk/pallas_call | solution.py:376
  98.3 2.8 %flow_chunk.11 = (f32[1280,128]{1,0:T(8,128)S(1)}, bf16[128,1280]{1,0:T(8,128)(2,1)S(1)}, f32[1,128]{1,0:T(1,128)S(1)}) custom-call(bf16[1280,2560]{1,0:T(8,128)(2,1)S(1)} %bitcast.61, bf16[656,128]{1,0:T(8,128)(2,1)S(1)} %collective-permute-done.12.b0, bf16[656,128]{1,0:T(8,128)(2,1)S(1)} %collective-permute-done.17.b1, ...), custom_call_target="tpu_custom_call" | custom-call | flops 2516582400 | bytes 6553600 | tf_op jit(solution)/shard_map/flow_chunk/pallas_call | solution.py:376
  109.3 2.8 %collective-permute-done.28 = bf16[128,640]{1,0:T(8,128)(2,1)S(1)} collective-permute-done((bf16[128,640]{1,0:T(8,128)(2,1)S(1)}, bf16[128,640]{1,0:T(8,128)(2,1)S(1)}, u32[]{:S(2)}, u32[]{:S(2)}) %collective-permute-start.28) | collective-permute-done | bytes 163872 | tf_op jit(solution)/shard_map/ppermute | solution.py:390
  121.1 3.5 %collective-permute-done.32 = bf16[128,640]{1,0:T(8,128)(2,1)S(1)} collective-permute-done((bf16[128,640]{1,0:T(8,128)(2,1)S(1)}, bf16[128,640]{1,0:T(8,128)(2,1)S(1)}, u32[]{:S(2)}, u32[]{:S(2)}) %collective-permute-start.32) | collective-permute-done | bytes 163872 | tf_op jit(solution)/shard_map/ppermute | solution.py:390
  126.4 3.6 %collective-permute-done.33.refs_1_ = bf16[128,640]{1,0:T(8,128)(2,1)S(1)} collective-permute-done((bf16[128,640]{1,0:T(8,128)(2,1)S(1)}, bf16[128,640]{1,0:T(8,128)(2,1)S(1)}, u32[]{:S(2)}, u32[]{:S(2)}) %collective-permute-start.33) | collective-permute-done | bytes 163872 | tf_op jit(solution)/shard_map/ppermute | solution.py:390
  130.0 7.1 %update_generators.3 = (bf16[16,144,128]{2,1,0:T(8,128)(2,1)}, bf16[656,128]{1,0:T(8,128)(2,1)S(1)}) custom-call(f32[128,640]{1,0:T(8,128)S(1)} %bitcast_add_fusion.2.refs_0_, bf16[128,640]{1,0:T(8,128)(2,1)S(1)} %collective-permute-done.33.refs_1_, bf16[128,640]{1,0:T(8,128)(2,1)S(1)} %collective-permute-done.36.refs_2_, ...), custom_call_target="tpu_custom_call" | custom-call | flops 1509949440 | bytes 4194304 | tf_op jit(solution)/shard_map/update_generators/pallas_call | solution.py:244
  142.5 4.3 %collective-permute-done.37.b0 = bf16[656,128]{1,0:T(8,128)(2,1)S(1)} collective-permute-done((bf16[656,128]{1,0:T(8,128)(2,1)S(1)}, bf16[656,128]{1,0:T(8,128)(2,1)S(1)}, u32[]{:S(2)}, u32[]{:S(2)}) %collective-permute-start.37) | collective-permute-done | bytes 167968 | tf_op jit(solution)/shard_map/ppermute | solution.py:390
  148.6 2.4 %flow_chunk.12 = (f32[1280,128]{1,0:T(8,128)S(1)}, f32[1,128]{1,0:T(1,128)S(1)}) custom-call(bf16[1280,2560]{1,0:T(8,128)(2,1)S(1)} %bitcast.69, bf16[656,128]{1,0:T(8,128)(2,1)S(1)} %get-tuple-element.113.b0, bf16[656,128]{1,0:T(8,128)(2,1)S(1)} %collective-permute-done.39.b1, bf16[656,128]{1,0:T(8,128)(2,1)S(1)} %collective-permute-done.40.b2, ...), custom_call_target="tpu_custom_call" | custom-call | flops 2516582400 | bytes 6553600 | tf_op jit(solution)/shard_map/flow_chunk/pallas_call | solution.py:376
  153.0 3.6 %all-to-all-start.1 = ((bf16[16,144,128]{2,1,0:T(8,128)(2,1)}), bf16[16,144,128]{2,1,0:T(8,128)(2,1)S(1)}, u32[]{:S(2)}, u32[]{:S(2)}) async-start(bf16[16,144,128]{2,1,0:T(8,128)(2,1)} %get-tuple-element.117), calls=%async_computation.1 | async-start | bytes 1179648 | tf_op jit(solution)/shard_map/all_to_all | solution.py:506
  159.7 8.8 %collective-permute-done.50.b2 = bf16[656,128]{1,0:T(8,128)(2,1)S(1)} collective-permute-done((bf16[656,128]{1,0:T(8,128)(2,1)S(1)}, bf16[656,128]{1,0:T(8,128)(2,1)S(1)}, u32[]{:S(2)}, u32[]{:S(2)}) %collective-permute-start.50) | collective-permute-done | bytes 167968 | tf_op jit(solution)/shard_map/ppermute | solution.py:390
  168.4 2.9 %copy-done.10 = bf16[1280,2560]{1,0:T(8,128)(2,1)S(1)} copy-done((bf16[1280,2560]{1,0:T(8,128)(2,1)S(1)}, bf16[1280,2560]{1,0:T(8,128)(2,1)}, u32[]{:S(2)}) %copy-start.10) | copy-done | bytes 6553624
  175.4 2.9 %copy-done.7 = bf16[1280,2560]{1,0:T(8,128)(2,1)S(1)} copy-done((bf16[1280,2560]{1,0:T(8,128)(2,1)S(1)}, bf16[1280,2560]{1,0:T(8,128)(2,1)}, u32[]{:S(2)}) %copy-start.7) | copy-done | bytes 6553624
  180.7 3.4 %flow_chunk.15 = (f32[1280,128]{1,0:T(8,128)}, bf16[128,1280]{1,0:T(8,128)(2,1)}, f32[1,128]{1,0:T(1,128)S(1)}) custom-call(bf16[1280,2560]{1,0:T(8,128)(2,1)S(1)} %bitcast.63, bf16[656,128]{1,0:T(8,128)(2,1)S(1)} %collective-permute-done.38.b0, bf16[656,128]{1,0:T(8,128)(2,1)S(1)} %collective-permute-done.43.b1, ...), custom_call_target="tpu_custom_call" | custom-call | flops 2516582400 | bytes 6553600 | tf_op jit(solution)/shard_map/flow_chunk/pallas_call | solution.py:376
  (187 shorter events, 68.0 us)
Async XLA Ops:
  8.0 17.8 %collective-permute-start = (bf16[2,128,640]{2,1,0:T(8,128)(2,1)S(1)}, bf16[2,128,640]{2,1,0:T(8,128)(2,1)}, u32[]{:S(2)}, u32[]{:S(2)}) collective-permute-start(bf16[2,128,640]{2,1,0:T(8,128)(2,1)S(1)} %get-tuple-element.73), channel_id=1, source_target_pairs={{0,1},{1,0},{2,3},{3,2},{4,5},{5,4},{6,7},{7,6},{8,9},{9,8},{10,11... | collective-permute-start | bytes 983048 | tf_op jit(solution)/shard_map/ppermute | solution.py:390
  12.0 47.7 %all-to-all-start = ((bf16[16,160,256]{2,1,0:T(8,128)(2,1)}), bf16[16,160,256]{2,1,0:T(8,128)(2,1)S(1)}, u32[]{:S(2)}, u32[]{:S(2)}) async-start(bf16[16,160,256]{2,1,0:T(8,128)(2,1)} %get-tuple-element.70), calls=%async_computation | async-start | bytes 2621440 | tf_op jit(solution)/shard_map/all_to_all | solution.py:427
  25.3 9.3 %collective-permute-start.1 = (bf16[2,128,640]{2,1,0:T(8,128)(2,1)S(1)}, bf16[2,128,640]{2,1,0:T(8,128)(2,1)S(1)}, u32[]{:S(2)}, u32[]{:S(2)}) collective-permute-start(bf16[2,128,640]{2,1,0:T(8,128)(2,1)S(1)} %get-tuple-element.76), channel_id=1, source_target_pairs={{0,1},{1,0},{2,3},{3,2},{4,5},{5,4},{6,7},{7,6},{8,9},{9,8},{10,11... | collective-permute-start | bytes 983048 | tf_op jit(solution)/shard_map/ppermute | solution.py:390
  26.7 10.3 %collective-permute-start.2 = (bf16[128,640]{1,0:T(8,128)(2,1)S(1)}, bf16[128,640]{1,0:T(8,128)(2,1)S(1)}, u32[]{:S(2)}, u32[]{:S(2)}) collective-permute-start(bf16[128,640]{1,0:T(8,128)(2,1)S(1)} %fusion.8), channel_id=1, source_target_pairs={{0,2},{1,3},{2,0},{3,1},{4,6},{5,7},{6,4},{7,5},{8,10},{9,11},{10,... | collective-permute-start | bytes 491528 | tf_op jit(solution)/shard_map/ppermute | solution.py:390
  34.5 10.5 %collective-permute-start.5 = (bf16[2,128,640]{2,1,0:T(8,128)(2,1)S(1)}, bf16[2,128,640]{2,1,0:T(8,128)(2,1)S(1)}, u32[]{:S(2)}, u32[]{:S(2)}) collective-permute-start(bf16[2,128,640]{2,1,0:T(8,128)(2,1)S(1)} %get-tuple-element.81), channel_id=1, source_target_pairs={{0,1},{1,0},{2,3},{3,2},{4,5},{5,4},{6,7},{7,6},{8,9},{9,8},{10,11... | collective-permute-start | bytes 983048 | tf_op jit(solution)/shard_map/ppermute | solution.py:390
  34.6 11.3 %collective-permute-start.8 = (bf16[128,640]{1,0:T(8,128)(2,1)S(1)}, bf16[128,640]{1,0:T(8,128)(2,1)S(1)}, u32[]{:S(2)}, u32[]{:S(2)}) collective-permute-start(bf16[128,640]{1,0:T(8,128)(2,1)S(1)} %fusion.9), channel_id=1, source_target_pairs={{0,2},{1,3},{2,0},{3,1},{4,6},{5,7},{6,4},{7,5},{8,10},{9,11},{10,... | collective-permute-start | bytes 491528 | tf_op jit(solution)/shard_map/ppermute | solution.py:390
  38.0 8.0 %collective-permute-start.9 = (bf16[128,640]{1,0:T(8,128)(2,1)S(1)}, bf16[128,640]{1,0:T(8,128)(2,1)S(1)}, u32[]{:S(2)}, u32[]{:S(2)}) collective-permute-start(bf16[128,640]{1,0:T(8,128)(2,1)S(1)} %fusion.7), channel_id=1, source_target_pairs={{0,4},{1,5},{2,6},{3,7},{4,0},{5,1},{6,2},{7,3},{8,12},{9,13},{10,... | collective-permute-start | bytes 491528 | tf_op jit(solution)/shard_map/ppermute | solution.py:390
  46.0 12.4 %collective-permute-start.10 = (bf16[128,640]{1,0:T(8,128)(2,1)S(1)}, bf16[128,640]{1,0:T(8,128)(2,1)S(1)}, u32[]{:S(2)}, u32[]{:S(2)}) collective-permute-start(bf16[128,640]{1,0:T(8,128)(2,1)S(1)} %fusion.5), channel_id=1, source_target_pairs={{0,8},{1,9},{2,10},{3,11},{4,12},{5,13},{6,14},{7,15},{8,0},{9,1},... | collective-permute-start | bytes 491528 | tf_op jit(solution)/shard_map/ppermute | solution.py:390
  51.8 8.0 %collective-permute-start.7 = (bf16[128,640]{1,0:T(8,128)(2,1)S(1)}, bf16[128,640]{1,0:T(8,128)(2,1)S(1)}, u32[]{:S(2)}, u32[]{:S(2)}) collective-permute-start(bf16[128,640]{1,0:T(8,128)(2,1)S(1)} %fusion.6), channel_id=1, source_target_pairs={{0,4},{1,5},{2,6},{3,7},{4,0},{5,1},{6,2},{7,3},{8,12},{9,13},{10,... | collective-permute-start | bytes 491528 | tf_op jit(solution)/shard_map/ppermute | solution.py:390
  66.1 7.1 %collective-permute-start.14 = (bf16[656,128]{1,0:T(8,128)(2,1)S(1)}, bf16[656,128]{1,0:T(8,128)(2,1)S(1)}, u32[]{:S(2)}, u32[]{:S(2)}) collective-permute-start(bf16[656,128]{1,0:T(8,128)(2,1)S(1)} %get-tuple-element.82.b0), channel_id=1, source_target_pairs={{0,2},{1,3},{2,0},{3,1},{4,6},{5,7},{6,4},{7,5},{8,10},{9,11},{10,... | collective-permute-start | bytes 503816 | tf_op jit(solution)/shard_map/ppermute | solution.py:390
  69.3 8.7 %collective-permute-start.16 = (bf16[656,128]{1,0:T(8,128)(2,1)S(1)}, bf16[656,128]{1,0:T(8,128)(2,1)S(1)}, u32[]{:S(2)}, u32[]{:S(2)}) collective-permute-start(bf16[656,128]{1,0:T(8,128)(2,1)S(1)} %get-tuple-element.82.b0), channel_id=1, source_target_pairs={{0,4},{1,5},{2,6},{3,7},{4,0},{5,1},{6,2},{7,3},{8,12},{9,13},{10,... | collective-permute-start | bytes 503816 | tf_op jit(solution)/shard_map/ppermute | solution.py:390
  69.3 10.5 %collective-permute-start.11 = (bf16[656,128]{1,0:T(8,128)(2,1)S(1)}, bf16[656,128]{1,0:T(8,128)(2,1)S(1)}, u32[]{:S(2)}, u32[]{:S(2)}) collective-permute-start(bf16[656,128]{1,0:T(8,128)(2,1)S(1)} %get-tuple-element.82.b0), channel_id=1, source_target_pairs={{0,8},{1,9},{2,10},{3,11},{4,12},{5,13},{6,14},{7,15},{8,0},{9,1},... | collective-permute-start | bytes 503816 | tf_op jit(solution)/shard_map/ppermute | solution.py:390
  71.9 8.2 %collective-permute-start.13 = (bf16[656,128]{1,0:T(8,128)(2,1)S(1)}, bf16[656,128]{1,0:T(8,128)(2,1)S(1)}, u32[]{:S(2)}, u32[]{:S(2)}) collective-permute-start(bf16[656,128]{1,0:T(8,128)(2,1)S(1)} %get-tuple-element.82.b0), channel_id=1, source_target_pairs={{0,1},{1,0},{2,3},{3,2},{4,5},{5,4},{6,7},{7,6},{8,9},{9,8},{10,11... | collective-permute-start | bytes 503816 | tf_op jit(solution)/shard_map/ppermute | solution.py:390
  73.2 8.6 %collective-permute-start.15 = (bf16[656,128]{1,0:T(8,128)(2,1)S(1)}, bf16[656,128]{1,0:T(8,128)(2,1)S(1)}, u32[]{:S(2)}, u32[]{:S(2)}) collective-permute-start(bf16[656,128]{1,0:T(8,128)(2,1)S(1)} %collective-permute-done.14.b2), channel_id=1, source_target_pairs={{0,1},{1,0},{2,3},{3,2},{4,5},{5,4},{6,7},{7,6},{8,9},{9,8},{10,11... | collective-permute-start | bytes 503816 | tf_op jit(solution)/shard_map/ppermute | solution.py:390
  79.8 9.2 %collective-permute-start.12 = (bf16[656,128]{1,0:T(8,128)(2,1)S(1)}, bf16[656,128]{1,0:T(8,128)(2,1)S(1)}, u32[]{:S(2)}, u32[]{:S(2)}) collective-permute-start(bf16[656,128]{1,0:T(8,128)(2,1)S(1)} %collective-permute-done.11.b0), channel_id=1, source_target_pairs={{0,4},{1,5},{2,6},{3,7},{4,0},{5,1},{6,2},{7,3},{8,12},{9,13},{10,... | collective-permute-start | bytes 503816 | tf_op jit(solution)/shard_map/ppermute | solution.py:390
  80.1 8.9 %collective-permute-start.19 = (bf16[656,128]{1,0:T(8,128)(2,1)S(1)}, bf16[656,128]{1,0:T(8,128)(2,1)S(1)}, u32[]{:S(2)}, u32[]{:S(2)}) collective-permute-start(bf16[656,128]{1,0:T(8,128)(2,1)S(1)} %collective-permute-done.16.b0), channel_id=1, source_target_pairs={{0,1},{1,0},{2,3},{3,2},{4,5},{5,4},{6,7},{7,6},{8,9},{9,8},{10,11... | collective-permute-start | bytes 503816 | tf_op jit(solution)/shard_map/ppermute | solution.py:390
  80.1 9.5 %collective-permute-start.24 = (bf16[656,128]{1,0:T(8,128)(2,1)S(1)}, bf16[656,128]{1,0:T(8,128)(2,1)S(1)}, u32[]{:S(2)}, u32[]{:S(2)}) collective-permute-start(bf16[656,128]{1,0:T(8,128)(2,1)S(1)} %collective-permute-done.11.b0), channel_id=1, source_target_pairs={{0,2},{1,3},{2,0},{3,1},{4,6},{5,7},{6,4},{7,5},{8,10},{9,11},{10,... | collective-permute-start | bytes 503816 | tf_op jit(solution)/shard_map/ppermute | solution.py:390
  81.8 13.9 %collective-permute-start.23 = (bf16[656,128]{1,0:T(8,128)(2,1)S(1)}, bf16[656,128]{1,0:T(8,128)(2,1)S(1)}, u32[]{:S(2)}, u32[]{:S(2)}) collective-permute-start(bf16[656,128]{1,0:T(8,128)(2,1)S(1)} %collective-permute-done.11.b0), channel_id=1, source_target_pairs={{0,1},{1,0},{2,3},{3,2},{4,5},{5,4},{6,7},{7,6},{8,9},{9,8},{10,11... | collective-permute-start | bytes 503816 | tf_op jit(solution)/shard_map/ppermute | solution.py:390
  89.1 9.1 %collective-permute-start.17 = (bf16[656,128]{1,0:T(8,128)(2,1)S(1)}, bf16[656,128]{1,0:T(8,128)(2,1)S(1)}, u32[]{:S(2)}, u32[]{:S(2)}) collective-permute-start(bf16[656,128]{1,0:T(8,128)(2,1)S(1)} %collective-permute-done.12.b0), channel_id=1, source_target_pairs={{0,1},{1,0},{2,3},{3,2},{4,5},{5,4},{6,7},{7,6},{8,9},{9,8},{10,11... | collective-permute-start | bytes 503816 | tf_op jit(solution)/shard_map/ppermute | solution.py:390
  106.7 8.5 %collective-permute-start.34 = (bf16[128,640]{1,0:T(8,128)(2,1)S(1)}, bf16[128,640]{1,0:T(8,128)(2,1)S(1)}, u32[]{:S(2)}, u32[]{:S(2)}) collective-permute-start(bf16[128,640]{1,0:T(8,128)(2,1)S(1)} %fusion.13), channel_id=1, source_target_pairs={{0,2},{1,3},{2,0},{3,1},{4,6},{5,7},{6,4},{7,5},{8,10},{9,11},{10,... | collective-permute-start | bytes 491528 | tf_op jit(solution)/shard_map/ppermute | solution.py:390
  109.3 9.6 %collective-permute-start.31 = (bf16[2,128,640]{2,1,0:T(8,128)(2,1)S(1)}, bf16[2,128,640]{2,1,0:T(8,128)(2,1)S(1)}, u32[]{:S(2)}, u32[]{:S(2)}) collective-permute-start(bf16[2,128,640]{2,1,0:T(8,128)(2,1)S(1)} %get-tuple-element.109), channel_id=1, source_target_pairs={{0,1},{1,0},{2,3},{3,2},{4,5},{5,4},{6,7},{7,6},{8,9},{9,8},{10,11... | collective-permute-start | bytes 983048 | tf_op jit(solution)/shard_map/ppermute | solution.py:390
  117.7 8.8 %collective-permute-start.36 = (bf16[128,640]{1,0:T(8,128)(2,1)S(1)}, bf16[128,640]{1,0:T(8,128)(2,1)S(1)}, u32[]{:S(2)}, u32[]{:S(2)}) collective-permute-start(bf16[128,640]{1,0:T(8,128)(2,1)S(1)} %fusion.1), channel_id=1, source_target_pairs={{0,8},{1,9},{2,10},{3,11},{4,12},{5,13},{6,14},{7,15},{8,0},{9,1},... | collective-permute-start | bytes 491528 | tf_op jit(solution)/shard_map/ppermute | solution.py:390
  138.7 8.1 %collective-permute-start.37 = (bf16[656,128]{1,0:T(8,128)(2,1)S(1)}, bf16[656,128]{1,0:T(8,128)(2,1)S(1)}, u32[]{:S(2)}, u32[]{:S(2)}) collective-permute-start(bf16[656,128]{1,0:T(8,128)(2,1)S(1)} %get-tuple-element.113.b0), channel_id=1, source_target_pairs={{0,8},{1,9},{2,10},{3,11},{4,12},{5,13},{6,14},{7,15},{8,0},{9,1},... | collective-permute-start | bytes 503816 | tf_op jit(solution)/shard_map/ppermute | solution.py:390
  140.1 7.5 %collective-permute-start.42 = (bf16[656,128]{1,0:T(8,128)(2,1)S(1)}, bf16[656,128]{1,0:T(8,128)(2,1)S(1)}, u32[]{:S(2)}, u32[]{:S(2)}) collective-permute-start(bf16[656,128]{1,0:T(8,128)(2,1)S(1)} %get-tuple-element.113.b0), channel_id=1, source_target_pairs={{0,4},{1,5},{2,6},{3,7},{4,0},{5,1},{6,2},{7,3},{8,12},{9,13},{10,... | collective-permute-start | bytes 503816 | tf_op jit(solution)/shard_map/ppermute | solution.py:390
  140.9 7.7 %collective-permute-start.39 = (bf16[656,128]{1,0:T(8,128)(2,1)S(1)}, bf16[656,128]{1,0:T(8,128)(2,1)S(1)}, u32[]{:S(2)}, u32[]{:S(2)}) collective-permute-start(bf16[656,128]{1,0:T(8,128)(2,1)S(1)} %get-tuple-element.113.b0), channel_id=1, source_target_pairs={{0,1},{1,0},{2,3},{3,2},{4,5},{5,4},{6,7},{7,6},{8,9},{9,8},{10,11... | collective-permute-start | bytes 503816 | tf_op jit(solution)/shard_map/ppermute | solution.py:390
  148.0 10.6 %collective-permute-start.46 = (bf16[656,128]{1,0:T(8,128)(2,1)S(1)}, bf16[656,128]{1,0:T(8,128)(2,1)S(1)}, u32[]{:S(2)}, u32[]{:S(2)}) collective-permute-start(bf16[656,128]{1,0:T(8,128)(2,1)S(1)} %collective-permute-done.42.b0), channel_id=1, source_target_pairs={{0,2},{1,3},{2,0},{3,1},{4,6},{5,7},{6,4},{7,5},{8,10},{9,11},{10,... | collective-permute-start | bytes 503816 | tf_op jit(solution)/shard_map/ppermute | solution.py:390
  153.0 31.6 %all-to-all-start.1 = ((bf16[16,144,128]{2,1,0:T(8,128)(2,1)}), bf16[16,144,128]{2,1,0:T(8,128)(2,1)S(1)}, u32[]{:S(2)}, u32[]{:S(2)}) async-start(bf16[16,144,128]{2,1,0:T(8,128)(2,1)} %get-tuple-element.117), calls=%async_computation.1 | async-start | bytes 1179648 | tf_op jit(solution)/shard_map/all_to_all | solution.py:506
  156.9 11.5 %collective-permute-start.50 = (bf16[656,128]{1,0:T(8,128)(2,1)S(1)}, bf16[656,128]{1,0:T(8,128)(2,1)S(1)}, u32[]{:S(2)}, u32[]{:S(2)}) collective-permute-start(bf16[656,128]{1,0:T(8,128)(2,1)S(1)} %collective-permute-done.37.b0), channel_id=1, source_target_pairs={{0,2},{1,3},{2,0},{3,1},{4,6},{5,7},{6,4},{7,5},{8,10},{9,11},{10,... | collective-permute-start | bytes 503816 | tf_op jit(solution)/shard_map/ppermute | solution.py:390
  158.6 9.9 %collective-permute-start.47 = (bf16[656,128]{1,0:T(8,128)(2,1)S(1)}, bf16[656,128]{1,0:T(8,128)(2,1)S(1)}, u32[]{:S(2)}, u32[]{:S(2)}) collective-permute-start(bf16[656,128]{1,0:T(8,128)(2,1)S(1)} %collective-permute-done.46.b2), channel_id=1, source_target_pairs={{0,1},{1,0},{2,3},{3,2},{4,5},{5,4},{6,7},{7,6},{8,9},{9,8},{10,11... | collective-permute-start | bytes 503816 | tf_op jit(solution)/shard_map/ppermute | solution.py:390
  158.8 16.6 %collective-permute-start.49 = (bf16[656,128]{1,0:T(8,128)(2,1)S(1)}, bf16[656,128]{1,0:T(8,128)(2,1)S(1)}, u32[]{:S(2)}, u32[]{:S(2)}) collective-permute-start(bf16[656,128]{1,0:T(8,128)(2,1)S(1)} %collective-permute-done.37.b0), channel_id=1, source_target_pairs={{0,1},{1,0},{2,3},{3,2},{4,5},{5,4},{6,7},{7,6},{8,9},{9,8},{10,11... | collective-permute-start | bytes 503816 | tf_op jit(solution)/shard_map/ppermute | solution.py:390
  159.3 15.5 %collective-permute-start.44 = (bf16[656,128]{1,0:T(8,128)(2,1)S(1)}, bf16[656,128]{1,0:T(8,128)(2,1)S(1)}, u32[]{:S(2)}, u32[]{:S(2)}) collective-permute-start(bf16[656,128]{1,0:T(8,128)(2,1)S(1)} %collective-permute-done.38.b0), channel_id=1, source_target_pairs={{0,2},{1,3},{2,0},{3,1},{4,6},{5,7},{6,4},{7,5},{8,10},{9,11},{10,... | collective-permute-start | bytes 503816 | tf_op jit(solution)/shard_map/ppermute | solution.py:390
  159.7 21.0 %collective-permute-start.43 = (bf16[656,128]{1,0:T(8,128)(2,1)S(1)}, bf16[656,128]{1,0:T(8,128)(2,1)S(1)}, u32[]{:S(2)}, u32[]{:S(2)}) collective-permute-start(bf16[656,128]{1,0:T(8,128)(2,1)S(1)} %collective-permute-done.38.b0), channel_id=1, source_target_pairs={{0,1},{1,0},{2,3},{3,2},{4,5},{5,4},{6,7},{7,6},{8,9},{9,8},{10,11... | collective-permute-start | bytes 503816 | tf_op jit(solution)/shard_map/ppermute | solution.py:390
  (55 other events, 334.6 us)

commit v6 on v5

--- a/solution.py
+++ b/solution.py
@@ -13,7 +13,7 @@
 sigma_step = 0.15
 
 GROUP = 4
-LIMIT = 12 << 20
+LIMIT = 16 << 20
 COST = 3
 META = 16
 F32 = jnp.float32
@@ -267,32 +267,35 @@
     )(*prices, balance_price, demand, recv, previous)
 
 
-def shadow_kernel(chunk, fetch, turn, place_ref, line_ref, ptdf_ref, keep_ref, send_ref, *rest):
+def shadow_kernel(chunk, stream, turn, place_ref, line_ref, ptdf_ref, keep_ref, send_ref, *rest):
     buses = keep_ref.shape[2]
     columns = [slice(rel * buses, (rel + 1) * buses) for rel in range(4)]
-    if turn:
-        *rest, line_t_ref, sems = rest
-        rest = [*rest, sems]
-    if fetch:
-        held_ref, sems = rest
+    if stream:
+        if turn:
+            line_t_ref, held_ref, sems, line_held_ref = rest
+            line_copy = pltpu.make_async_copy(line_ref, line_held_ref, sems.at[4])
+            line_copy.start()
+        else:
+            held_ref, sems = rest
         copies = []
         for rel in range(4):
             start = pl.multiple_of((place_ref[0] ^ (4 * chunk + rel)) * buses, 128)
             copies.append(
                 pltpu.make_async_copy(
-                    ptdf_ref.at[:, pl.ds(start, buses)], held_ref.at[:, pl.ds(rel * buses, buses)], sems.at[rel]
+                    ptdf_ref.at[:, pl.ds(start, buses)], held_ref.at[:, columns[rel]], sems.at[rel]
                 )
             )
         for rel in (3, 2, 1, 0):
             copies[rel].start()
+        if turn:
+            line_copy.wait()
+            line_t_ref[...] = line_held_ref[...].T.astype(BF16)
+            line_ref = line_t_ref
     else:
         held_ref = ptdf_ref
-    if turn:
-        line_t_ref[...] = line_ref[...].T.astype(BF16)
-        line_ref = line_t_ref
 
     def part(rel):
-        if fetch:
+        if stream:
             copies[rel].wait()
         return dot(line_ref[...], held_ref[:, columns[rel]])
 
@@ -302,49 +305,77 @@
     keep_ref[0] = part(0)
 
 
-def shadow_chunk(chunk, fetch, place, line, ptdf, buses):
+def in_hbm(x):
+    return pltpu.with_memory_space_constraint(x, pltpu.MemorySpace.HBM)
+
+
+HBM_SPEC = pl.BlockSpec(memory_space=pltpu.MemorySpace.HBM)
+VMEM_SPEC = pl.BlockSpec(memory_space=pltpu.VMEM)
+SMEM_SPEC = pl.BlockSpec(memory_space=pltpu.SMEM)
+
+
+def chunk_cost(hours, lines, buses):
+    return pl.CostEstimate(flops=COST * 8 * hours * lines * buses, bytes_accessed=8 * lines * buses, transcendentals=0)
+
+
+def shadow_chunk(chunk, stream, place, line, ptdf, buses):
     turn = line.dtype == F32
     lines, hours = line.shape if turn else line.shape[::-1]
-    vmem = pl.BlockSpec(memory_space=pltpu.VMEM)
     out_shape = [
         jax.ShapeDtypeStruct((2, hours, buses), F32),
         jax.ShapeDtypeStruct((2, hours, buses), BF16),
     ]
-    if fetch:
-        out_shape.append(pltpu.VMEM((lines, 4 * buses), BF16))
+    scratch = [pltpu.VMEM((lines, 4 * buses), BF16), pltpu.SemaphoreType.DMA((5,))] if stream else []
     if turn:
         out_shape.append(jax.ShapeDtypeStruct((hours, lines), BF16))
+        scratch.append(pltpu.VMEM((lines, hours), F32))
     return pl.pallas_call(
-        functools.partial(shadow_kernel, chunk, fetch, turn),
-        in_specs=[pl.BlockSpec(memory_space=pltpu.SMEM), vmem, pl.BlockSpec(memory_space=pltpu.MemorySpace.HBM) if fetch else vmem],
-        out_specs=tuple([vmem] * len(out_shape)),
+        functools.partial(shadow_kernel, chunk, stream, turn),
+        in_specs=[SMEM_SPEC, HBM_SPEC if turn else VMEM_SPEC, HBM_SPEC if stream else VMEM_SPEC],
+        out_specs=tuple([VMEM_SPEC] * len(out_shape)),
         out_shape=tuple(out_shape),
-        scratch_shapes=[pltpu.SemaphoreType.DMA((4,))] if fetch else [],
+        scratch_shapes=scratch,
         compiler_params=pltpu.CompilerParams(vmem_limit_bytes=LIMIT),
-        cost_estimate=pl.CostEstimate(
-            flops=COST * 8 * hours * lines * buses, bytes_accessed=8 * lines * buses, transcendentals=0
-        ),
+        cost_estimate=chunk_cost(hours, lines, buses),
         name="shadow_chunk",
-    )(place, line, pltpu.with_memory_space_constraint(ptdf, pltpu.MemorySpace.HBM) if fetch else ptdf)
-
-
-def flow_kernel(start, end, ptdf_ref, b0, b1, b2, b3, acc_ref, sum_ref, *rest):
+    )(place, in_hbm(line) if turn else line, in_hbm(ptdf) if stream else ptdf)
+
+
+TILES = 4
+
+
+def flow_kernel(chunk, start, end, keep, place_ref, ptdf_ref, b0, b1, b2, b3, acc_ref, sum_ref, *rest):
     if end:
-        limit_ref, line_ref, out_ref, half_ref, sum_out, inj_ref = rest
+        limit_ref, line_ref, out_ref, half_ref, sum_out, *rest = rest
     else:
-        out_ref, sum_out, inj_ref = rest
+        out_ref, sum_out, *rest = rest
+    held_ref, inj_ref, sems = rest
     buses = inj_ref.shape[0] // 4
+    tile = held_ref.shape[0] // TILES
+    copies = []
+    for i in range(TILES):
+        rows = pl.ds(i * tile, tile)
+        for rel in range(4):
+            first = pl.multiple_of((place_ref[0] ^ (4 * chunk + rel)) * buses, 128)
+            copies.append(
+                pltpu.make_async_copy(
+                    ptdf_ref.at[rows, pl.ds(first, buses)],
+                    held_ref.at[rows, pl.ds(rel * buses, buses)],
+                    sems.at[i, rel],
+                )
+            )
+            copies[-1].start()
     total = jnp.zeros(sum_ref.shape, F32) if start else sum_ref[...]
     for rel, ref in enumerate((b0, b1, b2, b3)):
         inj_ref[rel * buses : (rel + 1) * buses, :] = ref[:buses, :]
         tail = ref[buses:, :].astype(F32)
         total = total + jnp.sum(tail, axis=0, keepdims=True)
     sum_out[...] = total
-    tile = ptdf_ref.shape[0] // 4
-
-    def body(i, carry):
-        rows = pl.ds(pl.multiple_of(i * tile, tile), tile)
-        flow = dot(ptdf_ref[rows, :], inj_ref[...])
+    for i in range(TILES):
+        rows = slice(i * tile, (i + 1) * tile)
+        for copy in copies[4 * i : 4 * i + 4]:
+            copy.wait()
+        flow = dot(held_ref[rows, :], inj_ref[...])
         if not start:
             flow = flow + acc_ref[rows, :]
         if end:
@@ -354,36 +385,35 @@
             out_ref[rows, :] = line
         else:
             out_ref[rows, :] = flow
-        return carry
-
-    lax.fori_loop(0, 4, body, 0)
     if end:
         half_ref[...] = out_ref[...].T.astype(BF16)
 
 
-def flow_chunk(ptdf, blocks, acc, total, limit=None, line=None):
+def flow_chunk(chunk, keep, place, ptdf, blocks, acc, total, limit=None, line=None):
     lines = ptdf.shape[0]
     rows, hours = blocks[0].shape
     buses = rows - META
     start, end = acc is None, limit is not None
-    operands = [ptdf, *blocks, total if start else acc, total]
+    operands = [*blocks, total if start else acc, total]
     out_shape = [jax.ShapeDtypeStruct((lines, hours), F32)]
     if end:
         operands += [limit, line]
         out_shape += [jax.ShapeDtypeStruct((hours, lines), BF16)]
     out_shape += [jax.ShapeDtypeStruct((1, hours), F32)]
-    in_specs = [pl.BlockSpec(memory_space=pltpu.VMEM)] * len(operands)
+    held = pltpu.VMEM((lines, 4 * buses), BF16)
+    if keep:
+        out_shape.append(held)
     return pl.pallas_call(
-        functools.partial(flow_kernel, start, end),
-        in_specs=in_specs,
+        functools.partial(flow_kernel, chunk, start, end, keep),
+        in_specs=[SMEM_SPEC, HBM_SPEC] + [VMEM_SPEC] * len(operands),
+        out_specs=tuple([VMEM_SPEC] * len(out_shape)),
         out_shape=tuple(out_shape),
-        scratch_shapes=[pltpu.VMEM((4 * buses, hours), BF16)],
+        scratch_shapes=([] if keep else [held])
+        + [pltpu.VMEM((4 * buses, hours), BF16), pltpu.SemaphoreType.DMA((TILES, 4))],
         compiler_params=pltpu.CompilerParams(vmem_limit_bytes=LIMIT),
-        cost_estimate=pl.CostEstimate(
-            flops=COST * 8 * hours * lines * buses, bytes_accessed=8 * lines * buses, transcendentals=0
-        ),
+        cost_estimate=chunk_cost(hours, lines, buses),
         name="flow_chunk",
-    )(*operands)
+    )(place, in_hbm(ptdf), *operands)
 
 
 def swap(x, devices, mask):
@@ -449,15 +479,12 @@
                 return part
 
             def product(chunk, line_t):
-                if chunk in resident:
-                    keeps[chunk], send = shadow_chunk(chunk, False, place, line_t, resident[chunk], buses)
-                else:
-                    keeps[chunk], send, resident[chunk], *turned = shadow_chunk(
-                        chunk, True, place, line_t, ptdf, buses
-                    )
-                    line_t = turned[0] if turned else line_t
+                columns = resident.get(chunk, ptdf)
+                keeps[chunk], send, *turned = shadow_chunk(
+                    chunk, chunk not in resident, place, line_t, columns, buses
+                )
                 gots[chunk] = swap(send, devices, 1)
-                return line_t
+                return turned[0] if turned else line_t
 
             line_t = product(3, line_t)
             if iteration == 0:
@@ -467,9 +494,9 @@
             product(1, line_t)
             line_t, _, _ = lax.optimization_barrier((line_t, across(2), settle(3)))
             product(0, line_t)
-            across(1)
-            settle(2)
-            across(0)
+            gots[1], crossed[2] = lax.optimization_barrier((gots[1], crossed[2]))
+            parts[3], _, _ = lax.optimization_barrier((parts[3], across(1), across(0)))
+            crossed[1], _ = lax.optimization_barrier((crossed[1], settle(2)))
             settle(1)
             settle(0)
             prices = [parts[0], parts[1], parts[2]]
@@ -490,29 +517,35 @@
             def blocks(chunk):
                 return [near[chunk], cross[chunk], far[chunk], far_cross[chunk]]
 
+            def flow(chunk, acc, total, *rest):
+                acc, *given = flow_chunk(chunk, not last, place, ptdf, blocks(chunk), acc, total, *rest)
+                if not last:
+                    *given, resident[chunk] = given
+                return (acc, *given)
+
             near[2] = swap(block, devices, 8)
             near[1] = swap(block, devices, 4)
             spread(0)
+            near[1], near[2], far[0], cross[0], row = lax.optimization_barrier(
+                (near[1], near[2], far[0], cross[0], balance_row)
+            )
             near[3] = swap(near[2], devices, 4)
             spread(1)
             spread(2)
             settle_far(0)
-            near[1], near[2], row = lax.optimization_barrier((near[1], near[2], balance_row))
-            acc, total = flow_chunk(resident[0], blocks(0), None, row)
+            acc, total = flow(0, None, row)
             near[3], acc = lax.optimization_barrier((near[3], acc))
             spread(3)
-            if last:
-                held, _ = lax.optimization_barrier((held, near[3]))
-                back = lax.all_to_all(held, "bus", split_axis=0, concat_axis=0, tiled=True)
             settle_far(1)
-            acc, total = flow_chunk(resident[1], blocks(1), acc, total)
+            acc, total = flow(1, acc, total)
             settle_far(2)
             far[3], acc = lax.optimization_barrier((far[3], acc))
-            acc, total = flow_chunk(resident[2], blocks(2), acc, total)
+            if last:
+                held, _ = lax.optimization_barrier((held, far[2]))
+                back = lax.all_to_all(held, "bus", split_axis=0, concat_axis=0, tiled=True)
+            acc, total = flow(2, acc, total)
             settle_far(3)
-            line_price, line_half, total = flow_chunk(
-                resident[3], blocks(3), acc, total, limit, line_price
-            )
+            line_price, line_half, total = flow(3, acc, total, limit, line_price)
             balance = total
         else:
             if last:

time: 187 us -> 201 us (1.075)
  Pallas kernels: 58.3 us -> 87.5 us
  local copies, waits for them, and re-layouts: 26.9 us -> 3.6 us
  waiting for transfers between devices: 48.5 us -> 56.6 us
    pallas_call x16, Pallas kernels: 39.2 us -> 68.2 us  [the longest x8 49.1 us: flow_chunk(): pl.pallas_call(functools.partial(flow_kernel, chunk, start, end, keep), i...]
    unnamed x66 -> x34, local copies, waits for them, and re-layouts: 26.5 us -> 3.22 us
    ppermute x52, waiting for transfers between devices: 48.5 us -> 56.6 us  [swap(): return lax.ppermute(x, 'bus', [(i, i ^ mask) for i in range(devices)])]
    ppermute x52, starting transfers between devices: 38 us -> 34.9 us  [swap(): return lax.ppermute(x, 'bus', [(i, i ^ mask) for i in range(devices)])]
    all_to_all x1, starting transfers between devices: 3.58 us -> 6.2 us  [local(): back = lax.all_to_all(held, 'bus', split_axis=0, concat_axis=0, tiled=True)]
  transfers between devices with their start and end apart: 54 -> 54, of which waited for: 21 -> 15; matrix products, arithmetic and copies ran while one was open for 2% -> 2% of each run, Pallas kernels for 19% -> 31%
where the time goes in v6:
time: 201 us; the launch traced here: 200 us
  Pallas kernels  87.5 us (44%)
  waiting for transfers between devices  56.6 us (28%)
  starting transfers between devices  48.2 us (24%)
  local copies, waits for them, and re-layouts  3.6 us (2%)
  other arithmetic  3.14 us (2%)
    ppermute x52, waiting for transfers between devices, swap(): return lax.ppermute(x, 'bus', [(i, i ^ mask) for i in range(devices)])  56.6 us
    pallas_call x8, Pallas kernels, flow_chunk(): pl.pallas_call(functools.partial(flow_kernel, chunk, start, end, keep), i...  49.1 us
    ppermute x52, starting transfers between devices, swap(): return lax.ppermute(x, 'bus', [(i, i ^ mask) for i in range(devices)])  34.9 us
    pallas_call x8, Pallas kernels, shadow_chunk(): pl.pallas_call(functools.partial(shadow_kernel, chunk, stream, turn), in_...  19 us
    pallas_call x2, Pallas kernels, update(): pl.pallas_call(functools.partial(update_kernel, cap, first, last, len(pri...  13.6 us
    all_to_all x1, starting transfers between devices, local(): lax.all_to_all(outgoing, 'bus', split_axis=0, concat_axis=0, tiled=True)  7.04 us
    all_to_all x1, starting transfers between devices, local(): back = lax.all_to_all(held, 'bus', split_axis=0, concat_axis=0, tiled=True)  6.2 us
  transfers between devices with their start and end apart: 54, of which 15 were waited for; matrix products, arithmetic and copies ran while one was open for 2% of the time, Pallas kernels for 31%

profile of v6, /device:TPU:0, one launch (start us, length us, event | category | flops | bytes accessed | tf_op | source)
XLA Modules:
  0.0 200.2 jit_solution(17014763845269590431)
XLA Ops:
  0.7 3.7 %shadow_chunk.8 = (f32[2,128,640]{2,1,0:T(8,128)S(1)}, bf16[2,128,640]{2,1,0:T(8,128)(2,1)S(1)}, bf16[128,1280]{1,0:T(8,128)(2,1)S(1)}) custom-call(s32[1]{0:T(128)} %bitcast.4.place_ref, f32[1280,128]{1,0:T(8,128)} %rest_1_.1, bf16[1280,10240]{1,0:T(8,128)(2,1)} %ptdf_ref.23), custom_call_target="tpu_custom_call" | custom-call | flops 2516582400 | bytes 6553600 | tf_op jit(solution)/shard_map/shadow_chunk/pallas_call | solution.py:332
  4.9 3.6 %pack_generators.1 = (bf16[16,160,256]{2,1,0:T(8,128)(2,1)}, s32[1,768]{1,0:T(1,128)S(1)}) custom-call(s32[1,768]{1,0:T(1,128)S(1)} %bitcast.66, s32[6,128]{1,0:T(8,128)S(1)} %bitcast.64, f32[6,128]{1,0:T(8,128)S(1)} %bitcast.65, f32[768,128]{1,0:T(8,128)S(1)} %copy-done.1, f32[6,128]{1,0:T(8,128)S(1)} %bitcast.59, f32[768,128]{1,0:T(8,128)S(1)} %copy-done.2), custom_call_target="tpu_custom_call" | custom-call | flops 905969664 | bytes 3145728 | tf_op jit(solution)/shard_map/pack_generators/pallas_call | solution.py:102
  8.5 7.0 %all-to-all-start = ((bf16[16,160,256]{2,1,0:T(8,128)(2,1)}), bf16[16,160,256]{2,1,0:T(8,128)(2,1)S(1)}, u32[]{:S(2)}, u32[]{:S(2)}) async-start(bf16[16,160,256]{2,1,0:T(8,128)(2,1)} %get-tuple-element.81), calls=%async_computation | async-start | bytes 2621440 | tf_op jit(solution)/shard_map/all_to_all | solution.py:457
  15.6 3.4 %shadow_chunk.9 = (f32[2,128,640]{2,1,0:T(8,128)S(1)}, bf16[2,128,640]{2,1,0:T(8,128)(2,1)S(1)}) custom-call(s32[1]{0:T(128)} %bitcast.4.place_ref, bf16[128,1280]{1,0:T(8,128)(2,1)S(1)} %get-tuple-element.88.line_ref, bf16[1280,10240]{1,0:T(8,128)(2,1)} %ptdf_ref.23), custom_call_target="tpu_custom_call" | custom-call | flops 2516582400 | bytes 6553600 | tf_op jit(solution)/shard_map/shadow_chunk/pallas_call | solution.py:332
  22.2 3.4 %shadow_chunk.11 = (f32[2,128,640]{2,1,0:T(8,128)S(1)}, bf16[2,128,640]{2,1,0:T(8,128)(2,1)S(1)}) custom-call(s32[1]{0:T(128)} %bitcast.4.place_ref, bf16[128,1280]{1,0:T(8,128)(2,1)S(1)} %get-tuple-element.88.line_ref, bf16[1280,10240]{1,0:T(8,128)(2,1)} %ptdf_ref.23), custom_call_target="tpu_custom_call" | custom-call | flops 2516582400 | bytes 6553600 | tf_op jit(solution)/shard_map/shadow_chunk/pallas_call | solution.py:332
  26.2 6.9 %collective-permute-done.2 = bf16[128,640]{1,0:T(8,128)(2,1)S(1)} collective-permute-done((bf16[128,640]{1,0:T(8,128)(2,1)S(1)}, bf16[128,640]{1,0:T(8,128)(2,1)S(1)}, u32[]{:S(2)}, u32[]{:S(2)}) %collective-permute-start.2) | collective-permute-done | bytes 163872 | tf_op jit(solution)/shard_map/ppermute | solution.py:420
  34.1 3.5 %shadow_chunk.10 = (f32[2,128,640]{2,1,0:T(8,128)S(1)}, bf16[2,128,640]{2,1,0:T(8,128)(2,1)S(1)}) custom-call(s32[1]{0:T(128)} %bitcast.4.place_ref, bf16[128,1280]{1,0:T(8,128)(2,1)S(1)} %get-tuple-element.88.line_ref, bf16[1280,10240]{1,0:T(8,128)(2,1)} %ptdf_ref.23), custom_call_target="tpu_custom_call" | custom-call | flops 2516582400 | bytes 6553600 | tf_op jit(solution)/shard_map/shadow_chunk/pallas_call | solution.py:332
  40.0 7.5 %collective-permute-done.8 = bf16[128,640]{1,0:T(8,128)(2,1)S(1)} collective-permute-done((bf16[128,640]{1,0:T(8,128)(2,1)S(1)}, bf16[128,640]{1,0:T(8,128)(2,1)S(1)}, u32[]{:S(2)}, u32[]{:S(2)}) %collective-permute-start.8) | collective-permute-done | bytes 163872 | tf_op jit(solution)/shard_map/ppermute | solution.py:420
  49.5 2.5 %collective-permute-start.9 = (bf16[128,640]{1,0:T(8,128)(2,1)S(1)}, bf16[128,640]{1,0:T(8,128)(2,1)S(1)}, u32[]{:S(2)}, u32[]{:S(2)}) collective-permute-start(bf16[128,640]{1,0:T(8,128)(2,1)S(1)} %fusion.6), channel_id=1, source_target_pairs={{0,4},{1,5},{2,6},{3,7},{4,0},{5,1},{6,2},{7,3},{8,12},{9,13},{10,... | collective-permute-start | bytes 491528 | tf_op jit(solution)/shard_map/ppermute | solution.py:420
  52.1 6.3 %collective-permute-done.9.refs_1_ = bf16[128,640]{1,0:T(8,128)(2,1)S(1)} collective-permute-done((bf16[128,640]{1,0:T(8,128)(2,1)S(1)}, bf16[128,640]{1,0:T(8,128)(2,1)S(1)}, u32[]{:S(2)}, u32[]{:S(2)}) %collective-permute-start.9) | collective-permute-done | bytes 163872 | tf_op jit(solution)/shard_map/ppermute | solution.py:420
  58.4 6.5 %update_generators.2 = (f32[16,144,128]{2,1,0:T(8,128)S(1)}, bf16[656,128]{1,0:T(8,128)(2,1)S(1)}) custom-call(f32[128,640]{1,0:T(8,128)S(1)} %bitcast_add_fusion.6.refs_0_, bf16[128,640]{1,0:T(8,128)(2,1)S(1)} %collective-permute-done.9.refs_1_, bf16[128,640]{1,0:T(8,128)(2,1)S(1)} %collective-permute-done.10.refs_2_, f32[1,128]{1,0:T(1,128)S(1)} %bitcast.60, ...), custom_call_target="tpu_custom_call" | custom-call | flops 1509949440 | bytes 4194304 | tf_op jit(solution)/shard_map/update_generators/pallas_call | solution.py:244
  65.3 2.6 %collective-permute-start.12 = (bf16[656,128]{1,0:T(8,128)(2,1)S(1)}, bf16[656,128]{1,0:T(8,128)(2,1)S(1)}, u32[]{:S(2)}, u32[]{:S(2)}) collective-permute-start(bf16[656,128]{1,0:T(8,128)(2,1)S(1)} %get-tuple-element.97.b0), channel_id=1, source_target_pairs={{0,8},{1,9},{2,10},{3,11},{4,12},{5,13},{6,14},{7,15},{8,0},{9,1},... | collective-permute-start | bytes 503816 | tf_op jit(solution)/shard_map/ppermute | solution.py:420
  68.7 4.7 %collective-permute-done.11.b0 = bf16[656,128]{1,0:T(8,128)(2,1)S(1)} collective-permute-done((bf16[656,128]{1,0:T(8,128)(2,1)S(1)}, bf16[656,128]{1,0:T(8,128)(2,1)S(1)}, u32[]{:S(2)}, u32[]{:S(2)}) %collective-permute-start.11) | collective-permute-done | bytes 167968 | tf_op jit(solution)/shard_map/ppermute | solution.py:420
  78.5 4.2 %collective-permute-done.20.b2 = bf16[656,128]{1,0:T(8,128)(2,1)S(1)} collective-permute-done((bf16[656,128]{1,0:T(8,128)(2,1)S(1)}, bf16[656,128]{1,0:T(8,128)(2,1)S(1)}, u32[]{:S(2)}, u32[]{:S(2)}) %collective-permute-start.20) | collective-permute-done | bytes 167968 | tf_op jit(solution)/shard_map/ppermute | solution.py:420
  82.7 5.5 %flow_chunk.8 = (f32[1280,128]{1,0:T(8,128)S(1)}, f32[1,128]{1,0:T(1,128)S(1)}, bf16[1280,2560]{1,0:T(8,128)(2,1)S(1)}) custom-call(s32[1]{0:T(128)} %bitcast.4.place_ref, bf16[1280,10240]{1,0:T(8,128)(2,1)} %ptdf_ref.23, bf16[656,128]{1,0:T(8,128)(2,1)S(1)} %get-tuple-element.97.b0, bf16[656,128]{1,0:T(8,128)(2,1)S(1)} %collective-permute-done.14.b1, ...), custom_call_target="tpu_custom_call" | custom-call | flops 2516582400 | bytes 6553600 | tf_op jit(solution)/shard_map/flow_chunk/pallas_call | solution.py:406
  89.7 5.5 %flow_chunk.9 = (f32[1280,128]{1,0:T(8,128)S(1)}, f32[1,128]{1,0:T(1,128)S(1)}, bf16[1280,2560]{1,0:T(8,128)(2,1)S(1)}) custom-call(s32[1]{0:T(128)} %bitcast.4.place_ref, bf16[1280,10240]{1,0:T(8,128)(2,1)} %ptdf_ref.23, bf16[656,128]{1,0:T(8,128)(2,1)S(1)} %collective-permute-done.11.b0, bf16[656,128]{1,0:T(8,128)(2,1)S(1)} %collective-permute-done.19.b1, ...), custom_call_target="tpu_custom_call" | custom-call | flops 2516582400 | bytes 6553600 | tf_op jit(solution)/shard_map/flow_chunk/pallas_call | solution.py:406
  95.8 5.6 %flow_chunk.10 = (f32[1280,128]{1,0:T(8,128)S(1)}, f32[1,128]{1,0:T(1,128)S(1)}, bf16[1280,2560]{1,0:T(8,128)(2,1)S(1)}) custom-call(s32[1]{0:T(128)} %bitcast.4.place_ref, bf16[1280,10240]{1,0:T(8,128)(2,1)} %ptdf_ref.23, bf16[656,128]{1,0:T(8,128)(2,1)S(1)} %collective-permute-done.12.b0, bf16[656,128]{1,0:T(8,128)(2,1)S(1)} %collective-permute-done.23.b1, ...), custom_call_target="tpu_custom_call" | custom-call | flops 2516582400 | bytes 6553600 | tf_op jit(solution)/shard_map/flow_chunk/pallas_call | solution.py:406
  101.4 5.6 %flow_chunk.11 = (f32[1280,128]{1,0:T(8,128)S(1)}, bf16[128,1280]{1,0:T(8,128)(2,1)S(1)}, f32[1,128]{1,0:T(1,128)S(1)}, bf16[1280,2560]{1,0:T(8,128)(2,1)S(1)}) custom-call(s32[1]{0:T(128)} %bitcast.4.place_ref, bf16[1280,10240]{1,0:T(8,128)(2,1)} %ptdf_ref.23, bf16[656,128]{1,0:T(8,128)(2,1)S(1)} %collective-permute-done.15.b0, ...), custom_call_target="tpu_custom_call" | custom-call | flops 2516582400 | bytes 6553600 | tf_op jit(solution)/shard_map/flow_chunk/pallas_call | solution.py:406
  113.9 2.7 %collective-permute-done.28 = bf16[128,640]{1,0:T(8,128)(2,1)S(1)} collective-permute-done((bf16[128,640]{1,0:T(8,128)(2,1)S(1)}, bf16[128,640]{1,0:T(8,128)(2,1)S(1)}, u32[]{:S(2)}, u32[]{:S(2)}) %collective-permute-start.28) | collective-permute-done | bytes 163872 | tf_op jit(solution)/shard_map/ppermute | solution.py:420
  122.1 2.5 %collective-permute-done.34 = bf16[128,640]{1,0:T(8,128)(2,1)S(1)} collective-permute-done((bf16[128,640]{1,0:T(8,128)(2,1)S(1)}, bf16[128,640]{1,0:T(8,128)(2,1)S(1)}, u32[]{:S(2)}, u32[]{:S(2)}) %collective-permute-start.34) | collective-permute-done | bytes 163872 | tf_op jit(solution)/shard_map/ppermute | solution.py:420
  127.4 2.1 %collective-permute-done.30 = bf16[128,640]{1,0:T(8,128)(2,1)S(1)} collective-permute-done((bf16[128,640]{1,0:T(8,128)(2,1)S(1)}, bf16[128,640]{1,0:T(8,128)(2,1)S(1)}, u32[]{:S(2)}, u32[]{:S(2)}) %collective-permute-start.30) | collective-permute-done | bytes 163872 | tf_op jit(solution)/shard_map/ppermute | solution.py:420
  129.5 6.2 %collective-permute-done.35.refs_1_ = bf16[128,640]{1,0:T(8,128)(2,1)S(1)} collective-permute-done((bf16[128,640]{1,0:T(8,128)(2,1)S(1)}, bf16[128,640]{1,0:T(8,128)(2,1)S(1)}, u32[]{:S(2)}, u32[]{:S(2)}) %collective-permute-start.35) | collective-permute-done | bytes 163872 | tf_op jit(solution)/shard_map/ppermute | solution.py:420
  135.7 7.1 %update_generators.3 = (bf16[16,144,128]{2,1,0:T(8,128)(2,1)}, bf16[656,128]{1,0:T(8,128)(2,1)S(1)}) custom-call(f32[128,640]{1,0:T(8,128)S(1)} %bitcast_add_fusion.2.refs_0_, bf16[128,640]{1,0:T(8,128)(2,1)S(1)} %collective-permute-done.35.refs_1_, bf16[128,640]{1,0:T(8,128)(2,1)S(1)} %collective-permute-done.36.refs_2_, ...), custom_call_target="tpu_custom_call" | custom-call | flops 1509949440 | bytes 4194304 | tf_op jit(solution)/shard_map/update_generators/pallas_call | solution.py:244
  142.7 2.6 %collective-permute-start.38 = (bf16[656,128]{1,0:T(8,128)(2,1)S(1)}, bf16[656,128]{1,0:T(8,128)(2,1)S(1)}, u32[]{:S(2)}, u32[]{:S(2)}) collective-permute-start(bf16[656,128]{1,0:T(8,128)(2,1)S(1)} %get-tuple-element.135.b0), channel_id=1, source_target_pairs={{0,8},{1,9},{2,10},{3,11},{4,12},{5,13},{6,14},{7,15},{8,0},{9,1},... | collective-permute-start | bytes 503816 | tf_op jit(solution)/shard_map/ppermute | solution.py:420
  147.1 4.0 %collective-permute-done.37.b0 = bf16[656,128]{1,0:T(8,128)(2,1)} collective-permute-done((bf16[656,128]{1,0:T(8,128)(2,1)S(1)}, bf16[656,128]{1,0:T(8,128)(2,1)}, u32[]{:S(2)}, u32[]{:S(2)}) %collective-permute-start.37) | collective-permute-done | bytes 167968 | tf_op jit(solution)/shard_map/ppermute | solution.py:420
  156.2 2.5 %collective-permute-done.41.b2 = bf16[656,128]{1,0:T(8,128)(2,1)S(1)} collective-permute-done((bf16[656,128]{1,0:T(8,128)(2,1)S(1)}, bf16[656,128]{1,0:T(8,128)(2,1)S(1)}, u32[]{:S(2)}, u32[]{:S(2)}) %collective-permute-start.41) | collective-permute-done | bytes 167968 | tf_op jit(solution)/shard_map/ppermute | solution.py:420
  159.3 6.2 %all-to-all-start.1 = ((bf16[16,144,128]{2,1,0:T(8,128)(2,1)}), bf16[16,144,128]{2,1,0:T(8,128)(2,1)S(1)}, u32[]{:S(2)}, u32[]{:S(2)}) async-start(bf16[16,144,128]{2,1,0:T(8,128)(2,1)} %get-tuple-element.137), calls=%async_computation.1 | async-start | bytes 1179648 | tf_op jit(solution)/shard_map/all_to_all | solution.py:545
  167.9 6.5 %flow_chunk.12 = (f32[1280,128]{1,0:T(8,128)S(1)}, f32[1,128]{1,0:T(1,128)S(1)}) custom-call(s32[1]{0:T(128)} %bitcast.4.place_ref, bf16[1280,10240]{1,0:T(8,128)(2,1)} %ptdf_ref.23, bf16[656,128]{1,0:T(8,128)(2,1)S(1)} %copy-done.6, bf16[656,128]{1,0:T(8,128)(2,1)S(1)} %copy-done.8, bf16[656,128]{1,0:T(8,128)(2,1)} %collective-permute-done.39.b2, ...), custom_call_target="tpu_custom_call" | custom-call | flops 2516582400 | bytes 6553600 | tf_op jit(solution)/shard_map/flow_chunk/pallas_call | solution.py:406
  176.5 6.6 %flow_chunk.13 = (f32[1280,128]{1,0:T(8,128)S(1)}, f32[1,128]{1,0:T(1,128)S(1)}) custom-call(s32[1]{0:T(128)} %bitcast.4.place_ref, bf16[1280,10240]{1,0:T(8,128)(2,1)} %ptdf_ref.23, bf16[656,128]{1,0:T(8,128)(2,1)} %collective-permute-done.37.b0, bf16[656,128]{1,0:T(8,128)(2,1)} %collective-permute-done.46.b1, bf16[656,128]{1,0:T(8,128)(2,1)} %collective-permute-done.47.b2, ...), custom_call_target="tpu_custom_call" | custom-call | flops 2516582400 | bytes 6553600 | tf_op jit(solution)/shard_map/flow_chunk/pallas_call | solution.py:406
  183.7 6.4 %flow_chunk.14 = (f32[1280,128]{1,0:T(8,128)S(1)}, f32[1,128]{1,0:T(1,128)S(1)}) custom-call(s32[1]{0:T(128)} %bitcast.4.place_ref, bf16[1280,10240]{1,0:T(8,128)(2,1)} %ptdf_ref.23, bf16[656,128]{1,0:T(8,128)(2,1)S(1)} %collective-permute-done.38.b0, bf16[656,128]{1,0:T(8,128)(2,1)} %collective-permute-done.50.b1, bf16[656,128]{1,0:T(8,128)(2,1)S(1)} %copy-done.4, ...), custom_call_target="tpu_custom_call" | custom-call | flops 2516582400 | bytes 6553600 | tf_op jit(solution)/shard_map/flow_chunk/pallas_call | solution.py:406
  190.1 7.4 %flow_chunk.15 = (f32[1280,128]{1,0:T(8,128)}, bf16[128,1280]{1,0:T(8,128)(2,1)}, f32[1,128]{1,0:T(1,128)S(1)}) custom-call(s32[1]{0:T(128)} %bitcast.4.place_ref, bf16[1280,10240]{1,0:T(8,128)(2,1)} %ptdf_ref.23, bf16[656,128]{1,0:T(8,128)(2,1)} %collective-permute-done.42.b0, bf16[656,128]{1,0:T(8,128)(2,1)S(1)} %collective-permute-done.44.b1, ...), custom_call_target="tpu_custom_call" | custom-call | flops 2516582400 | bytes 6553600 | tf_op jit(solution)/shard_map/flow_chunk/pallas_call | solution.py:406
  198.1 2.1 %unpack_dispatch.1 = f32[768,128]{1,0:T(8,128)} custom-call(s32[1,768]{1,0:T(1,128)S(1)} %get-tuple-element.79.slot_ref, bf16[2304,128]{1,0:T(8,128)(2,1)S(1)} %bitcast.58, f32[768,128]{1,0:T(8,128)S(1)} %copy-done.1, f32[768,1]{1,0:T(8,128)S(1)} %reshape.87.max_ref, f32[768,128]{1,0:T(8,128)S(1)} %copy-done.2), custom_call_target="tpu_custom_call" | custom-call | flops 452984832 | bytes 1048576 | tf_op jit(solution)/shard_map/unpack_dispatch/pallas_call | solution.py:158
  (150 shorter events, 45.9 us)
Async XLA Ops:
  4.4 15.1 %collective-permute-start = (bf16[2,128,640]{2,1,0:T(8,128)(2,1)S(1)}, bf16[2,128,640]{2,1,0:T(8,128)(2,1)}, u32[]{:S(2)}, u32[]{:S(2)}) collective-permute-start(bf16[2,128,640]{2,1,0:T(8,128)(2,1)S(1)} %get-tuple-element.84), channel_id=1, source_target_pairs={{0,1},{1,0},{2,3},{3,2},{4,5},{5,4},{6,7},{7,6},{8,9},{9,8},{10,11... | collective-permute-start | bytes 983048 | tf_op jit(solution)/shard_map/ppermute | solution.py:420
  8.5 49.8 %all-to-all-start = ((bf16[16,160,256]{2,1,0:T(8,128)(2,1)}), bf16[16,160,256]{2,1,0:T(8,128)(2,1)S(1)}, u32[]{:S(2)}, u32[]{:S(2)}) async-start(bf16[16,160,256]{2,1,0:T(8,128)(2,1)} %get-tuple-element.81), calls=%async_computation | async-start | bytes 2621440 | tf_op jit(solution)/shard_map/all_to_all | solution.py:457
  20.5 12.7 %collective-permute-start.2 = (bf16[128,640]{1,0:T(8,128)(2,1)S(1)}, bf16[128,640]{1,0:T(8,128)(2,1)S(1)}, u32[]{:S(2)}, u32[]{:S(2)}) collective-permute-start(bf16[128,640]{1,0:T(8,128)(2,1)S(1)} %fusion.8), channel_id=1, source_target_pairs={{0,2},{1,3},{2,0},{3,1},{4,6},{5,7},{6,4},{7,5},{8,10},{9,11},{10,... | collective-permute-start | bytes 491528 | tf_op jit(solution)/shard_map/ppermute | solution.py:420
  25.6 12.2 %collective-permute-start.5 = (bf16[2,128,640]{2,1,0:T(8,128)(2,1)S(1)}, bf16[2,128,640]{2,1,0:T(8,128)(2,1)S(1)}, u32[]{:S(2)}, u32[]{:S(2)}) collective-permute-start(bf16[2,128,640]{2,1,0:T(8,128)(2,1)S(1)} %get-tuple-element.92), channel_id=1, source_target_pairs={{0,1},{1,0},{2,3},{3,2},{4,5},{5,4},{6,7},{7,6},{8,9},{9,8},{10,11... | collective-permute-start | bytes 983048 | tf_op jit(solution)/shard_map/ppermute | solution.py:420
  25.8 12.0 %collective-permute-start.6 = (bf16[128,640]{1,0:T(8,128)(2,1)S(1)}, bf16[128,640]{1,0:T(8,128)(2,1)S(1)}, u32[]{:S(2)}, u32[]{:S(2)}) collective-permute-start(bf16[128,640]{1,0:T(8,128)(2,1)S(1)} %fusion.9), channel_id=1, source_target_pairs={{0,2},{1,3},{2,0},{3,1},{4,6},{5,7},{6,4},{7,5},{8,10},{9,11},{10,... | collective-permute-start | bytes 491528 | tf_op jit(solution)/shard_map/ppermute | solution.py:420
  37.7 9.9 %collective-permute-start.8 = (bf16[128,640]{1,0:T(8,128)(2,1)S(1)}, bf16[128,640]{1,0:T(8,128)(2,1)S(1)}, u32[]{:S(2)}, u32[]{:S(2)}) collective-permute-start(bf16[128,640]{1,0:T(8,128)(2,1)S(1)} %fusion.7), channel_id=1, source_target_pairs={{0,4},{1,5},{2,6},{3,7},{4,0},{5,1},{6,2},{7,3},{8,12},{9,13},{10,... | collective-permute-start | bytes 491528 | tf_op jit(solution)/shard_map/ppermute | solution.py:420
  37.8 11.6 %collective-permute-start.7 = (bf16[128,640]{1,0:T(8,128)(2,1)S(1)}, bf16[128,640]{1,0:T(8,128)(2,1)S(1)}, u32[]{:S(2)}, u32[]{:S(2)}) collective-permute-start(bf16[128,640]{1,0:T(8,128)(2,1)S(1)} %fusion.11), channel_id=1, source_target_pairs={{0,2},{1,3},{2,0},{3,1},{4,6},{5,7},{6,4},{7,5},{8,10},{9,11},{10,... | collective-permute-start | bytes 491528 | tf_op jit(solution)/shard_map/ppermute | solution.py:420
  39.9 12.2 %collective-permute-start.4 = (bf16[128,640]{1,0:T(8,128)(2,1)S(1)}, bf16[128,640]{1,0:T(8,128)(2,1)S(1)}, u32[]{:S(2)}, u32[]{:S(2)}) collective-permute-start(bf16[128,640]{1,0:T(8,128)(2,1)S(1)} %fusion.10), channel_id=1, source_target_pairs={{0,2},{1,3},{2,0},{3,1},{4,6},{5,7},{6,4},{7,5},{8,10},{9,11},{10,... | collective-permute-start | bytes 491528 | tf_op jit(solution)/shard_map/ppermute | solution.py:420
  47.7 10.7 %collective-permute-start.10 = (bf16[128,640]{1,0:T(8,128)(2,1)S(1)}, bf16[128,640]{1,0:T(8,128)(2,1)S(1)}, u32[]{:S(2)}, u32[]{:S(2)}) collective-permute-start(bf16[128,640]{1,0:T(8,128)(2,1)S(1)} %fusion.5), channel_id=1, source_target_pairs={{0,8},{1,9},{2,10},{3,11},{4,12},{5,13},{6,14},{7,15},{8,0},{9,1},... | collective-permute-start | bytes 491528 | tf_op jit(solution)/shard_map/ppermute | solution.py:420
  49.5 8.9 %collective-permute-start.9 = (bf16[128,640]{1,0:T(8,128)(2,1)S(1)}, bf16[128,640]{1,0:T(8,128)(2,1)S(1)}, u32[]{:S(2)}, u32[]{:S(2)}) collective-permute-start(bf16[128,640]{1,0:T(8,128)(2,1)S(1)} %fusion.6), channel_id=1, source_target_pairs={{0,4},{1,5},{2,6},{3,7},{4,0},{5,1},{6,2},{7,3},{8,12},{9,13},{10,... | collective-permute-start | bytes 491528 | tf_op jit(solution)/shard_map/ppermute | solution.py:420
  64.9 8.6 %collective-permute-start.11 = (bf16[656,128]{1,0:T(8,128)(2,1)S(1)}, bf16[656,128]{1,0:T(8,128)(2,1)S(1)}, u32[]{:S(2)}, u32[]{:S(2)}) collective-permute-start(bf16[656,128]{1,0:T(8,128)(2,1)S(1)} %get-tuple-element.97.b0), channel_id=1, source_target_pairs={{0,4},{1,5},{2,6},{3,7},{4,0},{5,1},{6,2},{7,3},{8,12},{9,13},{10,... | collective-permute-start | bytes 503816 | tf_op jit(solution)/shard_map/ppermute | solution.py:420
  65.3 10.2 %collective-permute-start.12 = (bf16[656,128]{1,0:T(8,128)(2,1)S(1)}, bf16[656,128]{1,0:T(8,128)(2,1)S(1)}, u32[]{:S(2)}, u32[]{:S(2)}) collective-permute-start(bf16[656,128]{1,0:T(8,128)(2,1)S(1)} %get-tuple-element.97.b0), channel_id=1, source_target_pairs={{0,8},{1,9},{2,10},{3,11},{4,12},{5,13},{6,14},{7,15},{8,0},{9,1},... | collective-permute-start | bytes 503816 | tf_op jit(solution)/shard_map/ppermute | solution.py:420
  67.9 7.6 %collective-permute-start.13 = (bf16[656,128]{1,0:T(8,128)(2,1)S(1)}, bf16[656,128]{1,0:T(8,128)(2,1)S(1)}, u32[]{:S(2)}, u32[]{:S(2)}) collective-permute-start(bf16[656,128]{1,0:T(8,128)(2,1)S(1)} %get-tuple-element.97.b0), channel_id=1, source_target_pairs={{0,2},{1,3},{2,0},{3,1},{4,6},{5,7},{6,4},{7,5},{8,10},{9,11},{10,... | collective-permute-start | bytes 503816 | tf_op jit(solution)/shard_map/ppermute | solution.py:420
  76.7 12.1 %collective-permute-start.19 = (bf16[656,128]{1,0:T(8,128)(2,1)S(1)}, bf16[656,128]{1,0:T(8,128)(2,1)S(1)}, u32[]{:S(2)}, u32[]{:S(2)}) collective-permute-start(bf16[656,128]{1,0:T(8,128)(2,1)S(1)} %collective-permute-done.11.b0), channel_id=1, source_target_pairs={{0,1},{1,0},{2,3},{3,2},{4,5},{5,4},{6,7},{7,6},{8,9},{9,8},{10,11... | collective-permute-start | bytes 503816 | tf_op jit(solution)/shard_map/ppermute | solution.py:420
  77.0 11.2 %collective-permute-start.15 = (bf16[656,128]{1,0:T(8,128)(2,1)S(1)}, bf16[656,128]{1,0:T(8,128)(2,1)S(1)}, u32[]{:S(2)}, u32[]{:S(2)}) collective-permute-start(bf16[656,128]{1,0:T(8,128)(2,1)S(1)} %collective-permute-done.12.b0), channel_id=1, source_target_pairs={{0,4},{1,5},{2,6},{3,7},{4,0},{5,1},{6,2},{7,3},{8,12},{9,13},{10,... | collective-permute-start | bytes 503816 | tf_op jit(solution)/shard_map/ppermute | solution.py:420
  77.1 18.8 %collective-permute-start.23 = (bf16[656,128]{1,0:T(8,128)(2,1)S(1)}, bf16[656,128]{1,0:T(8,128)(2,1)S(1)}, u32[]{:S(2)}, u32[]{:S(2)}) collective-permute-start(bf16[656,128]{1,0:T(8,128)(2,1)S(1)} %collective-permute-done.12.b0), channel_id=1, source_target_pairs={{0,1},{1,0},{2,3},{3,2},{4,5},{5,4},{6,7},{7,6},{8,9},{9,8},{10,11... | collective-permute-start | bytes 503816 | tf_op jit(solution)/shard_map/ppermute | solution.py:420
  77.3 12.4 %collective-permute-start.24 = (bf16[656,128]{1,0:T(8,128)(2,1)S(1)}, bf16[656,128]{1,0:T(8,128)(2,1)S(1)}, u32[]{:S(2)}, u32[]{:S(2)}) collective-permute-start(bf16[656,128]{1,0:T(8,128)(2,1)S(1)} %collective-permute-done.12.b0), channel_id=1, source_target_pairs={{0,2},{1,3},{2,0},{3,1},{4,6},{5,7},{6,4},{7,5},{8,10},{9,11},{10,... | collective-permute-start | bytes 503816 | tf_op jit(solution)/shard_map/ppermute | solution.py:420
  88.2 13.2 %collective-permute-start.17 = (bf16[656,128]{1,0:T(8,128)(2,1)S(1)}, bf16[656,128]{1,0:T(8,128)(2,1)S(1)}, u32[]{:S(2)}, u32[]{:S(2)}) collective-permute-start(bf16[656,128]{1,0:T(8,128)(2,1)S(1)} %collective-permute-done.15.b0), channel_id=1, source_target_pairs={{0,1},{1,0},{2,3},{3,2},{4,5},{5,4},{6,7},{7,6},{8,9},{9,8},{10,11... | collective-permute-start | bytes 503816 | tf_op jit(solution)/shard_map/ppermute | solution.py:420
  121.1 8.3 %collective-permute-start.30 = (bf16[128,640]{1,0:T(8,128)(2,1)S(1)}, bf16[128,640]{1,0:T(8,128)(2,1)S(1)}, u32[]{:S(2)}, u32[]{:S(2)}) collective-permute-start(bf16[128,640]{1,0:T(8,128)(2,1)S(1)} %fusion.14), channel_id=1, source_target_pairs={{0,2},{1,3},{2,0},{3,1},{4,6},{5,7},{6,4},{7,5},{8,10},{9,11},{10,... | collective-permute-start | bytes 491528 | tf_op jit(solution)/shard_map/ppermute | solution.py:420
  124.7 11.0 %collective-permute-start.36 = (bf16[128,640]{1,0:T(8,128)(2,1)S(1)}, bf16[128,640]{1,0:T(8,128)(2,1)S(1)}, u32[]{:S(2)}, u32[]{:S(2)}) collective-permute-start(bf16[128,640]{1,0:T(8,128)(2,1)S(1)} %fusion.1), channel_id=1, source_target_pairs={{0,8},{1,9},{2,10},{3,11},{4,12},{5,13},{6,14},{7,15},{8,0},{9,1},... | collective-permute-start | bytes 491528 | tf_op jit(solution)/shard_map/ppermute | solution.py:420
  127.1 8.6 %collective-permute-start.35 = (bf16[128,640]{1,0:T(8,128)(2,1)S(1)}, bf16[128,640]{1,0:T(8,128)(2,1)S(1)}, u32[]{:S(2)}, u32[]{:S(2)}) collective-permute-start(bf16[128,640]{1,0:T(8,128)(2,1)S(1)} %fusion.2), channel_id=1, source_target_pairs={{0,4},{1,5},{2,6},{3,7},{4,0},{5,1},{6,2},{7,3},{8,12},{9,13},{10,... | collective-permute-start | bytes 491528 | tf_op jit(solution)/shard_map/ppermute | solution.py:420
  142.7 8.4 %collective-permute-start.37 = (bf16[656,128]{1,0:T(8,128)(2,1)S(1)}, bf16[656,128]{1,0:T(8,128)(2,1)}, u32[]{:S(2)}, u32[]{:S(2)}) collective-permute-start(bf16[656,128]{1,0:T(8,128)(2,1)S(1)} %get-tuple-element.135.b0), channel_id=1, source_target_pairs={{0,4},{1,5},{2,6},{3,7},{4,0},{5,1},{6,2},{7,3},{8,12},{9,13},{10,... | collective-permute-start | bytes 503816 | tf_op jit(solution)/shard_map/ppermute | solution.py:420
  142.7 9.9 %collective-permute-start.38 = (bf16[656,128]{1,0:T(8,128)(2,1)S(1)}, bf16[656,128]{1,0:T(8,128)(2,1)S(1)}, u32[]{:S(2)}, u32[]{:S(2)}) collective-permute-start(bf16[656,128]{1,0:T(8,128)(2,1)S(1)} %get-tuple-element.135.b0), channel_id=1, source_target_pairs={{0,8},{1,9},{2,10},{3,11},{4,12},{5,13},{6,14},{7,15},{8,0},{9,1},... | collective-permute-start | bytes 503816 | tf_op jit(solution)/shard_map/ppermute | solution.py:420
  155.0 10.6 %collective-permute-start.47 = (bf16[656,128]{1,0:T(8,128)(2,1)}, bf16[656,128]{1,0:T(8,128)(2,1)}, u32[]{:S(2)}, u32[]{:S(2)}) collective-permute-start(bf16[656,128]{1,0:T(8,128)(2,1)} %collective-permute-done.37.b0), channel_id=1, source_target_pairs={{0,2},{1,3},{2,0},{3,1},{4,6},{5,7},{6,4},{7,5},{8,10},{9,11},{10,... | collective-permute-start | bytes 503816 | tf_op jit(solution)/shard_map/ppermute | solution.py:420
  155.3 10.7 %collective-permute-start.43 = (bf16[656,128]{1,0:T(8,128)(2,1)}, bf16[656,128]{1,0:T(8,128)(2,1)}, u32[]{:S(2)}, u32[]{:S(2)}) collective-permute-start(bf16[656,128]{1,0:T(8,128)(2,1)} %collective-permute-done.39.b2), channel_id=1, source_target_pairs={{0,1},{1,0},{2,3},{3,2},{4,5},{5,4},{6,7},{7,6},{8,9},{9,8},{10,11... | collective-permute-start | bytes 503816 | tf_op jit(solution)/shard_map/ppermute | solution.py:420
  155.5 18.9 %collective-permute-start.42 = (bf16[656,128]{1,0:T(8,128)(2,1)S(1)}, bf16[656,128]{1,0:T(8,128)(2,1)}, u32[]{:S(2)}, u32[]{:S(2)}) collective-permute-start(bf16[656,128]{1,0:T(8,128)(2,1)S(1)} %collective-permute-done.38.b0), channel_id=1, source_target_pairs={{0,4},{1,5},{2,6},{3,7},{4,0},{5,1},{6,2},{7,3},{8,12},{9,13},{10,... | collective-permute-start | bytes 503816 | tf_op jit(solution)/shard_map/ppermute | solution.py:420
  155.6 20.9 %collective-permute-start.46 = (bf16[656,128]{1,0:T(8,128)(2,1)}, bf16[656,128]{1,0:T(8,128)(2,1)}, u32[]{:S(2)}, u32[]{:S(2)}) collective-permute-start(bf16[656,128]{1,0:T(8,128)(2,1)} %collective-permute-done.37.b0), channel_id=1, source_target_pairs={{0,1},{1,0},{2,3},{3,2},{4,5},{5,4},{6,7},{7,6},{8,9},{9,8},{10,11... | collective-permute-start | bytes 503816 | tf_op jit(solution)/shard_map/ppermute | solution.py:420
  158.7 25.0 %collective-permute-start.50 = (bf16[656,128]{1,0:T(8,128)(2,1)S(1)}, bf16[656,128]{1,0:T(8,128)(2,1)}, u32[]{:S(2)}, u32[]{:S(2)}) collective-permute-start(bf16[656,128]{1,0:T(8,128)(2,1)S(1)} %collective-permute-done.38.b0), channel_id=1, source_target_pairs={{0,1},{1,0},{2,3},{3,2},{4,5},{5,4},{6,7},{7,6},{8,9},{9,8},{10,11... | collective-permute-start | bytes 503816 | tf_op jit(solution)/shard_map/ppermute | solution.py:420
  159.3 38.7 %all-to-all-start.1 = ((bf16[16,144,128]{2,1,0:T(8,128)(2,1)}), bf16[16,144,128]{2,1,0:T(8,128)(2,1)S(1)}, u32[]{:S(2)}, u32[]{:S(2)}) async-start(bf16[16,144,128]{2,1,0:T(8,128)(2,1)} %get-tuple-element.137), calls=%async_computation.1 | async-start | bytes 1179648 | tf_op jit(solution)/shard_map/all_to_all | solution.py:545
  165.6 10.9 %collective-permute-start.48 = (bf16[656,128]{1,0:T(8,128)(2,1)}, bf16[656,128]{1,0:T(8,128)(2,1)S(1)}, u32[]{:S(2)}, u32[]{:S(2)}) collective-permute-start(bf16[656,128]{1,0:T(8,128)(2,1)} %collective-permute-done.47.b2), channel_id=1, source_target_pairs={{0,1},{1,0},{2,3},{3,2},{4,5},{5,4},{6,7},{7,6},{8,9},{9,8},{10,11... | collective-permute-start | bytes 503816 | tf_op jit(solution)/shard_map/ppermute | solution.py:420
  174.4 15.7 %collective-permute-start.44 = (bf16[656,128]{1,0:T(8,128)(2,1)}, bf16[656,128]{1,0:T(8,128)(2,1)S(1)}, u32[]{:S(2)}, u32[]{:S(2)}) collective-permute-start(bf16[656,128]{1,0:T(8,128)(2,1)} %collective-permute-done.42.b0), channel_id=1, source_target_pairs={{0,1},{1,0},{2,3},{3,2},{4,5},{5,4},{6,7},{7,6},{8,9},{9,8},{10,11... | collective-permute-start | bytes 503816 | tf_op jit(solution)/shard_map/ppermute | solution.py:420
  174.6 8.5 %collective-permute-start.45 = (bf16[656,128]{1,0:T(8,128)(2,1)}, bf16[656,128]{1,0:T(8,128)(2,1)S(1)}, u32[]{:S(2)}, u32[]{:S(2)}) collective-permute-start(bf16[656,128]{1,0:T(8,128)(2,1)} %collective-permute-done.42.b0), channel_id=1, source_target_pairs={{0,2},{1,3},{2,0},{3,1},{4,6},{5,7},{6,4},{7,5},{8,10},{9,11},{10,... | collective-permute-start | bytes 503816 | tf_op jit(solution)/shard_map/ppermute | solution.py:420
  (39 other events, 293.1 us)

commit v7 on v6

--- a/solution.py
+++ b/solution.py
@@ -16,6 +16,9 @@
 LIMIT = 16 << 20
 COST = 3
 META = 16
+HBM_SPEC = pl.BlockSpec(memory_space=pltpu.MemorySpace.HBM)
+VMEM_SPEC = pl.BlockSpec(memory_space=pltpu.VMEM)
+SMEM_SPEC = pl.BlockSpec(memory_space=pltpu.SMEM)
 F32 = jnp.float32
 BF16 = jnp.bfloat16
 NT = (((1,), (1,)), ((), ()))
@@ -45,7 +48,8 @@
 
 
 def pack_kernel(
-    cap, devices, owner_ref, local_ref, cost_ref, dispatch_ref, max_ref, avail_ref, out_ref, slot_ref, pay_ref, meta_ref
+    cap, devices, place_ref, owner_ref, local_ref, cost_ref, dispatch_ref, max_ref, avail_ref,
+    out_ref, near_ref, slot_ref, pay_ref, meta_ref,
 ):
     step = pl.program_id(0)
     gens, hours = dispatch_ref.shape
@@ -61,6 +65,7 @@
         count = dot(hits.astype(BF16), before.astype(BF16))
         rank = jnp.sum(count * hits, axis=0, keepdims=True).astype(jnp.int32)
         slot_ref[...] = owner * cap + rank
+        near_ref[...] = (owner ^ place_ref[0]) * cap + rank
         pay_ref[:, :hours] = dispatch_ref[...].astype(BF16)
         lanes = max_ref.shape[1]
         eye = (
@@ -95,7 +100,7 @@
         out_ref[i, cap:, :cap] = dot(meta_ref[...], picks[i], NT).astype(BF16)
 
 
-def pack(devices, cap, owner, local_bus, cost, dispatch, gen_max, availability):
+def pack(devices, cap, place, owner, local_bus, cost, dispatch, gen_max, availability):
     gens, hours = dispatch.shape
     full = lambda *shape: pl.BlockSpec(shape, lambda i: (0,) * len(shape))
     folded = (gens // 128, 128)
@@ -107,6 +112,7 @@
             jax.ShapeDtypeStruct((1, gens), jnp.int32),
         ),
         in_specs=[
+            SMEM_SPEC,
             full(1, gens),
             full(*folded),
             full(*folded),
@@ -116,6 +122,7 @@
         ],
         out_specs=(pl.BlockSpec((GROUP, cap + META, 2 * hours), lambda i: (i, 0, 0)), full(1, gens)),
         scratch_shapes=[
+            pltpu.VMEM((1, gens), jnp.int32),
             pltpu.VMEM((gens, 2 * hours), BF16),
             pltpu.VMEM((META, gens), BF16),
         ],
@@ -123,6 +130,7 @@
         cost_estimate=pl.CostEstimate(flops=4 * devices * cap * gens * hours, bytes_accessed=3 << 20, transcendentals=0),
         name="pack_generators",
     )(
+        place,
         owner.reshape(1, gens),
         local_bus.reshape(folded),
         cost.reshape(folded),
@@ -132,7 +140,13 @@
     )
 
 
-def unpack_kernel(block, slot_ref, back_ref, dispatch_ref, max_ref, avail_ref, out_ref):
+def unpack_kernel(block, slot_ref, *refs):
+    *back_refs, dispatch_ref, max_ref, avail_ref, out_ref, back_ref = refs
+    peers, cap, _ = back_refs[0].shape
+    for i, ref in enumerate(back_refs):
+        for j in range(peers):
+            start = (j * len(back_refs) + i) * cap
+            back_ref[start : start + cap, :] = ref[j]
     gens = slot_ref.shape[1]
     slot = jnp.broadcast_to(slot_ref[...].astype(F32), (128, gens)).T[:, 0:1].astype(jnp.int32)
     at = lax.broadcasted_iota(jnp.int32, (gens, block), 1)
@@ -150,121 +164,125 @@
     out_ref[...] = jnp.where(change == -sent, 0.0, moved)
 
 
-def unpack(slot, back, dispatch, gen_max, availability):
+def unpack(slot, backs, dispatch, gen_max, availability):
     gens = slot.shape[1]
-    devices, cap, hours = back.shape
-    slots = devices * cap
+    peers, cap, hours = backs[0].shape
+    slots = len(backs) * peers * cap
     block = next(size for size in (768, 256, 128, 16) if slots % size == 0)
     return pl.pallas_call(
         functools.partial(unpack_kernel, block),
         out_shape=jax.ShapeDtypeStruct((gens, hours), F32),
+        scratch_shapes=[pltpu.VMEM((slots, hours), BF16)],
         compiler_params=pltpu.CompilerParams(vmem_limit_bytes=LIMIT),
         cost_estimate=pl.CostEstimate(flops=2 * slots * gens * hours, bytes_accessed=1 << 20, transcendentals=0),
         name="unpack_dispatch",
-    )(slot, back.reshape(slots, hours), dispatch, gen_max, availability)
-
-
-def update_kernel(cap, first, last, parts, *refs):
-    price_refs = refs[:parts]
-    balance_ref, demand_ref, recv_ref, prev_ref, upd_ref, inj_ref, shadow_ref, acc_ref, extra_ref = refs[parts:]
-    step = pl.program_id(0)
+    )(slot, *backs, dispatch, gen_max, availability)
+
+
+def update_kernel(cap, devices, first, last, parts, chunks, place_ref, *refs):
+    price_refs, refs = refs[:parts], refs[parts:]
+    recv_ref, balance_ref, demand_ref, *refs = refs
+    if not first:
+        prev_ref, *refs = refs
+    copies = []
+    if chunks:
+        ptdf_ref, upd_ref, inj_ref, *held_refs, shadow_ref, acc_ref, extra_ref, sems = refs
+        copies = column_copies(place_ref, ptdf_ref, chunks, held_refs, sems)
+    else:
+        upd_ref, inj_ref, shadow_ref, acc_ref, extra_ref = refs
+    for copy in copies:
+        copy.start()
     buses, hours = demand_ref.shape
-
-    @pl.when(step == 0)
-    def _():
-        shadow = price_refs[0][...].astype(F32)
-        for ref in price_refs[1:]:
-            shadow = shadow + ref[...].astype(F32)
-        hi, lo = halves(shadow)
-        shadow_ref[:hours, :] = hi
-        shadow_ref[hours:, :] = lo
-        acc_ref[...] = jnp.zeros(acc_ref.shape, F32)
-        extra_ref[...] = jnp.zeros(extra_ref.shape, BF16)
-
-    group = recv_ref.shape[0]
-    pad = extra_ref.shape[0] // group
     wide = 2 * hours
-    meta = recv_ref[:, cap:, :].reshape(group * META, wide)
+    pad = extra_ref.shape[0] // devices
+    shadow = price_refs[0][...].astype(F32)
+    for ref in price_refs[1:]:
+        shadow = shadow + ref[...].astype(F32)
+    hi, lo = halves(shadow)
+    shadow_ref[:hours, :] = hi
+    shadow_ref[hours:, :] = lo
     eye = (
         lax.broadcasted_iota(jnp.int32, (cap, wide), 0) == lax.broadcasted_iota(jnp.int32, (cap, wide), 1)
     ).astype(F32)
-    columns = dot(eye.astype(BF16), meta, NT)
     buses_at = lax.broadcasted_iota(jnp.int32, (cap, buses), 1)
-    picks = []
-    for i in range(group):
-        at = i * META
-        bus_column = ((columns[:, at : at + 1] - 1.0) * 128.0 + columns[:, at + 1 : at + 2]).astype(jnp.int32)
-        picks.append((buses_at == bus_column).astype(F32).astype(BF16))
-    both = dot(jnp.concatenate(picks, axis=0), shadow_ref[...], NT)
-    for i in range(group):
-        at = i * META
-        cost = (columns[:, at + 2 : at + 3] + columns[:, at + 3 : at + 4]) + columns[:, at + 4 : at + 5]
-        rows = slice(i * cap, (i + 1) * cap)
-        price = both[rows, :hours] + both[rows, hours:] + balance_ref[...]
-        sent = recv_ref[i, :cap, :hours].astype(F32)
-        dispatch = sent if first else prev_ref[i]
-        upper = recv_ref[i, :cap, hours:].astype(F32)
-        updated = jnp.minimum(jnp.maximum(dispatch - tau_step * (cost + price), 0.0), upper)
-        if last:
-            upd_ref[i] = (updated - sent).astype(BF16)
-        else:
-            upd_ref[i] = updated
-        hi, lo = halves(2.0 * updated - dispatch)
-        extra_ref[i * pad : i * pad + cap, :hours] = hi
-        extra_ref[i * pad : i * pad + cap, hours:] = lo
     at_row = lax.broadcasted_iota(jnp.int32, (buses, pad), 0)
-    picks = []
-    for i in range(group):
-        row = recv_ref[i, cap:, :pad].astype(F32)
-        bus_row = ((row[0:1] - 1.0) * 128.0 + row[1:2]).astype(jnp.int32)
-        picks.append((at_row == bus_row).astype(F32).astype(BF16))
-    acc_ref[...] += dot(jnp.concatenate(picks, axis=1), extra_ref[...])
-
-    @pl.when(step == pl.num_programs(0) - 1)
-    def _():
-        injection = acc_ref[:, :hours] + acc_ref[:, hours:] - demand_ref[...]
-        inj_ref[:buses, :] = injection.astype(BF16)
-        hi, mid, low = thirds(jnp.sum(injection, axis=0, keepdims=True))
-        row = lax.broadcasted_iota(jnp.int32, (META, hours), 0)
-        tail = jnp.where(row == 0, hi.astype(F32), 0.0)
-        tail = jnp.where(row == 1, mid.astype(F32), tail)
-        tail = jnp.where(row == 2, low.astype(F32), tail)
-        inj_ref[buses:, :] = tail.astype(BF16)
-
-
-def update(cap, first, last, prices, balance_price, demand, recv, previous):
+    for start in range(0, devices, GROUP):
+        peers = range(start, start + GROUP)
+        meta = jnp.concatenate([recv_ref[peer, cap:, :] for peer in peers], axis=0)
+        columns = dot(eye.astype(BF16), meta, NT)
+        picks = []
+        for i in range(GROUP):
+            at = i * META
+            bus_column = ((columns[:, at : at + 1] - 1.0) * 128.0 + columns[:, at + 1 : at + 2]).astype(jnp.int32)
+            picks.append((buses_at == bus_column).astype(F32).astype(BF16))
+        both = dot(jnp.concatenate(picks, axis=0), shadow_ref[...], NT)
+        for i, peer in enumerate(peers):
+            at = i * META
+            cost = (columns[:, at + 2 : at + 3] + columns[:, at + 3 : at + 4]) + columns[:, at + 4 : at + 5]
+            rows = slice(i * cap, (i + 1) * cap)
+            price = both[rows, :hours] + both[rows, hours:] + balance_ref[...]
+            sent = recv_ref[peer, :cap, :hours].astype(F32)
+            dispatch = sent if first else prev_ref[peer]
+            upper = recv_ref[peer, :cap, hours:].astype(F32)
+            updated = jnp.minimum(jnp.maximum(dispatch - tau_step * (cost + price), 0.0), upper)
+            if last:
+                upd_ref[peer ^ place_ref[0]] = (updated - sent).astype(BF16)
+            else:
+                upd_ref[peer] = updated
+            hi, lo = halves(2.0 * updated - dispatch)
+            extra_ref[peer * pad : peer * pad + cap, :hours] = hi
+            extra_ref[peer * pad : peer * pad + cap, hours:] = lo
+            if pad > cap:
+                extra_ref[peer * pad + cap : (peer + 1) * pad, :] = jnp.zeros((pad - cap, wide), BF16)
+        picks = []
+        for peer in peers:
+            row = recv_ref[peer, cap:, :pad].astype(F32)
+            bus_row = ((row[0:1] - 1.0) * 128.0 + row[1:2]).astype(jnp.int32)
+            picks.append((at_row == bus_row).astype(F32).astype(BF16))
+        sums = dot(jnp.concatenate(picks, axis=1), extra_ref[start * pad : (start + GROUP) * pad, :])
+        acc_ref[...] = sums if start == 0 else acc_ref[...] + sums
+    injection = acc_ref[:, :hours] + acc_ref[:, hours:] - demand_ref[...]
+    inj_ref[:buses, :] = injection.astype(BF16)
+    hi, mid, low = thirds(jnp.sum(injection, axis=0, keepdims=True))
+    row = lax.broadcasted_iota(jnp.int32, (META, hours), 0)
+    tail = jnp.where(row == 0, hi.astype(F32), 0.0)
+    tail = jnp.where(row == 1, mid.astype(F32), tail)
+    tail = jnp.where(row == 2, low.astype(F32), tail)
+    inj_ref[buses:, :] = tail.astype(BF16)
+    for copy in copies:
+        copy.wait()
+
+
+def update(cap, place, last, prices, balance_price, demand, recv, previous, ptdf, chunks):
     devices = recv.shape[0]
     buses, hours = demand.shape
-    full = lambda *shape: pl.BlockSpec(shape, lambda i: (0,) * len(shape))
-    slots = lambda width: pl.BlockSpec((GROUP, cap, width), lambda i: (i, 0, 0))
-    if first:
-        previous, prev_spec = balance_price, full(1, hours)
-    else:
-        prev_spec = slots(hours)
+    first = previous is None
+    operands = [place, *prices, recv, balance_price, demand] + ([] if first else [previous])
+    in_specs = [SMEM_SPEC] + [VMEM_SPEC] * (len(operands) - 1)
+    out_shape = [
+        jax.ShapeDtypeStruct((devices, cap, hours), BF16 if last else F32),
+        jax.ShapeDtypeStruct((buses + META, hours), BF16),
+    ]
+    scratch = [
+        pltpu.VMEM((2 * hours, buses), BF16),
+        pltpu.VMEM((buses, 2 * hours), F32),
+        pltpu.VMEM((devices * (-(-cap // 128) * 128), 2 * hours), BF16),
+    ]
+    if chunks:
+        operands.append(in_hbm(ptdf))
+        in_specs.append(HBM_SPEC)
+        out_shape += [pltpu.VMEM((ptdf.shape[0], 4 * buses), BF16)] * len(chunks)
+        scratch.append(pltpu.SemaphoreType.DMA((len(chunks), 4)))
     return pl.pallas_call(
-        functools.partial(update_kernel, cap, first, last, len(prices)),
-        grid=(devices // GROUP,),
-        out_shape=(
-            jax.ShapeDtypeStruct((devices, cap, hours), BF16 if last else F32),
-            jax.ShapeDtypeStruct((buses + META, hours), BF16),
-        ),
-        in_specs=[full(hours, buses)] * len(prices)
-        + [
-            full(1, hours),
-            full(buses, hours),
-            pl.BlockSpec((GROUP, cap + META, 2 * hours), lambda i: (i, 0, 0)),
-            prev_spec,
-        ],
-        out_specs=(slots(hours), full(buses + META, hours)),
-        scratch_shapes=[
-            pltpu.VMEM((2 * hours, buses), BF16),
-            pltpu.VMEM((buses, 2 * hours), F32),
-            pltpu.VMEM((GROUP * (-(-cap // 128) * 128), 2 * hours), BF16),
-        ],
+        functools.partial(update_kernel, cap, devices, first, last, len(prices), chunks),
+        in_specs=in_specs,
+        out_specs=tuple([VMEM_SPEC] * len(out_shape)),
+        out_shape=tuple(out_shape),
+        scratch_shapes=scratch,
         compiler_params=pltpu.CompilerParams(vmem_limit_bytes=LIMIT),
         cost_estimate=pl.CostEstimate(flops=8 * devices * cap * buses * hours, bytes_accessed=4 << 20, transcendentals=0),
         name="update_generators",
-    )(*prices, balance_price, demand, recv, previous)
+    )(*operands)
 
 
 def shadow_kernel(chunk, stream, turn, place_ref, line_ref, ptdf_ref, keep_ref, send_ref, *rest):
@@ -309,11 +327,6 @@
     return pltpu.with_memory_space_constraint(x, pltpu.MemorySpace.HBM)
 
 
-HBM_SPEC = pl.BlockSpec(memory_space=pltpu.MemorySpace.HBM)
-VMEM_SPEC = pl.BlockSpec(memory_space=pltpu.VMEM)
-SMEM_SPEC = pl.BlockSpec(memory_space=pltpu.SMEM)
-
-
 def chunk_cost(hours, lines, buses):
     return pl.CostEstimate(flops=COST * 8 * hours * lines * buses, bytes_accessed=8 * lines * buses, transcendentals=0)
 
@@ -341,41 +354,65 @@
     )(place, in_hbm(line) if turn else line, in_hbm(ptdf) if stream else ptdf)
 
 
-TILES = 4
-
-
-def flow_kernel(chunk, start, end, keep, place_ref, ptdf_ref, b0, b1, b2, b3, acc_ref, sum_ref, *rest):
-    if end:
-        limit_ref, line_ref, out_ref, half_ref, sum_out, *rest = rest
-    else:
-        out_ref, sum_out, *rest = rest
-    held_ref, inj_ref, sems = rest
-    buses = inj_ref.shape[0] // 4
-    tile = held_ref.shape[0] // TILES
+def column_copies(place_ref, ptdf_ref, chunks, held_refs, sems):
+    buses = held_refs[0].shape[1] // 4
     copies = []
-    for i in range(TILES):
-        rows = pl.ds(i * tile, tile)
+    for i, chunk in enumerate(chunks):
         for rel in range(4):
-            first = pl.multiple_of((place_ref[0] ^ (4 * chunk + rel)) * buses, 128)
+            start = pl.multiple_of((place_ref[0] ^ (4 * chunk + rel)) * buses, 128)
             copies.append(
                 pltpu.make_async_copy(
-                    ptdf_ref.at[rows, pl.ds(first, buses)],
-                    held_ref.at[rows, pl.ds(rel * buses, buses)],
+                    ptdf_ref.at[:, pl.ds(start, buses)],
+                    held_refs[i].at[:, pl.ds(rel * buses, buses)],
                     sems.at[i, rel],
                 )
             )
-            copies[-1].start()
+    return copies
+
+
+def load_kernel(chunks, place_ref, ptdf_ref, token_ref, *rest):
+    *held_refs, sems = rest
+    copies = column_copies(place_ref, ptdf_ref, chunks, held_refs, sems)
+    for copy in copies:
+        copy.start()
+    token_ref[0] = place_ref[0]
+    for copy in copies:
+        copy.wait()
+
+
+def load_chunks(chunks, place, ptdf, buses):
+    lines = ptdf.shape[0]
+    count = len(chunks)
+    token, *held = pl.pallas_call(
+        functools.partial(load_kernel, chunks),
+        in_specs=[SMEM_SPEC, HBM_SPEC],
+        out_specs=tuple([SMEM_SPEC] + [VMEM_SPEC] * count),
+        out_shape=tuple([jax.ShapeDtypeStruct((1,), jnp.int32)] + [pltpu.VMEM((lines, 4 * buses), BF16)] * count),
+        scratch_shapes=[pltpu.SemaphoreType.DMA((count, 4))],
+        compiler_params=pltpu.CompilerParams(vmem_limit_bytes=LIMIT),
+        cost_estimate=pl.CostEstimate(flops=0, bytes_accessed=8 * count * lines * buses, transcendentals=0),
+        name="load_chunks",
+    )(place, in_hbm(ptdf))
+    return token, held
+
+
+def flow_kernel(start, end, ptdf_ref, b0, b1, b2, b3, acc_ref, sum_ref, *rest):
+    if end:
+        limit_ref, line_ref, out_ref, half_ref, sum_out, inj_ref = rest
+    else:
+        out_ref, sum_out, inj_ref = rest
+    buses = inj_ref.shape[0] // 4
     total = jnp.zeros(sum_ref.shape, F32) if start else sum_ref[...]
     for rel, ref in enumerate((b0, b1, b2, b3)):
         inj_ref[rel * buses : (rel + 1) * buses, :] = ref[:buses, :]
         tail = ref[buses:, :].astype(F32)
         total = total + jnp.sum(tail, axis=0, keepdims=True)
     sum_out[...] = total
-    for i in range(TILES):
-        rows = slice(i * tile, (i + 1) * tile)
-        for copy in copies[4 * i : 4 * i + 4]:
-            copy.wait()
-        flow = dot(held_ref[rows, :], inj_ref[...])
+    tile = ptdf_ref.shape[0] // 4
+
+    def body(i, carry):
+        rows = pl.ds(pl.multiple_of(i * tile, tile), tile)
+        flow = dot(ptdf_ref[rows, :], inj_ref[...])
         if not start:
             flow = flow + acc_ref[rows, :]
         if end:
@@ -385,35 +422,33 @@
             out_ref[rows, :] = line
         else:
             out_ref[rows, :] = flow
+        return carry
+
+    lax.fori_loop(0, 4, body, 0)
     if end:
         half_ref[...] = out_ref[...].T.astype(BF16)
 
 
-def flow_chunk(chunk, keep, place, ptdf, blocks, acc, total, limit=None, line=None):
+def flow_chunk(ptdf, blocks, acc, total, limit=None, line=None):
     lines = ptdf.shape[0]
     rows, hours = blocks[0].shape
     buses = rows - META
     start, end = acc is None, limit is not None
-    operands = [*blocks, total if start else acc, total]
+    operands = [ptdf, *blocks, total if start else acc, total]
     out_shape = [jax.ShapeDtypeStruct((lines, hours), F32)]
     if end:
         operands += [limit, line]
         out_shape += [jax.ShapeDtypeStruct((hours, lines), BF16)]
     out_shape += [jax.ShapeDtypeStruct((1, hours), F32)]
-    held = pltpu.VMEM((lines, 4 * buses), BF16)
-    if keep:
-        out_shape.append(held)
     return pl.pallas_call(
-        functools.partial(flow_kernel, chunk, start, end, keep),
-        in_specs=[SMEM_SPEC, HBM_SPEC] + [VMEM_SPEC] * len(operands),
-        out_specs=tuple([VMEM_SPEC] * len(out_shape)),
+        functools.partial(flow_kernel, start, end),
+        in_specs=[VMEM_SPEC] * len(operands),
         out_shape=tuple(out_shape),
-        scratch_shapes=([] if keep else [held])
-        + [pltpu.VMEM((4 * buses, hours), BF16), pltpu.SemaphoreType.DMA((TILES, 4))],
+        scratch_shapes=[pltpu.VMEM((4 * buses, hours), BF16)],
         compiler_params=pltpu.CompilerParams(vmem_limit_bytes=LIMIT),
         cost_estimate=chunk_cost(hours, lines, buses),
         name="flow_chunk",
-    )(place, in_hbm(ptdf), *operands)
+    )(*operands)
 
 
 def swap(x, devices, mask):
@@ -441,9 +476,11 @@
     cap = -(-max(2, 3 * gens // devices) // 16) * 16
     staged = devices == 16 and buses % 128 == 0
 
+    near_place = place if staged else jnp.zeros_like(place)
     outgoing, slot = pack(
         devices,
         cap,
+        near_place,
         gen_owner,
         gen_local,
         gen_cost,
@@ -503,7 +540,11 @@
         else:
             shadow = lax.dot_general(ptdf, line_half, (((0,), (0,)), ((), ())), preferred_element_type=F32)
             prices = [lax.psum_scatter(shadow, "bus", scatter_dimension=0, tiled=True).T]
-        held, block = update(cap, iteration == 0, last, prices, balance_row, demand, recv, held)
+        chunks = (0, 1) if staged and not last else ()
+        held, block, *loaded = update(
+            cap, place if staged else near_place, last, prices, balance_row, demand, recv, held, ptdf, chunks
+        )
+        resident.update(zip(chunks, loaded))
         if staged:
             near, far, cross, far_cross = {0: block}, {}, {}, {}
 
@@ -517,39 +558,44 @@
             def blocks(chunk):
                 return [near[chunk], cross[chunk], far[chunk], far_cross[chunk]]
 
-            def flow(chunk, acc, total, *rest):
-                acc, *given = flow_chunk(chunk, not last, place, ptdf, blocks(chunk), acc, total, *rest)
-                if not last:
-                    *given, resident[chunk] = given
-                return (acc, *given)
-
             near[2] = swap(block, devices, 8)
             near[1] = swap(block, devices, 4)
             spread(0)
-            near[1], near[2], far[0], cross[0], row = lax.optimization_barrier(
-                (near[1], near[2], far[0], cross[0], balance_row)
-            )
+            stage = [near[1], near[2], far[0]]
+            if not last:
+                cross[0], here = lax.optimization_barrier((cross[0], place))
+                place, (resident[2], resident[3]) = load_chunks((2, 3), here, ptdf, buses)
+                stage.append(place)
+            near[1], near[2], far[0], *rest = lax.optimization_barrier(stage)
+            place = rest[0] if rest else place
             near[3] = swap(near[2], devices, 4)
             spread(1)
             spread(2)
             settle_far(0)
-            acc, total = flow(0, None, row)
+            acc, total = flow_chunk(resident[0], blocks(0), None, balance_row)
             near[3], acc = lax.optimization_barrier((near[3], acc))
             spread(3)
+            if last:
+                home, _ = lax.optimization_barrier((held, cross[0]))
+                home = home.reshape(4, 4, *home.shape[1:])
+                home = [home[0]] + [swap(home[chunk], devices, 4 * chunk) for chunk in (1, 2, 3)]
             settle_far(1)
-            acc, total = flow(1, acc, total)
+            acc, total = flow_chunk(resident[1], blocks(1), acc, total)
             settle_far(2)
-            far[3], acc = lax.optimization_barrier((far[3], acc))
             if last:
-                held, _ = lax.optimization_barrier((held, far[2]))
-                back = lax.all_to_all(held, "bus", split_axis=0, concat_axis=0, tiled=True)
-            acc, total = flow(2, acc, total)
+                far[3], acc, *home = lax.optimization_barrier((far[3], acc, *home))
+            else:
+                far[3], acc = lax.optimization_barrier((far[3], acc))
             settle_far(3)
-            line_price, line_half, total = flow(3, acc, total, limit, line_price)
+            acc, total = flow_chunk(resident[2], blocks(2), acc, total)
+            if last:
+                back = [jnp.stack([home[chunk][rel] for chunk in range(4)]) for rel in range(4)]
+                back = [back[0]] + [swap(back[rel], devices, rel) for rel in (1, 2, 3)]
+            line_price, line_half, total = flow_chunk(resident[3], blocks(3), acc, total, limit, line_price)
             balance = total
         else:
             if last:
-                back = lax.all_to_all(held, "bus", split_axis=0, concat_axis=0, tiled=True)
+                back = [lax.all_to_all(held, "bus", split_axis=0, concat_axis=0, tiled=True)]
             every = lax.all_gather(block, "bus", axis=0, tiled=False)
             balance = jnp.sum(every[:, buses:].astype(F32), axis=(0, 1)).reshape(1, hours)
             flow = jnp.dot(ptdf, every[:, :buses].reshape(all_buses, hours), preferred_element_type=F32)

time: 201 us -> 186 us (0.925)
  Pallas kernels: 87.5 us -> 66.6 us
  waiting for transfers between devices: 56.6 us -> 65.8 us
  local copies, waits for them, and re-layouts: 3.6 us -> 0.51 us
    pallas_call x10 -> x11, Pallas kernels: 62.7 us -> 39.4 us  [the longest x8 20.7 us: flow_chunk(): pl.pallas_call(functools.partial(flow_kernel, start, end), in_specs=[VMEM...]
    ppermute x52 -> x58, waiting for transfers between devices: 56.6 us -> 65.8 us  [swap(): return lax.ppermute(x, 'bus', [(i, i ^ mask) for i in range(devices)])]
    all_to_all x1 -> x0, starting transfers between devices: 6.2 us -> none  [local(): back = lax.all_to_all(held, 'bus', split_axis=0, concat_axis=0, tiled=True)]
    ppermute x52 -> x58, starting transfers between devices: 34.9 us -> 40.3 us  [swap(): return lax.ppermute(x, 'bus', [(i, i ^ mask) for i in range(devices)])]
    unnamed x34 -> x20, local copies, waits for them, and re-layouts: 3.22 us -> 0.05 us
    pallas_call x8, Pallas kernels: 19 us -> 21.4 us  [shadow_chunk(): pl.pallas_call(functools.partial(shadow_kernel, chunk, stream, turn), in_...]
  transfers between devices with their start and end apart: 54 -> 59, of which waited for: 15 -> 20; matrix products, arithmetic and copies ran while one was open for 2% -> 2% of each run, Pallas kernels for 31% -> 22%
where the time goes in v7:
time: 186 us; the launch traced here: 185 us
  Pallas kernels  66.6 us (36%)
  waiting for transfers between devices  65.8 us (35%)
  starting transfers between devices  47.4 us (25%)
  other arithmetic  3.26 us (2%)
    ppermute x58, waiting for transfers between devices, swap(): return lax.ppermute(x, 'bus', [(i, i ^ mask) for i in range(devices)])  65.8 us
    ppermute x58, starting transfers between devices, swap(): return lax.ppermute(x, 'bus', [(i, i ^ mask) for i in range(devices)])  40.3 us
    pallas_call x8, Pallas kernels, shadow_chunk(): pl.pallas_call(functools.partial(shadow_kernel, chunk, stream, turn), in_...  21.4 us
    pallas_call x8, Pallas kernels, flow_chunk(): pl.pallas_call(functools.partial(flow_kernel, start, end), in_specs=[VMEM...  20.7 us
    pallas_call x2, Pallas kernels, update(): pl.pallas_call(functools.partial(update_kernel, cap, devices, first, last...  13.3 us
    all_to_all x1, starting transfers between devices, local(): lax.all_to_all(outgoing, 'bus', split_axis=0, concat_axis=0, tiled=True)  7.05 us
    pallas_call x1, Pallas kernels, load_chunks(): pl.pallas_call(functools.partial(load_kernel, chunks), in_specs=[SMEM_SPE...  5.44 us
  transfers between devices with their start and end apart: 59, of which 20 were waited for; matrix products, arithmetic and copies ran while one was open for 2% of the time, Pallas kernels for 22%

profile of v7, /device:TPU:0, one launch (start us, length us, event | category | flops | bytes accessed | tf_op | source)
XLA Modules:
  0.0 184.7 jit_solution(15208900830779488188)
XLA Ops:
  0.7 3.7 %shadow_chunk.8 = (f32[2,128,640]{2,1,0:T(8,128)S(1)}, bf16[2,128,640]{2,1,0:T(8,128)(2,1)S(1)}, bf16[128,1280]{1,0:T(8,128)(2,1)S(1)}) custom-call(s32[1]{0:T(128)} %bitcast.place_ref, f32[1280,128]{1,0:T(8,128)} %rest_1_.1, bf16[1280,10240]{1,0:T(8,128)(2,1)} %ptdf_ref.9), custom_call_target="tpu_custom_call" | custom-call | flops 2516582400 | bytes 6553600 | tf_op jit(solution)/shard_map/shadow_chunk/pallas_call | solution.py:345
  4.9 3.6 %pack_generators.1 = (bf16[16,160,256]{2,1,0:T(8,128)(2,1)}, s32[1,768]{1,0:T(1,128)S(1)}) custom-call(s32[1]{0:T(128)} %bitcast.place_ref, s32[1,768]{1,0:T(1,128)S(1)} %bitcast.63, s32[6,128]{1,0:T(8,128)S(1)} %bitcast.61, f32[6,128]{1,0:T(8,128)S(1)} %bitcast.62, f32[768,128]{1,0:T(8,128)S(1)} %copy-done.1, f32[6,128]{1,0:T(8,128)S(1)} %bitcast.57, ...), custom_call_target="tpu_custom_call" | custom-call | flops 905969664 | bytes 3145728 | tf_op jit(solution)/shard_map/pack_generators/pallas_call | solution.py:107
  8.5 7.1 %all-to-all-start = ((bf16[16,160,256]{2,1,0:T(8,128)(2,1)}), bf16[16,160,256]{2,1,0:T(8,128)(2,1)S(1)}, u32[]{:S(2)}, u32[]{:S(2)}) async-start(bf16[16,160,256]{2,1,0:T(8,128)(2,1)} %get-tuple-element.85), calls=%async_computation | async-start | bytes 2621440 | tf_op jit(solution)/shard_map/all_to_all | solution.py:494
  15.6 3.4 %shadow_chunk.9 = (f32[2,128,640]{2,1,0:T(8,128)S(1)}, bf16[2,128,640]{2,1,0:T(8,128)(2,1)S(1)}) custom-call(s32[1]{0:T(128)} %bitcast.place_ref, bf16[128,1280]{1,0:T(8,128)(2,1)S(1)} %get-tuple-element.92.line_ref, bf16[1280,10240]{1,0:T(8,128)(2,1)} %ptdf_ref.9), custom_call_target="tpu_custom_call" | custom-call | flops 2516582400 | bytes 6553600 | tf_op jit(solution)/shard_map/shadow_chunk/pallas_call | solution.py:345
  22.2 3.4 %shadow_chunk.11 = (f32[2,128,640]{2,1,0:T(8,128)S(1)}, bf16[2,128,640]{2,1,0:T(8,128)(2,1)S(1)}) custom-call(s32[1]{0:T(128)} %bitcast.place_ref, bf16[128,1280]{1,0:T(8,128)(2,1)S(1)} %get-tuple-element.92.line_ref, bf16[1280,10240]{1,0:T(8,128)(2,1)} %ptdf_ref.9), custom_call_target="tpu_custom_call" | custom-call | flops 2516582400 | bytes 6553600 | tf_op jit(solution)/shard_map/shadow_chunk/pallas_call | solution.py:345
  26.2 6.9 %collective-permute-done.2 = bf16[128,640]{1,0:T(8,128)(2,1)S(1)} collective-permute-done((bf16[128,640]{1,0:T(8,128)(2,1)S(1)}, bf16[128,640]{1,0:T(8,128)(2,1)S(1)}, u32[]{:S(2)}, u32[]{:S(2)}) %collective-permute-start.2) | collective-permute-done | bytes 163872 | tf_op jit(solution)/shard_map/ppermute | solution.py:455
  34.1 3.5 %shadow_chunk.10 = (f32[2,128,640]{2,1,0:T(8,128)S(1)}, bf16[2,128,640]{2,1,0:T(8,128)(2,1)S(1)}) custom-call(s32[1]{0:T(128)} %bitcast.place_ref, bf16[128,1280]{1,0:T(8,128)(2,1)S(1)} %get-tuple-element.92.line_ref, bf16[1280,10240]{1,0:T(8,128)(2,1)} %ptdf_ref.9), custom_call_target="tpu_custom_call" | custom-call | flops 2516582400 | bytes 6553600 | tf_op jit(solution)/shard_map/shadow_chunk/pallas_call | solution.py:345
  40.0 7.5 %collective-permute-done.8 = bf16[128,640]{1,0:T(8,128)(2,1)S(1)} collective-permute-done((bf16[128,640]{1,0:T(8,128)(2,1)S(1)}, bf16[128,640]{1,0:T(8,128)(2,1)S(1)}, u32[]{:S(2)}, u32[]{:S(2)}) %collective-permute-start.8) | collective-permute-done | bytes 163872 | tf_op jit(solution)/shard_map/ppermute | solution.py:455
  49.5 2.5 %collective-permute-start.9 = (bf16[128,640]{1,0:T(8,128)(2,1)S(1)}, bf16[128,640]{1,0:T(8,128)(2,1)S(1)}, u32[]{:S(2)}, u32[]{:S(2)}) collective-permute-start(bf16[128,640]{1,0:T(8,128)(2,1)S(1)} %fusion.6), channel_id=1, source_target_pairs={{0,4},{1,5},{2,6},{3,7},{4,0},{5,1},{6,2},{7,3},{8,12},{9,13},{10,... | collective-permute-start | bytes 491528 | tf_op jit(solution)/shard_map/ppermute | solution.py:455
  52.1 6.3 %collective-permute-done.9.refs_1_ = bf16[128,640]{1,0:T(8,128)(2,1)S(1)} collective-permute-done((bf16[128,640]{1,0:T(8,128)(2,1)S(1)}, bf16[128,640]{1,0:T(8,128)(2,1)S(1)}, u32[]{:S(2)}, u32[]{:S(2)}) %collective-permute-start.9) | collective-permute-done | bytes 163872 | tf_op jit(solution)/shard_map/ppermute | solution.py:455
  58.4 8.5 %update_generators.2 = (f32[16,144,128]{2,1,0:T(8,128)S(1)}, bf16[656,128]{1,0:T(8,128)(2,1)S(1)}, bf16[1280,2560]{1,0:T(8,128)(2,1)S(1)}, bf16[1280,2560]{1,0:T(8,128)(2,1)S(1)}) custom-call(s32[1]{0:T(128)} %bitcast.place_ref, f32[128,640]{1,0:T(8,128)S(1)} %bitcast_add_fusion.6.refs_0_, bf16[128,640]{1,0:T(8,128)(2,1)S(1)} %collective-permute-done.9.refs_1_, ...), custom_call_target="tpu_custom_call" | custom-call | flops 1509949440 | bytes 4194304 | tf_op jit(solution)/shard_map/update_generators/pallas_call | solution.py:276
  67.4 2.6 %collective-permute-start.12 = (bf16[656,128]{1,0:T(8,128)(2,1)S(1)}, bf16[656,128]{1,0:T(8,128)(2,1)S(1)}, u32[]{:S(2)}, u32[]{:S(2)}) collective-permute-start(bf16[656,128]{1,0:T(8,128)(2,1)S(1)} %get-tuple-element.101.b0), channel_id=1, source_target_pairs={{0,8},{1,9},{2,10},{3,11},{4,12},{5,13},{6,14},{7,15},{8,0},{9,1},... | collective-permute-start | bytes 503816 | tf_op jit(solution)/shard_map/ppermute | solution.py:455
  70.9 5.4 %load_chunks.1 = (s32[1]{0:T(128)}, bf16[1280,2560]{1,0:T(8,128)(2,1)S(1)}, bf16[1280,2560]{1,0:T(8,128)(2,1)S(1)}) custom-call(s32[1]{0:T(128)} %bitcast.place_ref, bf16[1280,10240]{1,0:T(8,128)(2,1)} %ptdf_ref.9), custom_call_target="tpu_custom_call" | custom-call | bytes 13107200 | tf_op jit(solution)/shard_map/load_chunks/pallas_call | solution.py:386
  81.2 4.2 %collective-permute-done.20.b2 = bf16[656,128]{1,0:T(8,128)(2,1)S(1)} collective-permute-done((bf16[656,128]{1,0:T(8,128)(2,1)S(1)}, bf16[656,128]{1,0:T(8,128)(2,1)S(1)}, u32[]{:S(2)}, u32[]{:S(2)}) %collective-permute-start.20) | collective-permute-done | bytes 167968 | tf_op jit(solution)/shard_map/ppermute | solution.py:455
  85.4 2.4 %flow_chunk.8 = (f32[1280,128]{1,0:T(8,128)S(1)}, f32[1,128]{1,0:T(1,128)S(1)}) custom-call(bf16[1280,2560]{1,0:T(8,128)(2,1)S(1)} %get-tuple-element.107.ptdf_ref, bf16[656,128]{1,0:T(8,128)(2,1)S(1)} %get-tuple-element.101.b0, bf16[656,128]{1,0:T(8,128)(2,1)S(1)} %collective-permute-done.14.b1, bf16[656,128]{1,0:T(8,128)(2,1)S(1)} %collective-permute-done.13.b2, ...), custom_call_target="tpu_custom_call" | custom-call | flops 2516582400 | bytes 6553600 | tf_op jit(solution)/shard_map/flow_chunk/pallas_call | solution.py:443
  89.4 2.4 %flow_chunk.9 = (f32[1280,128]{1,0:T(8,128)S(1)}, f32[1,128]{1,0:T(1,128)S(1)}) custom-call(bf16[1280,2560]{1,0:T(8,128)(2,1)S(1)} %get-tuple-element.112.ptdf_ref, bf16[656,128]{1,0:T(8,128)(2,1)S(1)} %collective-permute-done.11.b0, bf16[656,128]{1,0:T(8,128)(2,1)S(1)} %collective-permute-done.19.b1, bf16[656,128]{1,0:T(8,128)(2,1)S(1)} %collective-permute-done.20.b2, ...), custom_call_target="tpu_custom_call" | custom-call | flops 2516582400 | bytes 6553600 | tf_op jit(solution)/shard_map/flow_chunk/pallas_call | solution.py:443
  91.8 2.9 %collective-permute-done.18.b2 = bf16[656,128]{1,0:T(8,128)(2,1)S(1)} collective-permute-done((bf16[656,128]{1,0:T(8,128)(2,1)S(1)}, bf16[656,128]{1,0:T(8,128)(2,1)S(1)}, u32[]{:S(2)}, u32[]{:S(2)}) %collective-permute-start.18) | collective-permute-done | bytes 167968 | tf_op jit(solution)/shard_map/ppermute | solution.py:455
  94.7 2.4 %flow_chunk.10 = (f32[1280,128]{1,0:T(8,128)S(1)}, f32[1,128]{1,0:T(1,128)S(1)}) custom-call(bf16[1280,2560]{1,0:T(8,128)(2,1)S(1)} %get-tuple-element.118.ptdf_ref, bf16[656,128]{1,0:T(8,128)(2,1)S(1)} %collective-permute-done.12.b0, bf16[656,128]{1,0:T(8,128)(2,1)S(1)} %collective-permute-done.23.b1, bf16[656,128]{1,0:T(8,128)(2,1)S(1)} %collective-permute-done.24.b2, ...), custom_call_target="tpu_custom_call" | custom-call | flops 2516582400 | bytes 6553600 | tf_op jit(solution)/shard_map/flow_chunk/pallas_call | solution.py:443
  97.2 2.8 %flow_chunk.11 = (f32[1280,128]{1,0:T(8,128)S(1)}, bf16[128,1280]{1,0:T(8,128)(2,1)S(1)}, f32[1,128]{1,0:T(1,128)S(1)}) custom-call(bf16[1280,2560]{1,0:T(8,128)(2,1)S(1)} %get-tuple-element.105.ptdf_ref, bf16[656,128]{1,0:T(8,128)(2,1)S(1)} %collective-permute-done.15.b0, bf16[656,128]{1,0:T(8,128)(2,1)S(1)} %collective-permute-done.17.b1, ...), custom_call_target="tpu_custom_call" | custom-call | flops 2516582400 | bytes 6553600 | tf_op jit(solution)/shard_map/flow_chunk/pallas_call | solution.py:443
  108.7 2.7 %collective-permute-done.28 = bf16[128,640]{1,0:T(8,128)(2,1)S(1)} collective-permute-done((bf16[128,640]{1,0:T(8,128)(2,1)S(1)}, bf16[128,640]{1,0:T(8,128)(2,1)S(1)}, u32[]{:S(2)}, u32[]{:S(2)}) %collective-permute-start.28) | collective-permute-done | bytes 163872 | tf_op jit(solution)/shard_map/ppermute | solution.py:455
  116.8 3.3 %collective-permute-done.34 = bf16[128,640]{1,0:T(8,128)(2,1)S(1)} collective-permute-done((bf16[128,640]{1,0:T(8,128)(2,1)S(1)}, bf16[128,640]{1,0:T(8,128)(2,1)S(1)}, u32[]{:S(2)}, u32[]{:S(2)}) %collective-permute-start.34) | collective-permute-done | bytes 163872 | tf_op jit(solution)/shard_map/ppermute | solution.py:455
  124.1 6.6 %collective-permute-done.35.refs_1_ = bf16[128,640]{1,0:T(8,128)(2,1)S(1)} collective-permute-done((bf16[128,640]{1,0:T(8,128)(2,1)S(1)}, bf16[128,640]{1,0:T(8,128)(2,1)S(1)}, u32[]{:S(2)}, u32[]{:S(2)}) %collective-permute-start.35) | collective-permute-done | bytes 163872 | tf_op jit(solution)/shard_map/ppermute | solution.py:455
  130.7 4.8 %update_generators.3 = (bf16[16,144,128]{2,1,0:T(8,128)(2,1)S(1)}, bf16[656,128]{1,0:T(8,128)(2,1)S(1)}) custom-call(s32[1]{0:T(128)} %get-tuple-element.104.place_ref, f32[128,640]{1,0:T(8,128)S(1)} %bitcast_add_fusion.2.refs_0_, bf16[128,640]{1,0:T(8,128)(2,1)S(1)} %collective-permute-done.35.refs_1_, ...), custom_call_target="tpu_custom_call" | custom-call | flops 1509949440 | bytes 4194304 | tf_op jit(solution)/shard_map/update_generators/pallas_call | solution.py:276
  135.7 2.7 %collective-permute-start.38 = (bf16[656,128]{1,0:T(8,128)(2,1)S(1)}, bf16[656,128]{1,0:T(8,128)(2,1)S(1)}, u32[]{:S(2)}, u32[]{:S(2)}) collective-permute-start(bf16[656,128]{1,0:T(8,128)(2,1)S(1)} %get-tuple-element.140.b0), channel_id=1, source_target_pairs={{0,8},{1,9},{2,10},{3,11},{4,12},{5,13},{6,14},{7,15},{8,0},{9,1},... | collective-permute-start | bytes 503816 | tf_op jit(solution)/shard_map/ppermute | solution.py:455
  139.4 5.2 %collective-permute-done.37.b0 = bf16[656,128]{1,0:T(8,128)(2,1)S(1)} collective-permute-done((bf16[656,128]{1,0:T(8,128)(2,1)S(1)}, bf16[656,128]{1,0:T(8,128)(2,1)S(1)}, u32[]{:S(2)}, u32[]{:S(2)}) %collective-permute-start.37) | collective-permute-done | bytes 167968 | tf_op jit(solution)/shard_map/ppermute | solution.py:455
  153.0 2.4 %flow_chunk.12 = (f32[1280,128]{1,0:T(8,128)S(1)}, f32[1,128]{1,0:T(1,128)S(1)}) custom-call(bf16[1280,2560]{1,0:T(8,128)(2,1)S(1)} %get-tuple-element.107.ptdf_ref, bf16[656,128]{1,0:T(8,128)(2,1)S(1)} %get-tuple-element.140.b0, bf16[656,128]{1,0:T(8,128)(2,1)S(1)} %collective-permute-done.41.b1, bf16[656,128]{1,0:T(8,128)(2,1)S(1)} %collective-permute-done.39.b2, ...), custom_call_target="tpu_custom_call" | custom-call | flops 2516582400 | bytes 6553600 | tf_op jit(solution)/shard_map/flow_chunk/pallas_call | solution.py:443
  155.7 2.5 %collective-permute-start.49 = (bf16[4,144,128]{2,1,0:T(8,128)(2,1)S(1)}, bf16[4,144,128]{2,1,0:T(8,128)(2,1)S(1)}, u32[]{:S(2)}, u32[]{:S(2)}) collective-permute-start(bf16[4,144,128]{2,1,0:T(8,128)(2,1)S(1)} %get-tuple-element.163), channel_id=1, source_target_pairs={{0,12},{1,13},{2,14},{3,15},{4,8},{5,9},{6,10},{7,11},{8,4},{9,5},... | collective-permute-start | bytes 442376 | tf_op jit(solution)/shard_map/ppermute | solution.py:455
  158.8 2.4 %flow_chunk.13 = (f32[1280,128]{1,0:T(8,128)S(1)}, f32[1,128]{1,0:T(1,128)S(1)}) custom-call(bf16[1280,2560]{1,0:T(8,128)(2,1)S(1)} %get-tuple-element.112.ptdf_ref, bf16[656,128]{1,0:T(8,128)(2,1)S(1)} %collective-permute-done.37.b0, bf16[656,128]{1,0:T(8,128)(2,1)S(1)} %collective-permute-done.44.b1, bf16[656,128]{1,0:T(8,128)(2,1)S(1)} %collective-permute-done.45.b2, ...), custom_call_target="tpu_custom_call" | custom-call | flops 2516582400 | bytes 6553600 | tf_op jit(solution)/shard_map/flow_chunk/pallas_call | solution.py:443
  161.3 7.5 %collective-permute-done.48 = bf16[4,144,128]{2,1,0:T(8,128)(2,1)S(1)} collective-permute-done((bf16[4,144,128]{2,1,0:T(8,128)(2,1)S(1)}, bf16[4,144,128]{2,1,0:T(8,128)(2,1)S(1)}, u32[]{:S(2)}, u32[]{:S(2)}) %collective-permute-start.48) | collective-permute-done | bytes 147488 | tf_op jit(solution)/shard_map/ppermute | solution.py:455
  171.9 2.4 %flow_chunk.14 = (f32[1280,128]{1,0:T(8,128)S(1)}, f32[1,128]{1,0:T(1,128)S(1)}) custom-call(bf16[1280,2560]{1,0:T(8,128)(2,1)S(1)} %get-tuple-element.118.ptdf_ref, bf16[656,128]{1,0:T(8,128)(2,1)S(1)} %collective-permute-done.38.b0, bf16[656,128]{1,0:T(8,128)(2,1)S(1)} %collective-permute-done.55.b1, bf16[656,128]{1,0:T(8,128)(2,1)S(1)} %collective-permute-done.56.b2, ...), custom_call_target="tpu_custom_call" | custom-call | flops 2516582400 | bytes 6553600 | tf_op jit(solution)/shard_map/flow_chunk/pallas_call | solution.py:443
  176.3 2.3 %collective-permute-done.52.refs_3_ = bf16[4,144,128]{2,1,0:T(8,128)(2,1)S(1)} collective-permute-done((bf16[4,144,128]{2,1,0:T(8,128)(2,1)S(1)}, bf16[4,144,128]{2,1,0:T(8,128)(2,1)S(1)}, u32[]{:S(2)}, u32[]{:S(2)}) %collective-permute-start.52) | collective-permute-done | bytes 147488 | tf_op jit(solution)/shard_map/ppermute | solution.py:455
  180.8 3.4 %flow_chunk.15 = (f32[1280,128]{1,0:T(8,128)}, bf16[128,1280]{1,0:T(8,128)(2,1)}, f32[1,128]{1,0:T(1,128)S(1)}) custom-call(bf16[1280,2560]{1,0:T(8,128)(2,1)S(1)} %get-tuple-element.105.ptdf_ref, bf16[656,128]{1,0:T(8,128)(2,1)S(1)} %collective-permute-done.40.b0, bf16[656,128]{1,0:T(8,128)(2,1)S(1)} %collective-permute-done.53.b1, ...), custom_call_target="tpu_custom_call" | custom-call | flops 2516582400 | bytes 6553600 | tf_op jit(solution)/shard_map/flow_chunk/pallas_call | solution.py:443
  (154 shorter events, 53.5 us)
Async XLA Ops:
  4.4 15.1 %collective-permute-start = (bf16[2,128,640]{2,1,0:T(8,128)(2,1)S(1)}, bf16[2,128,640]{2,1,0:T(8,128)(2,1)}, u32[]{:S(2)}, u32[]{:S(2)}) collective-permute-start(bf16[2,128,640]{2,1,0:T(8,128)(2,1)S(1)} %get-tuple-element.88), channel_id=1, source_target_pairs={{0,1},{1,0},{2,3},{3,2},{4,5},{5,4},{6,7},{7,6},{8,9},{9,8},{10,11... | collective-permute-start | bytes 983048 | tf_op jit(solution)/shard_map/ppermute | solution.py:455
  8.5 49.8 %all-to-all-start = ((bf16[16,160,256]{2,1,0:T(8,128)(2,1)}), bf16[16,160,256]{2,1,0:T(8,128)(2,1)S(1)}, u32[]{:S(2)}, u32[]{:S(2)}) async-start(bf16[16,160,256]{2,1,0:T(8,128)(2,1)} %get-tuple-element.85), calls=%async_computation | async-start | bytes 2621440 | tf_op jit(solution)/shard_map/all_to_all | solution.py:494
  20.5 12.7 %collective-permute-start.2 = (bf16[128,640]{1,0:T(8,128)(2,1)S(1)}, bf16[128,640]{1,0:T(8,128)(2,1)S(1)}, u32[]{:S(2)}, u32[]{:S(2)}) collective-permute-start(bf16[128,640]{1,0:T(8,128)(2,1)S(1)} %fusion.8), channel_id=1, source_target_pairs={{0,2},{1,3},{2,0},{3,1},{4,6},{5,7},{6,4},{7,5},{8,10},{9,11},{10,... | collective-permute-start | bytes 491528 | tf_op jit(solution)/shard_map/ppermute | solution.py:455
  25.6 12.1 %collective-permute-start.5 = (bf16[2,128,640]{2,1,0:T(8,128)(2,1)S(1)}, bf16[2,128,640]{2,1,0:T(8,128)(2,1)S(1)}, u32[]{:S(2)}, u32[]{:S(2)}) collective-permute-start(bf16[2,128,640]{2,1,0:T(8,128)(2,1)S(1)} %get-tuple-element.96), channel_id=1, source_target_pairs={{0,1},{1,0},{2,3},{3,2},{4,5},{5,4},{6,7},{7,6},{8,9},{9,8},{10,11... | collective-permute-start | bytes 983048 | tf_op jit(solution)/shard_map/ppermute | solution.py:455
  25.8 12.0 %collective-permute-start.6 = (bf16[128,640]{1,0:T(8,128)(2,1)S(1)}, bf16[128,640]{1,0:T(8,128)(2,1)S(1)}, u32[]{:S(2)}, u32[]{:S(2)}) collective-permute-start(bf16[128,640]{1,0:T(8,128)(2,1)S(1)} %fusion.9), channel_id=1, source_target_pairs={{0,2},{1,3},{2,0},{3,1},{4,6},{5,7},{6,4},{7,5},{8,10},{9,11},{10,... | collective-permute-start | bytes 491528 | tf_op jit(solution)/shard_map/ppermute | solution.py:455
  37.7 9.9 %collective-permute-start.8 = (bf16[128,640]{1,0:T(8,128)(2,1)S(1)}, bf16[128,640]{1,0:T(8,128)(2,1)S(1)}, u32[]{:S(2)}, u32[]{:S(2)}) collective-permute-start(bf16[128,640]{1,0:T(8,128)(2,1)S(1)} %fusion.7), channel_id=1, source_target_pairs={{0,4},{1,5},{2,6},{3,7},{4,0},{5,1},{6,2},{7,3},{8,12},{9,13},{10,... | collective-permute-start | bytes 491528 | tf_op jit(solution)/shard_map/ppermute | solution.py:455
  37.8 11.6 %collective-permute-start.7 = (bf16[128,640]{1,0:T(8,128)(2,1)S(1)}, bf16[128,640]{1,0:T(8,128)(2,1)S(1)}, u32[]{:S(2)}, u32[]{:S(2)}) collective-permute-start(bf16[128,640]{1,0:T(8,128)(2,1)S(1)} %fusion.11), channel_id=1, source_target_pairs={{0,2},{1,3},{2,0},{3,1},{4,6},{5,7},{6,4},{7,5},{8,10},{9,11},{10,... | collective-permute-start | bytes 491528 | tf_op jit(solution)/shard_map/ppermute | solution.py:455
  39.9 12.2 %collective-permute-start.4 = (bf16[128,640]{1,0:T(8,128)(2,1)S(1)}, bf16[128,640]{1,0:T(8,128)(2,1)S(1)}, u32[]{:S(2)}, u32[]{:S(2)}) collective-permute-start(bf16[128,640]{1,0:T(8,128)(2,1)S(1)} %fusion.10), channel_id=1, source_target_pairs={{0,2},{1,3},{2,0},{3,1},{4,6},{5,7},{6,4},{7,5},{8,10},{9,11},{10,... | collective-permute-start | bytes 491528 | tf_op jit(solution)/shard_map/ppermute | solution.py:455
  47.6 10.7 %collective-permute-start.10 = (bf16[128,640]{1,0:T(8,128)(2,1)S(1)}, bf16[128,640]{1,0:T(8,128)(2,1)S(1)}, u32[]{:S(2)}, u32[]{:S(2)}) collective-permute-start(bf16[128,640]{1,0:T(8,128)(2,1)S(1)} %fusion.5), channel_id=1, source_target_pairs={{0,8},{1,9},{2,10},{3,11},{4,12},{5,13},{6,14},{7,15},{8,0},{9,1},... | collective-permute-start | bytes 491528 | tf_op jit(solution)/shard_map/ppermute | solution.py:455
  49.5 8.9 %collective-permute-start.9 = (bf16[128,640]{1,0:T(8,128)(2,1)S(1)}, bf16[128,640]{1,0:T(8,128)(2,1)S(1)}, u32[]{:S(2)}, u32[]{:S(2)}) collective-permute-start(bf16[128,640]{1,0:T(8,128)(2,1)S(1)} %fusion.6), channel_id=1, source_target_pairs={{0,4},{1,5},{2,6},{3,7},{4,0},{5,1},{6,2},{7,3},{8,12},{9,13},{10,... | collective-permute-start | bytes 491528 | tf_op jit(solution)/shard_map/ppermute | solution.py:455
  67.0 10.1 %collective-permute-start.11 = (bf16[656,128]{1,0:T(8,128)(2,1)S(1)}, bf16[656,128]{1,0:T(8,128)(2,1)S(1)}, u32[]{:S(2)}, u32[]{:S(2)}) collective-permute-start(bf16[656,128]{1,0:T(8,128)(2,1)S(1)} %get-tuple-element.101.b0), channel_id=1, source_target_pairs={{0,4},{1,5},{2,6},{3,7},{4,0},{5,1},{6,2},{7,3},{8,12},{9,13},{10,... | collective-permute-start | bytes 503816 | tf_op jit(solution)/shard_map/ppermute | solution.py:455
  67.4 10.9 %collective-permute-start.12 = (bf16[656,128]{1,0:T(8,128)(2,1)S(1)}, bf16[656,128]{1,0:T(8,128)(2,1)S(1)}, u32[]{:S(2)}, u32[]{:S(2)}) collective-permute-start(bf16[656,128]{1,0:T(8,128)(2,1)S(1)} %get-tuple-element.101.b0), channel_id=1, source_target_pairs={{0,8},{1,9},{2,10},{3,11},{4,12},{5,13},{6,14},{7,15},{8,0},{9,1},... | collective-permute-start | bytes 503816 | tf_op jit(solution)/shard_map/ppermute | solution.py:455
  79.5 8.9 %collective-permute-start.19 = (bf16[656,128]{1,0:T(8,128)(2,1)S(1)}, bf16[656,128]{1,0:T(8,128)(2,1)S(1)}, u32[]{:S(2)}, u32[]{:S(2)}) collective-permute-start(bf16[656,128]{1,0:T(8,128)(2,1)S(1)} %collective-permute-done.11.b0), channel_id=1, source_target_pairs={{0,1},{1,0},{2,3},{3,2},{4,5},{5,4},{6,7},{7,6},{8,9},{9,8},{10,11... | collective-permute-start | bytes 503816 | tf_op jit(solution)/shard_map/ppermute | solution.py:455
  80.0 14.7 %collective-permute-start.23 = (bf16[656,128]{1,0:T(8,128)(2,1)S(1)}, bf16[656,128]{1,0:T(8,128)(2,1)S(1)}, u32[]{:S(2)}, u32[]{:S(2)}) collective-permute-start(bf16[656,128]{1,0:T(8,128)(2,1)S(1)} %collective-permute-done.12.b0), channel_id=1, source_target_pairs={{0,1},{1,0},{2,3},{3,2},{4,5},{5,4},{6,7},{7,6},{8,9},{9,8},{10,11... | collective-permute-start | bytes 503816 | tf_op jit(solution)/shard_map/ppermute | solution.py:455
  80.1 9.3 %collective-permute-start.24 = (bf16[656,128]{1,0:T(8,128)(2,1)S(1)}, bf16[656,128]{1,0:T(8,128)(2,1)S(1)}, u32[]{:S(2)}, u32[]{:S(2)}) collective-permute-start(bf16[656,128]{1,0:T(8,128)(2,1)S(1)} %collective-permute-done.12.b0), channel_id=1, source_target_pairs={{0,2},{1,3},{2,0},{3,1},{4,6},{5,7},{6,4},{7,5},{8,10},{9,11},{10,... | collective-permute-start | bytes 503816 | tf_op jit(solution)/shard_map/ppermute | solution.py:455
  87.8 9.3 %collective-permute-start.17 = (bf16[656,128]{1,0:T(8,128)(2,1)S(1)}, bf16[656,128]{1,0:T(8,128)(2,1)S(1)}, u32[]{:S(2)}, u32[]{:S(2)}) collective-permute-start(bf16[656,128]{1,0:T(8,128)(2,1)S(1)} %collective-permute-done.15.b0), channel_id=1, source_target_pairs={{0,1},{1,0},{2,3},{3,2},{4,5},{5,4},{6,7},{7,6},{8,9},{9,8},{10,11... | collective-permute-start | bytes 503816 | tf_op jit(solution)/shard_map/ppermute | solution.py:455
  120.2 10.5 %collective-permute-start.36 = (bf16[128,640]{1,0:T(8,128)(2,1)S(1)}, bf16[128,640]{1,0:T(8,128)(2,1)S(1)}, u32[]{:S(2)}, u32[]{:S(2)}) collective-permute-start(bf16[128,640]{1,0:T(8,128)(2,1)S(1)} %fusion.1), channel_id=1, source_target_pairs={{0,8},{1,9},{2,10},{3,11},{4,12},{5,13},{6,14},{7,15},{8,0},{9,1},... | collective-permute-start | bytes 491528 | tf_op jit(solution)/shard_map/ppermute | solution.py:455
  121.9 8.8 %collective-permute-start.35 = (bf16[128,640]{1,0:T(8,128)(2,1)S(1)}, bf16[128,640]{1,0:T(8,128)(2,1)S(1)}, u32[]{:S(2)}, u32[]{:S(2)}) collective-permute-start(bf16[128,640]{1,0:T(8,128)(2,1)S(1)} %fusion.2), channel_id=1, source_target_pairs={{0,4},{1,5},{2,6},{3,7},{4,0},{5,1},{6,2},{7,3},{8,12},{9,13},{10,... | collective-permute-start | bytes 491528 | tf_op jit(solution)/shard_map/ppermute | solution.py:455
  135.5 9.2 %collective-permute-start.37 = (bf16[656,128]{1,0:T(8,128)(2,1)S(1)}, bf16[656,128]{1,0:T(8,128)(2,1)S(1)}, u32[]{:S(2)}, u32[]{:S(2)}) collective-permute-start(bf16[656,128]{1,0:T(8,128)(2,1)S(1)} %get-tuple-element.140.b0), channel_id=1, source_target_pairs={{0,4},{1,5},{2,6},{3,7},{4,0},{5,1},{6,2},{7,3},{8,12},{9,13},{10,... | collective-permute-start | bytes 503816 | tf_op jit(solution)/shard_map/ppermute | solution.py:455
  135.7 10.2 %collective-permute-start.38 = (bf16[656,128]{1,0:T(8,128)(2,1)S(1)}, bf16[656,128]{1,0:T(8,128)(2,1)S(1)}, u32[]{:S(2)}, u32[]{:S(2)}) collective-permute-start(bf16[656,128]{1,0:T(8,128)(2,1)S(1)} %get-tuple-element.140.b0), channel_id=1, source_target_pairs={{0,8},{1,9},{2,10},{3,11},{4,12},{5,13},{6,14},{7,15},{8,0},{9,1},... | collective-permute-start | bytes 503816 | tf_op jit(solution)/shard_map/ppermute | solution.py:455
  139.2 9.1 %collective-permute-start.41 = (bf16[656,128]{1,0:T(8,128)(2,1)S(1)}, bf16[656,128]{1,0:T(8,128)(2,1)S(1)}, u32[]{:S(2)}, u32[]{:S(2)}) collective-permute-start(bf16[656,128]{1,0:T(8,128)(2,1)S(1)} %get-tuple-element.140.b0), channel_id=1, source_target_pairs={{0,1},{1,0},{2,3},{3,2},{4,5},{5,4},{6,7},{7,6},{8,9},{9,8},{10,11... | collective-permute-start | bytes 503816 | tf_op jit(solution)/shard_map/ppermute | solution.py:455
  145.9 9.8 %collective-permute-start.44 = (bf16[656,128]{1,0:T(8,128)(2,1)S(1)}, bf16[656,128]{1,0:T(8,128)(2,1)S(1)}, u32[]{:S(2)}, u32[]{:S(2)}) collective-permute-start(bf16[656,128]{1,0:T(8,128)(2,1)S(1)} %collective-permute-done.37.b0), channel_id=1, source_target_pairs={{0,1},{1,0},{2,3},{3,2},{4,5},{5,4},{6,7},{7,6},{8,9},{9,8},{10,11... | collective-permute-start | bytes 503816 | tf_op jit(solution)/shard_map/ppermute | solution.py:455
  146.9 8.6 %collective-permute-start.40 = (bf16[656,128]{1,0:T(8,128)(2,1)S(1)}, bf16[656,128]{1,0:T(8,128)(2,1)S(1)}, u32[]{:S(2)}, u32[]{:S(2)}) collective-permute-start(bf16[656,128]{1,0:T(8,128)(2,1)S(1)} %collective-permute-done.38.b0), channel_id=1, source_target_pairs={{0,4},{1,5},{2,6},{3,7},{4,0},{5,1},{6,2},{7,3},{8,12},{9,13},{10,... | collective-permute-start | bytes 503816 | tf_op jit(solution)/shard_map/ppermute | solution.py:455
  146.9 22.0 %collective-permute-start.56 = (bf16[656,128]{1,0:T(8,128)(2,1)S(1)}, bf16[656,128]{1,0:T(8,128)(2,1)S(1)}, u32[]{:S(2)}, u32[]{:S(2)}) collective-permute-start(bf16[656,128]{1,0:T(8,128)(2,1)S(1)} %collective-permute-done.38.b0), channel_id=1, source_target_pairs={{0,2},{1,3},{2,0},{3,1},{4,6},{5,7},{6,4},{7,5},{8,10},{9,11},{10,... | collective-permute-start | bytes 503816 | tf_op jit(solution)/shard_map/ppermute | solution.py:455
  149.7 11.5 %collective-permute-start.47 = (bf16[4,144,128]{2,1,0:T(8,128)(2,1)S(1)}, bf16[4,144,128]{2,1,0:T(8,128)(2,1)S(1)}, u32[]{:S(2)}, u32[]{:S(2)}) collective-permute-start(bf16[4,144,128]{2,1,0:T(8,128)(2,1)S(1)} %get-tuple-element.165), channel_id=1, source_target_pairs={{0,4},{1,5},{2,6},{3,7},{4,0},{5,1},{6,2},{7,3},{8,12},{9,13},{10,... | collective-permute-start | bytes 442376 | tf_op jit(solution)/shard_map/ppermute | solution.py:455
  155.5 13.4 %collective-permute-start.48 = (bf16[4,144,128]{2,1,0:T(8,128)(2,1)S(1)}, bf16[4,144,128]{2,1,0:T(8,128)(2,1)S(1)}, u32[]{:S(2)}, u32[]{:S(2)}) collective-permute-start(bf16[4,144,128]{2,1,0:T(8,128)(2,1)S(1)} %get-tuple-element.164), channel_id=1, source_target_pairs={{0,8},{1,9},{2,10},{3,11},{4,12},{5,13},{6,14},{7,15},{8,0},{9,1},... | collective-permute-start | bytes 442376 | tf_op jit(solution)/shard_map/ppermute | solution.py:455
  155.7 13.6 %collective-permute-start.49 = (bf16[4,144,128]{2,1,0:T(8,128)(2,1)S(1)}, bf16[4,144,128]{2,1,0:T(8,128)(2,1)S(1)}, u32[]{:S(2)}, u32[]{:S(2)}) collective-permute-start(bf16[4,144,128]{2,1,0:T(8,128)(2,1)S(1)} %get-tuple-element.163), channel_id=1, source_target_pairs={{0,12},{1,13},{2,14},{3,15},{4,8},{5,9},{6,10},{7,11},{8,4},{9,5},... | collective-permute-start | bytes 442376 | tf_op jit(solution)/shard_map/ppermute | solution.py:455
  158.2 11.1 %collective-permute-start.43 = (bf16[656,128]{1,0:T(8,128)(2,1)S(1)}, bf16[656,128]{1,0:T(8,128)(2,1)S(1)}, u32[]{:S(2)}, u32[]{:S(2)}) collective-permute-start(bf16[656,128]{1,0:T(8,128)(2,1)S(1)} %collective-permute-done.40.b0), channel_id=1, source_target_pairs={{0,2},{1,3},{2,0},{3,1},{4,6},{5,7},{6,4},{7,5},{8,10},{9,11},{10,... | collective-permute-start | bytes 503816 | tf_op jit(solution)/shard_map/ppermute | solution.py:455
  161.2 9.0 %collective-permute-start.55 = (bf16[656,128]{1,0:T(8,128)(2,1)S(1)}, bf16[656,128]{1,0:T(8,128)(2,1)S(1)}, u32[]{:S(2)}, u32[]{:S(2)}) collective-permute-start(bf16[656,128]{1,0:T(8,128)(2,1)S(1)} %collective-permute-done.38.b0), channel_id=1, source_target_pairs={{0,1},{1,0},{2,3},{3,2},{4,5},{5,4},{6,7},{7,6},{8,9},{9,8},{10,11... | collective-permute-start | bytes 503816 | tf_op jit(solution)/shard_map/ppermute | solution.py:455
  168.8 12.0 %collective-permute-start.53 = (bf16[656,128]{1,0:T(8,128)(2,1)S(1)}, bf16[656,128]{1,0:T(8,128)(2,1)S(1)}, u32[]{:S(2)}, u32[]{:S(2)}) collective-permute-start(bf16[656,128]{1,0:T(8,128)(2,1)S(1)} %collective-permute-done.40.b0), channel_id=1, source_target_pairs={{0,1},{1,0},{2,3},{3,2},{4,5},{5,4},{6,7},{7,6},{8,9},{9,8},{10,11... | collective-permute-start | bytes 503816 | tf_op jit(solution)/shard_map/ppermute | solution.py:455
  170.2 8.4 %collective-permute-start.52 = (bf16[4,144,128]{2,1,0:T(8,128)(2,1)S(1)}, bf16[4,144,128]{2,1,0:T(8,128)(2,1)S(1)}, u32[]{:S(2)}, u32[]{:S(2)}) collective-permute-start(bf16[4,144,128]{2,1,0:T(8,128)(2,1)S(1)} %pad_maximum_fusion.3), channel_id=1, source_target_pairs={{0,3},{1,2},{2,1},{3,0},{4,7},{5,6},{6,5},{7,4},{8,11},{9,10},{10,... | collective-permute-start | bytes 442376 | tf_op jit(solution)/shard_map/ppermute | solution.py:455
  171.6 9.3 %collective-permute-start.54 = (bf16[656,128]{1,0:T(8,128)(2,1)S(1)}, bf16[656,128]{1,0:T(8,128)(2,1)S(1)}, u32[]{:S(2)}, u32[]{:S(2)}) collective-permute-start(bf16[656,128]{1,0:T(8,128)(2,1)S(1)} %collective-permute-done.43.b2), channel_id=1, source_target_pairs={{0,1},{1,0},{2,3},{3,2},{4,5},{5,4},{6,7},{7,6},{8,9},{9,8},{10,11... | collective-permute-start | bytes 503816 | tf_op jit(solution)/shard_map/ppermute | solution.py:455
  (37 other events, 234.9 us)

commit v8 on v7

--- a/solution.py
+++ b/solution.py
@@ -145,7 +145,7 @@
     peers, cap, _ = back_refs[0].shape
     for i, ref in enumerate(back_refs):
         for j in range(peers):
-            start = (j * len(back_refs) + i) * cap
+            start = (i * peers + j) * cap
             back_ref[start : start + cap, :] = ref[j]
     gens = slot_ref.shape[1]
     slot = jnp.broadcast_to(slot_ref[...].astype(F32), (128, gens)).T[:, 0:1].astype(jnp.int32)
@@ -491,8 +491,11 @@
     limit = line_limit.reshape(-1, 1)
     balance_row = balance_price.reshape(1, hours)
     line_half = line_price if staged else line_price.astype(BF16)
+    limit = line_limit.reshape(-1, 1)
+    balance_row = balance_price.reshape(1, hours)
+    line_half = line_price if staged else line_price.astype(BF16)
     recv = lax.all_to_all(outgoing, "bus", split_axis=0, concat_axis=0, tiled=True)
-    held, resident = None, {}
+    held, resident, recv = None, {}, None
     for iteration in range(ITERS):
         last = iteration == ITERS - 1
         if staged:
@@ -525,11 +528,20 @@
 
             line_t = product(3, line_t)
             if iteration == 0:
-                line_t, _ = lax.optimization_barrier((line_t, outgoing))
-            product(2, line_t)
-            line_t, _ = lax.optimization_barrier((line_t, across(3)))
+                line_t, gots[3], outgoing = lax.optimization_barrier((line_t, gots[3], outgoing))
+                outgoing, _ = lax.optimization_barrier((outgoing, across(3)))
+                recv = lax.all_to_all(outgoing, "bus", split_axis=0, concat_axis=0, tiled=True)
+                line_t, _ = lax.optimization_barrier((line_t, settle(3)))
+                product(2, line_t)
+            else:
+                product(2, line_t)
+                line_t, _ = lax.optimization_barrier((line_t, across(3)))
             product(1, line_t)
-            line_t, _, _ = lax.optimization_barrier((line_t, across(2), settle(3)))
+            line_t, _ = lax.optimization_barrier((line_t, across(2)))
+            if iteration:
+                line_t, _ = lax.optimization_barrier((line_t, settle(3)))
+            else:
+                line_t, parts[3] = lax.optimization_barrier((line_t, parts[3]))
             product(0, line_t)
             gots[1], crossed[2] = lax.optimization_barrier((gots[1], crossed[2]))
             parts[3], _, _ = lax.optimization_barrier((parts[3], across(1), across(0)))
@@ -538,6 +550,7 @@
             settle(0)
             prices = [parts[0], parts[1], parts[2]]
         else:
+            recv = lax.all_to_all(outgoing, "bus", split_axis=0, concat_axis=0, tiled=True) if recv is None else recv
             shadow = lax.dot_general(ptdf, line_half, (((0,), (0,)), ((), ())), preferred_element_type=F32)
             prices = [lax.psum_scatter(shadow, "bus", scatter_dimension=0, tiled=True).T]
         chunks = (0, 1) if staged and not last else ()
@@ -562,35 +575,34 @@
             near[1] = swap(block, devices, 4)
             spread(0)
             stage = [near[1], near[2], far[0]]
-            if not last:
+            if last:
+                home = held.reshape(4, 4, *held.shape[1:])
+                stage += [swap(home[:, rel], devices, rel) for rel in (1, 2, 3)]
+            else:
                 cross[0], here = lax.optimization_barrier((cross[0], place))
                 place, (resident[2], resident[3]) = load_chunks((2, 3), here, ptdf, buses)
                 stage.append(place)
             near[1], near[2], far[0], *rest = lax.optimization_barrier(stage)
-            place = rest[0] if rest else place
             near[3] = swap(near[2], devices, 4)
             spread(1)
             spread(2)
             settle_far(0)
+            if last:
+                home = jnp.stack([home[:, 0], *rest], axis=1)
+                back = [home[0]] + [swap(home[chunk], devices, 4 * chunk) for chunk in (1, 2, 3)]
+            else:
+                (place,) = rest
             acc, total = flow_chunk(resident[0], blocks(0), None, balance_row)
-            near[3], acc = lax.optimization_barrier((near[3], acc))
+            near[3], far[1], acc = lax.optimization_barrier((near[3], far[1], acc))
             spread(3)
-            if last:
-                home, _ = lax.optimization_barrier((held, cross[0]))
-                home = home.reshape(4, 4, *home.shape[1:])
-                home = [home[0]] + [swap(home[chunk], devices, 4 * chunk) for chunk in (1, 2, 3)]
             settle_far(1)
             acc, total = flow_chunk(resident[1], blocks(1), acc, total)
             settle_far(2)
-            if last:
-                far[3], acc, *home = lax.optimization_barrier((far[3], acc, *home))
-            else:
-                far[3], acc = lax.optimization_barrier((far[3], acc))
+            far[3], acc = lax.optimization_barrier((far[3], acc))
             settle_far(3)
             acc, total = flow_chunk(resident[2], blocks(2), acc, total)
             if last:
-                back = [jnp.stack([home[chunk][rel] for chunk in range(4)]) for rel in range(4)]
-                back = [back[0]] + [swap(back[rel], devices, rel) for rel in (1, 2, 3)]
+                acc, *back = lax.optimization_barrier((acc, *back))
             line_price, line_half, total = flow_chunk(resident[3], blocks(3), acc, total, limit, line_price)
             balance = total
         else:

time: 186 us -> 194 us (1.043)
  starting transfers between devices: 47.4 us -> 56.6 us
    ppermute x58, starting transfers between devices: 40.3 us -> 51.6 us  [swap(): return lax.ppermute(x, 'bus', [(i, i ^ mask) for i in range(devices)])]
    all_to_all x1, starting transfers between devices: 7.05 us -> 4.98 us  [local(): lax.all_to_all(outgoing, 'bus', split_axis=0, concat_axis=0, tiled=True)]
  transfers between devices with their start and end apart: 59 -> 59, of which waited for: 20 -> 22; matrix products, arithmetic and copies ran while one was open for 2% -> 1% of each run, Pallas kernels for 22% -> 21%
where the time goes in v8:
time: 194 us
  Pallas kernels  66.6 us (34%)
  waiting for transfers between devices  65.8 us (34%)
  starting transfers between devices  56.6 us (29%)
  other arithmetic  3 us (2%)
    ppermute x58, waiting for transfers between devices, swap(): return lax.ppermute(x, 'bus', [(i, i ^ mask) for i in range(devices)])  65.8 us
    ppermute x58, starting transfers between devices, swap(): return lax.ppermute(x, 'bus', [(i, i ^ mask) for i in range(devices)])  51.6 us
    pallas_call x8, Pallas kernels, shadow_chunk(): pl.pallas_call(functools.partial(shadow_kernel, chunk, stream, turn), in_...  21.3 us
    pallas_call x8, Pallas kernels, flow_chunk(): pl.pallas_call(functools.partial(flow_kernel, start, end), in_specs=[VMEM...  20.7 us
    pallas_call x2, Pallas kernels, update(): pl.pallas_call(functools.partial(update_kernel, cap, devices, first, last...  13.3 us
    pallas_call x1, Pallas kernels, load_chunks(): pl.pallas_call(functools.partial(load_kernel, chunks), in_specs=[SMEM_SPE...  5.44 us
    all_to_all x1, starting transfers between devices, local(): lax.all_to_all(outgoing, 'bus', split_axis=0, concat_axis=0, tiled=True)  4.98 us
  transfers between devices with their start and end apart: 59, of which 22 were waited for; matrix products, arithmetic and copies ran while one was open for 1% of the time, Pallas kernels for 21%

profile of v8, /device:TPU:0, one launch (start us, length us, event | category | flops | bytes accessed | tf_op | source)
XLA Modules:
  0.0 193.5 jit_solution(10588513332395894606)
XLA Ops:
  0.7 3.7 %shadow_chunk.8 = (f32[2,128,640]{2,1,0:T(8,128)S(1)}, bf16[2,128,640]{2,1,0:T(8,128)(2,1)S(1)}, bf16[128,1280]{1,0:T(8,128)(2,1)S(1)}) custom-call(s32[1]{0:T(128)} %bitcast.place_ref, f32[1280,128]{1,0:T(8,128)} %rest_1_.1, bf16[1280,10240]{1,0:T(8,128)(2,1)} %ptdf_ref.9), custom_call_target="tpu_custom_call" | custom-call | flops 2516582400 | bytes 6553600 | tf_op jit(solution)/shard_map/shadow_chunk/pallas_call | solution.py:345
  4.9 3.6 %pack_generators.1 = (bf16[16,160,256]{2,1,0:T(8,128)(2,1)}, s32[1,768]{1,0:T(1,128)S(1)}) custom-call(s32[1]{0:T(128)} %bitcast.place_ref, s32[1,768]{1,0:T(1,128)S(1)} %bitcast.88, s32[6,128]{1,0:T(8,128)S(1)} %bitcast.86, f32[6,128]{1,0:T(8,128)S(1)} %bitcast.87, f32[768,128]{1,0:T(8,128)S(1)} %copy-done.1, f32[6,128]{1,0:T(8,128)S(1)} %bitcast.82, ...), custom_call_target="tpu_custom_call" | custom-call | flops 905969664 | bytes 3145728 | tf_op jit(solution)/shard_map/pack_generators/pallas_call | solution.py:107
  9.2 2.6 %collective-permute-start.1 = (bf16[128,640]{1,0:T(8,128)(2,1)}, bf16[128,640]{1,0:T(8,128)(2,1)}, u32[]{:S(2)}, u32[]{:S(2)}) collective-permute-start(bf16[128,640]{1,0:T(8,128)(2,1)} %fusion.8), channel_id=1, source_target_pairs={{0,2},{1,3},{2,0},{3,1},{4,6},{5,7},{6,4},{7,5},{8,10},{9,11},{10,... | collective-permute-start | bytes 491528 | tf_op jit(solution)/shard_map/ppermute | solution.py:455
  11.8 5.0 %all-to-all-start = ((bf16[16,160,256]{2,1,0:T(8,128)(2,1)}), bf16[16,160,256]{2,1,0:T(8,128)(2,1)S(1)}, u32[]{:S(2)}, u32[]{:S(2)}) async-start(bf16[16,160,256]{2,1,0:T(8,128)(2,1)} %get-tuple-element.116), calls=%async_computation | async-start | bytes 2621440 | tf_op jit(solution)/shard_map/all_to_all | solution.py:533
  17.9 3.4 %shadow_chunk.9 = (f32[2,128,640]{2,1,0:T(8,128)S(1)}, bf16[2,128,640]{2,1,0:T(8,128)(2,1)S(1)}) custom-call(s32[1]{0:T(128)} %bitcast.place_ref, bf16[128,1280]{1,0:T(8,128)(2,1)S(1)} %get-tuple-element.105.line_ref, bf16[1280,10240]{1,0:T(8,128)(2,1)} %ptdf_ref.9), custom_call_target="tpu_custom_call" | custom-call | flops 2516582400 | bytes 6553600 | tf_op jit(solution)/shard_map/shadow_chunk/pallas_call | solution.py:345
  23.4 3.4 %shadow_chunk.11 = (f32[2,128,640]{2,1,0:T(8,128)S(1)}, bf16[2,128,640]{2,1,0:T(8,128)(2,1)S(1)}) custom-call(s32[1]{0:T(128)} %bitcast.place_ref, bf16[128,1280]{1,0:T(8,128)(2,1)S(1)} %get-tuple-element.105.line_ref, bf16[1280,10240]{1,0:T(8,128)(2,1)} %ptdf_ref.9), custom_call_target="tpu_custom_call" | custom-call | flops 2516582400 | bytes 6553600 | tf_op jit(solution)/shard_map/shadow_chunk/pallas_call | solution.py:345
  27.0 15.5 %collective-permute-done.3 = bf16[128,640]{1,0:T(8,128)(2,1)S(1)} collective-permute-done((bf16[128,640]{1,0:T(8,128)(2,1)S(1)}, bf16[128,640]{1,0:T(8,128)(2,1)S(1)}, u32[]{:S(2)}, u32[]{:S(2)}) %collective-permute-start.3) | collective-permute-done | bytes 163872 | tf_op jit(solution)/shard_map/ppermute | solution.py:455
  42.5 3.4 %shadow_chunk.10 = (f32[2,128,640]{2,1,0:T(8,128)S(1)}, bf16[2,128,640]{2,1,0:T(8,128)(2,1)S(1)}) custom-call(s32[1]{0:T(128)} %bitcast.place_ref, bf16[128,1280]{1,0:T(8,128)(2,1)S(1)} %get-tuple-element.105.line_ref, bf16[1280,10240]{1,0:T(8,128)(2,1)} %ptdf_ref.9), custom_call_target="tpu_custom_call" | custom-call | flops 2516582400 | bytes 6553600 | tf_op jit(solution)/shard_map/shadow_chunk/pallas_call | solution.py:345
  47.8 4.9 %collective-permute-done.7 = bf16[128,640]{1,0:T(8,128)(2,1)S(1)} collective-permute-done((bf16[128,640]{1,0:T(8,128)(2,1)S(1)}, bf16[128,640]{1,0:T(8,128)(2,1)S(1)}, u32[]{:S(2)}, u32[]{:S(2)}) %collective-permute-start.7) | collective-permute-done | bytes 163872 | tf_op jit(solution)/shard_map/ppermute | solution.py:455
  54.9 4.5 %collective-permute-start.10 = (bf16[128,640]{1,0:T(8,128)(2,1)S(1)}, bf16[128,640]{1,0:T(8,128)(2,1)S(1)}, u32[]{:S(2)}, u32[]{:S(2)}) collective-permute-start(bf16[128,640]{1,0:T(8,128)(2,1)S(1)} %fusion.5), channel_id=1, source_target_pairs={{0,8},{1,9},{2,10},{3,11},{4,12},{5,13},{6,14},{7,15},{8,0},{9,1},... | collective-permute-start | bytes 491528 | tf_op jit(solution)/shard_map/ppermute | solution.py:455
  59.4 2.6 %collective-permute-done.8 = bf16[128,640]{1,0:T(8,128)(2,1)S(1)} collective-permute-done((bf16[128,640]{1,0:T(8,128)(2,1)S(1)}, bf16[128,640]{1,0:T(8,128)(2,1)S(1)}, u32[]{:S(2)}, u32[]{:S(2)}) %collective-permute-start.8) | collective-permute-done | bytes 163872 | tf_op jit(solution)/shard_map/ppermute | solution.py:455
  62.1 2.6 %collective-permute-start.9 = (bf16[128,640]{1,0:T(8,128)(2,1)S(1)}, bf16[128,640]{1,0:T(8,128)(2,1)S(1)}, u32[]{:S(2)}, u32[]{:S(2)}) collective-permute-start(bf16[128,640]{1,0:T(8,128)(2,1)S(1)} %fusion.6), channel_id=1, source_target_pairs={{0,4},{1,5},{2,6},{3,7},{4,0},{5,1},{6,2},{7,3},{8,12},{9,13},{10,... | collective-permute-start | bytes 491528 | tf_op jit(solution)/shard_map/ppermute | solution.py:455
  66.5 3.4 %collective-permute-done.9.refs_1_ = bf16[128,640]{1,0:T(8,128)(2,1)S(1)} collective-permute-done((bf16[128,640]{1,0:T(8,128)(2,1)S(1)}, bf16[128,640]{1,0:T(8,128)(2,1)S(1)}, u32[]{:S(2)}, u32[]{:S(2)}) %collective-permute-start.9) | collective-permute-done | bytes 163872 | tf_op jit(solution)/shard_map/ppermute | solution.py:455
  69.9 8.5 %update_generators.2 = (f32[16,144,128]{2,1,0:T(8,128)S(1)}, bf16[656,128]{1,0:T(8,128)(2,1)S(1)}, bf16[1280,2560]{1,0:T(8,128)(2,1)S(1)}, bf16[1280,2560]{1,0:T(8,128)(2,1)S(1)}) custom-call(s32[1]{0:T(128)} %bitcast.place_ref, f32[128,640]{1,0:T(8,128)S(1)} %bitcast_add_fusion.6.refs_0_, bf16[128,640]{1,0:T(8,128)(2,1)S(1)} %collective-permute-done.9.refs_1_, ...), custom_call_target="tpu_custom_call" | custom-call | flops 1509949440 | bytes 4194304 | tf_op jit(solution)/shard_map/update_generators/pallas_call | solution.py:276
  82.4 5.4 %load_chunks.1 = (s32[1]{0:T(128)}, bf16[1280,2560]{1,0:T(8,128)(2,1)S(1)}, bf16[1280,2560]{1,0:T(8,128)(2,1)S(1)}) custom-call(s32[1]{0:T(128)} %bitcast.place_ref, bf16[1280,10240]{1,0:T(8,128)(2,1)} %ptdf_ref.9), custom_call_target="tpu_custom_call" | custom-call | bytes 13107200 | tf_op jit(solution)/shard_map/load_chunks/pallas_call | solution.py:386
  99.2 2.4 %flow_chunk.9 = (f32[1280,128]{1,0:T(8,128)S(1)}, f32[1,128]{1,0:T(1,128)S(1)}) custom-call(bf16[1280,2560]{1,0:T(8,128)(2,1)S(1)} %get-tuple-element.130.ptdf_ref, bf16[656,128]{1,0:T(8,128)(2,1)S(1)} %collective-permute-done.12.b0, bf16[656,128]{1,0:T(8,128)(2,1)S(1)} %collective-permute-done.20.b1, bf16[656,128]{1,0:T(8,128)(2,1)S(1)} %collective-permute-done.16.b2, ...), custom_call_target="tpu_custom_call" | custom-call | flops 2516582400 | bytes 6553600 | tf_op jit(solution)/shard_map/flow_chunk/pallas_call | solution.py:443
  101.6 3.3 %collective-permute-done.19.b2 = bf16[656,128]{1,0:T(8,128)(2,1)S(1)} collective-permute-done((bf16[656,128]{1,0:T(8,128)(2,1)S(1)}, bf16[656,128]{1,0:T(8,128)(2,1)S(1)}, u32[]{:S(2)}, u32[]{:S(2)}) %collective-permute-start.19) | collective-permute-done | bytes 167968 | tf_op jit(solution)/shard_map/ppermute | solution.py:455
  104.9 2.4 %flow_chunk.10 = (f32[1280,128]{1,0:T(8,128)S(1)}, f32[1,128]{1,0:T(1,128)S(1)}) custom-call(bf16[1280,2560]{1,0:T(8,128)(2,1)S(1)} %get-tuple-element.119.ptdf_ref, bf16[656,128]{1,0:T(8,128)(2,1)S(1)} %collective-permute-done.13.b0, bf16[656,128]{1,0:T(8,128)(2,1)S(1)} %collective-permute-done.23.b1, bf16[656,128]{1,0:T(8,128)(2,1)S(1)} %collective-permute-done.24.b2, ...), custom_call_target="tpu_custom_call" | custom-call | flops 2516582400 | bytes 6553600 | tf_op jit(solution)/shard_map/flow_chunk/pallas_call | solution.py:443
  107.4 2.8 %flow_chunk.11 = (f32[1280,128]{1,0:T(8,128)S(1)}, bf16[128,1280]{1,0:T(8,128)(2,1)S(1)}, f32[1,128]{1,0:T(1,128)S(1)}) custom-call(bf16[1280,2560]{1,0:T(8,128)(2,1)S(1)} %get-tuple-element.122.ptdf_ref, bf16[656,128]{1,0:T(8,128)(2,1)S(1)} %collective-permute-done.15.b0, bf16[656,128]{1,0:T(8,128)(2,1)S(1)} %collective-permute-done.18.b1, ...), custom_call_target="tpu_custom_call" | custom-call | flops 2516582400 | bytes 6553600 | tf_op jit(solution)/shard_map/flow_chunk/pallas_call | solution.py:443
  118.7 2.9 %collective-permute-done.28 = bf16[128,640]{1,0:T(8,128)(2,1)S(1)} collective-permute-done((bf16[128,640]{1,0:T(8,128)(2,1)S(1)}, bf16[128,640]{1,0:T(8,128)(2,1)S(1)}, u32[]{:S(2)}, u32[]{:S(2)}) %collective-permute-start.28) | collective-permute-done | bytes 163872 | tf_op jit(solution)/shard_map/ppermute | solution.py:455
  127.7 2.6 %collective-permute-done.34 = bf16[128,640]{1,0:T(8,128)(2,1)S(1)} collective-permute-done((bf16[128,640]{1,0:T(8,128)(2,1)S(1)}, bf16[128,640]{1,0:T(8,128)(2,1)S(1)}, u32[]{:S(2)}, u32[]{:S(2)}) %collective-permute-start.34) | collective-permute-done | bytes 163872 | tf_op jit(solution)/shard_map/ppermute | solution.py:455
  130.4 2.8 %collective-permute-start.36 = (bf16[128,640]{1,0:T(8,128)(2,1)S(1)}, bf16[128,640]{1,0:T(8,128)(2,1)S(1)}, u32[]{:S(2)}, u32[]{:S(2)}) collective-permute-start(bf16[128,640]{1,0:T(8,128)(2,1)S(1)} %fusion.1), channel_id=1, source_target_pairs={{0,8},{1,9},{2,10},{3,11},{4,12},{5,13},{6,14},{7,15},{8,0},{9,1},... | collective-permute-start | bytes 491528 | tf_op jit(solution)/shard_map/ppermute | solution.py:455
  135.4 5.5 %collective-permute-done.35.refs_1_ = bf16[128,640]{1,0:T(8,128)(2,1)S(1)} collective-permute-done((bf16[128,640]{1,0:T(8,128)(2,1)S(1)}, bf16[128,640]{1,0:T(8,128)(2,1)S(1)}, u32[]{:S(2)}, u32[]{:S(2)}) %collective-permute-start.35) | collective-permute-done | bytes 163872 | tf_op jit(solution)/shard_map/ppermute | solution.py:455
  141.0 4.8 %update_generators.3 = (bf16[16,144,128]{2,1,0:T(8,128)(2,1)S(1)}, bf16[656,128]{1,0:T(8,128)(2,1)S(1)}) custom-call(s32[1]{0:T(128)} %get-tuple-element.121.place_ref, f32[128,640]{1,0:T(8,128)S(1)} %bitcast_add_fusion.2.refs_0_, bf16[128,640]{1,0:T(8,128)(2,1)S(1)} %collective-permute-done.35.refs_1_, ...), custom_call_target="tpu_custom_call" | custom-call | flops 1509949440 | bytes 4194304 | tf_op jit(solution)/shard_map/update_generators/pallas_call | solution.py:276
  147.4 2.8 %collective-permute-start.38 = (bf16[656,128]{1,0:T(8,128)(2,1)S(1)}, bf16[656,128]{1,0:T(8,128)(2,1)S(1)}, u32[]{:S(2)}, u32[]{:S(2)}) collective-permute-start(bf16[656,128]{1,0:T(8,128)(2,1)S(1)} %get-tuple-element.158.b0), channel_id=1, source_target_pairs={{0,8},{1,9},{2,10},{3,11},{4,12},{5,13},{6,14},{7,15},{8,0},{9,1},... | collective-permute-start | bytes 503816 | tf_op jit(solution)/shard_map/ppermute | solution.py:455
  152.3 8.3 %collective-permute-done.41 = bf16[4,144,128]{2,1,0:T(8,128)(2,1)S(1)} collective-permute-done((bf16[4,144,128]{2,1,0:T(8,128)(2,1)S(1)}, bf16[4,144,128]{2,1,0:T(8,128)(2,1)S(1)}, u32[]{:S(2)}, u32[]{:S(2)}) %collective-permute-start.41) | collective-permute-done | bytes 147488 | tf_op jit(solution)/shard_map/ppermute | solution.py:455
  169.7 3.4 %collective-permute-done.47.b2 = bf16[656,128]{1,0:T(8,128)(2,1)S(1)} collective-permute-done((bf16[656,128]{1,0:T(8,128)(2,1)S(1)}, bf16[656,128]{1,0:T(8,128)(2,1)S(1)}, u32[]{:S(2)}, u32[]{:S(2)}) %collective-permute-start.47) | collective-permute-done | bytes 167968 | tf_op jit(solution)/shard_map/ppermute | solution.py:455
  174.6 2.4 %flow_chunk.13 = (f32[1280,128]{1,0:T(8,128)S(1)}, f32[1,128]{1,0:T(1,128)S(1)}) custom-call(bf16[1280,2560]{1,0:T(8,128)(2,1)S(1)} %get-tuple-element.130.ptdf_ref, bf16[656,128]{1,0:T(8,128)(2,1)S(1)} %collective-permute-done.37.b0, bf16[656,128]{1,0:T(8,128)(2,1)S(1)} %collective-permute-done.51.b1, bf16[656,128]{1,0:T(8,128)(2,1)S(1)} %collective-permute-done.47.b2, ...), custom_call_target="tpu_custom_call" | custom-call | flops 2516582400 | bytes 6553600 | tf_op jit(solution)/shard_map/flow_chunk/pallas_call | solution.py:443
  177.1 3.0 %collective-permute-done.50.b2 = bf16[656,128]{1,0:T(8,128)(2,1)S(1)} collective-permute-done((bf16[656,128]{1,0:T(8,128)(2,1)S(1)}, bf16[656,128]{1,0:T(8,128)(2,1)S(1)}, u32[]{:S(2)}, u32[]{:S(2)}) %collective-permute-start.50) | collective-permute-done | bytes 167968 | tf_op jit(solution)/shard_map/ppermute | solution.py:455
  180.1 3.7 %collective-permute-start.55 = (bf16[4,144,128]{2,1,0:T(8,128)(2,1)S(1)}, bf16[4,144,128]{2,1,0:T(8,128)(2,1)S(1)}, u32[]{:S(2)}, u32[]{:S(2)}) collective-permute-start(bf16[4,144,128]{2,1,0:T(8,128)(2,1)S(1)} %get-tuple-element.185), channel_id=1, source_target_pairs={{0,12},{1,13},{2,14},{3,15},{4,8},{5,9},{6,10},{7,11},{8,4},{9,5},... | collective-permute-start | bytes 442376 | tf_op jit(solution)/shard_map/ppermute | solution.py:455
  184.3 2.4 %flow_chunk.14 = (f32[1280,128]{1,0:T(8,128)S(1)}, f32[1,128]{1,0:T(1,128)S(1)}) custom-call(bf16[1280,2560]{1,0:T(8,128)(2,1)S(1)} %get-tuple-element.119.ptdf_ref, bf16[656,128]{1,0:T(8,128)(2,1)S(1)} %collective-permute-done.38.b0, bf16[656,128]{1,0:T(8,128)(2,1)S(1)} %collective-permute-done.43.b1, bf16[656,128]{1,0:T(8,128)(2,1)S(1)} %collective-permute-done.44.b2, ...), custom_call_target="tpu_custom_call" | custom-call | flops 2516582400 | bytes 6553600 | tf_op jit(solution)/shard_map/flow_chunk/pallas_call | solution.py:443
  189.6 3.4 %flow_chunk.15 = (f32[1280,128]{1,0:T(8,128)}, bf16[128,1280]{1,0:T(8,128)(2,1)}, f32[1,128]{1,0:T(1,128)S(1)}) custom-call(bf16[1280,2560]{1,0:T(8,128)(2,1)S(1)} %get-tuple-element.122.ptdf_ref, bf16[656,128]{1,0:T(8,128)(2,1)S(1)} %collective-permute-done.46.b0, bf16[656,128]{1,0:T(8,128)(2,1)S(1)} %collective-permute-done.56.b1, ...), custom_call_target="tpu_custom_call" | custom-call | flops 2516582400 | bytes 6553600 | tf_op jit(solution)/shard_map/flow_chunk/pallas_call | solution.py:443
  (149 shorter events, 60.9 us)
Async XLA Ops:
  9.2 7.7 %collective-permute-start.1 = (bf16[128,640]{1,0:T(8,128)(2,1)}, bf16[128,640]{1,0:T(8,128)(2,1)}, u32[]{:S(2)}, u32[]{:S(2)}) collective-permute-start(bf16[128,640]{1,0:T(8,128)(2,1)} %fusion.8), channel_id=1, source_target_pairs={{0,2},{1,3},{2,0},{3,1},{4,6},{5,7},{6,4},{7,5},{8,10},{9,11},{10,... | collective-permute-start | bytes 491528 | tf_op jit(solution)/shard_map/ppermute | solution.py:455
  11.8 58.1 %all-to-all-start = ((bf16[16,160,256]{2,1,0:T(8,128)(2,1)}), bf16[16,160,256]{2,1,0:T(8,128)(2,1)S(1)}, u32[]{:S(2)}, u32[]{:S(2)}) async-start(bf16[16,160,256]{2,1,0:T(8,128)(2,1)} %get-tuple-element.116), calls=%async_computation | async-start | bytes 2621440 | tf_op jit(solution)/shard_map/all_to_all | solution.py:533
  21.7 20.8 %collective-permute-start.3 = (bf16[128,640]{1,0:T(8,128)(2,1)S(1)}, bf16[128,640]{1,0:T(8,128)(2,1)S(1)}, u32[]{:S(2)}, u32[]{:S(2)}) collective-permute-start(bf16[128,640]{1,0:T(8,128)(2,1)S(1)} %fusion.7), channel_id=1, source_target_pairs={{0,4},{1,5},{2,6},{3,7},{4,0},{5,1},{6,2},{7,3},{8,12},{9,13},{10,... | collective-permute-start | bytes 491528 | tf_op jit(solution)/shard_map/ppermute | solution.py:455
  26.8 21.0 %collective-permute-start.6 = (bf16[2,128,640]{2,1,0:T(8,128)(2,1)S(1)}, bf16[2,128,640]{2,1,0:T(8,128)(2,1)S(1)}, u32[]{:S(2)}, u32[]{:S(2)}) collective-permute-start(bf16[2,128,640]{2,1,0:T(8,128)(2,1)S(1)} %get-tuple-element.109), channel_id=1, source_target_pairs={{0,1},{1,0},{2,3},{3,2},{4,5},{5,4},{6,7},{7,6},{8,9},{9,8},{10,11... | collective-permute-start | bytes 983048 | tf_op jit(solution)/shard_map/ppermute | solution.py:455
  52.7 12.0 %collective-permute-start.5 = (bf16[128,640]{1,0:T(8,128)(2,1)S(1)}, bf16[128,640]{1,0:T(8,128)(2,1)S(1)}, u32[]{:S(2)}, u32[]{:S(2)}) collective-permute-start(bf16[128,640]{1,0:T(8,128)(2,1)S(1)} %get-tuple-element.193), channel_id=1, source_target_pairs={{0,2},{1,3},{2,0},{3,1},{4,6},{5,7},{6,4},{7,5},{8,10},{9,11},{10,... | collective-permute-start | bytes 491528 | tf_op jit(solution)/shard_map/ppermute | solution.py:455
  54.5 7.6 %collective-permute-start.8 = (bf16[128,640]{1,0:T(8,128)(2,1)S(1)}, bf16[128,640]{1,0:T(8,128)(2,1)S(1)}, u32[]{:S(2)}, u32[]{:S(2)}) collective-permute-start(bf16[128,640]{1,0:T(8,128)(2,1)S(1)} %get-tuple-element.194), channel_id=1, source_target_pairs={{0,2},{1,3},{2,0},{3,1},{4,6},{5,7},{6,4},{7,5},{8,10},{9,11},{10,... | collective-permute-start | bytes 491528 | tf_op jit(solution)/shard_map/ppermute | solution.py:455
  54.9 11.6 %collective-permute-start.10 = (bf16[128,640]{1,0:T(8,128)(2,1)S(1)}, bf16[128,640]{1,0:T(8,128)(2,1)S(1)}, u32[]{:S(2)}, u32[]{:S(2)}) collective-permute-start(bf16[128,640]{1,0:T(8,128)(2,1)S(1)} %fusion.5), channel_id=1, source_target_pairs={{0,8},{1,9},{2,10},{3,11},{4,12},{5,13},{6,14},{7,15},{8,0},{9,1},... | collective-permute-start | bytes 491528 | tf_op jit(solution)/shard_map/ppermute | solution.py:455
  62.1 7.8 %collective-permute-start.9 = (bf16[128,640]{1,0:T(8,128)(2,1)S(1)}, bf16[128,640]{1,0:T(8,128)(2,1)S(1)}, u32[]{:S(2)}, u32[]{:S(2)}) collective-permute-start(bf16[128,640]{1,0:T(8,128)(2,1)S(1)} %fusion.6), channel_id=1, source_target_pairs={{0,4},{1,5},{2,6},{3,7},{4,0},{5,1},{6,2},{7,3},{8,12},{9,13},{10,... | collective-permute-start | bytes 491528 | tf_op jit(solution)/shard_map/ppermute | solution.py:455
  78.6 10.3 %collective-permute-start.12 = (bf16[656,128]{1,0:T(8,128)(2,1)S(1)}, bf16[656,128]{1,0:T(8,128)(2,1)S(1)}, u32[]{:S(2)}, u32[]{:S(2)}) collective-permute-start(bf16[656,128]{1,0:T(8,128)(2,1)S(1)} %get-tuple-element.117.b0), channel_id=1, source_target_pairs={{0,4},{1,5},{2,6},{3,7},{4,0},{5,1},{6,2},{7,3},{8,12},{9,13},{10,... | collective-permute-start | bytes 503816 | tf_op jit(solution)/shard_map/ppermute | solution.py:455
  78.7 10.1 %collective-permute-start.13 = (bf16[656,128]{1,0:T(8,128)(2,1)S(1)}, bf16[656,128]{1,0:T(8,128)(2,1)S(1)}, u32[]{:S(2)}, u32[]{:S(2)}) collective-permute-start(bf16[656,128]{1,0:T(8,128)(2,1)S(1)} %get-tuple-element.117.b0), channel_id=1, source_target_pairs={{0,8},{1,9},{2,10},{3,11},{4,12},{5,13},{6,14},{7,15},{8,0},{9,1},... | collective-permute-start | bytes 503816 | tf_op jit(solution)/shard_map/ppermute | solution.py:455
  80.9 7.9 %collective-permute-start.14 = (bf16[656,128]{1,0:T(8,128)(2,1)S(1)}, bf16[656,128]{1,0:T(8,128)(2,1)S(1)}, u32[]{:S(2)}, u32[]{:S(2)}) collective-permute-start(bf16[656,128]{1,0:T(8,128)(2,1)S(1)} %get-tuple-element.117.b0), channel_id=1, source_target_pairs={{0,2},{1,3},{2,0},{3,1},{4,6},{5,7},{6,4},{7,5},{8,10},{9,11},{10,... | collective-permute-start | bytes 503816 | tf_op jit(solution)/shard_map/ppermute | solution.py:455
  88.9 8.5 %collective-permute-start.16 = (bf16[656,128]{1,0:T(8,128)(2,1)S(1)}, bf16[656,128]{1,0:T(8,128)(2,1)S(1)}, u32[]{:S(2)}, u32[]{:S(2)}) collective-permute-start(bf16[656,128]{1,0:T(8,128)(2,1)S(1)} %collective-permute-done.12.b0), channel_id=1, source_target_pairs={{0,2},{1,3},{2,0},{3,1},{4,6},{5,7},{6,4},{7,5},{8,10},{9,11},{10,... | collective-permute-start | bytes 503816 | tf_op jit(solution)/shard_map/ppermute | solution.py:455
  90.4 7.8 %collective-permute-start.20 = (bf16[656,128]{1,0:T(8,128)(2,1)S(1)}, bf16[656,128]{1,0:T(8,128)(2,1)S(1)}, u32[]{:S(2)}, u32[]{:S(2)}) collective-permute-start(bf16[656,128]{1,0:T(8,128)(2,1)S(1)} %collective-permute-done.12.b0), channel_id=1, source_target_pairs={{0,1},{1,0},{2,3},{3,2},{4,5},{5,4},{6,7},{7,6},{8,9},{9,8},{10,11... | collective-permute-start | bytes 503816 | tf_op jit(solution)/shard_map/ppermute | solution.py:455
  98.2 9.2 %collective-permute-start.18 = (bf16[656,128]{1,0:T(8,128)(2,1)S(1)}, bf16[656,128]{1,0:T(8,128)(2,1)S(1)}, u32[]{:S(2)}, u32[]{:S(2)}) collective-permute-start(bf16[656,128]{1,0:T(8,128)(2,1)S(1)} %collective-permute-done.15.b0), channel_id=1, source_target_pairs={{0,1},{1,0},{2,3},{3,2},{4,5},{5,4},{6,7},{7,6},{8,9},{9,8},{10,11... | collective-permute-start | bytes 503816 | tf_op jit(solution)/shard_map/ppermute | solution.py:455
  116.2 9.3 %collective-permute-start.32 = (bf16[128,640]{1,0:T(8,128)(2,1)S(1)}, bf16[128,640]{1,0:T(8,128)(2,1)S(1)}, u32[]{:S(2)}, u32[]{:S(2)}) collective-permute-start(bf16[128,640]{1,0:T(8,128)(2,1)S(1)} %fusion.13), channel_id=1, source_target_pairs={{0,2},{1,3},{2,0},{3,1},{4,6},{5,7},{6,4},{7,5},{8,10},{9,11},{10,... | collective-permute-start | bytes 491528 | tf_op jit(solution)/shard_map/ppermute | solution.py:455
  125.5 7.6 %collective-permute-start.33 = (bf16[128,640]{1,0:T(8,128)(2,1)S(1)}, bf16[128,640]{1,0:T(8,128)(2,1)S(1)}, u32[]{:S(2)}, u32[]{:S(2)}) collective-permute-start(bf16[128,640]{1,0:T(8,128)(2,1)S(1)} %fusion.15), channel_id=1, source_target_pairs={{0,2},{1,3},{2,0},{3,1},{4,6},{5,7},{6,4},{7,5},{8,10},{9,11},{10,... | collective-permute-start | bytes 491528 | tf_op jit(solution)/shard_map/ppermute | solution.py:455
  126.2 9.2 %collective-permute-start.30 = (bf16[128,640]{1,0:T(8,128)(2,1)S(1)}, bf16[128,640]{1,0:T(8,128)(2,1)S(1)}, u32[]{:S(2)}, u32[]{:S(2)}) collective-permute-start(bf16[128,640]{1,0:T(8,128)(2,1)S(1)} %fusion.14), channel_id=1, source_target_pairs={{0,2},{1,3},{2,0},{3,1},{4,6},{5,7},{6,4},{7,5},{8,10},{9,11},{10,... | collective-permute-start | bytes 491528 | tf_op jit(solution)/shard_map/ppermute | solution.py:455
  130.4 10.6 %collective-permute-start.36 = (bf16[128,640]{1,0:T(8,128)(2,1)S(1)}, bf16[128,640]{1,0:T(8,128)(2,1)S(1)}, u32[]{:S(2)}, u32[]{:S(2)}) collective-permute-start(bf16[128,640]{1,0:T(8,128)(2,1)S(1)} %fusion.1), channel_id=1, source_target_pairs={{0,8},{1,9},{2,10},{3,11},{4,12},{5,13},{6,14},{7,15},{8,0},{9,1},... | collective-permute-start | bytes 491528 | tf_op jit(solution)/shard_map/ppermute | solution.py:455
  133.2 7.8 %collective-permute-start.35 = (bf16[128,640]{1,0:T(8,128)(2,1)S(1)}, bf16[128,640]{1,0:T(8,128)(2,1)S(1)}, u32[]{:S(2)}, u32[]{:S(2)}) collective-permute-start(bf16[128,640]{1,0:T(8,128)(2,1)S(1)} %fusion.2), channel_id=1, source_target_pairs={{0,4},{1,5},{2,6},{3,7},{4,0},{5,1},{6,2},{7,3},{8,12},{9,13},{10,... | collective-permute-start | bytes 491528 | tf_op jit(solution)/shard_map/ppermute | solution.py:455
  145.9 15.6 %collective-permute-start.37 = (bf16[656,128]{1,0:T(8,128)(2,1)S(1)}, bf16[656,128]{1,0:T(8,128)(2,1)S(1)}, u32[]{:S(2)}, u32[]{:S(2)}) collective-permute-start(bf16[656,128]{1,0:T(8,128)(2,1)S(1)} %get-tuple-element.158.b0), channel_id=1, source_target_pairs={{0,4},{1,5},{2,6},{3,7},{4,0},{5,1},{6,2},{7,3},{8,12},{9,13},{10,... | collective-permute-start | bytes 503816 | tf_op jit(solution)/shard_map/ppermute | solution.py:455
  147.4 14.1 %collective-permute-start.38 = (bf16[656,128]{1,0:T(8,128)(2,1)S(1)}, bf16[656,128]{1,0:T(8,128)(2,1)S(1)}, u32[]{:S(2)}, u32[]{:S(2)}) collective-permute-start(bf16[656,128]{1,0:T(8,128)(2,1)S(1)} %get-tuple-element.158.b0), channel_id=1, source_target_pairs={{0,8},{1,9},{2,10},{3,11},{4,12},{5,13},{6,14},{7,15},{8,0},{9,1},... | collective-permute-start | bytes 503816 | tf_op jit(solution)/shard_map/ppermute | solution.py:455
  150.2 11.3 %collective-permute-start.39 = (bf16[656,128]{1,0:T(8,128)(2,1)S(1)}, bf16[656,128]{1,0:T(8,128)(2,1)S(1)}, u32[]{:S(2)}, u32[]{:S(2)}) collective-permute-start(bf16[656,128]{1,0:T(8,128)(2,1)S(1)} %get-tuple-element.158.b0), channel_id=1, source_target_pairs={{0,2},{1,3},{2,0},{3,1},{4,6},{5,7},{6,4},{7,5},{8,10},{9,11},{10,... | collective-permute-start | bytes 503816 | tf_op jit(solution)/shard_map/ppermute | solution.py:455
  150.8 9.8 %collective-permute-start.41 = (bf16[4,144,128]{2,1,0:T(8,128)(2,1)S(1)}, bf16[4,144,128]{2,1,0:T(8,128)(2,1)S(1)}, u32[]{:S(2)}, u32[]{:S(2)}) collective-permute-start(bf16[4,144,128]{2,1,0:T(8,128)(2,1)S(1)} %get-tuple-element.190), channel_id=1, source_target_pairs={{0,2},{1,3},{2,0},{3,1},{4,6},{5,7},{6,4},{7,5},{8,10},{9,11},{10,... | collective-permute-start | bytes 442376 | tf_op jit(solution)/shard_map/ppermute | solution.py:455
  152.3 9.3 %collective-permute-start.42 = (bf16[4,144,128]{2,1,0:T(8,128)(2,1)S(1)}, bf16[4,144,128]{2,1,0:T(8,128)(2,1)S(1)}, u32[]{:S(2)}, u32[]{:S(2)}) collective-permute-start(bf16[4,144,128]{2,1,0:T(8,128)(2,1)S(1)} %get-tuple-element.192), channel_id=1, source_target_pairs={{0,3},{1,2},{2,1},{3,0},{4,7},{5,6},{6,5},{7,4},{8,11},{9,10},{10,... | collective-permute-start | bytes 442376 | tf_op jit(solution)/shard_map/ppermute | solution.py:455
  162.7 21.0 %collective-permute-start.43 = (bf16[656,128]{1,0:T(8,128)(2,1)S(1)}, bf16[656,128]{1,0:T(8,128)(2,1)S(1)}, u32[]{:S(2)}, u32[]{:S(2)}) collective-permute-start(bf16[656,128]{1,0:T(8,128)(2,1)S(1)} %collective-permute-done.38.b0), channel_id=1, source_target_pairs={{0,1},{1,0},{2,3},{3,2},{4,5},{5,4},{6,7},{7,6},{8,9},{9,8},{10,11... | collective-permute-start | bytes 503816 | tf_op jit(solution)/shard_map/ppermute | solution.py:455
  162.8 10.7 %collective-permute-start.44 = (bf16[656,128]{1,0:T(8,128)(2,1)S(1)}, bf16[656,128]{1,0:T(8,128)(2,1)S(1)}, u32[]{:S(2)}, u32[]{:S(2)}) collective-permute-start(bf16[656,128]{1,0:T(8,128)(2,1)S(1)} %collective-permute-done.38.b0), channel_id=1, source_target_pairs={{0,2},{1,3},{2,0},{3,1},{4,6},{5,7},{6,4},{7,5},{8,10},{9,11},{10,... | collective-permute-start | bytes 503816 | tf_op jit(solution)/shard_map/ppermute | solution.py:455
  163.7 9.4 %collective-permute-start.47 = (bf16[656,128]{1,0:T(8,128)(2,1)S(1)}, bf16[656,128]{1,0:T(8,128)(2,1)S(1)}, u32[]{:S(2)}, u32[]{:S(2)}) collective-permute-start(bf16[656,128]{1,0:T(8,128)(2,1)S(1)} %collective-permute-done.37.b0), channel_id=1, source_target_pairs={{0,2},{1,3},{2,0},{3,1},{4,6},{5,7},{6,4},{7,5},{8,10},{9,11},{10,... | collective-permute-start | bytes 503816 | tf_op jit(solution)/shard_map/ppermute | solution.py:455
  165.3 8.6 %collective-permute-start.51 = (bf16[656,128]{1,0:T(8,128)(2,1)S(1)}, bf16[656,128]{1,0:T(8,128)(2,1)S(1)}, u32[]{:S(2)}, u32[]{:S(2)}) collective-permute-start(bf16[656,128]{1,0:T(8,128)(2,1)S(1)} %collective-permute-done.37.b0), channel_id=1, source_target_pairs={{0,1},{1,0},{2,3},{3,2},{4,5},{5,4},{6,7},{7,6},{8,9},{9,8},{10,11... | collective-permute-start | bytes 503816 | tf_op jit(solution)/shard_map/ppermute | solution.py:455
  173.1 13.5 %collective-permute-start.53 = (bf16[4,144,128]{2,1,0:T(8,128)(2,1)S(1)}, bf16[4,144,128]{2,1,0:T(8,128)(2,1)S(1)}, u32[]{:S(2)}, u32[]{:S(2)}) collective-permute-start(bf16[4,144,128]{2,1,0:T(8,128)(2,1)S(1)} %get-tuple-element.187), channel_id=1, source_target_pairs={{0,4},{1,5},{2,6},{3,7},{4,0},{5,1},{6,2},{7,3},{8,12},{9,13},{10,... | collective-permute-start | bytes 442376 | tf_op jit(solution)/shard_map/ppermute | solution.py:455
  173.5 13.9 %collective-permute-start.54 = (bf16[4,144,128]{2,1,0:T(8,128)(2,1)S(1)}, bf16[4,144,128]{2,1,0:T(8,128)(2,1)S(1)}, u32[]{:S(2)}, u32[]{:S(2)}) collective-permute-start(bf16[4,144,128]{2,1,0:T(8,128)(2,1)S(1)} %get-tuple-element.186), channel_id=1, source_target_pairs={{0,8},{1,9},{2,10},{3,11},{4,12},{5,13},{6,14},{7,15},{8,0},{9,1},... | collective-permute-start | bytes 442376 | tf_op jit(solution)/shard_map/ppermute | solution.py:455
  174.5 9.3 %collective-permute-start.45 = (bf16[656,128]{1,0:T(8,128)(2,1)S(1)}, bf16[656,128]{1,0:T(8,128)(2,1)S(1)}, u32[]{:S(2)}, u32[]{:S(2)}) collective-permute-start(bf16[656,128]{1,0:T(8,128)(2,1)S(1)} %collective-permute-done.44.b2), channel_id=1, source_target_pairs={{0,1},{1,0},{2,3},{3,2},{4,5},{5,4},{6,7},{7,6},{8,9},{9,8},{10,11... | collective-permute-start | bytes 503816 | tf_op jit(solution)/shard_map/ppermute | solution.py:455
  180.1 7.3 %collective-permute-start.55 = (bf16[4,144,128]{2,1,0:T(8,128)(2,1)S(1)}, bf16[4,144,128]{2,1,0:T(8,128)(2,1)S(1)}, u32[]{:S(2)}, u32[]{:S(2)}) collective-permute-start(bf16[4,144,128]{2,1,0:T(8,128)(2,1)S(1)} %get-tuple-element.185), channel_id=1, source_target_pairs={{0,12},{1,13},{2,14},{3,15},{4,8},{5,9},{6,10},{7,11},{8,4},{9,5},... | collective-permute-start | bytes 442376 | tf_op jit(solution)/shard_map/ppermute | solution.py:455
  (37 other events, 261.5 us)

commit v9 on v8

--- a/solution.py
+++ b/solution.py
@@ -14,7 +14,6 @@
 
 GROUP = 4
 LIMIT = 16 << 20
-COST = 3
 META = 16
 HBM_SPEC = pl.BlockSpec(memory_space=pltpu.MemorySpace.HBM)
 VMEM_SPEC = pl.BlockSpec(memory_space=pltpu.VMEM)
@@ -328,7 +327,7 @@
 
 
 def chunk_cost(hours, lines, buses):
-    return pl.CostEstimate(flops=COST * 8 * hours * lines * buses, bytes_accessed=8 * lines * buses, transcendentals=0)
+    return pl.CostEstimate(flops=hours * lines * buses, bytes_accessed=lines * buses, transcendentals=0)
 
 
 def shadow_chunk(chunk, stream, place, line, ptdf, buses):
@@ -390,7 +389,7 @@
         out_shape=tuple([jax.ShapeDtypeStruct((1,), jnp.int32)] + [pltpu.VMEM((lines, 4 * buses), BF16)] * count),
         scratch_shapes=[pltpu.SemaphoreType.DMA((count, 4))],
         compiler_params=pltpu.CompilerParams(vmem_limit_bytes=LIMIT),
-        cost_estimate=pl.CostEstimate(flops=0, bytes_accessed=8 * count * lines * buses, transcendentals=0),
+        cost_estimate=pl.CostEstimate(flops=0, bytes_accessed=lines * buses, transcendentals=0),
         name="load_chunks",
     )(place, in_hbm(ptdf))
     return token, held
@@ -540,8 +539,6 @@
             line_t, _ = lax.optimization_barrier((line_t, across(2)))
             if iteration:
                 line_t, _ = lax.optimization_barrier((line_t, settle(3)))
-            else:
-                line_t, parts[3] = lax.optimization_barrier((line_t, parts[3]))
             product(0, line_t)
             gots[1], crossed[2] = lax.optimization_barrier((gots[1], crossed[2]))
             parts[3], _, _ = lax.optimization_barrier((parts[3], across(1), across(0)))
@@ -561,45 +558,45 @@
         if staged:
             near, far, cross, far_cross = {0: block}, {}, {}, {}
 
-            def spread(chunk):
-                far[chunk] = swap(near[chunk], devices, 2)
-                cross[chunk] = swap(near[chunk], devices, 1)
-
-            def settle_far(chunk):
-                far_cross[chunk] = swap(far[chunk], devices, 1)
+            def to_core(*xs):
+                if len(xs) == 1:
+                    return [swap(xs[0], devices, 1)]
+                moved = swap(jnp.stack(xs), devices, 1)
+                return [moved[i] for i in range(len(xs))]
 
             def blocks(chunk):
                 return [near[chunk], cross[chunk], far[chunk], far_cross[chunk]]
 
             near[2] = swap(block, devices, 8)
             near[1] = swap(block, devices, 4)
-            spread(0)
+            far[0] = swap(block, devices, 2)
+            (cross[0],) = to_core(block)
             stage = [near[1], near[2], far[0]]
             if last:
                 home = held.reshape(4, 4, *held.shape[1:])
-                stage += [swap(home[:, rel], devices, rel) for rel in (1, 2, 3)]
+                side = [swap(home[:, rel], devices, rel) for rel in (1, 2, 3)]
             else:
                 cross[0], here = lax.optimization_barrier((cross[0], place))
                 place, (resident[2], resident[3]) = load_chunks((2, 3), here, ptdf, buses)
                 stage.append(place)
             near[1], near[2], far[0], *rest = lax.optimization_barrier(stage)
             near[3] = swap(near[2], devices, 4)
-            spread(1)
-            spread(2)
-            settle_far(0)
+            far[1] = swap(near[1], devices, 2)
+            far[2] = swap(near[2], devices, 2)
+            cross[1], cross[2], far_cross[0] = to_core(near[1], near[2], far[0])
+            acc, total = flow_chunk(resident[0], blocks(0), None, balance_row)
+            if not last:
+                (place,) = rest
+                side = []
+            near[3], far[1], far[2], acc, *side = lax.optimization_barrier((near[3], far[1], far[2], acc, *side))
+            far[3] = swap(near[3], devices, 2)
+            cross[3], far_cross[1], far_cross[2] = to_core(near[3], far[1], far[2])
             if last:
-                home = jnp.stack([home[:, 0], *rest], axis=1)
+                home = jnp.stack([home[:, 0], *side], axis=1)
                 back = [home[0]] + [swap(home[chunk], devices, 4 * chunk) for chunk in (1, 2, 3)]
-            else:
-                (place,) = rest
-            acc, total = flow_chunk(resident[0], blocks(0), None, balance_row)
-            near[3], far[1], acc = lax.optimization_barrier((near[3], far[1], acc))
-            spread(3)
-            settle_far(1)
             acc, total = flow_chunk(resident[1], blocks(1), acc, total)
-            settle_far(2)
             far[3], acc = lax.optimization_barrier((far[3], acc))
-            settle_far(3)
+            (far_cross[3],) = to_core(far[3])
             acc, total = flow_chunk(resident[2], blocks(2), acc, total)
             if last:
                 acc, *back = lax.optimization_barrier((acc, *back))

time: 194 us -> 193 us (level)
  starting transfers between devices: 56.6 us -> 52.8 us
  waiting for transfers between devices: 65.8 us -> 69.1 us
    ppermute x58 -> x50, starting transfers between devices: 51.6 us -> 45.7 us  [swap(): return lax.ppermute(x, 'bus', [(i, i ^ mask) for i in range(devices)])]
    ppermute x58 -> x50, waiting for transfers between devices: 65.8 us -> 69.1 us  [swap(): return lax.ppermute(x, 'bus', [(i, i ^ mask) for i in range(devices)])]
    all_to_all x1, starting transfers between devices: 4.98 us -> 7.05 us  [local(): lax.all_to_all(outgoing, 'bus', split_axis=0, concat_axis=0, tiled=True)]
  transfers between devices with their start and end apart: 59 -> 51, of which waited for: 22 -> 23; matrix products, arithmetic and copies ran while one was open for 1% -> 1% of each run, Pallas kernels for 21% -> 22%
where the time goes in v9:
time: 193 us
  waiting for transfers between devices  69.1 us (36%)
  Pallas kernels  66.6 us (35%)
  starting transfers between devices  52.8 us (27%)
  other arithmetic  2.27 us (1%)
    ppermute x50, waiting for transfers between devices, swap(): return lax.ppermute(x, 'bus', [(i, i ^ mask) for i in range(devices)])  69.1 us
    ppermute x50, starting transfers between devices, swap(): return lax.ppermute(x, 'bus', [(i, i ^ mask) for i in range(devices)])  45.7 us
    pallas_call x8, Pallas kernels, shadow_chunk(): pl.pallas_call(functools.partial(shadow_kernel, chunk, stream, turn), in_...  21.4 us
    pallas_call x8, Pallas kernels, flow_chunk(): pl.pallas_call(functools.partial(flow_kernel, start, end), in_specs=[VMEM...  20.7 us
    pallas_call x2, Pallas kernels, update(): pl.pallas_call(functools.partial(update_kernel, cap, devices, first, last...  13.4 us
    all_to_all x1, starting transfers between devices, local(): lax.all_to_all(outgoing, 'bus', split_axis=0, concat_axis=0, tiled=True)  7.05 us
    pallas_call x1, Pallas kernels, load_chunks(): pl.pallas_call(functools.partial(load_kernel, chunks), in_specs=[SMEM_SPE...  5.44 us
  transfers between devices with their start and end apart: 51, of which 23 were waited for; matrix products, arithmetic and copies ran while one was open for 1% of the time, Pallas kernels for 22%

profile of v9, /device:TPU:0, one launch (start us, length us, event | category | flops | bytes accessed | tf_op | source)
XLA Modules:
  0.0 192.7 jit_solution(7844583512993536516)
XLA Ops:
  0.7 3.7 %shadow_chunk.8 = (f32[2,128,640]{2,1,0:T(8,128)S(1)}, bf16[2,128,640]{2,1,0:T(8,128)(2,1)S(1)}, bf16[128,1280]{1,0:T(8,128)(2,1)S(1)}) custom-call(s32[1]{0:T(128)} %bitcast.place_ref, f32[1280,128]{1,0:T(8,128)} %rest_1_.1, bf16[1280,10240]{1,0:T(8,128)(2,1)} %ptdf_ref.9), custom_call_target="tpu_custom_call" | custom-call | flops 104857600 | bytes 819200 | tf_op jit(solution)/shard_map/shadow_chunk/pallas_call | solution.py:344
  4.9 3.6 %pack_generators.1 = (bf16[16,160,256]{2,1,0:T(8,128)(2,1)}, s32[1,768]{1,0:T(1,128)S(1)}) custom-call(s32[1]{0:T(128)} %bitcast.place_ref, s32[1,768]{1,0:T(1,128)S(1)} %bitcast.136, s32[6,128]{1,0:T(8,128)S(1)} %bitcast.134, f32[6,128]{1,0:T(8,128)S(1)} %bitcast.135, f32[768,128]{1,0:T(8,128)S(1)} %copy-done.1, f32[6,128]{1,0:T(8,128)S(1)} %bitcast.133, ...), custom_call_target="tpu_custom_call" | custom-call | flops 905969664 | bytes 3145728 | tf_op jit(solution)/shard_map/pack_generators/pallas_call | solution.py:106
  9.2 7.0 %all-to-all-start = ((bf16[16,160,256]{2,1,0:T(8,128)(2,1)}), bf16[16,160,256]{2,1,0:T(8,128)(2,1)S(1)}, u32[]{:S(2)}, u32[]{:S(2)}) async-start(bf16[16,160,256]{2,1,0:T(8,128)(2,1)} %get-tuple-element.114), calls=%async_computation | async-start | bytes 2621440 | tf_op jit(solution)/shard_map/all_to_all | solution.py:532
  18.3 15.0 %collective-permute-done.1 = bf16[128,640]{1,0:T(8,128)(2,1)S(1)} collective-permute-done((bf16[128,640]{1,0:T(8,128)(2,1)}, bf16[128,640]{1,0:T(8,128)(2,1)S(1)}, u32[]{:S(2)}, u32[]{:S(2)}) %collective-permute-start.1) | collective-permute-done | bytes 163872 | tf_op jit(solution)/shard_map/ppermute | solution.py:454
  33.4 3.4 %shadow_chunk.9 = (f32[2,128,640]{2,1,0:T(8,128)S(1)}, bf16[2,128,640]{2,1,0:T(8,128)(2,1)S(1)}) custom-call(s32[1]{0:T(128)} %bitcast.place_ref, bf16[128,1280]{1,0:T(8,128)(2,1)S(1)} %get-tuple-element.104.line_ref, bf16[1280,10240]{1,0:T(8,128)(2,1)} %ptdf_ref.9), custom_call_target="tpu_custom_call" | custom-call | flops 104857600 | bytes 819200 | tf_op jit(solution)/shard_map/shadow_chunk/pallas_call | solution.py:344
  36.9 3.4 %shadow_chunk.11 = (f32[2,128,640]{2,1,0:T(8,128)S(1)}, bf16[2,128,640]{2,1,0:T(8,128)(2,1)S(1)}) custom-call(s32[1]{0:T(128)} %bitcast.place_ref, bf16[128,1280]{1,0:T(8,128)(2,1)S(1)} %get-tuple-element.104.line_ref, bf16[1280,10240]{1,0:T(8,128)(2,1)} %ptdf_ref.9), custom_call_target="tpu_custom_call" | custom-call | flops 104857600 | bytes 819200 | tf_op jit(solution)/shard_map/shadow_chunk/pallas_call | solution.py:344
  41.1 3.4 %shadow_chunk.10 = (f32[2,128,640]{2,1,0:T(8,128)S(1)}, bf16[2,128,640]{2,1,0:T(8,128)(2,1)S(1)}) custom-call(s32[1]{0:T(128)} %bitcast.place_ref, bf16[128,1280]{1,0:T(8,128)(2,1)S(1)} %get-tuple-element.104.line_ref, bf16[1280,10240]{1,0:T(8,128)(2,1)} %ptdf_ref.9), custom_call_target="tpu_custom_call" | custom-call | flops 104857600 | bytes 819200 | tf_op jit(solution)/shard_map/shadow_chunk/pallas_call | solution.py:344
  44.7 3.0 %collective-permute-done.6 = bf16[128,640]{1,0:T(8,128)(2,1)S(1)} collective-permute-done((bf16[128,640]{1,0:T(8,128)(2,1)S(1)}, bf16[128,640]{1,0:T(8,128)(2,1)S(1)}, u32[]{:S(2)}, u32[]{:S(2)}) %collective-permute-start.6) | collective-permute-done | bytes 163872 | tf_op jit(solution)/shard_map/ppermute | solution.py:454
  57.2 5.5 %collective-permute-done.9.refs_1_ = bf16[128,640]{1,0:T(8,128)(2,1)S(1)} collective-permute-done((bf16[128,640]{1,0:T(8,128)(2,1)S(1)}, bf16[128,640]{1,0:T(8,128)(2,1)S(1)}, u32[]{:S(2)}, u32[]{:S(2)}) %collective-permute-start.9) | collective-permute-done | bytes 163872 | tf_op jit(solution)/shard_map/ppermute | solution.py:454
  62.7 8.5 %update_generators.2 = (f32[16,144,128]{2,1,0:T(8,128)S(1)}, bf16[656,128]{1,0:T(8,128)(2,1)S(1)}, bf16[1280,2560]{1,0:T(8,128)(2,1)S(1)}, bf16[1280,2560]{1,0:T(8,128)(2,1)S(1)}) custom-call(s32[1]{0:T(128)} %bitcast.place_ref, f32[128,640]{1,0:T(8,128)S(1)} %bitcast_add_fusion.6.refs_0_, bf16[128,640]{1,0:T(8,128)(2,1)S(1)} %collective-permute-done.9.refs_1_, ...), custom_call_target="tpu_custom_call" | custom-call | flops 1509949440 | bytes 4194304 | tf_op jit(solution)/shard_map/update_generators/pallas_call | solution.py:275
  71.8 3.7 %collective-permute-start.13 = (bf16[656,128]{1,0:T(8,128)(2,1)S(1)}, bf16[656,128]{1,0:T(8,128)(2,1)S(1)}, u32[]{:S(2)}, u32[]{:S(2)}) collective-permute-start(bf16[656,128]{1,0:T(8,128)(2,1)S(1)} %get-tuple-element.115.b0), channel_id=1, source_target_pairs={{0,8},{1,9},{2,10},{3,11},{4,12},{5,13},{6,14},{7,15},{8,0},{9,1},... | collective-permute-start | bytes 503816 | tf_op jit(solution)/shard_map/ppermute | solution.py:454
  77.4 5.4 %load_chunks.1 = (s32[1]{0:T(128)}, bf16[1280,2560]{1,0:T(8,128)(2,1)S(1)}, bf16[1280,2560]{1,0:T(8,128)(2,1)S(1)}) custom-call(s32[1]{0:T(128)} %bitcast.place_ref, bf16[1280,10240]{1,0:T(8,128)(2,1)} %ptdf_ref.9), custom_call_target="tpu_custom_call" | custom-call | bytes 819200 | tf_op jit(solution)/shard_map/load_chunks/pallas_call | solution.py:385
  86.4 2.4 %flow_chunk.8 = (f32[1280,128]{1,0:T(8,128)S(1)}, f32[1,128]{1,0:T(1,128)S(1)}) custom-call(bf16[1280,2560]{1,0:T(8,128)(2,1)S(1)} %get-tuple-element.123.ptdf_ref, bf16[656,128]{1,0:T(8,128)(2,1)S(1)} %get-tuple-element.115.b0, bf16[656,128]{1,0:T(8,128)(2,1)S(1)} %collective-permute-done.11.b1, bf16[656,128]{1,0:T(8,128)(2,1)S(1)} %collective-permute-done.14.b2, ...), custom_call_target="tpu_custom_call" | custom-call | flops 104857600 | bytes 819200 | tf_op jit(solution)/shard_map/flow_chunk/pallas_call | solution.py:442
  91.5 2.9 %collective-permute-done.17.b2 = bf16[656,128]{1,0:T(8,128)(2,1)S(1)} collective-permute-done((bf16[656,128]{1,0:T(8,128)(2,1)S(1)}, bf16[656,128]{1,0:T(8,128)(2,1)S(1)}, u32[]{:S(2)}, u32[]{:S(2)}) %collective-permute-start.17) | collective-permute-done | bytes 167968 | tf_op jit(solution)/shard_map/ppermute | solution.py:454
  96.5 2.4 %flow_chunk.9 = (f32[1280,128]{1,0:T(8,128)S(1)}, f32[1,128]{1,0:T(1,128)S(1)}) custom-call(bf16[1280,2560]{1,0:T(8,128)(2,1)S(1)} %get-tuple-element.130.ptdf_ref, bf16[656,128]{1,0:T(8,128)(2,1)S(1)} %collective-permute-done.12.b0, bf16[656,128]{1,0:T(8,128)(2,1)S(1)} %get-tuple-element.203.b1, bf16[656,128]{1,0:T(8,128)(2,1)S(1)} %collective-permute-done.16.b2, ...), custom_call_target="tpu_custom_call" | custom-call | flops 104857600 | bytes 819200 | tf_op jit(solution)/shard_map/flow_chunk/pallas_call | solution.py:442
  98.9 2.4 %collective-permute-done.20.b2 = bf16[656,128]{1,0:T(8,128)(2,1)S(1)} collective-permute-done((bf16[656,128]{1,0:T(8,128)(2,1)S(1)}, bf16[656,128]{1,0:T(8,128)(2,1)S(1)}, u32[]{:S(2)}, u32[]{:S(2)}) %collective-permute-start.20) | collective-permute-done | bytes 167968 | tf_op jit(solution)/shard_map/ppermute | solution.py:454
  101.5 2.4 %flow_chunk.10 = (f32[1280,128]{1,0:T(8,128)S(1)}, f32[1,128]{1,0:T(1,128)S(1)}) custom-call(bf16[1280,2560]{1,0:T(8,128)(2,1)S(1)} %get-tuple-element.117.ptdf_ref, bf16[656,128]{1,0:T(8,128)(2,1)S(1)} %collective-permute-done.13.b0, bf16[656,128]{1,0:T(8,128)(2,1)S(1)} %get-tuple-element.202.b1, bf16[656,128]{1,0:T(8,128)(2,1)S(1)} %collective-permute-done.17.b2, ...), custom_call_target="tpu_custom_call" | custom-call | flops 104857600 | bytes 819200 | tf_op jit(solution)/shard_map/flow_chunk/pallas_call | solution.py:442
  103.9 2.8 %flow_chunk.11 = (f32[1280,128]{1,0:T(8,128)S(1)}, bf16[128,1280]{1,0:T(8,128)(2,1)S(1)}, f32[1,128]{1,0:T(1,128)S(1)}) custom-call(bf16[1280,2560]{1,0:T(8,128)(2,1)S(1)} %get-tuple-element.120.ptdf_ref, bf16[656,128]{1,0:T(8,128)(2,1)S(1)} %collective-permute-done.15.b0, bf16[656,128]{1,0:T(8,128)(2,1)S(1)} %get-tuple-element.201.b1, ...), custom_call_target="tpu_custom_call" | custom-call | flops 104857600 | bytes 819200 | tf_op jit(solution)/shard_map/flow_chunk/pallas_call | solution.py:442
  124.2 2.6 %collective-permute-done.30 = bf16[128,640]{1,0:T(8,128)(2,1)S(1)} collective-permute-done((bf16[128,640]{1,0:T(8,128)(2,1)S(1)}, bf16[128,640]{1,0:T(8,128)(2,1)S(1)}, u32[]{:S(2)}, u32[]{:S(2)}) %collective-permute-start.30) | collective-permute-done | bytes 163872 | tf_op jit(solution)/shard_map/ppermute | solution.py:454
  126.9 2.7 %collective-permute-start.32 = (bf16[128,640]{1,0:T(8,128)(2,1)S(1)}, bf16[128,640]{1,0:T(8,128)(2,1)S(1)}, u32[]{:S(2)}, u32[]{:S(2)}) collective-permute-start(bf16[128,640]{1,0:T(8,128)(2,1)S(1)} %fusion.1), channel_id=1, source_target_pairs={{0,8},{1,9},{2,10},{3,11},{4,12},{5,13},{6,14},{7,15},{8,0},{9,1},... | collective-permute-start | bytes 491528 | tf_op jit(solution)/shard_map/ppermute | solution.py:454
  131.9 5.5 %collective-permute-done.31.refs_1_ = bf16[128,640]{1,0:T(8,128)(2,1)S(1)} collective-permute-done((bf16[128,640]{1,0:T(8,128)(2,1)S(1)}, bf16[128,640]{1,0:T(8,128)(2,1)S(1)}, u32[]{:S(2)}, u32[]{:S(2)}) %collective-permute-start.31) | collective-permute-done | bytes 163872 | tf_op jit(solution)/shard_map/ppermute | solution.py:454
  137.5 4.8 %update_generators.3 = (bf16[16,144,128]{2,1,0:T(8,128)(2,1)S(1)}, bf16[656,128]{1,0:T(8,128)(2,1)S(1)}) custom-call(s32[1]{0:T(128)} %get-tuple-element.119.place_ref, f32[128,640]{1,0:T(8,128)S(1)} %bitcast_add_fusion.2.refs_0_, bf16[128,640]{1,0:T(8,128)(2,1)S(1)} %collective-permute-done.31.refs_1_, ...), custom_call_target="tpu_custom_call" | custom-call | flops 1509949440 | bytes 4194304 | tf_op jit(solution)/shard_map/update_generators/pallas_call | solution.py:275
  146.6 2.9 %collective-permute-done.33.b0 = bf16[656,128]{1,0:T(8,128)(2,1)S(1)} collective-permute-done((bf16[656,128]{1,0:T(8,128)(2,1)S(1)}, bf16[656,128]{1,0:T(8,128)(2,1)S(1)}, u32[]{:S(2)}, u32[]{:S(2)}) %collective-permute-start.33) | collective-permute-done | bytes 167968 | tf_op jit(solution)/shard_map/ppermute | solution.py:454
  149.6 3.4 %collective-permute-done.34.b0 = bf16[656,128]{1,0:T(8,128)(2,1)S(1)} collective-permute-done((bf16[656,128]{1,0:T(8,128)(2,1)S(1)}, bf16[656,128]{1,0:T(8,128)(2,1)S(1)}, u32[]{:S(2)}, u32[]{:S(2)}) %collective-permute-start.34) | collective-permute-done | bytes 167968 | tf_op jit(solution)/shard_map/ppermute | solution.py:454
  157.8 2.4 %flow_chunk.12 = (f32[1280,128]{1,0:T(8,128)S(1)}, f32[1,128]{1,0:T(1,128)S(1)}) custom-call(bf16[1280,2560]{1,0:T(8,128)(2,1)S(1)} %get-tuple-element.123.ptdf_ref, bf16[656,128]{1,0:T(8,128)(2,1)S(1)} %get-tuple-element.157.b0, bf16[656,128]{1,0:T(8,128)(2,1)S(1)} %collective-permute-done.40.b1, bf16[656,128]{1,0:T(8,128)(2,1)S(1)} %collective-permute-done.35.b2, ...), custom_call_target="tpu_custom_call" | custom-call | flops 104857600 | bytes 819200 | tf_op jit(solution)/shard_map/flow_chunk/pallas_call | solution.py:442
  160.5 2.4 %collective-permute-done.43 = bf16[4,144,128]{2,1,0:T(8,128)(2,1)S(1)} collective-permute-done((bf16[4,144,128]{2,1,0:T(8,128)(2,1)S(1)}, bf16[4,144,128]{2,1,0:T(8,128)(2,1)S(1)}, u32[]{:S(2)}, u32[]{:S(2)}) %collective-permute-start.43) | collective-permute-done | bytes 147488 | tf_op jit(solution)/shard_map/ppermute | solution.py:454
  162.9 4.3 %collective-permute-done.38.b2 = bf16[656,128]{1,0:T(8,128)(2,1)S(1)} collective-permute-done((bf16[656,128]{1,0:T(8,128)(2,1)S(1)}, bf16[656,128]{1,0:T(8,128)(2,1)S(1)}, u32[]{:S(2)}, u32[]{:S(2)}) %collective-permute-start.38) | collective-permute-done | bytes 167968 | tf_op jit(solution)/shard_map/ppermute | solution.py:454
  167.2 3.1 %collective-permute-done.39.b2 = bf16[656,128]{1,0:T(8,128)(2,1)S(1)} collective-permute-done((bf16[656,128]{1,0:T(8,128)(2,1)S(1)}, bf16[656,128]{1,0:T(8,128)(2,1)S(1)}, u32[]{:S(2)}, u32[]{:S(2)}) %collective-permute-start.39) | collective-permute-done | bytes 167968 | tf_op jit(solution)/shard_map/ppermute | solution.py:454
  176.9 2.4 %flow_chunk.13 = (f32[1280,128]{1,0:T(8,128)S(1)}, f32[1,128]{1,0:T(1,128)S(1)}) custom-call(bf16[1280,2560]{1,0:T(8,128)(2,1)S(1)} %get-tuple-element.130.ptdf_ref, bf16[656,128]{1,0:T(8,128)(2,1)S(1)} %collective-permute-done.33.b0, bf16[656,128]{1,0:T(8,128)(2,1)S(1)} %get-tuple-element.196.b1, bf16[656,128]{1,0:T(8,128)(2,1)S(1)} %collective-permute-done.38.b2, ...), custom_call_target="tpu_custom_call" | custom-call | flops 104857600 | bytes 819200 | tf_op jit(solution)/shard_map/flow_chunk/pallas_call | solution.py:442
  179.6 2.4 %flow_chunk.14 = (f32[1280,128]{1,0:T(8,128)S(1)}, f32[1,128]{1,0:T(1,128)S(1)}) custom-call(bf16[1280,2560]{1,0:T(8,128)(2,1)S(1)} %get-tuple-element.117.ptdf_ref, bf16[656,128]{1,0:T(8,128)(2,1)S(1)} %collective-permute-done.34.b0, bf16[656,128]{1,0:T(8,128)(2,1)S(1)} %get-tuple-element.198.b1, bf16[656,128]{1,0:T(8,128)(2,1)S(1)} %collective-permute-done.39.b2, ...), custom_call_target="tpu_custom_call" | custom-call | flops 104857600 | bytes 819200 | tf_op jit(solution)/shard_map/flow_chunk/pallas_call | solution.py:442
  182.0 4.5 %collective-permute-done.47.refs_2_ = bf16[4,144,128]{2,1,0:T(8,128)(2,1)S(1)} collective-permute-done((bf16[4,144,128]{2,1,0:T(8,128)(2,1)S(1)}, bf16[4,144,128]{2,1,0:T(8,128)(2,1)S(1)}, u32[]{:S(2)}, u32[]{:S(2)}) %collective-permute-start.47) | collective-permute-done | bytes 147488 | tf_op jit(solution)/shard_map/ppermute | solution.py:454
  188.8 3.4 %flow_chunk.15 = (f32[1280,128]{1,0:T(8,128)}, bf16[128,1280]{1,0:T(8,128)(2,1)}, f32[1,128]{1,0:T(1,128)S(1)}) custom-call(bf16[1280,2560]{1,0:T(8,128)(2,1)S(1)} %get-tuple-element.120.ptdf_ref, bf16[656,128]{1,0:T(8,128)(2,1)S(1)} %collective-permute-done.37.b0, bf16[656,128]{1,0:T(8,128)(2,1)S(1)} %get-tuple-element.193.b1, ...), custom_call_target="tpu_custom_call" | custom-call | flops 104857600 | bytes 819200 | tf_op jit(solution)/shard_map/flow_chunk/pallas_call | solution.py:442
  (142 shorter events, 63.2 us)
Async XLA Ops:
  9.2 53.4 %all-to-all-start = ((bf16[16,160,256]{2,1,0:T(8,128)(2,1)}), bf16[16,160,256]{2,1,0:T(8,128)(2,1)S(1)}, u32[]{:S(2)}, u32[]{:S(2)}) async-start(bf16[16,160,256]{2,1,0:T(8,128)(2,1)} %get-tuple-element.114), calls=%async_computation | async-start | bytes 2621440 | tf_op jit(solution)/shard_map/all_to_all | solution.py:532
  16.3 17.0 %collective-permute-start.1 = (bf16[128,640]{1,0:T(8,128)(2,1)}, bf16[128,640]{1,0:T(8,128)(2,1)S(1)}, u32[]{:S(2)}, u32[]{:S(2)}) collective-permute-start(bf16[128,640]{1,0:T(8,128)(2,1)} %fusion.8), channel_id=1, source_target_pairs={{0,2},{1,3},{2,0},{3,1},{4,6},{5,7},{6,4},{7,5},{8,10},{9,11},{10,... | collective-permute-start | bytes 491528 | tf_op jit(solution)/shard_map/ppermute | solution.py:454
  41.0 6.7 %collective-permute-start.6 = (bf16[128,640]{1,0:T(8,128)(2,1)S(1)}, bf16[128,640]{1,0:T(8,128)(2,1)S(1)}, u32[]{:S(2)}, u32[]{:S(2)}) collective-permute-start(bf16[128,640]{1,0:T(8,128)(2,1)S(1)} %fusion.9), channel_id=1, source_target_pairs={{0,2},{1,3},{2,0},{3,1},{4,6},{5,7},{6,4},{7,5},{8,10},{9,11},{10,... | collective-permute-start | bytes 491528 | tf_op jit(solution)/shard_map/ppermute | solution.py:454
  47.7 7.2 %collective-permute-start.7 = (bf16[128,640]{1,0:T(8,128)(2,1)S(1)}, bf16[128,640]{1,0:T(8,128)(2,1)S(1)}, u32[]{:S(2)}, u32[]{:S(2)}) collective-permute-start(bf16[128,640]{1,0:T(8,128)(2,1)S(1)} %fusion.11), channel_id=1, source_target_pairs={{0,2},{1,3},{2,0},{3,1},{4,6},{5,7},{6,4},{7,5},{8,10},{9,11},{10,... | collective-permute-start | bytes 491528 | tf_op jit(solution)/shard_map/ppermute | solution.py:454
  49.4 7.7 %collective-permute-start.4 = (bf16[128,640]{1,0:T(8,128)(2,1)S(1)}, bf16[128,640]{1,0:T(8,128)(2,1)S(1)}, u32[]{:S(2)}, u32[]{:S(2)}) collective-permute-start(bf16[128,640]{1,0:T(8,128)(2,1)S(1)} %fusion.10), channel_id=1, source_target_pairs={{0,2},{1,3},{2,0},{3,1},{4,6},{5,7},{6,4},{7,5},{8,10},{9,11},{10,... | collective-permute-start | bytes 491528 | tf_op jit(solution)/shard_map/ppermute | solution.py:454
  51.3 11.4 %collective-permute-start.10 = (bf16[128,640]{1,0:T(8,128)(2,1)S(1)}, bf16[128,640]{1,0:T(8,128)(2,1)S(1)}, u32[]{:S(2)}, u32[]{:S(2)}) collective-permute-start(bf16[128,640]{1,0:T(8,128)(2,1)S(1)} %fusion.5), channel_id=1, source_target_pairs={{0,8},{1,9},{2,10},{3,11},{4,12},{5,13},{6,14},{7,15},{8,0},{9,1},... | collective-permute-start | bytes 491528 | tf_op jit(solution)/shard_map/ppermute | solution.py:454
  55.0 7.7 %collective-permute-start.9 = (bf16[128,640]{1,0:T(8,128)(2,1)S(1)}, bf16[128,640]{1,0:T(8,128)(2,1)S(1)}, u32[]{:S(2)}, u32[]{:S(2)}) collective-permute-start(bf16[128,640]{1,0:T(8,128)(2,1)S(1)} %fusion.6), channel_id=1, source_target_pairs={{0,4},{1,5},{2,6},{3,7},{4,0},{5,1},{6,2},{7,3},{8,12},{9,13},{10,... | collective-permute-start | bytes 491528 | tf_op jit(solution)/shard_map/ppermute | solution.py:454
  71.3 11.6 %collective-permute-start.12 = (bf16[656,128]{1,0:T(8,128)(2,1)S(1)}, bf16[656,128]{1,0:T(8,128)(2,1)S(1)}, u32[]{:S(2)}, u32[]{:S(2)}) collective-permute-start(bf16[656,128]{1,0:T(8,128)(2,1)S(1)} %get-tuple-element.115.b0), channel_id=1, source_target_pairs={{0,4},{1,5},{2,6},{3,7},{4,0},{5,1},{6,2},{7,3},{8,12},{9,13},{10,... | collective-permute-start | bytes 503816 | tf_op jit(solution)/shard_map/ppermute | solution.py:454
  71.8 12.0 %collective-permute-start.13 = (bf16[656,128]{1,0:T(8,128)(2,1)S(1)}, bf16[656,128]{1,0:T(8,128)(2,1)S(1)}, u32[]{:S(2)}, u32[]{:S(2)}) collective-permute-start(bf16[656,128]{1,0:T(8,128)(2,1)S(1)} %get-tuple-element.115.b0), channel_id=1, source_target_pairs={{0,8},{1,9},{2,10},{3,11},{4,12},{5,13},{6,14},{7,15},{8,0},{9,1},... | collective-permute-start | bytes 503816 | tf_op jit(solution)/shard_map/ppermute | solution.py:454
  75.6 8.3 %collective-permute-start.14 = (bf16[656,128]{1,0:T(8,128)(2,1)S(1)}, bf16[656,128]{1,0:T(8,128)(2,1)S(1)}, u32[]{:S(2)}, u32[]{:S(2)}) collective-permute-start(bf16[656,128]{1,0:T(8,128)(2,1)S(1)} %get-tuple-element.115.b0), channel_id=1, source_target_pairs={{0,2},{1,3},{2,0},{3,1},{4,6},{5,7},{6,4},{7,5},{8,10},{9,11},{10,... | collective-permute-start | bytes 503816 | tf_op jit(solution)/shard_map/ppermute | solution.py:454
  84.0 6.7 %collective-permute-start.15 = (bf16[656,128]{1,0:T(8,128)(2,1)S(1)}, bf16[656,128]{1,0:T(8,128)(2,1)S(1)}, u32[]{:S(2)}, u32[]{:S(2)}) collective-permute-start(bf16[656,128]{1,0:T(8,128)(2,1)S(1)} %collective-permute-done.13.b0), channel_id=1, source_target_pairs={{0,4},{1,5},{2,6},{3,7},{4,0},{5,1},{6,2},{7,3},{8,12},{9,13},{10,... | collective-permute-start | bytes 503816 | tf_op jit(solution)/shard_map/ppermute | solution.py:454
  84.4 7.1 %collective-permute-start.16 = (bf16[656,128]{1,0:T(8,128)(2,1)S(1)}, bf16[656,128]{1,0:T(8,128)(2,1)S(1)}, u32[]{:S(2)}, u32[]{:S(2)}) collective-permute-start(bf16[656,128]{1,0:T(8,128)(2,1)S(1)} %collective-permute-done.12.b0), channel_id=1, source_target_pairs={{0,2},{1,3},{2,0},{3,1},{4,6},{5,7},{6,4},{7,5},{8,10},{9,11},{10,... | collective-permute-start | bytes 503816 | tf_op jit(solution)/shard_map/ppermute | solution.py:454
  86.2 8.2 %collective-permute-start.17 = (bf16[656,128]{1,0:T(8,128)(2,1)S(1)}, bf16[656,128]{1,0:T(8,128)(2,1)S(1)}, u32[]{:S(2)}, u32[]{:S(2)}) collective-permute-start(bf16[656,128]{1,0:T(8,128)(2,1)S(1)} %collective-permute-done.13.b0), channel_id=1, source_target_pairs={{0,2},{1,3},{2,0},{3,1},{4,6},{5,7},{6,4},{7,5},{8,10},{9,11},{10,... | collective-permute-start | bytes 503816 | tf_op jit(solution)/shard_map/ppermute | solution.py:454
  94.6 6.7 %collective-permute-start.20 = (bf16[656,128]{1,0:T(8,128)(2,1)S(1)}, bf16[656,128]{1,0:T(8,128)(2,1)S(1)}, u32[]{:S(2)}, u32[]{:S(2)}) collective-permute-start(bf16[656,128]{1,0:T(8,128)(2,1)S(1)} %collective-permute-done.15.b0), channel_id=1, source_target_pairs={{0,2},{1,3},{2,0},{3,1},{4,6},{5,7},{6,4},{7,5},{8,10},{9,11},{10,... | collective-permute-start | bytes 503816 | tf_op jit(solution)/shard_map/ppermute | solution.py:454
  111.2 7.1 %collective-permute-start.24 = (bf16[128,640]{1,0:T(8,128)(2,1)S(1)}, bf16[128,640]{1,0:T(8,128)(2,1)S(1)}, u32[]{:S(2)}, u32[]{:S(2)}) collective-permute-start(bf16[128,640]{1,0:T(8,128)(2,1)S(1)} %fusion.12), channel_id=1, source_target_pairs={{0,2},{1,3},{2,0},{3,1},{4,6},{5,7},{6,4},{7,5},{8,10},{9,11},{10,... | collective-permute-start | bytes 491528 | tf_op jit(solution)/shard_map/ppermute | solution.py:454
  113.0 9.0 %collective-permute-start.28 = (bf16[128,640]{1,0:T(8,128)(2,1)S(1)}, bf16[128,640]{1,0:T(8,128)(2,1)S(1)}, u32[]{:S(2)}, u32[]{:S(2)}) collective-permute-start(bf16[128,640]{1,0:T(8,128)(2,1)S(1)} %fusion.13), channel_id=1, source_target_pairs={{0,2},{1,3},{2,0},{3,1},{4,6},{5,7},{6,4},{7,5},{8,10},{9,11},{10,... | collective-permute-start | bytes 491528 | tf_op jit(solution)/shard_map/ppermute | solution.py:454
  122.0 7.5 %collective-permute-start.29 = (bf16[128,640]{1,0:T(8,128)(2,1)S(1)}, bf16[128,640]{1,0:T(8,128)(2,1)S(1)}, u32[]{:S(2)}, u32[]{:S(2)}) collective-permute-start(bf16[128,640]{1,0:T(8,128)(2,1)S(1)} %fusion.15), channel_id=1, source_target_pairs={{0,2},{1,3},{2,0},{3,1},{4,6},{5,7},{6,4},{7,5},{8,10},{9,11},{10,... | collective-permute-start | bytes 491528 | tf_op jit(solution)/shard_map/ppermute | solution.py:454
  123.9 8.0 %collective-permute-start.26 = (bf16[128,640]{1,0:T(8,128)(2,1)S(1)}, bf16[128,640]{1,0:T(8,128)(2,1)S(1)}, u32[]{:S(2)}, u32[]{:S(2)}) collective-permute-start(bf16[128,640]{1,0:T(8,128)(2,1)S(1)} %fusion.14), channel_id=1, source_target_pairs={{0,2},{1,3},{2,0},{3,1},{4,6},{5,7},{6,4},{7,5},{8,10},{9,11},{10,... | collective-permute-start | bytes 491528 | tf_op jit(solution)/shard_map/ppermute | solution.py:454
  126.9 10.5 %collective-permute-start.32 = (bf16[128,640]{1,0:T(8,128)(2,1)S(1)}, bf16[128,640]{1,0:T(8,128)(2,1)S(1)}, u32[]{:S(2)}, u32[]{:S(2)}) collective-permute-start(bf16[128,640]{1,0:T(8,128)(2,1)S(1)} %fusion.1), channel_id=1, source_target_pairs={{0,8},{1,9},{2,10},{3,11},{4,12},{5,13},{6,14},{7,15},{8,0},{9,1},... | collective-permute-start | bytes 491528 | tf_op jit(solution)/shard_map/ppermute | solution.py:454
  129.6 7.8 %collective-permute-start.31 = (bf16[128,640]{1,0:T(8,128)(2,1)S(1)}, bf16[128,640]{1,0:T(8,128)(2,1)S(1)}, u32[]{:S(2)}, u32[]{:S(2)}) collective-permute-start(bf16[128,640]{1,0:T(8,128)(2,1)S(1)} %fusion.2), channel_id=1, source_target_pairs={{0,4},{1,5},{2,6},{3,7},{4,0},{5,1},{6,2},{7,3},{8,12},{9,13},{10,... | collective-permute-start | bytes 491528 | tf_op jit(solution)/shard_map/ppermute | solution.py:454
  142.3 7.3 %collective-permute-start.33 = (bf16[656,128]{1,0:T(8,128)(2,1)S(1)}, bf16[656,128]{1,0:T(8,128)(2,1)S(1)}, u32[]{:S(2)}, u32[]{:S(2)}) collective-permute-start(bf16[656,128]{1,0:T(8,128)(2,1)S(1)} %get-tuple-element.157.b0), channel_id=1, source_target_pairs={{0,4},{1,5},{2,6},{3,7},{4,0},{5,1},{6,2},{7,3},{8,12},{9,13},{10,... | collective-permute-start | bytes 503816 | tf_op jit(solution)/shard_map/ppermute | solution.py:454
  143.8 9.2 %collective-permute-start.34 = (bf16[656,128]{1,0:T(8,128)(2,1)S(1)}, bf16[656,128]{1,0:T(8,128)(2,1)S(1)}, u32[]{:S(2)}, u32[]{:S(2)}) collective-permute-start(bf16[656,128]{1,0:T(8,128)(2,1)S(1)} %get-tuple-element.157.b0), channel_id=1, source_target_pairs={{0,8},{1,9},{2,10},{3,11},{4,12},{5,13},{6,14},{7,15},{8,0},{9,1},... | collective-permute-start | bytes 503816 | tf_op jit(solution)/shard_map/ppermute | solution.py:454
  144.9 8.1 %collective-permute-start.35 = (bf16[656,128]{1,0:T(8,128)(2,1)S(1)}, bf16[656,128]{1,0:T(8,128)(2,1)S(1)}, u32[]{:S(2)}, u32[]{:S(2)}) collective-permute-start(bf16[656,128]{1,0:T(8,128)(2,1)S(1)} %get-tuple-element.157.b0), channel_id=1, source_target_pairs={{0,2},{1,3},{2,0},{3,1},{4,6},{5,7},{6,4},{7,5},{8,10},{9,11},{10,... | collective-permute-start | bytes 503816 | tf_op jit(solution)/shard_map/ppermute | solution.py:454
  155.5 7.3 %collective-permute-start.43 = (bf16[4,144,128]{2,1,0:T(8,128)(2,1)S(1)}, bf16[4,144,128]{2,1,0:T(8,128)(2,1)S(1)}, u32[]{:S(2)}, u32[]{:S(2)}) collective-permute-start(bf16[4,144,128]{2,1,0:T(8,128)(2,1)S(1)} %get-tuple-element.192), channel_id=1, source_target_pairs={{0,3},{1,2},{2,1},{3,0},{4,7},{5,6},{6,5},{7,4},{8,11},{9,10},{10,... | collective-permute-start | bytes 442376 | tf_op jit(solution)/shard_map/ppermute | solution.py:454
  155.6 7.3 %collective-permute-start.37 = (bf16[656,128]{1,0:T(8,128)(2,1)S(1)}, bf16[656,128]{1,0:T(8,128)(2,1)S(1)}, u32[]{:S(2)}, u32[]{:S(2)}) collective-permute-start(bf16[656,128]{1,0:T(8,128)(2,1)S(1)} %collective-permute-done.34.b0), channel_id=1, source_target_pairs={{0,4},{1,5},{2,6},{3,7},{4,0},{5,1},{6,2},{7,3},{8,12},{9,13},{10,... | collective-permute-start | bytes 503816 | tf_op jit(solution)/shard_map/ppermute | solution.py:454
  155.6 11.6 %collective-permute-start.38 = (bf16[656,128]{1,0:T(8,128)(2,1)S(1)}, bf16[656,128]{1,0:T(8,128)(2,1)S(1)}, u32[]{:S(2)}, u32[]{:S(2)}) collective-permute-start(bf16[656,128]{1,0:T(8,128)(2,1)S(1)} %collective-permute-done.33.b0), channel_id=1, source_target_pairs={{0,2},{1,3},{2,0},{3,1},{4,6},{5,7},{6,4},{7,5},{8,10},{9,11},{10,... | collective-permute-start | bytes 503816 | tf_op jit(solution)/shard_map/ppermute | solution.py:454
  157.4 12.9 %collective-permute-start.39 = (bf16[656,128]{1,0:T(8,128)(2,1)S(1)}, bf16[656,128]{1,0:T(8,128)(2,1)S(1)}, u32[]{:S(2)}, u32[]{:S(2)}) collective-permute-start(bf16[656,128]{1,0:T(8,128)(2,1)S(1)} %collective-permute-done.34.b0), channel_id=1, source_target_pairs={{0,2},{1,3},{2,0},{3,1},{4,6},{5,7},{6,4},{7,5},{8,10},{9,11},{10,... | collective-permute-start | bytes 503816 | tf_op jit(solution)/shard_map/ppermute | solution.py:454
  170.5 8.8 %collective-permute-start.45 = (bf16[656,128]{1,0:T(8,128)(2,1)S(1)}, bf16[656,128]{1,0:T(8,128)(2,1)S(1)}, u32[]{:S(2)}, u32[]{:S(2)}) collective-permute-start(bf16[656,128]{1,0:T(8,128)(2,1)S(1)} %collective-permute-done.37.b0), channel_id=1, source_target_pairs={{0,2},{1,3},{2,0},{3,1},{4,6},{5,7},{6,4},{7,5},{8,10},{9,11},{10,... | collective-permute-start | bytes 503816 | tf_op jit(solution)/shard_map/ppermute | solution.py:454
  172.4 9.6 %collective-permute-start.46 = (bf16[4,144,128]{2,1,0:T(8,128)(2,1)S(1)}, bf16[4,144,128]{2,1,0:T(8,128)(2,1)S(1)}, u32[]{:S(2)}, u32[]{:S(2)}) collective-permute-start(bf16[4,144,128]{2,1,0:T(8,128)(2,1)S(1)} %get-tuple-element.187), channel_id=1, source_target_pairs={{0,4},{1,5},{2,6},{3,7},{4,0},{5,1},{6,2},{7,3},{8,12},{9,13},{10,... | collective-permute-start | bytes 442376 | tf_op jit(solution)/shard_map/ppermute | solution.py:454
  172.5 14.0 %collective-permute-start.47 = (bf16[4,144,128]{2,1,0:T(8,128)(2,1)S(1)}, bf16[4,144,128]{2,1,0:T(8,128)(2,1)S(1)}, u32[]{:S(2)}, u32[]{:S(2)}) collective-permute-start(bf16[4,144,128]{2,1,0:T(8,128)(2,1)S(1)} %get-tuple-element.186), channel_id=1, source_target_pairs={{0,8},{1,9},{2,10},{3,11},{4,12},{5,13},{6,14},{7,15},{8,0},{9,1},... | collective-permute-start | bytes 442376 | tf_op jit(solution)/shard_map/ppermute | solution.py:454
  174.5 12.0 %collective-permute-start.48 = (bf16[4,144,128]{2,1,0:T(8,128)(2,1)S(1)}, bf16[4,144,128]{2,1,0:T(8,128)(2,1)S(1)}, u32[]{:S(2)}, u32[]{:S(2)}) collective-permute-start(bf16[4,144,128]{2,1,0:T(8,128)(2,1)S(1)} %get-tuple-element.185), channel_id=1, source_target_pairs={{0,12},{1,13},{2,14},{3,15},{4,8},{5,9},{6,10},{7,11},{8,4},{9,5},... | collective-permute-start | bytes 442376 | tf_op jit(solution)/shard_map/ppermute | solution.py:454
  179.4 9.4 %collective-permute-start.49 = (bf16[656,128]{1,0:T(8,128)(2,1)S(1)}, bf16[656,128]{1,0:T(8,128)(2,1)S(1)}, u32[]{:S(2)}, u32[]{:S(2)}) collective-permute-start(bf16[656,128]{1,0:T(8,128)(2,1)S(1)} %collective-permute-done.45.b2), channel_id=1, source_target_pairs={{0,1},{1,0},{2,3},{3,2},{4,5},{5,4},{6,7},{7,6},{8,9},{9,8},{10,11... | collective-permute-start | bytes 503816 | tf_op jit(solution)/shard_map/ppermute | solution.py:454
  (29 other events, 168.4 us)

commit v10 on v8

--- a/solution.py
+++ b/solution.py
@@ -327,8 +327,9 @@
     return pltpu.with_memory_space_constraint(x, pltpu.MemorySpace.HBM)
 
 
-def chunk_cost(hours, lines, buses):
-    return pl.CostEstimate(flops=COST * 8 * hours * lines * buses, bytes_accessed=8 * lines * buses, transcendentals=0)
+def chunk_cost(hours, lines, buses, weight=COST):
+    flops = max(1, 8 * weight) * hours * lines * buses
+    return pl.CostEstimate(flops=flops, bytes_accessed=(8 if weight else 1) * lines * buses, transcendentals=0)
 
 
 def shadow_chunk(chunk, stream, place, line, ptdf, buses):
@@ -429,7 +430,7 @@
         half_ref[...] = out_ref[...].T.astype(BF16)
 
 
-def flow_chunk(ptdf, blocks, acc, total, limit=None, line=None):
+def flow_chunk(ptdf, blocks, acc, total, limit=None, line=None, weight=COST):
     lines = ptdf.shape[0]
     rows, hours = blocks[0].shape
     buses = rows - META
@@ -446,7 +447,7 @@
         out_shape=tuple(out_shape),
         scratch_shapes=[pltpu.VMEM((4 * buses, hours), BF16)],
         compiler_params=pltpu.CompilerParams(vmem_limit_bytes=LIMIT),
-        cost_estimate=chunk_cost(hours, lines, buses),
+        cost_estimate=chunk_cost(hours, lines, buses, weight),
         name="flow_chunk",
     )(*operands)
 
@@ -498,6 +499,7 @@
     held, resident, recv = None, {}, None
     for iteration in range(ITERS):
         last = iteration == ITERS - 1
+        weight = 0 if last else COST
         if staged:
             line_t = line_half
             keeps, gots, crossed, parts = {}, {}, {}, {}
@@ -540,8 +542,6 @@
             line_t, _ = lax.optimization_barrier((line_t, across(2)))
             if iteration:
                 line_t, _ = lax.optimization_barrier((line_t, settle(3)))
-            else:
-                line_t, parts[3] = lax.optimization_barrier((line_t, parts[3]))
             product(0, line_t)
             gots[1], crossed[2] = lax.optimization_barrier((gots[1], crossed[2]))
             parts[3], _, _ = lax.optimization_barrier((parts[3], across(1), across(0)))
@@ -592,18 +592,18 @@
                 back = [home[0]] + [swap(home[chunk], devices, 4 * chunk) for chunk in (1, 2, 3)]
             else:
                 (place,) = rest
-            acc, total = flow_chunk(resident[0], blocks(0), None, balance_row)
+            acc, total = flow_chunk(resident[0], blocks(0), None, balance_row, weight=weight)
             near[3], far[1], acc = lax.optimization_barrier((near[3], far[1], acc))
             spread(3)
             settle_far(1)
-            acc, total = flow_chunk(resident[1], blocks(1), acc, total)
+            acc, total = flow_chunk(resident[1], blocks(1), acc, total, weight=weight)
             settle_far(2)
             far[3], acc = lax.optimization_barrier((far[3], acc))
             settle_far(3)
-            acc, total = flow_chunk(resident[2], blocks(2), acc, total)
-            if last:
-                acc, *back = lax.optimization_barrier((acc, *back))
-            line_price, line_half, total = flow_chunk(resident[3], blocks(3), acc, total, limit, line_price)
+            acc, total = flow_chunk(resident[2], blocks(2), acc, total, weight=weight)
+            line_price, line_half, total = flow_chunk(
+                resident[3], blocks(3), acc, total, limit, line_price, weight
+            )
             balance = total
         else:
             if last:

time: 194 us -> 180 us (0.928)
  starting transfers between devices: 56.6 us -> 45.4 us
  waiting for transfers between devices: 65.8 us -> 62.7 us
    ppermute x58, starting transfers between devices: 51.6 us -> 40.4 us  [swap(): return lax.ppermute(x, 'bus', [(i, i ^ mask) for i in range(devices)])]
    ppermute x58, waiting for transfers between devices: 65.8 us -> 62.7 us  [swap(): return lax.ppermute(x, 'bus', [(i, i ^ mask) for i in range(devices)])]
  transfers between devices with their start and end apart: 59 -> 59, of which waited for: 22 -> 25; matrix products, arithmetic and copies ran while one was open for 1% -> 1% of each run, Pallas kernels for 21% -> 23%
where the time goes in v10:
time: 180 us
  Pallas kernels  66.9 us (37%)
  waiting for transfers between devices  62.7 us (35%)
  starting transfers between devices  45.4 us (25%)
  other arithmetic  2.97 us (2%)
    ppermute x58, waiting for transfers between devices, swap(): return lax.ppermute(x, 'bus', [(i, i ^ mask) for i in range(devices)])  62.7 us
    ppermute x58, starting transfers between devices, swap(): return lax.ppermute(x, 'bus', [(i, i ^ mask) for i in range(devices)])  40.4 us
    pallas_call x8, Pallas kernels, shadow_chunk(): pl.pallas_call(functools.partial(shadow_kernel, chunk, stream, turn), in_...  21.3 us
    pallas_call x8, Pallas kernels, flow_chunk(): pl.pallas_call(functools.partial(flow_kernel, start, end), in_specs=[VMEM...  20.9 us
    pallas_call x2, Pallas kernels, update(): pl.pallas_call(functools.partial(update_kernel, cap, devices, first, last...  13.3 us
    pallas_call x1, Pallas kernels, load_chunks(): pl.pallas_call(functools.partial(load_kernel, chunks), in_specs=[SMEM_SPE...  5.44 us
    all_to_all x1, starting transfers between devices, local(): lax.all_to_all(outgoing, 'bus', split_axis=0, concat_axis=0, tiled=True)  4.98 us
  transfers between devices with their start and end apart: 59, of which 25 were waited for; matrix products, arithmetic and copies ran while one was open for 1% of the time, Pallas kernels for 23%

profile of v10, /device:TPU:0, one launch (start us, length us, event | category | flops | bytes accessed | tf_op | source)
XLA Modules:
  0.0 179.7 jit_solution(3084753224060025868)
XLA Ops:
  0.7 3.7 %shadow_chunk.8 = (f32[2,128,640]{2,1,0:T(8,128)S(1)}, bf16[2,128,640]{2,1,0:T(8,128)(2,1)S(1)}, bf16[128,1280]{1,0:T(8,128)(2,1)S(1)}) custom-call(s32[1]{0:T(128)} %bitcast.place_ref, f32[1280,128]{1,0:T(8,128)} %rest_1_.1, bf16[1280,10240]{1,0:T(8,128)(2,1)} %ptdf_ref.9), custom_call_target="tpu_custom_call" | custom-call | flops 2516582400 | bytes 6553600 | tf_op jit(solution)/shard_map/shadow_chunk/pallas_call | solution.py:346
  4.9 3.6 %pack_generators.1 = (bf16[16,160,256]{2,1,0:T(8,128)(2,1)}, s32[1,768]{1,0:T(1,128)S(1)}) custom-call(s32[1]{0:T(128)} %bitcast.place_ref, s32[1,768]{1,0:T(1,128)S(1)} %bitcast.88, s32[6,128]{1,0:T(8,128)S(1)} %bitcast.86, f32[6,128]{1,0:T(8,128)S(1)} %bitcast.87, f32[768,128]{1,0:T(8,128)S(1)} %copy-done.1, f32[6,128]{1,0:T(8,128)S(1)} %bitcast.82, ...), custom_call_target="tpu_custom_call" | custom-call | flops 905969664 | bytes 3145728 | tf_op jit(solution)/shard_map/pack_generators/pallas_call | solution.py:107
  9.2 2.6 %collective-permute-start.1 = (bf16[128,640]{1,0:T(8,128)(2,1)}, bf16[128,640]{1,0:T(8,128)(2,1)}, u32[]{:S(2)}, u32[]{:S(2)}) collective-permute-start(bf16[128,640]{1,0:T(8,128)(2,1)} %fusion.8), channel_id=1, source_target_pairs={{0,2},{1,3},{2,0},{3,1},{4,6},{5,7},{6,4},{7,5},{8,10},{9,11},{10,... | collective-permute-start | bytes 491528 | tf_op jit(solution)/shard_map/ppermute | solution.py:456
  11.8 5.0 %all-to-all-start = ((bf16[16,160,256]{2,1,0:T(8,128)(2,1)}), bf16[16,160,256]{2,1,0:T(8,128)(2,1)S(1)}, u32[]{:S(2)}, u32[]{:S(2)}) async-start(bf16[16,160,256]{2,1,0:T(8,128)(2,1)} %get-tuple-element.107), calls=%async_computation | async-start | bytes 2621440 | tf_op jit(solution)/shard_map/all_to_all | solution.py:535
  17.9 3.4 %shadow_chunk.9 = (f32[2,128,640]{2,1,0:T(8,128)S(1)}, bf16[2,128,640]{2,1,0:T(8,128)(2,1)S(1)}) custom-call(s32[1]{0:T(128)} %bitcast.place_ref, bf16[128,1280]{1,0:T(8,128)(2,1)S(1)} %get-tuple-element.97.line_ref, bf16[1280,10240]{1,0:T(8,128)(2,1)} %ptdf_ref.9), custom_call_target="tpu_custom_call" | custom-call | flops 2516582400 | bytes 6553600 | tf_op jit(solution)/shard_map/shadow_chunk/pallas_call | solution.py:346
  21.7 3.4 %shadow_chunk.11 = (f32[2,128,640]{2,1,0:T(8,128)S(1)}, bf16[2,128,640]{2,1,0:T(8,128)(2,1)S(1)}) custom-call(s32[1]{0:T(128)} %bitcast.place_ref, bf16[128,1280]{1,0:T(8,128)(2,1)S(1)} %get-tuple-element.97.line_ref, bf16[1280,10240]{1,0:T(8,128)(2,1)} %ptdf_ref.9), custom_call_target="tpu_custom_call" | custom-call | flops 2516582400 | bytes 6553600 | tf_op jit(solution)/shard_map/shadow_chunk/pallas_call | solution.py:346
  27.4 3.4 %shadow_chunk.10 = (f32[2,128,640]{2,1,0:T(8,128)S(1)}, bf16[2,128,640]{2,1,0:T(8,128)(2,1)S(1)}) custom-call(s32[1]{0:T(128)} %bitcast.place_ref, bf16[128,1280]{1,0:T(8,128)(2,1)S(1)} %get-tuple-element.97.line_ref, bf16[1280,10240]{1,0:T(8,128)(2,1)} %ptdf_ref.9), custom_call_target="tpu_custom_call" | custom-call | flops 2516582400 | bytes 6553600 | tf_op jit(solution)/shard_map/shadow_chunk/pallas_call | solution.py:346
  32.5 2.4 %collective-permute-done.6 = bf16[128,640]{1,0:T(8,128)(2,1)S(1)} collective-permute-done((bf16[128,640]{1,0:T(8,128)(2,1)S(1)}, bf16[128,640]{1,0:T(8,128)(2,1)S(1)}, u32[]{:S(2)}, u32[]{:S(2)}) %collective-permute-start.6) | collective-permute-done | bytes 163872 | tf_op jit(solution)/shard_map/ppermute | solution.py:456
  37.1 5.5 %collective-permute-done.8 = bf16[128,640]{1,0:T(8,128)(2,1)S(1)} collective-permute-done((bf16[128,640]{1,0:T(8,128)(2,1)S(1)}, bf16[128,640]{1,0:T(8,128)(2,1)S(1)}, u32[]{:S(2)}, u32[]{:S(2)}) %collective-permute-start.8) | collective-permute-done | bytes 163872 | tf_op jit(solution)/shard_map/ppermute | solution.py:456
  42.7 4.4 %collective-permute-start.10 = (bf16[128,640]{1,0:T(8,128)(2,1)S(1)}, bf16[128,640]{1,0:T(8,128)(2,1)S(1)}, u32[]{:S(2)}, u32[]{:S(2)}) collective-permute-start(bf16[128,640]{1,0:T(8,128)(2,1)S(1)} %fusion.5), channel_id=1, source_target_pairs={{0,8},{1,9},{2,10},{3,11},{4,12},{5,13},{6,14},{7,15},{8,0},{9,1},... | collective-permute-start | bytes 491528 | tf_op jit(solution)/shard_map/ppermute | solution.py:456
  47.9 8.3 %collective-permute-done.9.refs_1_ = bf16[128,640]{1,0:T(8,128)(2,1)S(1)} collective-permute-done((bf16[128,640]{1,0:T(8,128)(2,1)S(1)}, bf16[128,640]{1,0:T(8,128)(2,1)S(1)}, u32[]{:S(2)}, u32[]{:S(2)}) %collective-permute-start.9) | collective-permute-done | bytes 163872 | tf_op jit(solution)/shard_map/ppermute | solution.py:456
  56.3 8.5 %update_generators.2 = (f32[16,144,128]{2,1,0:T(8,128)S(1)}, bf16[656,128]{1,0:T(8,128)(2,1)S(1)}, bf16[1280,2560]{1,0:T(8,128)(2,1)S(1)}, bf16[1280,2560]{1,0:T(8,128)(2,1)S(1)}) custom-call(s32[1]{0:T(128)} %bitcast.place_ref, f32[128,640]{1,0:T(8,128)S(1)} %bitcast_add_fusion.6.refs_0_, bf16[128,640]{1,0:T(8,128)(2,1)S(1)} %collective-permute-done.9.refs_1_, ...), custom_call_target="tpu_custom_call" | custom-call | flops 1509949440 | bytes 4194304 | tf_op jit(solution)/shard_map/update_generators/pallas_call | solution.py:276
  68.2 5.4 %load_chunks.1 = (s32[1]{0:T(128)}, bf16[1280,2560]{1,0:T(8,128)(2,1)S(1)}, bf16[1280,2560]{1,0:T(8,128)(2,1)S(1)}) custom-call(s32[1]{0:T(128)} %bitcast.place_ref, bf16[1280,10240]{1,0:T(8,128)(2,1)} %ptdf_ref.9), custom_call_target="tpu_custom_call" | custom-call | bytes 13107200 | tf_op jit(solution)/shard_map/load_chunks/pallas_call | solution.py:387
  73.8 2.3 %collective-permute-done.12.b0 = bf16[656,128]{1,0:T(8,128)(2,1)S(1)} collective-permute-done((bf16[656,128]{1,0:T(8,128)(2,1)S(1)}, bf16[656,128]{1,0:T(8,128)(2,1)S(1)}, u32[]{:S(2)}, u32[]{:S(2)}) %collective-permute-start.12) | collective-permute-done | bytes 167968 | tf_op jit(solution)/shard_map/ppermute | solution.py:456
  78.4 2.4 %flow_chunk.8 = (f32[1280,128]{1,0:T(8,128)S(1)}, f32[1,128]{1,0:T(1,128)S(1)}) custom-call(bf16[1280,2560]{1,0:T(8,128)(2,1)S(1)} %get-tuple-element.115.ptdf_ref, bf16[656,128]{1,0:T(8,128)(2,1)S(1)} %get-tuple-element.108.b0, bf16[656,128]{1,0:T(8,128)(2,1)S(1)} %collective-permute-done.14.b1, bf16[656,128]{1,0:T(8,128)(2,1)S(1)} %collective-permute-done.13.b2, ...), custom_call_target="tpu_custom_call" | custom-call | flops 2516582400 | bytes 6553600 | tf_op jit(solution)/shard_map/flow_chunk/pallas_call | solution.py:444
  80.8 3.5 %collective-permute-done.15.b0 = bf16[656,128]{1,0:T(8,128)(2,1)S(1)} collective-permute-done((bf16[656,128]{1,0:T(8,128)(2,1)S(1)}, bf16[656,128]{1,0:T(8,128)(2,1)S(1)}, u32[]{:S(2)}, u32[]{:S(2)}) %collective-permute-start.15) | collective-permute-done | bytes 167968 | tf_op jit(solution)/shard_map/ppermute | solution.py:456
  86.4 2.4 %flow_chunk.9 = (f32[1280,128]{1,0:T(8,128)S(1)}, f32[1,128]{1,0:T(1,128)S(1)}) custom-call(bf16[1280,2560]{1,0:T(8,128)(2,1)S(1)} %get-tuple-element.120.ptdf_ref, bf16[656,128]{1,0:T(8,128)(2,1)S(1)} %collective-permute-done.11.b0, bf16[656,128]{1,0:T(8,128)(2,1)S(1)} %collective-permute-done.20.b1, bf16[656,128]{1,0:T(8,128)(2,1)S(1)} %collective-permute-done.16.b2, ...), custom_call_target="tpu_custom_call" | custom-call | flops 2516582400 | bytes 6553600 | tf_op jit(solution)/shard_map/flow_chunk/pallas_call | solution.py:444
  88.9 3.0 %collective-permute-done.19.b2 = bf16[656,128]{1,0:T(8,128)(2,1)S(1)} collective-permute-done((bf16[656,128]{1,0:T(8,128)(2,1)S(1)}, bf16[656,128]{1,0:T(8,128)(2,1)S(1)}, u32[]{:S(2)}, u32[]{:S(2)}) %collective-permute-start.19) | collective-permute-done | bytes 167968 | tf_op jit(solution)/shard_map/ppermute | solution.py:456
  91.9 2.4 %flow_chunk.10 = (f32[1280,128]{1,0:T(8,128)S(1)}, f32[1,128]{1,0:T(1,128)S(1)}) custom-call(bf16[1280,2560]{1,0:T(8,128)(2,1)S(1)} %get-tuple-element.126.ptdf_ref, bf16[656,128]{1,0:T(8,128)(2,1)S(1)} %collective-permute-done.12.b0, bf16[656,128]{1,0:T(8,128)(2,1)S(1)} %collective-permute-done.23.b1, bf16[656,128]{1,0:T(8,128)(2,1)S(1)} %collective-permute-done.24.b2, ...), custom_call_target="tpu_custom_call" | custom-call | flops 2516582400 | bytes 6553600 | tf_op jit(solution)/shard_map/flow_chunk/pallas_call | solution.py:444
  94.3 2.8 %flow_chunk.11 = (f32[1280,128]{1,0:T(8,128)S(1)}, bf16[128,1280]{1,0:T(8,128)(2,1)S(1)}, f32[1,128]{1,0:T(1,128)S(1)}) custom-call(bf16[1280,2560]{1,0:T(8,128)(2,1)S(1)} %get-tuple-element.112.ptdf_ref, bf16[656,128]{1,0:T(8,128)(2,1)S(1)} %collective-permute-done.15.b0, bf16[656,128]{1,0:T(8,128)(2,1)S(1)} %collective-permute-done.18.b1, ...), custom_call_target="tpu_custom_call" | custom-call | flops 2516582400 | bytes 6553600 | tf_op jit(solution)/shard_map/flow_chunk/pallas_call | solution.py:444
  105.7 2.9 %collective-permute-done.28 = bf16[128,640]{1,0:T(8,128)(2,1)S(1)} collective-permute-done((bf16[128,640]{1,0:T(8,128)(2,1)S(1)}, bf16[128,640]{1,0:T(8,128)(2,1)S(1)}, u32[]{:S(2)}, u32[]{:S(2)}) %collective-permute-start.28) | collective-permute-done | bytes 163872 | tf_op jit(solution)/shard_map/ppermute | solution.py:456
  114.0 3.3 %collective-permute-done.34 = bf16[128,640]{1,0:T(8,128)(2,1)S(1)} collective-permute-done((bf16[128,640]{1,0:T(8,128)(2,1)S(1)}, bf16[128,640]{1,0:T(8,128)(2,1)S(1)}, u32[]{:S(2)}, u32[]{:S(2)}) %collective-permute-start.34) | collective-permute-done | bytes 163872 | tf_op jit(solution)/shard_map/ppermute | solution.py:456
  121.2 6.5 %collective-permute-done.35.refs_1_ = bf16[128,640]{1,0:T(8,128)(2,1)S(1)} collective-permute-done((bf16[128,640]{1,0:T(8,128)(2,1)S(1)}, bf16[128,640]{1,0:T(8,128)(2,1)S(1)}, u32[]{:S(2)}, u32[]{:S(2)}) %collective-permute-start.35) | collective-permute-done | bytes 163872 | tf_op jit(solution)/shard_map/ppermute | solution.py:456
  127.8 4.8 %update_generators.3 = (bf16[16,144,128]{2,1,0:T(8,128)(2,1)S(1)}, bf16[656,128]{1,0:T(8,128)(2,1)S(1)}) custom-call(s32[1]{0:T(128)} %get-tuple-element.111.place_ref, f32[128,640]{1,0:T(8,128)S(1)} %bitcast_add_fusion.2.refs_0_, bf16[128,640]{1,0:T(8,128)(2,1)S(1)} %collective-permute-done.35.refs_1_, ...), custom_call_target="tpu_custom_call" | custom-call | flops 1509949440 | bytes 4194304 | tf_op jit(solution)/shard_map/update_generators/pallas_call | solution.py:276
  136.9 8.3 %collective-permute-done.41 = bf16[4,144,128]{2,1,0:T(8,128)(2,1)S(1)} collective-permute-done((bf16[4,144,128]{2,1,0:T(8,128)(2,1)S(1)}, bf16[4,144,128]{2,1,0:T(8,128)(2,1)S(1)}, u32[]{:S(2)}, u32[]{:S(2)}) %collective-permute-start.41) | collective-permute-done | bytes 147488 | tf_op jit(solution)/shard_map/ppermute | solution.py:456
  149.6 2.4 %flow_chunk.12 = (f32[1280,128]{1,0:T(8,128)S(1)}, f32[1,128]{1,0:T(1,128)S(1)}) custom-call(bf16[1280,2560]{1,0:T(8,128)(2,1)S(1)} %get-tuple-element.115.ptdf_ref, bf16[656,128]{1,0:T(8,128)(2,1)S(1)} %get-tuple-element.150.b0, bf16[656,128]{1,0:T(8,128)(2,1)S(1)} %collective-permute-done.48.b1, bf16[656,128]{1,0:T(8,128)(2,1)S(1)} %collective-permute-done.39.b2, ...), custom_call_target="tpu_custom_call" | custom-call | flops 104857600 | bytes 819200 | tf_op jit(solution)/shard_map/flow_chunk/pallas_call | solution.py:444
  158.2 2.3 %collective-permute-start.45 = (bf16[4,144,128]{2,1,0:T(8,128)(2,1)S(1)}, bf16[4,144,128]{2,1,0:T(8,128)(2,1)S(1)}, u32[]{:S(2)}, u32[]{:S(2)}) collective-permute-start(bf16[4,144,128]{2,1,0:T(8,128)(2,1)S(1)} %get-tuple-element.171), channel_id=1, source_target_pairs={{0,12},{1,13},{2,14},{3,15},{4,8},{5,9},{6,10},{7,11},{8,4},{9,5},... | collective-permute-start | bytes 442376 | tf_op jit(solution)/shard_map/ppermute | solution.py:456
  161.2 2.7 %flow_chunk.13 = (f32[1280,128]{1,0:T(8,128)S(1)}, f32[1,128]{1,0:T(1,128)S(1)}) custom-call(bf16[1280,2560]{1,0:T(8,128)(2,1)S(1)} %get-tuple-element.120.ptdf_ref, bf16[656,128]{1,0:T(8,128)(2,1)S(1)} %collective-permute-done.37.b0, bf16[656,128]{1,0:T(8,128)(2,1)S(1)} %collective-permute-done.52.b1, bf16[656,128]{1,0:T(8,128)(2,1)S(1)} %collective-permute-done.47.b2, ...), custom_call_target="tpu_custom_call" | custom-call | flops 104857600 | bytes 819200 | tf_op jit(solution)/shard_map/flow_chunk/pallas_call | solution.py:444
  164.2 6.7 %collective-permute-done.44.refs_2_ = bf16[4,144,128]{2,1,0:T(8,128)(2,1)S(1)} collective-permute-done((bf16[4,144,128]{2,1,0:T(8,128)(2,1)S(1)}, bf16[4,144,128]{2,1,0:T(8,128)(2,1)S(1)}, u32[]{:S(2)}, u32[]{:S(2)}) %collective-permute-start.44) | collective-permute-done | bytes 147488 | tf_op jit(solution)/shard_map/ppermute | solution.py:456
  171.1 2.2 %unpack_dispatch.1 = f32[768,128]{1,0:T(8,128)} custom-call(s32[1,768]{1,0:T(1,128)S(1)} %get-tuple-element.87.slot_ref, bf16[4,144,128]{2,1,0:T(8,128)(2,1)S(1)} %get-tuple-element.174.refs_0_, bf16[4,144,128]{2,1,0:T(8,128)(2,1)S(1)} %collective-permute-done.43.refs_1_, bf16[4,144,128]{2,1,0:T(8,128)(2,1)S(1)} %collective-permute-done.44.refs_2_, ...), custom_call_target="tpu_custom_call" | custom-call | flops 452984832 | bytes 1048576 | tf_op jit(solution)/shard_map/unpack_dispatch/pallas_call | solution.py:172
  173.3 2.4 %flow_chunk.14 = (f32[1280,128]{1,0:T(8,128)S(1)}, f32[1,128]{1,0:T(1,128)S(1)}) custom-call(bf16[1280,2560]{1,0:T(8,128)(2,1)S(1)} %get-tuple-element.126.ptdf_ref, bf16[656,128]{1,0:T(8,128)(2,1)S(1)} %collective-permute-done.38.b0, bf16[656,128]{1,0:T(8,128)(2,1)S(1)} %collective-permute-done.55.b1, bf16[656,128]{1,0:T(8,128)(2,1)S(1)} %collective-permute-done.56.b2, ...), custom_call_target="tpu_custom_call" | custom-call | flops 104857600 | bytes 819200 | tf_op jit(solution)/shard_map/flow_chunk/pallas_call | solution.py:444
  175.8 3.4 %flow_chunk.15 = (f32[1280,128]{1,0:T(8,128)}, bf16[128,1280]{1,0:T(8,128)(2,1)}, f32[1,128]{1,0:T(1,128)S(1)}) custom-call(bf16[1280,2560]{1,0:T(8,128)(2,1)S(1)} %get-tuple-element.112.ptdf_ref, bf16[656,128]{1,0:T(8,128)(2,1)S(1)} %collective-permute-done.46.b0, bf16[656,128]{1,0:T(8,128)(2,1)S(1)} %collective-permute-done.50.b1, ...), custom_call_target="tpu_custom_call" | custom-call | flops 104857600 | bytes 819200 | tf_op jit(solution)/shard_map/flow_chunk/pallas_call | solution.py:444
  (150 shorter events, 51.8 us)
Async XLA Ops:
  9.2 7.7 %collective-permute-start.1 = (bf16[128,640]{1,0:T(8,128)(2,1)}, bf16[128,640]{1,0:T(8,128)(2,1)}, u32[]{:S(2)}, u32[]{:S(2)}) collective-permute-start(bf16[128,640]{1,0:T(8,128)(2,1)} %fusion.8), channel_id=1, source_target_pairs={{0,2},{1,3},{2,0},{3,1},{4,6},{5,7},{6,4},{7,5},{8,10},{9,11},{10,... | collective-permute-start | bytes 491528 | tf_op jit(solution)/shard_map/ppermute | solution.py:456
  11.8 44.5 %all-to-all-start = ((bf16[16,160,256]{2,1,0:T(8,128)(2,1)}), bf16[16,160,256]{2,1,0:T(8,128)(2,1)S(1)}, u32[]{:S(2)}, u32[]{:S(2)}) async-start(bf16[16,160,256]{2,1,0:T(8,128)(2,1)} %get-tuple-element.107), calls=%async_computation | async-start | bytes 2621440 | tf_op jit(solution)/shard_map/all_to_all | solution.py:535
  25.5 9.4 %collective-permute-start.6 = (bf16[128,640]{1,0:T(8,128)(2,1)S(1)}, bf16[128,640]{1,0:T(8,128)(2,1)S(1)}, u32[]{:S(2)}, u32[]{:S(2)}) collective-permute-start(bf16[128,640]{1,0:T(8,128)(2,1)S(1)} %fusion.9), channel_id=1, source_target_pairs={{0,2},{1,3},{2,0},{3,1},{4,6},{5,7},{6,4},{7,5},{8,10},{9,11},{10,... | collective-permute-start | bytes 491528 | tf_op jit(solution)/shard_map/ppermute | solution.py:456
  30.9 11.8 %collective-permute-start.8 = (bf16[128,640]{1,0:T(8,128)(2,1)S(1)}, bf16[128,640]{1,0:T(8,128)(2,1)S(1)}, u32[]{:S(2)}, u32[]{:S(2)}) collective-permute-start(bf16[128,640]{1,0:T(8,128)(2,1)S(1)} %fusion.7), channel_id=1, source_target_pairs={{0,4},{1,5},{2,6},{3,7},{4,0},{5,1},{6,2},{7,3},{8,12},{9,13},{10,... | collective-permute-start | bytes 491528 | tf_op jit(solution)/shard_map/ppermute | solution.py:456
  34.9 12.2 %collective-permute-start.7 = (bf16[128,640]{1,0:T(8,128)(2,1)S(1)}, bf16[128,640]{1,0:T(8,128)(2,1)S(1)}, u32[]{:S(2)}, u32[]{:S(2)}) collective-permute-start(bf16[128,640]{1,0:T(8,128)(2,1)S(1)} %fusion.11), channel_id=1, source_target_pairs={{0,2},{1,3},{2,0},{3,1},{4,6},{5,7},{6,4},{7,5},{8,10},{9,11},{10,... | collective-permute-start | bytes 491528 | tf_op jit(solution)/shard_map/ppermute | solution.py:456
  36.3 11.5 %collective-permute-start.4 = (bf16[128,640]{1,0:T(8,128)(2,1)S(1)}, bf16[128,640]{1,0:T(8,128)(2,1)S(1)}, u32[]{:S(2)}, u32[]{:S(2)}) collective-permute-start(bf16[128,640]{1,0:T(8,128)(2,1)S(1)} %fusion.10), channel_id=1, source_target_pairs={{0,2},{1,3},{2,0},{3,1},{4,6},{5,7},{6,4},{7,5},{8,10},{9,11},{10,... | collective-permute-start | bytes 491528 | tf_op jit(solution)/shard_map/ppermute | solution.py:456
  42.7 13.5 %collective-permute-start.10 = (bf16[128,640]{1,0:T(8,128)(2,1)S(1)}, bf16[128,640]{1,0:T(8,128)(2,1)S(1)}, u32[]{:S(2)}, u32[]{:S(2)}) collective-permute-start(bf16[128,640]{1,0:T(8,128)(2,1)S(1)} %fusion.5), channel_id=1, source_target_pairs={{0,8},{1,9},{2,10},{3,11},{4,12},{5,13},{6,14},{7,15},{8,0},{9,1},... | collective-permute-start | bytes 491528 | tf_op jit(solution)/shard_map/ppermute | solution.py:456
  47.2 9.0 %collective-permute-start.9 = (bf16[128,640]{1,0:T(8,128)(2,1)S(1)}, bf16[128,640]{1,0:T(8,128)(2,1)S(1)}, u32[]{:S(2)}, u32[]{:S(2)}) collective-permute-start(bf16[128,640]{1,0:T(8,128)(2,1)S(1)} %fusion.6), channel_id=1, source_target_pairs={{0,4},{1,5},{2,6},{3,7},{4,0},{5,1},{6,2},{7,3},{8,12},{9,13},{10,... | collective-permute-start | bytes 491528 | tf_op jit(solution)/shard_map/ppermute | solution.py:456
  64.9 8.9 %collective-permute-start.11 = (bf16[656,128]{1,0:T(8,128)(2,1)S(1)}, bf16[656,128]{1,0:T(8,128)(2,1)S(1)}, u32[]{:S(2)}, u32[]{:S(2)}) collective-permute-start(bf16[656,128]{1,0:T(8,128)(2,1)S(1)} %get-tuple-element.108.b0), channel_id=1, source_target_pairs={{0,4},{1,5},{2,6},{3,7},{4,0},{5,1},{6,2},{7,3},{8,12},{9,13},{10,... | collective-permute-start | bytes 503816 | tf_op jit(solution)/shard_map/ppermute | solution.py:456
  65.2 11.0 %collective-permute-start.12 = (bf16[656,128]{1,0:T(8,128)(2,1)S(1)}, bf16[656,128]{1,0:T(8,128)(2,1)S(1)}, u32[]{:S(2)}, u32[]{:S(2)}) collective-permute-start(bf16[656,128]{1,0:T(8,128)(2,1)S(1)} %get-tuple-element.108.b0), channel_id=1, source_target_pairs={{0,8},{1,9},{2,10},{3,11},{4,12},{5,13},{6,14},{7,15},{8,0},{9,1},... | collective-permute-start | bytes 503816 | tf_op jit(solution)/shard_map/ppermute | solution.py:456
  66.7 9.4 %collective-permute-start.13 = (bf16[656,128]{1,0:T(8,128)(2,1)S(1)}, bf16[656,128]{1,0:T(8,128)(2,1)S(1)}, u32[]{:S(2)}, u32[]{:S(2)}) collective-permute-start(bf16[656,128]{1,0:T(8,128)(2,1)S(1)} %get-tuple-element.108.b0), channel_id=1, source_target_pairs={{0,2},{1,3},{2,0},{3,1},{4,6},{5,7},{6,4},{7,5},{8,10},{9,11},{10,... | collective-permute-start | bytes 503816 | tf_op jit(solution)/shard_map/ppermute | solution.py:456
  76.1 8.2 %collective-permute-start.16 = (bf16[656,128]{1,0:T(8,128)(2,1)S(1)}, bf16[656,128]{1,0:T(8,128)(2,1)S(1)}, u32[]{:S(2)}, u32[]{:S(2)}) collective-permute-start(bf16[656,128]{1,0:T(8,128)(2,1)S(1)} %collective-permute-done.11.b0), channel_id=1, source_target_pairs={{0,2},{1,3},{2,0},{3,1},{4,6},{5,7},{6,4},{7,5},{8,10},{9,11},{10,... | collective-permute-start | bytes 503816 | tf_op jit(solution)/shard_map/ppermute | solution.py:456
  77.6 7.6 %collective-permute-start.20 = (bf16[656,128]{1,0:T(8,128)(2,1)S(1)}, bf16[656,128]{1,0:T(8,128)(2,1)S(1)}, u32[]{:S(2)}, u32[]{:S(2)}) collective-permute-start(bf16[656,128]{1,0:T(8,128)(2,1)S(1)} %collective-permute-done.11.b0), channel_id=1, source_target_pairs={{0,1},{1,0},{2,3},{3,2},{4,5},{5,4},{6,7},{7,6},{8,9},{9,8},{10,11... | collective-permute-start | bytes 503816 | tf_op jit(solution)/shard_map/ppermute | solution.py:456
  77.9 8.6 %collective-permute-start.24 = (bf16[656,128]{1,0:T(8,128)(2,1)S(1)}, bf16[656,128]{1,0:T(8,128)(2,1)S(1)}, u32[]{:S(2)}, u32[]{:S(2)}) collective-permute-start(bf16[656,128]{1,0:T(8,128)(2,1)S(1)} %collective-permute-done.12.b0), channel_id=1, source_target_pairs={{0,2},{1,3},{2,0},{3,1},{4,6},{5,7},{6,4},{7,5},{8,10},{9,11},{10,... | collective-permute-start | bytes 503816 | tf_op jit(solution)/shard_map/ppermute | solution.py:456
  85.2 9.2 %collective-permute-start.18 = (bf16[656,128]{1,0:T(8,128)(2,1)S(1)}, bf16[656,128]{1,0:T(8,128)(2,1)S(1)}, u32[]{:S(2)}, u32[]{:S(2)}) collective-permute-start(bf16[656,128]{1,0:T(8,128)(2,1)S(1)} %collective-permute-done.15.b0), channel_id=1, source_target_pairs={{0,1},{1,0},{2,3},{3,2},{4,5},{5,4},{6,7},{7,6},{8,9},{9,8},{10,11... | collective-permute-start | bytes 503816 | tf_op jit(solution)/shard_map/ppermute | solution.py:456
  103.2 8.6 %collective-permute-start.32 = (bf16[128,640]{1,0:T(8,128)(2,1)S(1)}, bf16[128,640]{1,0:T(8,128)(2,1)S(1)}, u32[]{:S(2)}, u32[]{:S(2)}) collective-permute-start(bf16[128,640]{1,0:T(8,128)(2,1)S(1)} %fusion.13), channel_id=1, source_target_pairs={{0,2},{1,3},{2,0},{3,1},{4,6},{5,7},{6,4},{7,5},{8,10},{9,11},{10,... | collective-permute-start | bytes 491528 | tf_op jit(solution)/shard_map/ppermute | solution.py:456
  112.4 8.8 %collective-permute-start.30 = (bf16[128,640]{1,0:T(8,128)(2,1)S(1)}, bf16[128,640]{1,0:T(8,128)(2,1)S(1)}, u32[]{:S(2)}, u32[]{:S(2)}) collective-permute-start(bf16[128,640]{1,0:T(8,128)(2,1)S(1)} %fusion.14), channel_id=1, source_target_pairs={{0,2},{1,3},{2,0},{3,1},{4,6},{5,7},{6,4},{7,5},{8,10},{9,11},{10,... | collective-permute-start | bytes 491528 | tf_op jit(solution)/shard_map/ppermute | solution.py:456
  117.3 10.4 %collective-permute-start.36 = (bf16[128,640]{1,0:T(8,128)(2,1)S(1)}, bf16[128,640]{1,0:T(8,128)(2,1)S(1)}, u32[]{:S(2)}, u32[]{:S(2)}) collective-permute-start(bf16[128,640]{1,0:T(8,128)(2,1)S(1)} %fusion.1), channel_id=1, source_target_pairs={{0,8},{1,9},{2,10},{3,11},{4,12},{5,13},{6,14},{7,15},{8,0},{9,1},... | collective-permute-start | bytes 491528 | tf_op jit(solution)/shard_map/ppermute | solution.py:456
  119.0 8.8 %collective-permute-start.35 = (bf16[128,640]{1,0:T(8,128)(2,1)S(1)}, bf16[128,640]{1,0:T(8,128)(2,1)S(1)}, u32[]{:S(2)}, u32[]{:S(2)}) collective-permute-start(bf16[128,640]{1,0:T(8,128)(2,1)S(1)} %fusion.2), channel_id=1, source_target_pairs={{0,4},{1,5},{2,6},{3,7},{4,0},{5,1},{6,2},{7,3},{8,12},{9,13},{10,... | collective-permute-start | bytes 491528 | tf_op jit(solution)/shard_map/ppermute | solution.py:456
  132.7 13.4 %collective-permute-start.37 = (bf16[656,128]{1,0:T(8,128)(2,1)S(1)}, bf16[656,128]{1,0:T(8,128)(2,1)S(1)}, u32[]{:S(2)}, u32[]{:S(2)}) collective-permute-start(bf16[656,128]{1,0:T(8,128)(2,1)S(1)} %get-tuple-element.150.b0), channel_id=1, source_target_pairs={{0,4},{1,5},{2,6},{3,7},{4,0},{5,1},{6,2},{7,3},{8,12},{9,13},{10,... | collective-permute-start | bytes 503816 | tf_op jit(solution)/shard_map/ppermute | solution.py:456
  132.8 13.4 %collective-permute-start.38 = (bf16[656,128]{1,0:T(8,128)(2,1)S(1)}, bf16[656,128]{1,0:T(8,128)(2,1)S(1)}, u32[]{:S(2)}, u32[]{:S(2)}) collective-permute-start(bf16[656,128]{1,0:T(8,128)(2,1)S(1)} %get-tuple-element.150.b0), channel_id=1, source_target_pairs={{0,8},{1,9},{2,10},{3,11},{4,12},{5,13},{6,14},{7,15},{8,0},{9,1},... | collective-permute-start | bytes 503816 | tf_op jit(solution)/shard_map/ppermute | solution.py:456
  134.8 11.3 %collective-permute-start.39 = (bf16[656,128]{1,0:T(8,128)(2,1)S(1)}, bf16[656,128]{1,0:T(8,128)(2,1)S(1)}, u32[]{:S(2)}, u32[]{:S(2)}) collective-permute-start(bf16[656,128]{1,0:T(8,128)(2,1)S(1)} %get-tuple-element.150.b0), channel_id=1, source_target_pairs={{0,2},{1,3},{2,0},{3,1},{4,6},{5,7},{6,4},{7,5},{8,10},{9,11},{10,... | collective-permute-start | bytes 503816 | tf_op jit(solution)/shard_map/ppermute | solution.py:456
  135.3 9.8 %collective-permute-start.41 = (bf16[4,144,128]{2,1,0:T(8,128)(2,1)S(1)}, bf16[4,144,128]{2,1,0:T(8,128)(2,1)S(1)}, u32[]{:S(2)}, u32[]{:S(2)}) collective-permute-start(bf16[4,144,128]{2,1,0:T(8,128)(2,1)S(1)} %get-tuple-element.176), channel_id=1, source_target_pairs={{0,2},{1,3},{2,0},{3,1},{4,6},{5,7},{6,4},{7,5},{8,10},{9,11},{10,... | collective-permute-start | bytes 442376 | tf_op jit(solution)/shard_map/ppermute | solution.py:456
  136.9 9.3 %collective-permute-start.42 = (bf16[4,144,128]{2,1,0:T(8,128)(2,1)S(1)}, bf16[4,144,128]{2,1,0:T(8,128)(2,1)S(1)}, u32[]{:S(2)}, u32[]{:S(2)}) collective-permute-start(bf16[4,144,128]{2,1,0:T(8,128)(2,1)S(1)} %get-tuple-element.178), channel_id=1, source_target_pairs={{0,3},{1,2},{2,1},{3,0},{4,7},{5,6},{6,5},{7,4},{8,11},{9,10},{10,... | collective-permute-start | bytes 442376 | tf_op jit(solution)/shard_map/ppermute | solution.py:456
  147.9 9.1 %collective-permute-start.52 = (bf16[656,128]{1,0:T(8,128)(2,1)S(1)}, bf16[656,128]{1,0:T(8,128)(2,1)S(1)}, u32[]{:S(2)}, u32[]{:S(2)}) collective-permute-start(bf16[656,128]{1,0:T(8,128)(2,1)S(1)} %collective-permute-done.37.b0), channel_id=1, source_target_pairs={{0,1},{1,0},{2,3},{3,2},{4,5},{5,4},{6,7},{7,6},{8,9},{9,8},{10,11... | collective-permute-start | bytes 503816 | tf_op jit(solution)/shard_map/ppermute | solution.py:456
  148.0 10.2 %collective-permute-start.56 = (bf16[656,128]{1,0:T(8,128)(2,1)S(1)}, bf16[656,128]{1,0:T(8,128)(2,1)S(1)}, u32[]{:S(2)}, u32[]{:S(2)}) collective-permute-start(bf16[656,128]{1,0:T(8,128)(2,1)S(1)} %collective-permute-done.38.b0), channel_id=1, source_target_pairs={{0,2},{1,3},{2,0},{3,1},{4,6},{5,7},{6,4},{7,5},{8,10},{9,11},{10,... | collective-permute-start | bytes 503816 | tf_op jit(solution)/shard_map/ppermute | solution.py:456
  155.1 9.0 %collective-permute-start.43 = (bf16[4,144,128]{2,1,0:T(8,128)(2,1)S(1)}, bf16[4,144,128]{2,1,0:T(8,128)(2,1)S(1)}, u32[]{:S(2)}, u32[]{:S(2)}) collective-permute-start(bf16[4,144,128]{2,1,0:T(8,128)(2,1)S(1)} %get-tuple-element.173), channel_id=1, source_target_pairs={{0,4},{1,5},{2,6},{3,7},{4,0},{5,1},{6,2},{7,3},{8,12},{9,13},{10,... | collective-permute-start | bytes 442376 | tf_op jit(solution)/shard_map/ppermute | solution.py:456
  157.0 13.9 %collective-permute-start.44 = (bf16[4,144,128]{2,1,0:T(8,128)(2,1)S(1)}, bf16[4,144,128]{2,1,0:T(8,128)(2,1)S(1)}, u32[]{:S(2)}, u32[]{:S(2)}) collective-permute-start(bf16[4,144,128]{2,1,0:T(8,128)(2,1)S(1)} %get-tuple-element.172), channel_id=1, source_target_pairs={{0,8},{1,9},{2,10},{3,11},{4,12},{5,13},{6,14},{7,15},{8,0},{9,1},... | collective-permute-start | bytes 442376 | tf_op jit(solution)/shard_map/ppermute | solution.py:456
  158.2 12.9 %collective-permute-start.45 = (bf16[4,144,128]{2,1,0:T(8,128)(2,1)S(1)}, bf16[4,144,128]{2,1,0:T(8,128)(2,1)S(1)}, u32[]{:S(2)}, u32[]{:S(2)}) collective-permute-start(bf16[4,144,128]{2,1,0:T(8,128)(2,1)S(1)} %get-tuple-element.171), channel_id=1, source_target_pairs={{0,12},{1,13},{2,14},{3,15},{4,8},{5,9},{6,10},{7,11},{8,4},{9,5},... | collective-permute-start | bytes 442376 | tf_op jit(solution)/shard_map/ppermute | solution.py:456
  160.7 12.6 %collective-permute-start.55 = (bf16[656,128]{1,0:T(8,128)(2,1)S(1)}, bf16[656,128]{1,0:T(8,128)(2,1)S(1)}, u32[]{:S(2)}, u32[]{:S(2)}) collective-permute-start(bf16[656,128]{1,0:T(8,128)(2,1)S(1)} %collective-permute-done.38.b0), channel_id=1, source_target_pairs={{0,1},{1,0},{2,3},{3,2},{4,5},{5,4},{6,7},{7,6},{8,9},{9,8},{10,11... | collective-permute-start | bytes 503816 | tf_op jit(solution)/shard_map/ppermute | solution.py:456
  160.7 12.6 %collective-permute-start.57 = (bf16[656,128]{1,0:T(8,128)(2,1)S(1)}, bf16[656,128]{1,0:T(8,128)(2,1)S(1)}, u32[]{:S(2)}, u32[]{:S(2)}) collective-permute-start(bf16[656,128]{1,0:T(8,128)(2,1)S(1)} %collective-permute-done.56.b2), channel_id=1, source_target_pairs={{0,1},{1,0},{2,3},{3,2},{4,5},{5,4},{6,7},{7,6},{8,9},{9,8},{10,11... | collective-permute-start | bytes 503816 | tf_op jit(solution)/shard_map/ppermute | solution.py:456
  164.2 11.6 %collective-permute-start.50 = (bf16[656,128]{1,0:T(8,128)(2,1)S(1)}, bf16[656,128]{1,0:T(8,128)(2,1)S(1)}, u32[]{:S(2)}, u32[]{:S(2)}) collective-permute-start(bf16[656,128]{1,0:T(8,128)(2,1)S(1)} %collective-permute-done.46.b0), channel_id=1, source_target_pairs={{0,1},{1,0},{2,3},{3,2},{4,5},{5,4},{6,7},{7,6},{8,9},{9,8},{10,11... | collective-permute-start | bytes 503816 | tf_op jit(solution)/shard_map/ppermute | solution.py:456
  (37 other events, 233.9 us)

commit v11 on v10

--- a/solution.py
+++ b/solution.py
@@ -553,7 +553,7 @@
             recv = lax.all_to_all(outgoing, "bus", split_axis=0, concat_axis=0, tiled=True) if recv is None else recv
             shadow = lax.dot_general(ptdf, line_half, (((0,), (0,)), ((), ())), preferred_element_type=F32)
             prices = [lax.psum_scatter(shadow, "bus", scatter_dimension=0, tiled=True).T]
-        chunks = (0, 1) if staged and not last else ()
+        chunks = (0,) if staged and not last else ()
         held, block, *loaded = update(
             cap, place if staged else near_place, last, prices, balance_row, demand, recv, held, ptdf, chunks
         )
@@ -580,7 +580,7 @@
                 stage += [swap(home[:, rel], devices, rel) for rel in (1, 2, 3)]
             else:
                 cross[0], here = lax.optimization_barrier((cross[0], place))
-                place, (resident[2], resident[3]) = load_chunks((2, 3), here, ptdf, buses)
+                place, (resident[1], resident[2]) = load_chunks((1, 2), here, ptdf, buses)
                 stage.append(place)
             near[1], near[2], far[0], *rest = lax.optimization_barrier(stage)
             near[3] = swap(near[2], devices, 4)
@@ -593,7 +593,10 @@
             else:
                 (place,) = rest
             acc, total = flow_chunk(resident[0], blocks(0), None, balance_row, weight=weight)
-            near[3], far[1], acc = lax.optimization_barrier((near[3], far[1], acc))
+            if not last:
+                acc, here = lax.optimization_barrier((acc, place))
+                place, (resident[3],) = load_chunks((3,), here, ptdf, buses)
+            near[3], far[1], acc, place = lax.optimization_barrier((near[3], far[1], acc, place))
             spread(3)
             settle_far(1)
             acc, total = flow_chunk(resident[1], blocks(1), acc, total, weight=weight)

time: 180 us -> 180 us (level)
  waiting for transfers between devices: 62.7 us -> 52.4 us
  starting transfers between devices: 45.4 us -> 53.7 us
  Pallas kernels: 66.9 us -> 69 us
    ppermute x58, waiting for transfers between devices: 62.7 us -> 52.4 us  [swap(): return lax.ppermute(x, 'bus', [(i, i ^ mask) for i in range(devices)])]
    ppermute x58, starting transfers between devices: 40.4 us -> 48.7 us  [swap(): return lax.ppermute(x, 'bus', [(i, i ^ mask) for i in range(devices)])]
    pallas_call x1 -> x2, Pallas kernels: 5.44 us -> 9.58 us  [load_chunks(): pl.pallas_call(functools.partial(load_kernel, chunks), in_specs=[SMEM_SPE...]
    pallas_call x2, Pallas kernels: 13.3 us -> 11.3 us  [update(): pl.pallas_call(functools.partial(update_kernel, cap, devices, first, last...]
  transfers between devices with their start and end apart: 59 -> 59, of which waited for: 25 -> 20; matrix products, arithmetic and copies ran while one was open for 1% -> 1% of each run, Pallas kernels for 23% -> 26%
where the time goes in v11:
time: 180 us
  Pallas kernels  69 us (38%)
  starting transfers between devices  53.7 us (30%)
  waiting for transfers between devices  52.4 us (29%)
  other arithmetic  2.97 us (2%)
    ppermute x58, waiting for transfers between devices, swap(): return lax.ppermute(x, 'bus', [(i, i ^ mask) for i in range(devices)])  52.4 us
    ppermute x58, starting transfers between devices, swap(): return lax.ppermute(x, 'bus', [(i, i ^ mask) for i in range(devices)])  48.7 us
    pallas_call x8, Pallas kernels, shadow_chunk(): pl.pallas_call(functools.partial(shadow_kernel, chunk, stream, turn), in_...  21.4 us
    pallas_call x8, Pallas kernels, flow_chunk(): pl.pallas_call(functools.partial(flow_kernel, start, end), in_specs=[VMEM...  20.9 us
    pallas_call x2, Pallas kernels, update(): pl.pallas_call(functools.partial(update_kernel, cap, devices, first, last...  11.3 us
    pallas_call x2, Pallas kernels, load_chunks(): pl.pallas_call(functools.partial(load_kernel, chunks), in_specs=[SMEM_SPE...  9.58 us
    all_to_all x1, starting transfers between devices, local(): lax.all_to_all(outgoing, 'bus', split_axis=0, concat_axis=0, tiled=True)  4.98 us
  transfers between devices with their start and end apart: 59, of which 20 were waited for; matrix products, arithmetic and copies ran while one was open for 1% of the time, Pallas kernels for 26%

profile of v11, /device:TPU:0, one launch (start us, length us, event | category | flops | bytes accessed | tf_op | source)
XLA Modules:
  0.0 179.7 jit_solution(6513781325626010942)
XLA Ops:
  0.7 3.7 %shadow_chunk.8 = (f32[2,128,640]{2,1,0:T(8,128)S(1)}, bf16[2,128,640]{2,1,0:T(8,128)(2,1)S(1)}, bf16[128,1280]{1,0:T(8,128)(2,1)S(1)}) custom-call(s32[1]{0:T(128)} %bitcast.place_ref, f32[1280,128]{1,0:T(8,128)} %rest_1_.1, bf16[1280,10240]{1,0:T(8,128)(2,1)} %ptdf_ref.11), custom_call_target="tpu_custom_call" | custom-call | flops 2516582400 | bytes 6553600 | tf_op jit(solution)/shard_map/shadow_chunk/pallas_call | solution.py:346
  4.9 3.6 %pack_generators.1 = (bf16[16,160,256]{2,1,0:T(8,128)(2,1)}, s32[1,768]{1,0:T(1,128)S(1)}) custom-call(s32[1]{0:T(128)} %bitcast.place_ref, s32[1,768]{1,0:T(1,128)S(1)} %bitcast.88, s32[6,128]{1,0:T(8,128)S(1)} %bitcast.86, f32[6,128]{1,0:T(8,128)S(1)} %bitcast.87, f32[768,128]{1,0:T(8,128)S(1)} %copy-done.1, f32[6,128]{1,0:T(8,128)S(1)} %bitcast.82, ...), custom_call_target="tpu_custom_call" | custom-call | flops 905969664 | bytes 3145728 | tf_op jit(solution)/shard_map/pack_generators/pallas_call | solution.py:107
  9.2 2.6 %collective-permute-start.1 = (bf16[128,640]{1,0:T(8,128)(2,1)}, bf16[128,640]{1,0:T(8,128)(2,1)}, u32[]{:S(2)}, u32[]{:S(2)}) collective-permute-start(bf16[128,640]{1,0:T(8,128)(2,1)} %fusion.8), channel_id=1, source_target_pairs={{0,2},{1,3},{2,0},{3,1},{4,6},{5,7},{6,4},{7,5},{8,10},{9,11},{10,... | collective-permute-start | bytes 491528 | tf_op jit(solution)/shard_map/ppermute | solution.py:456
  11.8 5.0 %all-to-all-start = ((bf16[16,160,256]{2,1,0:T(8,128)(2,1)}), bf16[16,160,256]{2,1,0:T(8,128)(2,1)S(1)}, u32[]{:S(2)}, u32[]{:S(2)}) async-start(bf16[16,160,256]{2,1,0:T(8,128)(2,1)} %get-tuple-element.111), calls=%async_computation | async-start | bytes 2621440 | tf_op jit(solution)/shard_map/all_to_all | solution.py:535
  17.9 3.4 %shadow_chunk.9 = (f32[2,128,640]{2,1,0:T(8,128)S(1)}, bf16[2,128,640]{2,1,0:T(8,128)(2,1)S(1)}) custom-call(s32[1]{0:T(128)} %bitcast.place_ref, bf16[128,1280]{1,0:T(8,128)(2,1)S(1)} %get-tuple-element.101.line_ref, bf16[1280,10240]{1,0:T(8,128)(2,1)} %ptdf_ref.11), custom_call_target="tpu_custom_call" | custom-call | flops 2516582400 | bytes 6553600 | tf_op jit(solution)/shard_map/shadow_chunk/pallas_call | solution.py:346
  21.7 3.4 %shadow_chunk.11 = (f32[2,128,640]{2,1,0:T(8,128)S(1)}, bf16[2,128,640]{2,1,0:T(8,128)(2,1)S(1)}) custom-call(s32[1]{0:T(128)} %bitcast.place_ref, bf16[128,1280]{1,0:T(8,128)(2,1)S(1)} %get-tuple-element.101.line_ref, bf16[1280,10240]{1,0:T(8,128)(2,1)} %ptdf_ref.11), custom_call_target="tpu_custom_call" | custom-call | flops 2516582400 | bytes 6553600 | tf_op jit(solution)/shard_map/shadow_chunk/pallas_call | solution.py:346
  27.3 3.4 %shadow_chunk.10 = (f32[2,128,640]{2,1,0:T(8,128)S(1)}, bf16[2,128,640]{2,1,0:T(8,128)(2,1)S(1)}) custom-call(s32[1]{0:T(128)} %bitcast.place_ref, bf16[128,1280]{1,0:T(8,128)(2,1)S(1)} %get-tuple-element.101.line_ref, bf16[1280,10240]{1,0:T(8,128)(2,1)} %ptdf_ref.11), custom_call_target="tpu_custom_call" | custom-call | flops 2516582400 | bytes 6553600 | tf_op jit(solution)/shard_map/shadow_chunk/pallas_call | solution.py:346
  32.5 2.4 %collective-permute-done.6 = bf16[128,640]{1,0:T(8,128)(2,1)S(1)} collective-permute-done((bf16[128,640]{1,0:T(8,128)(2,1)S(1)}, bf16[128,640]{1,0:T(8,128)(2,1)S(1)}, u32[]{:S(2)}, u32[]{:S(2)}) %collective-permute-start.6) | collective-permute-done | bytes 163872 | tf_op jit(solution)/shard_map/ppermute | solution.py:456
  37.1 5.5 %collective-permute-done.8 = bf16[128,640]{1,0:T(8,128)(2,1)S(1)} collective-permute-done((bf16[128,640]{1,0:T(8,128)(2,1)S(1)}, bf16[128,640]{1,0:T(8,128)(2,1)S(1)}, u32[]{:S(2)}, u32[]{:S(2)}) %collective-permute-start.8) | collective-permute-done | bytes 163872 | tf_op jit(solution)/shard_map/ppermute | solution.py:456
  42.7 4.4 %collective-permute-start.10 = (bf16[128,640]{1,0:T(8,128)(2,1)S(1)}, bf16[128,640]{1,0:T(8,128)(2,1)S(1)}, u32[]{:S(2)}, u32[]{:S(2)}) collective-permute-start(bf16[128,640]{1,0:T(8,128)(2,1)S(1)} %fusion.5), channel_id=1, source_target_pairs={{0,8},{1,9},{2,10},{3,11},{4,12},{5,13},{6,14},{7,15},{8,0},{9,1},... | collective-permute-start | bytes 491528 | tf_op jit(solution)/shard_map/ppermute | solution.py:456
  47.9 8.3 %collective-permute-done.9.refs_1_ = bf16[128,640]{1,0:T(8,128)(2,1)S(1)} collective-permute-done((bf16[128,640]{1,0:T(8,128)(2,1)S(1)}, bf16[128,640]{1,0:T(8,128)(2,1)S(1)}, u32[]{:S(2)}, u32[]{:S(2)}) %collective-permute-start.9) | collective-permute-done | bytes 163872 | tf_op jit(solution)/shard_map/ppermute | solution.py:456
  56.3 6.5 %update_generators.2 = (f32[16,144,128]{2,1,0:T(8,128)S(1)}, bf16[656,128]{1,0:T(8,128)(2,1)S(1)}, bf16[1280,2560]{1,0:T(8,128)(2,1)S(1)}) custom-call(s32[1]{0:T(128)} %bitcast.place_ref, f32[128,640]{1,0:T(8,128)S(1)} %bitcast_add_fusion.6.refs_0_, bf16[128,640]{1,0:T(8,128)(2,1)S(1)} %collective-permute-done.9.refs_1_, ...), custom_call_target="tpu_custom_call" | custom-call | flops 1509949440 | bytes 4194304 | tf_op jit(solution)/shard_map/update_generators/pallas_call | solution.py:276
  66.2 5.4 %load_chunks.2 = (s32[1]{0:T(128)}, bf16[1280,2560]{1,0:T(8,128)(2,1)S(1)}, bf16[1280,2560]{1,0:T(8,128)(2,1)S(1)}) custom-call(s32[1]{0:T(128)} %bitcast.place_ref, bf16[1280,10240]{1,0:T(8,128)(2,1)} %ptdf_ref.11), custom_call_target="tpu_custom_call" | custom-call | bytes 13107200 | tf_op jit(solution)/shard_map/load_chunks/pallas_call | solution.py:387
  71.8 2.3 %collective-permute-done.12.b0 = bf16[656,128]{1,0:T(8,128)(2,1)S(1)} collective-permute-done((bf16[656,128]{1,0:T(8,128)(2,1)S(1)}, bf16[656,128]{1,0:T(8,128)(2,1)S(1)}, u32[]{:S(2)}, u32[]{:S(2)}) %collective-permute-start.12) | collective-permute-done | bytes 167968 | tf_op jit(solution)/shard_map/ppermute | solution.py:456
  76.4 2.4 %flow_chunk.8 = (f32[1280,128]{1,0:T(8,128)S(1)}, f32[1,128]{1,0:T(1,128)S(1)}) custom-call(bf16[1280,2560]{1,0:T(8,128)(2,1)S(1)} %get-tuple-element.117.ptdf_ref, bf16[656,128]{1,0:T(8,128)(2,1)S(1)} %get-tuple-element.112.b0, bf16[656,128]{1,0:T(8,128)(2,1)S(1)} %collective-permute-done.14.b1, bf16[656,128]{1,0:T(8,128)(2,1)S(1)} %collective-permute-done.13.b2, ...), custom_call_target="tpu_custom_call" | custom-call | flops 2516582400 | bytes 6553600 | tf_op jit(solution)/shard_map/flow_chunk/pallas_call | solution.py:444
  78.8 4.1 %load_chunks.3 = (s32[1]{0:T(128)}, bf16[1280,2560]{1,0:T(8,128)(2,1)S(1)}) custom-call(s32[1]{0:T(128)} %get-tuple-element.123.place_ref, bf16[1280,10240]{1,0:T(8,128)(2,1)} %ptdf_ref.11), custom_call_target="tpu_custom_call" | custom-call | bytes 6553600 | tf_op jit(solution)/shard_map/load_chunks/pallas_call | solution.py:387
  85.6 2.4 %flow_chunk.9 = (f32[1280,128]{1,0:T(8,128)S(1)}, f32[1,128]{1,0:T(1,128)S(1)}) custom-call(bf16[1280,2560]{1,0:T(8,128)(2,1)S(1)} %get-tuple-element.128.ptdf_ref, bf16[656,128]{1,0:T(8,128)(2,1)S(1)} %collective-permute-done.11.b0, bf16[656,128]{1,0:T(8,128)(2,1)S(1)} %collective-permute-done.20.b1, bf16[656,128]{1,0:T(8,128)(2,1)S(1)} %collective-permute-done.16.b2, ...), custom_call_target="tpu_custom_call" | custom-call | flops 2516582400 | bytes 6553600 | tf_op jit(solution)/shard_map/flow_chunk/pallas_call | solution.py:444
  88.0 2.5 %collective-permute-done.19.b2 = bf16[656,128]{1,0:T(8,128)(2,1)S(1)} collective-permute-done((bf16[656,128]{1,0:T(8,128)(2,1)S(1)}, bf16[656,128]{1,0:T(8,128)(2,1)S(1)}, u32[]{:S(2)}, u32[]{:S(2)}) %collective-permute-start.19) | collective-permute-done | bytes 167968 | tf_op jit(solution)/shard_map/ppermute | solution.py:456
  90.6 2.4 %flow_chunk.10 = (f32[1280,128]{1,0:T(8,128)S(1)}, f32[1,128]{1,0:T(1,128)S(1)}) custom-call(bf16[1280,2560]{1,0:T(8,128)(2,1)S(1)} %get-tuple-element.134.ptdf_ref, bf16[656,128]{1,0:T(8,128)(2,1)S(1)} %collective-permute-done.12.b0, bf16[656,128]{1,0:T(8,128)(2,1)S(1)} %collective-permute-done.23.b1, bf16[656,128]{1,0:T(8,128)(2,1)S(1)} %collective-permute-done.24.b2, ...), custom_call_target="tpu_custom_call" | custom-call | flops 2516582400 | bytes 6553600 | tf_op jit(solution)/shard_map/flow_chunk/pallas_call | solution.py:444
  93.0 2.8 %flow_chunk.11 = (f32[1280,128]{1,0:T(8,128)S(1)}, bf16[128,1280]{1,0:T(8,128)(2,1)S(1)}, f32[1,128]{1,0:T(1,128)S(1)}) custom-call(bf16[1280,2560]{1,0:T(8,128)(2,1)S(1)} %get-tuple-element.126.ptdf_ref, bf16[656,128]{1,0:T(8,128)(2,1)S(1)} %collective-permute-done.15.b0, bf16[656,128]{1,0:T(8,128)(2,1)S(1)} %collective-permute-done.18.b1, ...), custom_call_target="tpu_custom_call" | custom-call | flops 2516582400 | bytes 6553600 | tf_op jit(solution)/shard_map/flow_chunk/pallas_call | solution.py:444
  113.7 2.5 %collective-permute-done.34 = bf16[128,640]{1,0:T(8,128)(2,1)S(1)} collective-permute-done((bf16[128,640]{1,0:T(8,128)(2,1)S(1)}, bf16[128,640]{1,0:T(8,128)(2,1)S(1)}, u32[]{:S(2)}, u32[]{:S(2)}) %collective-permute-start.34) | collective-permute-done | bytes 163872 | tf_op jit(solution)/shard_map/ppermute | solution.py:456
  121.4 4.2 %collective-permute-done.35.refs_1_ = bf16[128,640]{1,0:T(8,128)(2,1)S(1)} collective-permute-done((bf16[128,640]{1,0:T(8,128)(2,1)S(1)}, bf16[128,640]{1,0:T(8,128)(2,1)S(1)}, u32[]{:S(2)}, u32[]{:S(2)}) %collective-permute-start.35) | collective-permute-done | bytes 163872 | tf_op jit(solution)/shard_map/ppermute | solution.py:456
  126.7 4.8 %update_generators.3 = (bf16[16,144,128]{2,1,0:T(8,128)(2,1)S(1)}, bf16[656,128]{1,0:T(8,128)(2,1)S(1)}) custom-call(s32[1]{0:T(128)} %get-tuple-element.125.place_ref, f32[128,640]{1,0:T(8,128)S(1)} %bitcast_add_fusion.2.refs_0_, bf16[128,640]{1,0:T(8,128)(2,1)S(1)} %collective-permute-done.35.refs_1_, ...), custom_call_target="tpu_custom_call" | custom-call | flops 1509949440 | bytes 4194304 | tf_op jit(solution)/shard_map/update_generators/pallas_call | solution.py:276
  136.4 7.9 %collective-permute-done.41 = bf16[4,144,128]{2,1,0:T(8,128)(2,1)S(1)} collective-permute-done((bf16[4,144,128]{2,1,0:T(8,128)(2,1)S(1)}, bf16[4,144,128]{2,1,0:T(8,128)(2,1)S(1)}, u32[]{:S(2)}, u32[]{:S(2)}) %collective-permute-start.41) | collective-permute-done | bytes 147488 | tf_op jit(solution)/shard_map/ppermute | solution.py:456
  149.8 2.4 %flow_chunk.12 = (f32[1280,128]{1,0:T(8,128)S(1)}, f32[1,128]{1,0:T(1,128)S(1)}) custom-call(bf16[1280,2560]{1,0:T(8,128)(2,1)S(1)} %get-tuple-element.117.ptdf_ref, bf16[656,128]{1,0:T(8,128)(2,1)S(1)} %get-tuple-element.158.b0, bf16[656,128]{1,0:T(8,128)(2,1)S(1)} %collective-permute-done.48.b1, bf16[656,128]{1,0:T(8,128)(2,1)S(1)} %collective-permute-done.39.b2, ...), custom_call_target="tpu_custom_call" | custom-call | flops 104857600 | bytes 819200 | tf_op jit(solution)/shard_map/flow_chunk/pallas_call | solution.py:444
  152.5 2.3 %collective-permute-done.47.b2 = bf16[656,128]{1,0:T(8,128)(2,1)S(1)} collective-permute-done((bf16[656,128]{1,0:T(8,128)(2,1)S(1)}, bf16[656,128]{1,0:T(8,128)(2,1)S(1)}, u32[]{:S(2)}, u32[]{:S(2)}) %collective-permute-start.47) | collective-permute-done | bytes 167968 | tf_op jit(solution)/shard_map/ppermute | solution.py:456
  158.5 2.3 %collective-permute-start.45 = (bf16[4,144,128]{2,1,0:T(8,128)(2,1)S(1)}, bf16[4,144,128]{2,1,0:T(8,128)(2,1)S(1)}, u32[]{:S(2)}, u32[]{:S(2)}) collective-permute-start(bf16[4,144,128]{2,1,0:T(8,128)(2,1)S(1)} %get-tuple-element.179), channel_id=1, source_target_pairs={{0,12},{1,13},{2,14},{3,15},{4,8},{5,9},{6,10},{7,11},{8,4},{9,5},... | collective-permute-start | bytes 442376 | tf_op jit(solution)/shard_map/ppermute | solution.py:456
  161.3 2.7 %flow_chunk.13 = (f32[1280,128]{1,0:T(8,128)S(1)}, f32[1,128]{1,0:T(1,128)S(1)}) custom-call(bf16[1280,2560]{1,0:T(8,128)(2,1)S(1)} %get-tuple-element.128.ptdf_ref, bf16[656,128]{1,0:T(8,128)(2,1)S(1)} %collective-permute-done.37.b0, bf16[656,128]{1,0:T(8,128)(2,1)S(1)} %collective-permute-done.52.b1, bf16[656,128]{1,0:T(8,128)(2,1)S(1)} %collective-permute-done.47.b2, ...), custom_call_target="tpu_custom_call" | custom-call | flops 104857600 | bytes 819200 | tf_op jit(solution)/shard_map/flow_chunk/pallas_call | solution.py:444
  165.3 5.7 %collective-permute-done.44.refs_2_ = bf16[4,144,128]{2,1,0:T(8,128)(2,1)S(1)} collective-permute-done((bf16[4,144,128]{2,1,0:T(8,128)(2,1)S(1)}, bf16[4,144,128]{2,1,0:T(8,128)(2,1)S(1)}, u32[]{:S(2)}, u32[]{:S(2)}) %collective-permute-start.44) | collective-permute-done | bytes 147488 | tf_op jit(solution)/shard_map/ppermute | solution.py:456
  171.1 2.2 %unpack_dispatch.1 = f32[768,128]{1,0:T(8,128)} custom-call(s32[1,768]{1,0:T(1,128)S(1)} %get-tuple-element.91.slot_ref, bf16[4,144,128]{2,1,0:T(8,128)(2,1)S(1)} %get-tuple-element.182.refs_0_, bf16[4,144,128]{2,1,0:T(8,128)(2,1)S(1)} %collective-permute-done.43.refs_1_, bf16[4,144,128]{2,1,0:T(8,128)(2,1)S(1)} %collective-permute-done.44.refs_2_, ...), custom_call_target="tpu_custom_call" | custom-call | flops 452984832 | bytes 1048576 | tf_op jit(solution)/shard_map/unpack_dispatch/pallas_call | solution.py:172
  173.4 2.4 %flow_chunk.14 = (f32[1280,128]{1,0:T(8,128)S(1)}, f32[1,128]{1,0:T(1,128)S(1)}) custom-call(bf16[1280,2560]{1,0:T(8,128)(2,1)S(1)} %get-tuple-element.134.ptdf_ref, bf16[656,128]{1,0:T(8,128)(2,1)S(1)} %collective-permute-done.38.b0, bf16[656,128]{1,0:T(8,128)(2,1)S(1)} %collective-permute-done.55.b1, bf16[656,128]{1,0:T(8,128)(2,1)S(1)} %collective-permute-done.56.b2, ...), custom_call_target="tpu_custom_call" | custom-call | flops 104857600 | bytes 819200 | tf_op jit(solution)/shard_map/flow_chunk/pallas_call | solution.py:444
  175.8 3.4 %flow_chunk.15 = (f32[1280,128]{1,0:T(8,128)}, bf16[128,1280]{1,0:T(8,128)(2,1)}, f32[1,128]{1,0:T(1,128)S(1)}) custom-call(bf16[1280,2560]{1,0:T(8,128)(2,1)S(1)} %get-tuple-element.126.ptdf_ref, bf16[656,128]{1,0:T(8,128)(2,1)S(1)} %collective-permute-done.46.b0, bf16[656,128]{1,0:T(8,128)(2,1)S(1)} %collective-permute-done.50.b1, ...), custom_call_target="tpu_custom_call" | custom-call | flops 104857600 | bytes 819200 | tf_op jit(solution)/shard_map/flow_chunk/pallas_call | solution.py:444
  (151 shorter events, 59.0 us)
Async XLA Ops:
  9.2 7.7 %collective-permute-start.1 = (bf16[128,640]{1,0:T(8,128)(2,1)}, bf16[128,640]{1,0:T(8,128)(2,1)}, u32[]{:S(2)}, u32[]{:S(2)}) collective-permute-start(bf16[128,640]{1,0:T(8,128)(2,1)} %fusion.8), channel_id=1, source_target_pairs={{0,2},{1,3},{2,0},{3,1},{4,6},{5,7},{6,4},{7,5},{8,10},{9,11},{10,... | collective-permute-start | bytes 491528 | tf_op jit(solution)/shard_map/ppermute | solution.py:456
  11.8 44.5 %all-to-all-start = ((bf16[16,160,256]{2,1,0:T(8,128)(2,1)}), bf16[16,160,256]{2,1,0:T(8,128)(2,1)S(1)}, u32[]{:S(2)}, u32[]{:S(2)}) async-start(bf16[16,160,256]{2,1,0:T(8,128)(2,1)} %get-tuple-element.111), calls=%async_computation | async-start | bytes 2621440 | tf_op jit(solution)/shard_map/all_to_all | solution.py:535
  25.1 7.3 %collective-permute-start.5 = (bf16[2,128,640]{2,1,0:T(8,128)(2,1)S(1)}, bf16[2,128,640]{2,1,0:T(8,128)(2,1)S(1)}, u32[]{:S(2)}, u32[]{:S(2)}) collective-permute-start(bf16[2,128,640]{2,1,0:T(8,128)(2,1)S(1)} %get-tuple-element.105), channel_id=1, source_target_pairs={{0,1},{1,0},{2,3},{3,2},{4,5},{5,4},{6,7},{7,6},{8,9},{9,8},{10,11... | collective-permute-start | bytes 983048 | tf_op jit(solution)/shard_map/ppermute | solution.py:456
  25.5 9.4 %collective-permute-start.6 = (bf16[128,640]{1,0:T(8,128)(2,1)S(1)}, bf16[128,640]{1,0:T(8,128)(2,1)S(1)}, u32[]{:S(2)}, u32[]{:S(2)}) collective-permute-start(bf16[128,640]{1,0:T(8,128)(2,1)S(1)} %fusion.9), channel_id=1, source_target_pairs={{0,2},{1,3},{2,0},{3,1},{4,6},{5,7},{6,4},{7,5},{8,10},{9,11},{10,... | collective-permute-start | bytes 491528 | tf_op jit(solution)/shard_map/ppermute | solution.py:456
  30.9 11.8 %collective-permute-start.8 = (bf16[128,640]{1,0:T(8,128)(2,1)S(1)}, bf16[128,640]{1,0:T(8,128)(2,1)S(1)}, u32[]{:S(2)}, u32[]{:S(2)}) collective-permute-start(bf16[128,640]{1,0:T(8,128)(2,1)S(1)} %fusion.7), channel_id=1, source_target_pairs={{0,4},{1,5},{2,6},{3,7},{4,0},{5,1},{6,2},{7,3},{8,12},{9,13},{10,... | collective-permute-start | bytes 491528 | tf_op jit(solution)/shard_map/ppermute | solution.py:456
  34.9 12.2 %collective-permute-start.7 = (bf16[128,640]{1,0:T(8,128)(2,1)S(1)}, bf16[128,640]{1,0:T(8,128)(2,1)S(1)}, u32[]{:S(2)}, u32[]{:S(2)}) collective-permute-start(bf16[128,640]{1,0:T(8,128)(2,1)S(1)} %fusion.11), channel_id=1, source_target_pairs={{0,2},{1,3},{2,0},{3,1},{4,6},{5,7},{6,4},{7,5},{8,10},{9,11},{10,... | collective-permute-start | bytes 491528 | tf_op jit(solution)/shard_map/ppermute | solution.py:456
  36.3 11.6 %collective-permute-start.4 = (bf16[128,640]{1,0:T(8,128)(2,1)S(1)}, bf16[128,640]{1,0:T(8,128)(2,1)S(1)}, u32[]{:S(2)}, u32[]{:S(2)}) collective-permute-start(bf16[128,640]{1,0:T(8,128)(2,1)S(1)} %fusion.10), channel_id=1, source_target_pairs={{0,2},{1,3},{2,0},{3,1},{4,6},{5,7},{6,4},{7,5},{8,10},{9,11},{10,... | collective-permute-start | bytes 491528 | tf_op jit(solution)/shard_map/ppermute | solution.py:456
  42.7 13.5 %collective-permute-start.10 = (bf16[128,640]{1,0:T(8,128)(2,1)S(1)}, bf16[128,640]{1,0:T(8,128)(2,1)S(1)}, u32[]{:S(2)}, u32[]{:S(2)}) collective-permute-start(bf16[128,640]{1,0:T(8,128)(2,1)S(1)} %fusion.5), channel_id=1, source_target_pairs={{0,8},{1,9},{2,10},{3,11},{4,12},{5,13},{6,14},{7,15},{8,0},{9,1},... | collective-permute-start | bytes 491528 | tf_op jit(solution)/shard_map/ppermute | solution.py:456
  47.2 9.0 %collective-permute-start.9 = (bf16[128,640]{1,0:T(8,128)(2,1)S(1)}, bf16[128,640]{1,0:T(8,128)(2,1)S(1)}, u32[]{:S(2)}, u32[]{:S(2)}) collective-permute-start(bf16[128,640]{1,0:T(8,128)(2,1)S(1)} %fusion.6), channel_id=1, source_target_pairs={{0,4},{1,5},{2,6},{3,7},{4,0},{5,1},{6,2},{7,3},{8,12},{9,13},{10,... | collective-permute-start | bytes 491528 | tf_op jit(solution)/shard_map/ppermute | solution.py:456
  62.9 8.9 %collective-permute-start.11 = (bf16[656,128]{1,0:T(8,128)(2,1)S(1)}, bf16[656,128]{1,0:T(8,128)(2,1)S(1)}, u32[]{:S(2)}, u32[]{:S(2)}) collective-permute-start(bf16[656,128]{1,0:T(8,128)(2,1)S(1)} %get-tuple-element.112.b0), channel_id=1, source_target_pairs={{0,4},{1,5},{2,6},{3,7},{4,0},{5,1},{6,2},{7,3},{8,12},{9,13},{10,... | collective-permute-start | bytes 503816 | tf_op jit(solution)/shard_map/ppermute | solution.py:456
  63.1 11.0 %collective-permute-start.12 = (bf16[656,128]{1,0:T(8,128)(2,1)S(1)}, bf16[656,128]{1,0:T(8,128)(2,1)S(1)}, u32[]{:S(2)}, u32[]{:S(2)}) collective-permute-start(bf16[656,128]{1,0:T(8,128)(2,1)S(1)} %get-tuple-element.112.b0), channel_id=1, source_target_pairs={{0,8},{1,9},{2,10},{3,11},{4,12},{5,13},{6,14},{7,15},{8,0},{9,1},... | collective-permute-start | bytes 503816 | tf_op jit(solution)/shard_map/ppermute | solution.py:456
  64.7 9.4 %collective-permute-start.13 = (bf16[656,128]{1,0:T(8,128)(2,1)S(1)}, bf16[656,128]{1,0:T(8,128)(2,1)S(1)}, u32[]{:S(2)}, u32[]{:S(2)}) collective-permute-start(bf16[656,128]{1,0:T(8,128)(2,1)S(1)} %get-tuple-element.112.b0), channel_id=1, source_target_pairs={{0,2},{1,3},{2,0},{3,1},{4,6},{5,7},{6,4},{7,5},{8,10},{9,11},{10,... | collective-permute-start | bytes 503816 | tf_op jit(solution)/shard_map/ppermute | solution.py:456
  74.1 8.9 %collective-permute-start.16 = (bf16[656,128]{1,0:T(8,128)(2,1)S(1)}, bf16[656,128]{1,0:T(8,128)(2,1)S(1)}, u32[]{:S(2)}, u32[]{:S(2)}) collective-permute-start(bf16[656,128]{1,0:T(8,128)(2,1)S(1)} %collective-permute-done.11.b0), channel_id=1, source_target_pairs={{0,2},{1,3},{2,0},{3,1},{4,6},{5,7},{6,4},{7,5},{8,10},{9,11},{10,... | collective-permute-start | bytes 503816 | tf_op jit(solution)/shard_map/ppermute | solution.py:456
  75.6 8.3 %collective-permute-start.20 = (bf16[656,128]{1,0:T(8,128)(2,1)S(1)}, bf16[656,128]{1,0:T(8,128)(2,1)S(1)}, u32[]{:S(2)}, u32[]{:S(2)}) collective-permute-start(bf16[656,128]{1,0:T(8,128)(2,1)S(1)} %collective-permute-done.11.b0), channel_id=1, source_target_pairs={{0,1},{1,0},{2,3},{3,2},{4,5},{5,4},{6,7},{7,6},{8,9},{9,8},{10,11... | collective-permute-start | bytes 503816 | tf_op jit(solution)/shard_map/ppermute | solution.py:456
  75.8 9.6 %collective-permute-start.24 = (bf16[656,128]{1,0:T(8,128)(2,1)S(1)}, bf16[656,128]{1,0:T(8,128)(2,1)S(1)}, u32[]{:S(2)}, u32[]{:S(2)}) collective-permute-start(bf16[656,128]{1,0:T(8,128)(2,1)S(1)} %collective-permute-done.12.b0), channel_id=1, source_target_pairs={{0,2},{1,3},{2,0},{3,1},{4,6},{5,7},{6,4},{7,5},{8,10},{9,11},{10,... | collective-permute-start | bytes 503816 | tf_op jit(solution)/shard_map/ppermute | solution.py:456
  83.8 9.2 %collective-permute-start.18 = (bf16[656,128]{1,0:T(8,128)(2,1)S(1)}, bf16[656,128]{1,0:T(8,128)(2,1)S(1)}, u32[]{:S(2)}, u32[]{:S(2)}) collective-permute-start(bf16[656,128]{1,0:T(8,128)(2,1)S(1)} %collective-permute-done.15.b0), channel_id=1, source_target_pairs={{0,1},{1,0},{2,3},{3,2},{4,5},{5,4},{6,7},{7,6},{8,9},{9,8},{10,11... | collective-permute-start | bytes 503816 | tf_op jit(solution)/shard_map/ppermute | solution.py:456
  101.9 9.5 %collective-permute-start.32 = (bf16[128,640]{1,0:T(8,128)(2,1)S(1)}, bf16[128,640]{1,0:T(8,128)(2,1)S(1)}, u32[]{:S(2)}, u32[]{:S(2)}) collective-permute-start(bf16[128,640]{1,0:T(8,128)(2,1)S(1)} %fusion.13), channel_id=1, source_target_pairs={{0,2},{1,3},{2,0},{3,1},{4,6},{5,7},{6,4},{7,5},{8,10},{9,11},{10,... | collective-permute-start | bytes 491528 | tf_op jit(solution)/shard_map/ppermute | solution.py:456
  113.1 8.2 %collective-permute-start.30 = (bf16[128,640]{1,0:T(8,128)(2,1)S(1)}, bf16[128,640]{1,0:T(8,128)(2,1)S(1)}, u32[]{:S(2)}, u32[]{:S(2)}) collective-permute-start(bf16[128,640]{1,0:T(8,128)(2,1)S(1)} %fusion.14), channel_id=1, source_target_pairs={{0,2},{1,3},{2,0},{3,1},{4,6},{5,7},{6,4},{7,5},{8,10},{9,11},{10,... | collective-permute-start | bytes 491528 | tf_op jit(solution)/shard_map/ppermute | solution.py:456
  116.3 10.4 %collective-permute-start.36 = (bf16[128,640]{1,0:T(8,128)(2,1)S(1)}, bf16[128,640]{1,0:T(8,128)(2,1)S(1)}, u32[]{:S(2)}, u32[]{:S(2)}) collective-permute-start(bf16[128,640]{1,0:T(8,128)(2,1)S(1)} %fusion.1), channel_id=1, source_target_pairs={{0,8},{1,9},{2,10},{3,11},{4,12},{5,13},{6,14},{7,15},{8,0},{9,1},... | collective-permute-start | bytes 491528 | tf_op jit(solution)/shard_map/ppermute | solution.py:456
  131.6 13.7 %collective-permute-start.37 = (bf16[656,128]{1,0:T(8,128)(2,1)S(1)}, bf16[656,128]{1,0:T(8,128)(2,1)S(1)}, u32[]{:S(2)}, u32[]{:S(2)}) collective-permute-start(bf16[656,128]{1,0:T(8,128)(2,1)S(1)} %get-tuple-element.158.b0), channel_id=1, source_target_pairs={{0,4},{1,5},{2,6},{3,7},{4,0},{5,1},{6,2},{7,3},{8,12},{9,13},{10,... | collective-permute-start | bytes 503816 | tf_op jit(solution)/shard_map/ppermute | solution.py:456
  132.4 12.9 %collective-permute-start.38 = (bf16[656,128]{1,0:T(8,128)(2,1)S(1)}, bf16[656,128]{1,0:T(8,128)(2,1)S(1)}, u32[]{:S(2)}, u32[]{:S(2)}) collective-permute-start(bf16[656,128]{1,0:T(8,128)(2,1)S(1)} %get-tuple-element.158.b0), channel_id=1, source_target_pairs={{0,8},{1,9},{2,10},{3,11},{4,12},{5,13},{6,14},{7,15},{8,0},{9,1},... | collective-permute-start | bytes 503816 | tf_op jit(solution)/shard_map/ppermute | solution.py:456
  133.9 11.4 %collective-permute-start.39 = (bf16[656,128]{1,0:T(8,128)(2,1)S(1)}, bf16[656,128]{1,0:T(8,128)(2,1)S(1)}, u32[]{:S(2)}, u32[]{:S(2)}) collective-permute-start(bf16[656,128]{1,0:T(8,128)(2,1)S(1)} %get-tuple-element.158.b0), channel_id=1, source_target_pairs={{0,2},{1,3},{2,0},{3,1},{4,6},{5,7},{6,4},{7,5},{8,10},{9,11},{10,... | collective-permute-start | bytes 503816 | tf_op jit(solution)/shard_map/ppermute | solution.py:456
  135.4 8.8 %collective-permute-start.41 = (bf16[4,144,128]{2,1,0:T(8,128)(2,1)S(1)}, bf16[4,144,128]{2,1,0:T(8,128)(2,1)S(1)}, u32[]{:S(2)}, u32[]{:S(2)}) collective-permute-start(bf16[4,144,128]{2,1,0:T(8,128)(2,1)S(1)} %get-tuple-element.184), channel_id=1, source_target_pairs={{0,2},{1,3},{2,0},{3,1},{4,6},{5,7},{6,4},{7,5},{8,10},{9,11},{10,... | collective-permute-start | bytes 442376 | tf_op jit(solution)/shard_map/ppermute | solution.py:456
  135.9 9.4 %collective-permute-start.42 = (bf16[4,144,128]{2,1,0:T(8,128)(2,1)S(1)}, bf16[4,144,128]{2,1,0:T(8,128)(2,1)S(1)}, u32[]{:S(2)}, u32[]{:S(2)}) collective-permute-start(bf16[4,144,128]{2,1,0:T(8,128)(2,1)S(1)} %get-tuple-element.186), channel_id=1, source_target_pairs={{0,3},{1,2},{2,1},{3,0},{4,7},{5,6},{6,5},{7,4},{8,11},{9,10},{10,... | collective-permute-start | bytes 442376 | tf_op jit(solution)/shard_map/ppermute | solution.py:456
  149.1 7.9 %collective-permute-start.52 = (bf16[656,128]{1,0:T(8,128)(2,1)S(1)}, bf16[656,128]{1,0:T(8,128)(2,1)S(1)}, u32[]{:S(2)}, u32[]{:S(2)}) collective-permute-start(bf16[656,128]{1,0:T(8,128)(2,1)S(1)} %collective-permute-done.37.b0), channel_id=1, source_target_pairs={{0,1},{1,0},{2,3},{3,2},{4,5},{5,4},{6,7},{7,6},{8,9},{9,8},{10,11... | collective-permute-start | bytes 503816 | tf_op jit(solution)/shard_map/ppermute | solution.py:456
  149.2 9.3 %collective-permute-start.56 = (bf16[656,128]{1,0:T(8,128)(2,1)S(1)}, bf16[656,128]{1,0:T(8,128)(2,1)S(1)}, u32[]{:S(2)}, u32[]{:S(2)}) collective-permute-start(bf16[656,128]{1,0:T(8,128)(2,1)S(1)} %collective-permute-done.38.b0), channel_id=1, source_target_pairs={{0,2},{1,3},{2,0},{3,1},{4,6},{5,7},{6,4},{7,5},{8,10},{9,11},{10,... | collective-permute-start | bytes 503816 | tf_op jit(solution)/shard_map/ppermute | solution.py:456
  156.4 8.9 %collective-permute-start.43 = (bf16[4,144,128]{2,1,0:T(8,128)(2,1)S(1)}, bf16[4,144,128]{2,1,0:T(8,128)(2,1)S(1)}, u32[]{:S(2)}, u32[]{:S(2)}) collective-permute-start(bf16[4,144,128]{2,1,0:T(8,128)(2,1)S(1)} %get-tuple-element.181), channel_id=1, source_target_pairs={{0,4},{1,5},{2,6},{3,7},{4,0},{5,1},{6,2},{7,3},{8,12},{9,13},{10,... | collective-permute-start | bytes 442376 | tf_op jit(solution)/shard_map/ppermute | solution.py:456
  157.0 13.9 %collective-permute-start.44 = (bf16[4,144,128]{2,1,0:T(8,128)(2,1)S(1)}, bf16[4,144,128]{2,1,0:T(8,128)(2,1)S(1)}, u32[]{:S(2)}, u32[]{:S(2)}) collective-permute-start(bf16[4,144,128]{2,1,0:T(8,128)(2,1)S(1)} %get-tuple-element.180), channel_id=1, source_target_pairs={{0,8},{1,9},{2,10},{3,11},{4,12},{5,13},{6,14},{7,15},{8,0},{9,1},... | collective-permute-start | bytes 442376 | tf_op jit(solution)/shard_map/ppermute | solution.py:456
  158.5 12.7 %collective-permute-start.45 = (bf16[4,144,128]{2,1,0:T(8,128)(2,1)S(1)}, bf16[4,144,128]{2,1,0:T(8,128)(2,1)S(1)}, u32[]{:S(2)}, u32[]{:S(2)}) collective-permute-start(bf16[4,144,128]{2,1,0:T(8,128)(2,1)S(1)} %get-tuple-element.179), channel_id=1, source_target_pairs={{0,12},{1,13},{2,14},{3,15},{4,8},{5,9},{6,10},{7,11},{8,4},{9,5},... | collective-permute-start | bytes 442376 | tf_op jit(solution)/shard_map/ppermute | solution.py:456
  160.8 12.5 %collective-permute-start.55 = (bf16[656,128]{1,0:T(8,128)(2,1)S(1)}, bf16[656,128]{1,0:T(8,128)(2,1)S(1)}, u32[]{:S(2)}, u32[]{:S(2)}) collective-permute-start(bf16[656,128]{1,0:T(8,128)(2,1)S(1)} %collective-permute-done.38.b0), channel_id=1, source_target_pairs={{0,1},{1,0},{2,3},{3,2},{4,5},{5,4},{6,7},{7,6},{8,9},{9,8},{10,11... | collective-permute-start | bytes 503816 | tf_op jit(solution)/shard_map/ppermute | solution.py:456
  160.8 12.5 %collective-permute-start.57 = (bf16[656,128]{1,0:T(8,128)(2,1)S(1)}, bf16[656,128]{1,0:T(8,128)(2,1)S(1)}, u32[]{:S(2)}, u32[]{:S(2)}) collective-permute-start(bf16[656,128]{1,0:T(8,128)(2,1)S(1)} %collective-permute-done.56.b2), channel_id=1, source_target_pairs={{0,1},{1,0},{2,3},{3,2},{4,5},{5,4},{6,7},{7,6},{8,9},{9,8},{10,11... | collective-permute-start | bytes 503816 | tf_op jit(solution)/shard_map/ppermute | solution.py:456
  165.3 10.5 %collective-permute-start.50 = (bf16[656,128]{1,0:T(8,128)(2,1)S(1)}, bf16[656,128]{1,0:T(8,128)(2,1)S(1)}, u32[]{:S(2)}, u32[]{:S(2)}) collective-permute-start(bf16[656,128]{1,0:T(8,128)(2,1)S(1)} %collective-permute-done.46.b0), channel_id=1, source_target_pairs={{0,1},{1,0},{2,3},{3,2},{4,5},{5,4},{6,7},{7,6},{8,9},{9,8},{10,11... | collective-permute-start | bytes 503816 | tf_op jit(solution)/shard_map/ppermute | solution.py:456
  (37 other events, 231.8 us)

commit v12 on v11

--- a/solution.py
+++ b/solution.py
@@ -599,6 +599,8 @@
             near[3], far[1], acc, place = lax.optimization_barrier((near[3], far[1], acc, place))
             spread(3)
             settle_far(1)
+            if last:
+                acc, *back = lax.optimization_barrier((acc, *back))
             acc, total = flow_chunk(resident[1], blocks(1), acc, total, weight=weight)
             settle_far(2)
             far[3], acc = lax.optimization_barrier((far[3], acc))
@@ -607,6 +609,8 @@
             line_price, line_half, total = flow_chunk(
                 resident[3], blocks(3), acc, total, limit, line_price, weight
             )
+            if last:
+                line_price, *back = lax.optimization_barrier((line_price, *back))
             balance = total
         else:
             if last:

time: 180 us -> 180 us (level)
  starting transfers between devices: 53.7 us -> 56.8 us
  waiting for transfers between devices: 52.4 us -> 49.7 us
    ppermute x58, starting transfers between devices: 48.7 us -> 51.8 us  [swap(): return lax.ppermute(x, 'bus', [(i, i ^ mask) for i in range(devices)])]
    ppermute x58, waiting for transfers between devices: 52.4 us -> 49.7 us  [swap(): return lax.ppermute(x, 'bus', [(i, i ^ mask) for i in range(devices)])]
  transfers between devices with their start and end apart: 59 -> 59, of which waited for: 20 -> 18; matrix products, arithmetic and copies ran while one was open for 1% -> 1% of each run, Pallas kernels for 26% -> 24%
where the time goes in v12:
time: 180 us
  Pallas kernels  68.7 us (38%)
  starting transfers between devices  56.8 us (32%)
  waiting for transfers between devices  49.7 us (28%)
  other arithmetic  2.99 us (2%)
    ppermute x58, starting transfers between devices, swap(): return lax.ppermute(x, 'bus', [(i, i ^ mask) for i in range(devices)])  51.8 us
    ppermute x58, waiting for transfers between devices, swap(): return lax.ppermute(x, 'bus', [(i, i ^ mask) for i in range(devices)])  49.7 us
    pallas_call x8, Pallas kernels, shadow_chunk(): pl.pallas_call(functools.partial(shadow_kernel, chunk, stream, turn), in_...  21.4 us
    pallas_call x8, Pallas kernels, flow_chunk(): pl.pallas_call(functools.partial(flow_kernel, start, end), in_specs=[VMEM...  20.7 us
    pallas_call x2, Pallas kernels, update(): pl.pallas_call(functools.partial(update_kernel, cap, devices, first, last...  11.3 us
    pallas_call x2, Pallas kernels, load_chunks(): pl.pallas_call(functools.partial(load_kernel, chunks), in_specs=[SMEM_SPE...  9.58 us
    all_to_all x1, starting transfers between devices, local(): lax.all_to_all(outgoing, 'bus', split_axis=0, concat_axis=0, tiled=True)  4.98 us
  transfers between devices with their start and end apart: 59, of which 18 were waited for; matrix products, arithmetic and copies ran while one was open for 1% of the time, Pallas kernels for 24%

profile of v12, /device:TPU:0, one launch (start us, length us, event | category | flops | bytes accessed | tf_op | source)
XLA Modules:
  0.0 179.9 jit_solution(6194588597320657595)
XLA Ops:
  0.7 3.7 %shadow_chunk.8 = (f32[2,128,640]{2,1,0:T(8,128)S(1)}, bf16[2,128,640]{2,1,0:T(8,128)(2,1)S(1)}, bf16[128,1280]{1,0:T(8,128)(2,1)S(1)}) custom-call(s32[1]{0:T(128)} %bitcast.place_ref, f32[1280,128]{1,0:T(8,128)} %rest_1_.1, bf16[1280,10240]{1,0:T(8,128)(2,1)} %ptdf_ref.11), custom_call_target="tpu_custom_call" | custom-call | flops 2516582400 | bytes 6553600 | tf_op jit(solution)/shard_map/shadow_chunk/pallas_call | solution.py:346
  4.9 3.6 %pack_generators.1 = (bf16[16,160,256]{2,1,0:T(8,128)(2,1)}, s32[1,768]{1,0:T(1,128)S(1)}) custom-call(s32[1]{0:T(128)} %bitcast.place_ref, s32[1,768]{1,0:T(1,128)S(1)} %bitcast.88, s32[6,128]{1,0:T(8,128)S(1)} %bitcast.86, f32[6,128]{1,0:T(8,128)S(1)} %bitcast.87, f32[768,128]{1,0:T(8,128)S(1)} %copy-done.1, f32[6,128]{1,0:T(8,128)S(1)} %bitcast.82, ...), custom_call_target="tpu_custom_call" | custom-call | flops 905969664 | bytes 3145728 | tf_op jit(solution)/shard_map/pack_generators/pallas_call | solution.py:107
  9.2 2.6 %collective-permute-start.1 = (bf16[128,640]{1,0:T(8,128)(2,1)}, bf16[128,640]{1,0:T(8,128)(2,1)}, u32[]{:S(2)}, u32[]{:S(2)}) collective-permute-start(bf16[128,640]{1,0:T(8,128)(2,1)} %fusion.8), channel_id=1, source_target_pairs={{0,2},{1,3},{2,0},{3,1},{4,6},{5,7},{6,4},{7,5},{8,10},{9,11},{10,... | collective-permute-start | bytes 491528 | tf_op jit(solution)/shard_map/ppermute | solution.py:456
  11.8 5.0 %all-to-all-start = ((bf16[16,160,256]{2,1,0:T(8,128)(2,1)}), bf16[16,160,256]{2,1,0:T(8,128)(2,1)S(1)}, u32[]{:S(2)}, u32[]{:S(2)}) async-start(bf16[16,160,256]{2,1,0:T(8,128)(2,1)} %get-tuple-element.121), calls=%async_computation | async-start | bytes 2621440 | tf_op jit(solution)/shard_map/all_to_all | solution.py:535
  17.9 3.4 %shadow_chunk.9 = (f32[2,128,640]{2,1,0:T(8,128)S(1)}, bf16[2,128,640]{2,1,0:T(8,128)(2,1)S(1)}) custom-call(s32[1]{0:T(128)} %bitcast.place_ref, bf16[128,1280]{1,0:T(8,128)(2,1)S(1)} %get-tuple-element.111.line_ref, bf16[1280,10240]{1,0:T(8,128)(2,1)} %ptdf_ref.11), custom_call_target="tpu_custom_call" | custom-call | flops 2516582400 | bytes 6553600 | tf_op jit(solution)/shard_map/shadow_chunk/pallas_call | solution.py:346
  21.7 3.4 %shadow_chunk.11 = (f32[2,128,640]{2,1,0:T(8,128)S(1)}, bf16[2,128,640]{2,1,0:T(8,128)(2,1)S(1)}) custom-call(s32[1]{0:T(128)} %bitcast.place_ref, bf16[128,1280]{1,0:T(8,128)(2,1)S(1)} %get-tuple-element.111.line_ref, bf16[1280,10240]{1,0:T(8,128)(2,1)} %ptdf_ref.11), custom_call_target="tpu_custom_call" | custom-call | flops 2516582400 | bytes 6553600 | tf_op jit(solution)/shard_map/shadow_chunk/pallas_call | solution.py:346
  27.3 3.4 %shadow_chunk.10 = (f32[2,128,640]{2,1,0:T(8,128)S(1)}, bf16[2,128,640]{2,1,0:T(8,128)(2,1)S(1)}) custom-call(s32[1]{0:T(128)} %bitcast.place_ref, bf16[128,1280]{1,0:T(8,128)(2,1)S(1)} %get-tuple-element.111.line_ref, bf16[1280,10240]{1,0:T(8,128)(2,1)} %ptdf_ref.11), custom_call_target="tpu_custom_call" | custom-call | flops 2516582400 | bytes 6553600 | tf_op jit(solution)/shard_map/shadow_chunk/pallas_call | solution.py:346
  32.5 2.4 %collective-permute-done.6 = bf16[128,640]{1,0:T(8,128)(2,1)S(1)} collective-permute-done((bf16[128,640]{1,0:T(8,128)(2,1)S(1)}, bf16[128,640]{1,0:T(8,128)(2,1)S(1)}, u32[]{:S(2)}, u32[]{:S(2)}) %collective-permute-start.6) | collective-permute-done | bytes 163872 | tf_op jit(solution)/shard_map/ppermute | solution.py:456
  37.1 5.5 %collective-permute-done.8 = bf16[128,640]{1,0:T(8,128)(2,1)S(1)} collective-permute-done((bf16[128,640]{1,0:T(8,128)(2,1)S(1)}, bf16[128,640]{1,0:T(8,128)(2,1)S(1)}, u32[]{:S(2)}, u32[]{:S(2)}) %collective-permute-start.8) | collective-permute-done | bytes 163872 | tf_op jit(solution)/shard_map/ppermute | solution.py:456
  42.7 4.4 %collective-permute-start.10 = (bf16[128,640]{1,0:T(8,128)(2,1)S(1)}, bf16[128,640]{1,0:T(8,128)(2,1)S(1)}, u32[]{:S(2)}, u32[]{:S(2)}) collective-permute-start(bf16[128,640]{1,0:T(8,128)(2,1)S(1)} %fusion.5), channel_id=1, source_target_pairs={{0,8},{1,9},{2,10},{3,11},{4,12},{5,13},{6,14},{7,15},{8,0},{9,1},... | collective-permute-start | bytes 491528 | tf_op jit(solution)/shard_map/ppermute | solution.py:456
  47.9 8.3 %collective-permute-done.9.refs_1_ = bf16[128,640]{1,0:T(8,128)(2,1)S(1)} collective-permute-done((bf16[128,640]{1,0:T(8,128)(2,1)S(1)}, bf16[128,640]{1,0:T(8,128)(2,1)S(1)}, u32[]{:S(2)}, u32[]{:S(2)}) %collective-permute-start.9) | collective-permute-done | bytes 163872 | tf_op jit(solution)/shard_map/ppermute | solution.py:456
  56.3 6.5 %update_generators.2 = (f32[16,144,128]{2,1,0:T(8,128)S(1)}, bf16[656,128]{1,0:T(8,128)(2,1)S(1)}, bf16[1280,2560]{1,0:T(8,128)(2,1)S(1)}) custom-call(s32[1]{0:T(128)} %bitcast.place_ref, f32[128,640]{1,0:T(8,128)S(1)} %bitcast_add_fusion.6.refs_0_, bf16[128,640]{1,0:T(8,128)(2,1)S(1)} %collective-permute-done.9.refs_1_, ...), custom_call_target="tpu_custom_call" | custom-call | flops 1509949440 | bytes 4194304 | tf_op jit(solution)/shard_map/update_generators/pallas_call | solution.py:276
  66.2 5.4 %load_chunks.2 = (s32[1]{0:T(128)}, bf16[1280,2560]{1,0:T(8,128)(2,1)S(1)}, bf16[1280,2560]{1,0:T(8,128)(2,1)S(1)}) custom-call(s32[1]{0:T(128)} %bitcast.place_ref, bf16[1280,10240]{1,0:T(8,128)(2,1)} %ptdf_ref.11), custom_call_target="tpu_custom_call" | custom-call | bytes 13107200 | tf_op jit(solution)/shard_map/load_chunks/pallas_call | solution.py:387
  71.8 2.3 %collective-permute-done.13.b0 = bf16[656,128]{1,0:T(8,128)(2,1)S(1)} collective-permute-done((bf16[656,128]{1,0:T(8,128)(2,1)S(1)}, bf16[656,128]{1,0:T(8,128)(2,1)S(1)}, u32[]{:S(2)}, u32[]{:S(2)}) %collective-permute-start.13) | collective-permute-done | bytes 167968 | tf_op jit(solution)/shard_map/ppermute | solution.py:456
  76.4 2.4 %flow_chunk.8 = (f32[1280,128]{1,0:T(8,128)S(1)}, f32[1,128]{1,0:T(1,128)S(1)}) custom-call(bf16[1280,2560]{1,0:T(8,128)(2,1)S(1)} %get-tuple-element.122.ptdf_ref, bf16[656,128]{1,0:T(8,128)(2,1)S(1)} %get-tuple-element.123.b0, bf16[656,128]{1,0:T(8,128)(2,1)S(1)} %collective-permute-done.11.b1, bf16[656,128]{1,0:T(8,128)(2,1)S(1)} %collective-permute-done.14.b2, ...), custom_call_target="tpu_custom_call" | custom-call | flops 2516582400 | bytes 6553600 | tf_op jit(solution)/shard_map/flow_chunk/pallas_call | solution.py:444
  78.8 4.1 %load_chunks.3 = (s32[1]{0:T(128)}, bf16[1280,2560]{1,0:T(8,128)(2,1)S(1)}) custom-call(s32[1]{0:T(128)} %get-tuple-element.130.place_ref, bf16[1280,10240]{1,0:T(8,128)(2,1)} %ptdf_ref.11), custom_call_target="tpu_custom_call" | custom-call | bytes 6553600 | tf_op jit(solution)/shard_map/load_chunks/pallas_call | solution.py:387
  85.6 2.4 %flow_chunk.9 = (f32[1280,128]{1,0:T(8,128)S(1)}, f32[1,128]{1,0:T(1,128)S(1)}) custom-call(bf16[1280,2560]{1,0:T(8,128)(2,1)S(1)} %get-tuple-element.138.ptdf_ref, bf16[656,128]{1,0:T(8,128)(2,1)S(1)} %collective-permute-done.12.b0, bf16[656,128]{1,0:T(8,128)(2,1)S(1)} %collective-permute-done.20.b1, bf16[656,128]{1,0:T(8,128)(2,1)S(1)} %collective-permute-done.17.b2, ...), custom_call_target="tpu_custom_call" | custom-call | flops 2516582400 | bytes 6553600 | tf_op jit(solution)/shard_map/flow_chunk/pallas_call | solution.py:444
  88.0 2.5 %collective-permute-done.19.b2 = bf16[656,128]{1,0:T(8,128)(2,1)S(1)} collective-permute-done((bf16[656,128]{1,0:T(8,128)(2,1)S(1)}, bf16[656,128]{1,0:T(8,128)(2,1)S(1)}, u32[]{:S(2)}, u32[]{:S(2)}) %collective-permute-start.19) | collective-permute-done | bytes 167968 | tf_op jit(solution)/shard_map/ppermute | solution.py:456
  90.6 2.4 %flow_chunk.10 = (f32[1280,128]{1,0:T(8,128)S(1)}, f32[1,128]{1,0:T(1,128)S(1)}) custom-call(bf16[1280,2560]{1,0:T(8,128)(2,1)S(1)} %get-tuple-element.144.ptdf_ref, bf16[656,128]{1,0:T(8,128)(2,1)S(1)} %collective-permute-done.13.b0, bf16[656,128]{1,0:T(8,128)(2,1)S(1)} %collective-permute-done.23.b1, bf16[656,128]{1,0:T(8,128)(2,1)S(1)} %collective-permute-done.24.b2, ...), custom_call_target="tpu_custom_call" | custom-call | flops 2516582400 | bytes 6553600 | tf_op jit(solution)/shard_map/flow_chunk/pallas_call | solution.py:444
  93.0 2.8 %flow_chunk.11 = (f32[1280,128]{1,0:T(8,128)S(1)}, bf16[128,1280]{1,0:T(8,128)(2,1)S(1)}, f32[1,128]{1,0:T(1,128)S(1)}) custom-call(bf16[1280,2560]{1,0:T(8,128)(2,1)S(1)} %get-tuple-element.131.ptdf_ref, bf16[656,128]{1,0:T(8,128)(2,1)S(1)} %collective-permute-done.16.b0, bf16[656,128]{1,0:T(8,128)(2,1)S(1)} %collective-permute-done.18.b1, ...), custom_call_target="tpu_custom_call" | custom-call | flops 2516582400 | bytes 6553600 | tf_op jit(solution)/shard_map/flow_chunk/pallas_call | solution.py:444
  113.7 2.5 %collective-permute-done.34 = bf16[128,640]{1,0:T(8,128)(2,1)S(1)} collective-permute-done((bf16[128,640]{1,0:T(8,128)(2,1)S(1)}, bf16[128,640]{1,0:T(8,128)(2,1)S(1)}, u32[]{:S(2)}, u32[]{:S(2)}) %collective-permute-start.34) | collective-permute-done | bytes 163872 | tf_op jit(solution)/shard_map/ppermute | solution.py:456
  121.4 4.2 %collective-permute-done.35.refs_1_ = bf16[128,640]{1,0:T(8,128)(2,1)S(1)} collective-permute-done((bf16[128,640]{1,0:T(8,128)(2,1)S(1)}, bf16[128,640]{1,0:T(8,128)(2,1)S(1)}, u32[]{:S(2)}, u32[]{:S(2)}) %collective-permute-start.35) | collective-permute-done | bytes 163872 | tf_op jit(solution)/shard_map/ppermute | solution.py:456
  126.7 4.8 %update_generators.3 = (bf16[16,144,128]{2,1,0:T(8,128)(2,1)S(1)}, bf16[656,128]{1,0:T(8,128)(2,1)S(1)}) custom-call(s32[1]{0:T(128)} %get-tuple-element.136.place_ref, f32[128,640]{1,0:T(8,128)S(1)} %bitcast_add_fusion.2.refs_0_, bf16[128,640]{1,0:T(8,128)(2,1)S(1)} %collective-permute-done.35.refs_1_, ...), custom_call_target="tpu_custom_call" | custom-call | flops 1509949440 | bytes 4194304 | tf_op jit(solution)/shard_map/update_generators/pallas_call | solution.py:276
  136.4 7.9 %collective-permute-done.41 = bf16[4,144,128]{2,1,0:T(8,128)(2,1)S(1)} collective-permute-done((bf16[4,144,128]{2,1,0:T(8,128)(2,1)S(1)}, bf16[4,144,128]{2,1,0:T(8,128)(2,1)S(1)}, u32[]{:S(2)}, u32[]{:S(2)}) %collective-permute-start.41) | collective-permute-done | bytes 147488 | tf_op jit(solution)/shard_map/ppermute | solution.py:456
  150.8 2.4 %flow_chunk.12 = (f32[1280,128]{1,0:T(8,128)S(1)}, f32[1,128]{1,0:T(1,128)S(1)}) custom-call(bf16[1280,2560]{1,0:T(8,128)(2,1)S(1)} %get-tuple-element.122.ptdf_ref, bf16[656,128]{1,0:T(8,128)(2,1)S(1)} %get-tuple-element.167.b0, bf16[656,128]{1,0:T(8,128)(2,1)S(1)} %collective-permute-done.45.b1, bf16[656,128]{1,0:T(8,128)(2,1)S(1)} %collective-permute-done.39.b2, ...), custom_call_target="tpu_custom_call" | custom-call | flops 104857600 | bytes 819200 | tf_op jit(solution)/shard_map/flow_chunk/pallas_call | solution.py:444
  153.2 3.9 %collective-permute-start.56 = (bf16[656,128]{1,0:T(8,128)(2,1)S(1)}, bf16[656,128]{1,0:T(8,128)(2,1)S(1)}, u32[]{:S(2)}, u32[]{:S(2)}) collective-permute-start(bf16[656,128]{1,0:T(8,128)(2,1)S(1)} %collective-permute-done.38.b0), channel_id=1, source_target_pairs={{0,2},{1,3},{2,0},{3,1},{4,6},{5,7},{6,4},{7,5},{8,10},{9,11},{10,... | collective-permute-start | bytes 503816 | tf_op jit(solution)/shard_map/ppermute | solution.py:456
  160.2 2.2 %collective-permute-start.53 = (bf16[4,144,128]{2,1,0:T(8,128)(2,1)S(1)}, bf16[4,144,128]{2,1,0:T(8,128)(2,1)S(1)}, u32[]{:S(2)}, u32[]{:S(2)}) collective-permute-start(bf16[4,144,128]{2,1,0:T(8,128)(2,1)S(1)} %get-tuple-element.199), channel_id=1, source_target_pairs={{0,12},{1,13},{2,14},{3,15},{4,8},{5,9},{6,10},{7,11},{8,4},{9,5},... | collective-permute-start | bytes 442376 | tf_op jit(solution)/shard_map/ppermute | solution.py:456
  162.4 5.3 %collective-permute-done.53.refs_3_ = bf16[4,144,128]{2,1,0:T(8,128)(2,1)S(1)} collective-permute-done((bf16[4,144,128]{2,1,0:T(8,128)(2,1)S(1)}, bf16[4,144,128]{2,1,0:T(8,128)(2,1)S(1)}, u32[]{:S(2)}, u32[]{:S(2)}) %collective-permute-start.53) | collective-permute-done | bytes 147488 | tf_op jit(solution)/shard_map/ppermute | solution.py:456
  168.3 2.4 %flow_chunk.13 = (f32[1280,128]{1,0:T(8,128)S(1)}, f32[1,128]{1,0:T(1,128)S(1)}) custom-call(bf16[1280,2560]{1,0:T(8,128)(2,1)S(1)} %get-tuple-element.138.ptdf_ref, bf16[656,128]{1,0:T(8,128)(2,1)S(1)} %collective-permute-done.37.b0, bf16[656,128]{1,0:T(8,128)(2,1)S(1)} %collective-permute-done.49.b1, bf16[656,128]{1,0:T(8,128)(2,1)S(1)} %collective-permute-done.44.b2, ...), custom_call_target="tpu_custom_call" | custom-call | flops 104857600 | bytes 819200 | tf_op jit(solution)/shard_map/flow_chunk/pallas_call | solution.py:444
  171.4 2.4 %flow_chunk.14 = (f32[1280,128]{1,0:T(8,128)S(1)}, f32[1,128]{1,0:T(1,128)S(1)}) custom-call(bf16[1280,2560]{1,0:T(8,128)(2,1)S(1)} %get-tuple-element.144.ptdf_ref, bf16[656,128]{1,0:T(8,128)(2,1)S(1)} %collective-permute-done.38.b0, bf16[656,128]{1,0:T(8,128)(2,1)S(1)} %collective-permute-done.55.b1, bf16[656,128]{1,0:T(8,128)(2,1)S(1)} %collective-permute-done.56.b2, ...), custom_call_target="tpu_custom_call" | custom-call | flops 104857600 | bytes 819200 | tf_op jit(solution)/shard_map/flow_chunk/pallas_call | solution.py:444
  173.8 3.4 %flow_chunk.15 = (f32[1280,128]{1,0:T(8,128)}, bf16[128,1280]{1,0:T(8,128)(2,1)}, f32[1,128]{1,0:T(1,128)S(1)}) custom-call(bf16[1280,2560]{1,0:T(8,128)(2,1)S(1)} %get-tuple-element.131.ptdf_ref, bf16[656,128]{1,0:T(8,128)(2,1)S(1)} %collective-permute-done.43.b0, bf16[656,128]{1,0:T(8,128)(2,1)S(1)} %collective-permute-done.47.b1, ...), custom_call_target="tpu_custom_call" | custom-call | flops 104857600 | bytes 819200 | tf_op jit(solution)/shard_map/flow_chunk/pallas_call | solution.py:444
  177.7 2.2 %unpack_dispatch.1 = f32[768,128]{1,0:T(8,128)} custom-call(s32[1,768]{1,0:T(1,128)S(1)} %get-tuple-element.101.slot_ref, bf16[4,144,128]{2,1,0:T(8,128)(2,1)S(1)} %get-tuple-element.193.refs_0_, bf16[4,144,128]{2,1,0:T(8,128)(2,1)S(1)} %collective-permute-done.51.refs_1_, bf16[4,144,128]{2,1,0:T(8,128)(2,1)S(1)} %collective-permute-done.52.refs_2_, ...), custom_call_target="tpu_custom_call" | custom-call | flops 452984832 | bytes 1048576 | tf_op jit(solution)/shard_map/unpack_dispatch/pallas_call | solution.py:172
  (151 shorter events, 58.5 us)
Async XLA Ops:
  9.2 7.7 %collective-permute-start.1 = (bf16[128,640]{1,0:T(8,128)(2,1)}, bf16[128,640]{1,0:T(8,128)(2,1)}, u32[]{:S(2)}, u32[]{:S(2)}) collective-permute-start(bf16[128,640]{1,0:T(8,128)(2,1)} %fusion.8), channel_id=1, source_target_pairs={{0,2},{1,3},{2,0},{3,1},{4,6},{5,7},{6,4},{7,5},{8,10},{9,11},{10,... | collective-permute-start | bytes 491528 | tf_op jit(solution)/shard_map/ppermute | solution.py:456
  11.8 44.5 %all-to-all-start = ((bf16[16,160,256]{2,1,0:T(8,128)(2,1)}), bf16[16,160,256]{2,1,0:T(8,128)(2,1)S(1)}, u32[]{:S(2)}, u32[]{:S(2)}) async-start(bf16[16,160,256]{2,1,0:T(8,128)(2,1)} %get-tuple-element.121), calls=%async_computation | async-start | bytes 2621440 | tf_op jit(solution)/shard_map/all_to_all | solution.py:535
  25.5 9.4 %collective-permute-start.6 = (bf16[128,640]{1,0:T(8,128)(2,1)S(1)}, bf16[128,640]{1,0:T(8,128)(2,1)S(1)}, u32[]{:S(2)}, u32[]{:S(2)}) collective-permute-start(bf16[128,640]{1,0:T(8,128)(2,1)S(1)} %fusion.9), channel_id=1, source_target_pairs={{0,2},{1,3},{2,0},{3,1},{4,6},{5,7},{6,4},{7,5},{8,10},{9,11},{10,... | collective-permute-start | bytes 491528 | tf_op jit(solution)/shard_map/ppermute | solution.py:456
  30.9 11.8 %collective-permute-start.8 = (bf16[128,640]{1,0:T(8,128)(2,1)S(1)}, bf16[128,640]{1,0:T(8,128)(2,1)S(1)}, u32[]{:S(2)}, u32[]{:S(2)}) collective-permute-start(bf16[128,640]{1,0:T(8,128)(2,1)S(1)} %fusion.7), channel_id=1, source_target_pairs={{0,4},{1,5},{2,6},{3,7},{4,0},{5,1},{6,2},{7,3},{8,12},{9,13},{10,... | collective-permute-start | bytes 491528 | tf_op jit(solution)/shard_map/ppermute | solution.py:456
  34.9 12.2 %collective-permute-start.7 = (bf16[128,640]{1,0:T(8,128)(2,1)S(1)}, bf16[128,640]{1,0:T(8,128)(2,1)S(1)}, u32[]{:S(2)}, u32[]{:S(2)}) collective-permute-start(bf16[128,640]{1,0:T(8,128)(2,1)S(1)} %fusion.11), channel_id=1, source_target_pairs={{0,2},{1,3},{2,0},{3,1},{4,6},{5,7},{6,4},{7,5},{8,10},{9,11},{10,... | collective-permute-start | bytes 491528 | tf_op jit(solution)/shard_map/ppermute | solution.py:456
  36.3 11.6 %collective-permute-start.4 = (bf16[128,640]{1,0:T(8,128)(2,1)S(1)}, bf16[128,640]{1,0:T(8,128)(2,1)S(1)}, u32[]{:S(2)}, u32[]{:S(2)}) collective-permute-start(bf16[128,640]{1,0:T(8,128)(2,1)S(1)} %fusion.10), channel_id=1, source_target_pairs={{0,2},{1,3},{2,0},{3,1},{4,6},{5,7},{6,4},{7,5},{8,10},{9,11},{10,... | collective-permute-start | bytes 491528 | tf_op jit(solution)/shard_map/ppermute | solution.py:456
  42.7 13.5 %collective-permute-start.10 = (bf16[128,640]{1,0:T(8,128)(2,1)S(1)}, bf16[128,640]{1,0:T(8,128)(2,1)S(1)}, u32[]{:S(2)}, u32[]{:S(2)}) collective-permute-start(bf16[128,640]{1,0:T(8,128)(2,1)S(1)} %fusion.5), channel_id=1, source_target_pairs={{0,8},{1,9},{2,10},{3,11},{4,12},{5,13},{6,14},{7,15},{8,0},{9,1},... | collective-permute-start | bytes 491528 | tf_op jit(solution)/shard_map/ppermute | solution.py:456
  47.2 9.0 %collective-permute-start.9 = (bf16[128,640]{1,0:T(8,128)(2,1)S(1)}, bf16[128,640]{1,0:T(8,128)(2,1)S(1)}, u32[]{:S(2)}, u32[]{:S(2)}) collective-permute-start(bf16[128,640]{1,0:T(8,128)(2,1)S(1)} %fusion.6), channel_id=1, source_target_pairs={{0,4},{1,5},{2,6},{3,7},{4,0},{5,1},{6,2},{7,3},{8,12},{9,13},{10,... | collective-permute-start | bytes 491528 | tf_op jit(solution)/shard_map/ppermute | solution.py:456
  62.9 8.9 %collective-permute-start.12 = (bf16[656,128]{1,0:T(8,128)(2,1)S(1)}, bf16[656,128]{1,0:T(8,128)(2,1)S(1)}, u32[]{:S(2)}, u32[]{:S(2)}) collective-permute-start(bf16[656,128]{1,0:T(8,128)(2,1)S(1)} %get-tuple-element.123.b0), channel_id=1, source_target_pairs={{0,4},{1,5},{2,6},{3,7},{4,0},{5,1},{6,2},{7,3},{8,12},{9,13},{10,... | collective-permute-start | bytes 503816 | tf_op jit(solution)/shard_map/ppermute | solution.py:456
  63.1 11.0 %collective-permute-start.13 = (bf16[656,128]{1,0:T(8,128)(2,1)S(1)}, bf16[656,128]{1,0:T(8,128)(2,1)S(1)}, u32[]{:S(2)}, u32[]{:S(2)}) collective-permute-start(bf16[656,128]{1,0:T(8,128)(2,1)S(1)} %get-tuple-element.123.b0), channel_id=1, source_target_pairs={{0,8},{1,9},{2,10},{3,11},{4,12},{5,13},{6,14},{7,15},{8,0},{9,1},... | collective-permute-start | bytes 503816 | tf_op jit(solution)/shard_map/ppermute | solution.py:456
  64.7 9.4 %collective-permute-start.14 = (bf16[656,128]{1,0:T(8,128)(2,1)S(1)}, bf16[656,128]{1,0:T(8,128)(2,1)S(1)}, u32[]{:S(2)}, u32[]{:S(2)}) collective-permute-start(bf16[656,128]{1,0:T(8,128)(2,1)S(1)} %get-tuple-element.123.b0), channel_id=1, source_target_pairs={{0,2},{1,3},{2,0},{3,1},{4,6},{5,7},{6,4},{7,5},{8,10},{9,11},{10,... | collective-permute-start | bytes 503816 | tf_op jit(solution)/shard_map/ppermute | solution.py:456
  74.1 8.9 %collective-permute-start.17 = (bf16[656,128]{1,0:T(8,128)(2,1)S(1)}, bf16[656,128]{1,0:T(8,128)(2,1)S(1)}, u32[]{:S(2)}, u32[]{:S(2)}) collective-permute-start(bf16[656,128]{1,0:T(8,128)(2,1)S(1)} %collective-permute-done.12.b0), channel_id=1, source_target_pairs={{0,2},{1,3},{2,0},{3,1},{4,6},{5,7},{6,4},{7,5},{8,10},{9,11},{10,... | collective-permute-start | bytes 503816 | tf_op jit(solution)/shard_map/ppermute | solution.py:456
  75.6 8.3 %collective-permute-start.20 = (bf16[656,128]{1,0:T(8,128)(2,1)S(1)}, bf16[656,128]{1,0:T(8,128)(2,1)S(1)}, u32[]{:S(2)}, u32[]{:S(2)}) collective-permute-start(bf16[656,128]{1,0:T(8,128)(2,1)S(1)} %collective-permute-done.12.b0), channel_id=1, source_target_pairs={{0,1},{1,0},{2,3},{3,2},{4,5},{5,4},{6,7},{7,6},{8,9},{9,8},{10,11... | collective-permute-start | bytes 503816 | tf_op jit(solution)/shard_map/ppermute | solution.py:456
  75.8 9.6 %collective-permute-start.24 = (bf16[656,128]{1,0:T(8,128)(2,1)S(1)}, bf16[656,128]{1,0:T(8,128)(2,1)S(1)}, u32[]{:S(2)}, u32[]{:S(2)}) collective-permute-start(bf16[656,128]{1,0:T(8,128)(2,1)S(1)} %collective-permute-done.13.b0), channel_id=1, source_target_pairs={{0,2},{1,3},{2,0},{3,1},{4,6},{5,7},{6,4},{7,5},{8,10},{9,11},{10,... | collective-permute-start | bytes 503816 | tf_op jit(solution)/shard_map/ppermute | solution.py:456
  83.8 9.2 %collective-permute-start.18 = (bf16[656,128]{1,0:T(8,128)(2,1)S(1)}, bf16[656,128]{1,0:T(8,128)(2,1)S(1)}, u32[]{:S(2)}, u32[]{:S(2)}) collective-permute-start(bf16[656,128]{1,0:T(8,128)(2,1)S(1)} %collective-permute-done.16.b0), channel_id=1, source_target_pairs={{0,1},{1,0},{2,3},{3,2},{4,5},{5,4},{6,7},{7,6},{8,9},{9,8},{10,11... | collective-permute-start | bytes 503816 | tf_op jit(solution)/shard_map/ppermute | solution.py:456
  101.9 9.5 %collective-permute-start.32 = (bf16[128,640]{1,0:T(8,128)(2,1)S(1)}, bf16[128,640]{1,0:T(8,128)(2,1)S(1)}, u32[]{:S(2)}, u32[]{:S(2)}) collective-permute-start(bf16[128,640]{1,0:T(8,128)(2,1)S(1)} %fusion.13), channel_id=1, source_target_pairs={{0,2},{1,3},{2,0},{3,1},{4,6},{5,7},{6,4},{7,5},{8,10},{9,11},{10,... | collective-permute-start | bytes 491528 | tf_op jit(solution)/shard_map/ppermute | solution.py:456
  113.1 8.2 %collective-permute-start.30 = (bf16[128,640]{1,0:T(8,128)(2,1)S(1)}, bf16[128,640]{1,0:T(8,128)(2,1)S(1)}, u32[]{:S(2)}, u32[]{:S(2)}) collective-permute-start(bf16[128,640]{1,0:T(8,128)(2,1)S(1)} %fusion.14), channel_id=1, source_target_pairs={{0,2},{1,3},{2,0},{3,1},{4,6},{5,7},{6,4},{7,5},{8,10},{9,11},{10,... | collective-permute-start | bytes 491528 | tf_op jit(solution)/shard_map/ppermute | solution.py:456
  116.3 10.4 %collective-permute-start.36 = (bf16[128,640]{1,0:T(8,128)(2,1)S(1)}, bf16[128,640]{1,0:T(8,128)(2,1)S(1)}, u32[]{:S(2)}, u32[]{:S(2)}) collective-permute-start(bf16[128,640]{1,0:T(8,128)(2,1)S(1)} %fusion.1), channel_id=1, source_target_pairs={{0,8},{1,9},{2,10},{3,11},{4,12},{5,13},{6,14},{7,15},{8,0},{9,1},... | collective-permute-start | bytes 491528 | tf_op jit(solution)/shard_map/ppermute | solution.py:456
  131.6 13.7 %collective-permute-start.37 = (bf16[656,128]{1,0:T(8,128)(2,1)S(1)}, bf16[656,128]{1,0:T(8,128)(2,1)S(1)}, u32[]{:S(2)}, u32[]{:S(2)}) collective-permute-start(bf16[656,128]{1,0:T(8,128)(2,1)S(1)} %get-tuple-element.167.b0), channel_id=1, source_target_pairs={{0,4},{1,5},{2,6},{3,7},{4,0},{5,1},{6,2},{7,3},{8,12},{9,13},{10,... | collective-permute-start | bytes 503816 | tf_op jit(solution)/shard_map/ppermute | solution.py:456
  132.4 12.9 %collective-permute-start.38 = (bf16[656,128]{1,0:T(8,128)(2,1)S(1)}, bf16[656,128]{1,0:T(8,128)(2,1)S(1)}, u32[]{:S(2)}, u32[]{:S(2)}) collective-permute-start(bf16[656,128]{1,0:T(8,128)(2,1)S(1)} %get-tuple-element.167.b0), channel_id=1, source_target_pairs={{0,8},{1,9},{2,10},{3,11},{4,12},{5,13},{6,14},{7,15},{8,0},{9,1},... | collective-permute-start | bytes 503816 | tf_op jit(solution)/shard_map/ppermute | solution.py:456
  133.9 11.4 %collective-permute-start.39 = (bf16[656,128]{1,0:T(8,128)(2,1)S(1)}, bf16[656,128]{1,0:T(8,128)(2,1)S(1)}, u32[]{:S(2)}, u32[]{:S(2)}) collective-permute-start(bf16[656,128]{1,0:T(8,128)(2,1)S(1)} %get-tuple-element.167.b0), channel_id=1, source_target_pairs={{0,2},{1,3},{2,0},{3,1},{4,6},{5,7},{6,4},{7,5},{8,10},{9,11},{10,... | collective-permute-start | bytes 503816 | tf_op jit(solution)/shard_map/ppermute | solution.py:456
  135.4 8.8 %collective-permute-start.41 = (bf16[4,144,128]{2,1,0:T(8,128)(2,1)S(1)}, bf16[4,144,128]{2,1,0:T(8,128)(2,1)S(1)}, u32[]{:S(2)}, u32[]{:S(2)}) collective-permute-start(bf16[4,144,128]{2,1,0:T(8,128)(2,1)S(1)} %get-tuple-element.204), channel_id=1, source_target_pairs={{0,2},{1,3},{2,0},{3,1},{4,6},{5,7},{6,4},{7,5},{8,10},{9,11},{10,... | collective-permute-start | bytes 442376 | tf_op jit(solution)/shard_map/ppermute | solution.py:456
  135.9 9.4 %collective-permute-start.42 = (bf16[4,144,128]{2,1,0:T(8,128)(2,1)S(1)}, bf16[4,144,128]{2,1,0:T(8,128)(2,1)S(1)}, u32[]{:S(2)}, u32[]{:S(2)}) collective-permute-start(bf16[4,144,128]{2,1,0:T(8,128)(2,1)S(1)} %get-tuple-element.206), channel_id=1, source_target_pairs={{0,3},{1,2},{2,1},{3,0},{4,7},{5,6},{6,5},{7,4},{8,11},{9,10},{10,... | collective-permute-start | bytes 442376 | tf_op jit(solution)/shard_map/ppermute | solution.py:456
  145.3 7.9 %collective-permute-start.43 = (bf16[656,128]{1,0:T(8,128)(2,1)S(1)}, bf16[656,128]{1,0:T(8,128)(2,1)S(1)}, u32[]{:S(2)}, u32[]{:S(2)}) collective-permute-start(bf16[656,128]{1,0:T(8,128)(2,1)S(1)} %collective-permute-done.38.b0), channel_id=1, source_target_pairs={{0,4},{1,5},{2,6},{3,7},{4,0},{5,1},{6,2},{7,3},{8,12},{9,13},{10,... | collective-permute-start | bytes 503816 | tf_op jit(solution)/shard_map/ppermute | solution.py:456
  146.8 10.3 %collective-permute-start.44 = (bf16[656,128]{1,0:T(8,128)(2,1)S(1)}, bf16[656,128]{1,0:T(8,128)(2,1)S(1)}, u32[]{:S(2)}, u32[]{:S(2)}) collective-permute-start(bf16[656,128]{1,0:T(8,128)(2,1)S(1)} %collective-permute-done.37.b0), channel_id=1, source_target_pairs={{0,2},{1,3},{2,0},{3,1},{4,6},{5,7},{6,4},{7,5},{8,10},{9,11},{10,... | collective-permute-start | bytes 503816 | tf_op jit(solution)/shard_map/ppermute | solution.py:456
  148.7 10.0 %collective-permute-start.51 = (bf16[4,144,128]{2,1,0:T(8,128)(2,1)S(1)}, bf16[4,144,128]{2,1,0:T(8,128)(2,1)S(1)}, u32[]{:S(2)}, u32[]{:S(2)}) collective-permute-start(bf16[4,144,128]{2,1,0:T(8,128)(2,1)S(1)} %get-tuple-element.201), channel_id=1, source_target_pairs={{0,4},{1,5},{2,6},{3,7},{4,0},{5,1},{6,2},{7,3},{8,12},{9,13},{10,... | collective-permute-start | bytes 442376 | tf_op jit(solution)/shard_map/ppermute | solution.py:456
  149.4 10.9 %collective-permute-start.52 = (bf16[4,144,128]{2,1,0:T(8,128)(2,1)S(1)}, bf16[4,144,128]{2,1,0:T(8,128)(2,1)S(1)}, u32[]{:S(2)}, u32[]{:S(2)}) collective-permute-start(bf16[4,144,128]{2,1,0:T(8,128)(2,1)S(1)} %get-tuple-element.200), channel_id=1, source_target_pairs={{0,8},{1,9},{2,10},{3,11},{4,12},{5,13},{6,14},{7,15},{8,0},{9,1},... | collective-permute-start | bytes 442376 | tf_op jit(solution)/shard_map/ppermute | solution.py:456
  150.8 16.8 %collective-permute-start.49 = (bf16[656,128]{1,0:T(8,128)(2,1)S(1)}, bf16[656,128]{1,0:T(8,128)(2,1)S(1)}, u32[]{:S(2)}, u32[]{:S(2)}) collective-permute-start(bf16[656,128]{1,0:T(8,128)(2,1)S(1)} %collective-permute-done.37.b0), channel_id=1, source_target_pairs={{0,1},{1,0},{2,3},{3,2},{4,5},{5,4},{6,7},{7,6},{8,9},{9,8},{10,11... | collective-permute-start | bytes 503816 | tf_op jit(solution)/shard_map/ppermute | solution.py:456
  153.2 14.9 %collective-permute-start.56 = (bf16[656,128]{1,0:T(8,128)(2,1)S(1)}, bf16[656,128]{1,0:T(8,128)(2,1)S(1)}, u32[]{:S(2)}, u32[]{:S(2)}) collective-permute-start(bf16[656,128]{1,0:T(8,128)(2,1)S(1)} %collective-permute-done.38.b0), channel_id=1, source_target_pairs={{0,2},{1,3},{2,0},{3,1},{4,6},{5,7},{6,4},{7,5},{8,10},{9,11},{10,... | collective-permute-start | bytes 503816 | tf_op jit(solution)/shard_map/ppermute | solution.py:456
  157.1 11.1 %collective-permute-start.50 = (bf16[656,128]{1,0:T(8,128)(2,1)S(1)}, bf16[656,128]{1,0:T(8,128)(2,1)S(1)}, u32[]{:S(2)}, u32[]{:S(2)}) collective-permute-start(bf16[656,128]{1,0:T(8,128)(2,1)S(1)} %collective-permute-done.44.b2), channel_id=1, source_target_pairs={{0,1},{1,0},{2,3},{3,2},{4,5},{5,4},{6,7},{7,6},{8,9},{9,8},{10,11... | collective-permute-start | bytes 503816 | tf_op jit(solution)/shard_map/ppermute | solution.py:456
  158.7 12.0 %collective-permute-start.48 = (bf16[656,128]{1,0:T(8,128)(2,1)S(1)}, bf16[656,128]{1,0:T(8,128)(2,1)S(1)}, u32[]{:S(2)}, u32[]{:S(2)}) collective-permute-start(bf16[656,128]{1,0:T(8,128)(2,1)S(1)} %collective-permute-done.43.b0), channel_id=1, source_target_pairs={{0,2},{1,3},{2,0},{3,1},{4,6},{5,7},{6,4},{7,5},{8,10},{9,11},{10,... | collective-permute-start | bytes 503816 | tf_op jit(solution)/shard_map/ppermute | solution.py:456
  160.2 7.4 %collective-permute-start.53 = (bf16[4,144,128]{2,1,0:T(8,128)(2,1)S(1)}, bf16[4,144,128]{2,1,0:T(8,128)(2,1)S(1)}, u32[]{:S(2)}, u32[]{:S(2)}) collective-permute-start(bf16[4,144,128]{2,1,0:T(8,128)(2,1)S(1)} %get-tuple-element.199), channel_id=1, source_target_pairs={{0,12},{1,13},{2,14},{3,15},{4,8},{5,9},{6,10},{7,11},{8,4},{9,5},... | collective-permute-start | bytes 442376 | tf_op jit(solution)/shard_map/ppermute | solution.py:456
  (37 other events, 224.6 us)

commit v13 on v12

--- a/solution.py
+++ b/solution.py
@@ -600,7 +600,8 @@
             spread(3)
             settle_far(1)
             if last:
-                acc, *back = lax.optimization_barrier((acc, *back))
+                acc, *back = lax.optimization_barrier((acc, *back[::-1]))
+                back = back[::-1]
             acc, total = flow_chunk(resident[1], blocks(1), acc, total, weight=weight)
             settle_far(2)
             far[3], acc = lax.optimization_barrier((far[3], acc))

time: 180 us -> 182 us (1.011)
  waiting for transfers between devices: 49.7 us -> 57.4 us
  starting transfers between devices: 56.8 us -> 50.8 us
    ppermute x58, waiting for transfers between devices: 49.7 us -> 57.4 us  [swap(): return lax.ppermute(x, 'bus', [(i, i ^ mask) for i in range(devices)])]
    ppermute x58, starting transfers between devices: 51.8 us -> 45.8 us  [swap(): return lax.ppermute(x, 'bus', [(i, i ^ mask) for i in range(devices)])]
  transfers between devices with their start and end apart: 59 -> 59, of which waited for: 18 -> 19; matrix products, arithmetic and copies ran while one was open for 1% -> 1% of each run, Pallas kernels for 24% -> 24%
where the time goes in v13:
time: 182 us
  Pallas kernels  68.7 us (38%)
  waiting for transfers between devices  57.4 us (32%)
  starting transfers between devices  50.8 us (28%)
  other arithmetic  2.99 us (2%)
    ppermute x58, waiting for transfers between devices, swap(): return lax.ppermute(x, 'bus', [(i, i ^ mask) for i in range(devices)])  57.4 us
    ppermute x58, starting transfers between devices, swap(): return lax.ppermute(x, 'bus', [(i, i ^ mask) for i in range(devices)])  45.8 us
    pallas_call x8, Pallas kernels, shadow_chunk(): pl.pallas_call(functools.partial(shadow_kernel, chunk, stream, turn), in_...  21.4 us
    pallas_call x8, Pallas kernels, flow_chunk(): pl.pallas_call(functools.partial(flow_kernel, start, end), in_specs=[VMEM...  20.7 us
    pallas_call x2, Pallas kernels, update(): pl.pallas_call(functools.partial(update_kernel, cap, devices, first, last...  11.3 us
    pallas_call x2, Pallas kernels, load_chunks(): pl.pallas_call(functools.partial(load_kernel, chunks), in_specs=[SMEM_SPE...  9.58 us
    all_to_all x1, starting transfers between devices, local(): lax.all_to_all(outgoing, 'bus', split_axis=0, concat_axis=0, tiled=True)  4.98 us
  transfers between devices with their start and end apart: 59, of which 19 were waited for; matrix products, arithmetic and copies ran while one was open for 1% of the time, Pallas kernels for 24%

profile of v13, /device:TPU:0, one launch (start us, length us, event | category | flops | bytes accessed | tf_op | source)
XLA Modules:
  0.0 181.6 jit_solution(2508055423121124810)
XLA Ops:
  0.7 3.7 %shadow_chunk.8 = (f32[2,128,640]{2,1,0:T(8,128)S(1)}, bf16[2,128,640]{2,1,0:T(8,128)(2,1)S(1)}, bf16[128,1280]{1,0:T(8,128)(2,1)S(1)}) custom-call(s32[1]{0:T(128)} %bitcast.place_ref, f32[1280,128]{1,0:T(8,128)} %rest_1_.1, bf16[1280,10240]{1,0:T(8,128)(2,1)} %ptdf_ref.11), custom_call_target="tpu_custom_call" | custom-call | flops 2516582400 | bytes 6553600 | tf_op jit(solution)/shard_map/shadow_chunk/pallas_call | solution.py:346
  4.9 3.6 %pack_generators.1 = (bf16[16,160,256]{2,1,0:T(8,128)(2,1)}, s32[1,768]{1,0:T(1,128)S(1)}) custom-call(s32[1]{0:T(128)} %bitcast.place_ref, s32[1,768]{1,0:T(1,128)S(1)} %bitcast.88, s32[6,128]{1,0:T(8,128)S(1)} %bitcast.86, f32[6,128]{1,0:T(8,128)S(1)} %bitcast.87, f32[768,128]{1,0:T(8,128)S(1)} %copy-done.1, f32[6,128]{1,0:T(8,128)S(1)} %bitcast.82, ...), custom_call_target="tpu_custom_call" | custom-call | flops 905969664 | bytes 3145728 | tf_op jit(solution)/shard_map/pack_generators/pallas_call | solution.py:107
  9.2 2.6 %collective-permute-start.1 = (bf16[128,640]{1,0:T(8,128)(2,1)}, bf16[128,640]{1,0:T(8,128)(2,1)}, u32[]{:S(2)}, u32[]{:S(2)}) collective-permute-start(bf16[128,640]{1,0:T(8,128)(2,1)} %fusion.8), channel_id=1, source_target_pairs={{0,2},{1,3},{2,0},{3,1},{4,6},{5,7},{6,4},{7,5},{8,10},{9,11},{10,... | collective-permute-start | bytes 491528 | tf_op jit(solution)/shard_map/ppermute | solution.py:456
  11.8 5.0 %all-to-all-start = ((bf16[16,160,256]{2,1,0:T(8,128)(2,1)}), bf16[16,160,256]{2,1,0:T(8,128)(2,1)S(1)}, u32[]{:S(2)}, u32[]{:S(2)}) async-start(bf16[16,160,256]{2,1,0:T(8,128)(2,1)} %get-tuple-element.121), calls=%async_computation | async-start | bytes 2621440 | tf_op jit(solution)/shard_map/all_to_all | solution.py:535
  17.9 3.4 %shadow_chunk.9 = (f32[2,128,640]{2,1,0:T(8,128)S(1)}, bf16[2,128,640]{2,1,0:T(8,128)(2,1)S(1)}) custom-call(s32[1]{0:T(128)} %bitcast.place_ref, bf16[128,1280]{1,0:T(8,128)(2,1)S(1)} %get-tuple-element.111.line_ref, bf16[1280,10240]{1,0:T(8,128)(2,1)} %ptdf_ref.11), custom_call_target="tpu_custom_call" | custom-call | flops 2516582400 | bytes 6553600 | tf_op jit(solution)/shard_map/shadow_chunk/pallas_call | solution.py:346
  21.7 3.4 %shadow_chunk.11 = (f32[2,128,640]{2,1,0:T(8,128)S(1)}, bf16[2,128,640]{2,1,0:T(8,128)(2,1)S(1)}) custom-call(s32[1]{0:T(128)} %bitcast.place_ref, bf16[128,1280]{1,0:T(8,128)(2,1)S(1)} %get-tuple-element.111.line_ref, bf16[1280,10240]{1,0:T(8,128)(2,1)} %ptdf_ref.11), custom_call_target="tpu_custom_call" | custom-call | flops 2516582400 | bytes 6553600 | tf_op jit(solution)/shard_map/shadow_chunk/pallas_call | solution.py:346
  27.3 3.4 %shadow_chunk.10 = (f32[2,128,640]{2,1,0:T(8,128)S(1)}, bf16[2,128,640]{2,1,0:T(8,128)(2,1)S(1)}) custom-call(s32[1]{0:T(128)} %bitcast.place_ref, bf16[128,1280]{1,0:T(8,128)(2,1)S(1)} %get-tuple-element.111.line_ref, bf16[1280,10240]{1,0:T(8,128)(2,1)} %ptdf_ref.11), custom_call_target="tpu_custom_call" | custom-call | flops 2516582400 | bytes 6553600 | tf_op jit(solution)/shard_map/shadow_chunk/pallas_call | solution.py:346
  32.5 2.4 %collective-permute-done.6 = bf16[128,640]{1,0:T(8,128)(2,1)S(1)} collective-permute-done((bf16[128,640]{1,0:T(8,128)(2,1)S(1)}, bf16[128,640]{1,0:T(8,128)(2,1)S(1)}, u32[]{:S(2)}, u32[]{:S(2)}) %collective-permute-start.6) | collective-permute-done | bytes 163872 | tf_op jit(solution)/shard_map/ppermute | solution.py:456
  37.1 5.5 %collective-permute-done.8 = bf16[128,640]{1,0:T(8,128)(2,1)S(1)} collective-permute-done((bf16[128,640]{1,0:T(8,128)(2,1)S(1)}, bf16[128,640]{1,0:T(8,128)(2,1)S(1)}, u32[]{:S(2)}, u32[]{:S(2)}) %collective-permute-start.8) | collective-permute-done | bytes 163872 | tf_op jit(solution)/shard_map/ppermute | solution.py:456
  42.7 4.4 %collective-permute-start.10 = (bf16[128,640]{1,0:T(8,128)(2,1)S(1)}, bf16[128,640]{1,0:T(8,128)(2,1)S(1)}, u32[]{:S(2)}, u32[]{:S(2)}) collective-permute-start(bf16[128,640]{1,0:T(8,128)(2,1)S(1)} %fusion.5), channel_id=1, source_target_pairs={{0,8},{1,9},{2,10},{3,11},{4,12},{5,13},{6,14},{7,15},{8,0},{9,1},... | collective-permute-start | bytes 491528 | tf_op jit(solution)/shard_map/ppermute | solution.py:456
  47.9 8.3 %collective-permute-done.9.refs_1_ = bf16[128,640]{1,0:T(8,128)(2,1)S(1)} collective-permute-done((bf16[128,640]{1,0:T(8,128)(2,1)S(1)}, bf16[128,640]{1,0:T(8,128)(2,1)S(1)}, u32[]{:S(2)}, u32[]{:S(2)}) %collective-permute-start.9) | collective-permute-done | bytes 163872 | tf_op jit(solution)/shard_map/ppermute | solution.py:456
  56.3 6.5 %update_generators.2 = (f32[16,144,128]{2,1,0:T(8,128)S(1)}, bf16[656,128]{1,0:T(8,128)(2,1)S(1)}, bf16[1280,2560]{1,0:T(8,128)(2,1)S(1)}) custom-call(s32[1]{0:T(128)} %bitcast.place_ref, f32[128,640]{1,0:T(8,128)S(1)} %bitcast_add_fusion.6.refs_0_, bf16[128,640]{1,0:T(8,128)(2,1)S(1)} %collective-permute-done.9.refs_1_, ...), custom_call_target="tpu_custom_call" | custom-call | flops 1509949440 | bytes 4194304 | tf_op jit(solution)/shard_map/update_generators/pallas_call | solution.py:276
  66.2 5.4 %load_chunks.2 = (s32[1]{0:T(128)}, bf16[1280,2560]{1,0:T(8,128)(2,1)S(1)}, bf16[1280,2560]{1,0:T(8,128)(2,1)S(1)}) custom-call(s32[1]{0:T(128)} %bitcast.place_ref, bf16[1280,10240]{1,0:T(8,128)(2,1)} %ptdf_ref.11), custom_call_target="tpu_custom_call" | custom-call | bytes 13107200 | tf_op jit(solution)/shard_map/load_chunks/pallas_call | solution.py:387
  71.8 2.3 %collective-permute-done.13.b0 = bf16[656,128]{1,0:T(8,128)(2,1)S(1)} collective-permute-done((bf16[656,128]{1,0:T(8,128)(2,1)S(1)}, bf16[656,128]{1,0:T(8,128)(2,1)S(1)}, u32[]{:S(2)}, u32[]{:S(2)}) %collective-permute-start.13) | collective-permute-done | bytes 167968 | tf_op jit(solution)/shard_map/ppermute | solution.py:456
  76.4 2.4 %flow_chunk.8 = (f32[1280,128]{1,0:T(8,128)S(1)}, f32[1,128]{1,0:T(1,128)S(1)}) custom-call(bf16[1280,2560]{1,0:T(8,128)(2,1)S(1)} %get-tuple-element.122.ptdf_ref, bf16[656,128]{1,0:T(8,128)(2,1)S(1)} %get-tuple-element.123.b0, bf16[656,128]{1,0:T(8,128)(2,1)S(1)} %collective-permute-done.11.b1, bf16[656,128]{1,0:T(8,128)(2,1)S(1)} %collective-permute-done.14.b2, ...), custom_call_target="tpu_custom_call" | custom-call | flops 2516582400 | bytes 6553600 | tf_op jit(solution)/shard_map/flow_chunk/pallas_call | solution.py:444
  78.8 4.1 %load_chunks.3 = (s32[1]{0:T(128)}, bf16[1280,2560]{1,0:T(8,128)(2,1)S(1)}) custom-call(s32[1]{0:T(128)} %get-tuple-element.130.place_ref, bf16[1280,10240]{1,0:T(8,128)(2,1)} %ptdf_ref.11), custom_call_target="tpu_custom_call" | custom-call | bytes 6553600 | tf_op jit(solution)/shard_map/load_chunks/pallas_call | solution.py:387
  85.6 2.4 %flow_chunk.9 = (f32[1280,128]{1,0:T(8,128)S(1)}, f32[1,128]{1,0:T(1,128)S(1)}) custom-call(bf16[1280,2560]{1,0:T(8,128)(2,1)S(1)} %get-tuple-element.138.ptdf_ref, bf16[656,128]{1,0:T(8,128)(2,1)S(1)} %collective-permute-done.12.b0, bf16[656,128]{1,0:T(8,128)(2,1)S(1)} %collective-permute-done.20.b1, bf16[656,128]{1,0:T(8,128)(2,1)S(1)} %collective-permute-done.17.b2, ...), custom_call_target="tpu_custom_call" | custom-call | flops 2516582400 | bytes 6553600 | tf_op jit(solution)/shard_map/flow_chunk/pallas_call | solution.py:444
  88.0 2.5 %collective-permute-done.19.b2 = bf16[656,128]{1,0:T(8,128)(2,1)S(1)} collective-permute-done((bf16[656,128]{1,0:T(8,128)(2,1)S(1)}, bf16[656,128]{1,0:T(8,128)(2,1)S(1)}, u32[]{:S(2)}, u32[]{:S(2)}) %collective-permute-start.19) | collective-permute-done | bytes 167968 | tf_op jit(solution)/shard_map/ppermute | solution.py:456
  90.6 2.4 %flow_chunk.10 = (f32[1280,128]{1,0:T(8,128)S(1)}, f32[1,128]{1,0:T(1,128)S(1)}) custom-call(bf16[1280,2560]{1,0:T(8,128)(2,1)S(1)} %get-tuple-element.144.ptdf_ref, bf16[656,128]{1,0:T(8,128)(2,1)S(1)} %collective-permute-done.13.b0, bf16[656,128]{1,0:T(8,128)(2,1)S(1)} %collective-permute-done.23.b1, bf16[656,128]{1,0:T(8,128)(2,1)S(1)} %collective-permute-done.24.b2, ...), custom_call_target="tpu_custom_call" | custom-call | flops 2516582400 | bytes 6553600 | tf_op jit(solution)/shard_map/flow_chunk/pallas_call | solution.py:444
  93.0 2.8 %flow_chunk.11 = (f32[1280,128]{1,0:T(8,128)S(1)}, bf16[128,1280]{1,0:T(8,128)(2,1)S(1)}, f32[1,128]{1,0:T(1,128)S(1)}) custom-call(bf16[1280,2560]{1,0:T(8,128)(2,1)S(1)} %get-tuple-element.131.ptdf_ref, bf16[656,128]{1,0:T(8,128)(2,1)S(1)} %collective-permute-done.16.b0, bf16[656,128]{1,0:T(8,128)(2,1)S(1)} %collective-permute-done.18.b1, ...), custom_call_target="tpu_custom_call" | custom-call | flops 2516582400 | bytes 6553600 | tf_op jit(solution)/shard_map/flow_chunk/pallas_call | solution.py:444
  113.7 2.5 %collective-permute-done.34 = bf16[128,640]{1,0:T(8,128)(2,1)S(1)} collective-permute-done((bf16[128,640]{1,0:T(8,128)(2,1)S(1)}, bf16[128,640]{1,0:T(8,128)(2,1)S(1)}, u32[]{:S(2)}, u32[]{:S(2)}) %collective-permute-start.34) | collective-permute-done | bytes 163872 | tf_op jit(solution)/shard_map/ppermute | solution.py:456
  121.4 4.2 %collective-permute-done.35.refs_1_ = bf16[128,640]{1,0:T(8,128)(2,1)S(1)} collective-permute-done((bf16[128,640]{1,0:T(8,128)(2,1)S(1)}, bf16[128,640]{1,0:T(8,128)(2,1)S(1)}, u32[]{:S(2)}, u32[]{:S(2)}) %collective-permute-start.35) | collective-permute-done | bytes 163872 | tf_op jit(solution)/shard_map/ppermute | solution.py:456
  126.7 4.8 %update_generators.3 = (bf16[16,144,128]{2,1,0:T(8,128)(2,1)S(1)}, bf16[656,128]{1,0:T(8,128)(2,1)S(1)}) custom-call(s32[1]{0:T(128)} %get-tuple-element.136.place_ref, f32[128,640]{1,0:T(8,128)S(1)} %bitcast_add_fusion.2.refs_0_, bf16[128,640]{1,0:T(8,128)(2,1)S(1)} %collective-permute-done.35.refs_1_, ...), custom_call_target="tpu_custom_call" | custom-call | flops 1509949440 | bytes 4194304 | tf_op jit(solution)/shard_map/update_generators/pallas_call | solution.py:276
  136.4 7.9 %collective-permute-done.41 = bf16[4,144,128]{2,1,0:T(8,128)(2,1)S(1)} collective-permute-done((bf16[4,144,128]{2,1,0:T(8,128)(2,1)S(1)}, bf16[4,144,128]{2,1,0:T(8,128)(2,1)S(1)}, u32[]{:S(2)}, u32[]{:S(2)}) %collective-permute-start.41) | collective-permute-done | bytes 147488 | tf_op jit(solution)/shard_map/ppermute | solution.py:456
  150.8 2.4 %flow_chunk.12 = (f32[1280,128]{1,0:T(8,128)S(1)}, f32[1,128]{1,0:T(1,128)S(1)}) custom-call(bf16[1280,2560]{1,0:T(8,128)(2,1)S(1)} %get-tuple-element.122.ptdf_ref, bf16[656,128]{1,0:T(8,128)(2,1)S(1)} %get-tuple-element.167.b0, bf16[656,128]{1,0:T(8,128)(2,1)S(1)} %collective-permute-done.45.b1, bf16[656,128]{1,0:T(8,128)(2,1)S(1)} %collective-permute-done.39.b2, ...), custom_call_target="tpu_custom_call" | custom-call | flops 104857600 | bytes 819200 | tf_op jit(solution)/shard_map/flow_chunk/pallas_call | solution.py:444
  154.1 3.3 %collective-permute-done.51.refs_3_ = bf16[4,144,128]{2,1,0:T(8,128)(2,1)S(1)} collective-permute-done((bf16[4,144,128]{2,1,0:T(8,128)(2,1)S(1)}, bf16[4,144,128]{2,1,0:T(8,128)(2,1)S(1)}, u32[]{:S(2)}, u32[]{:S(2)}) %collective-permute-start.51) | collective-permute-done | bytes 147488 | tf_op jit(solution)/shard_map/ppermute | solution.py:456
  158.1 6.1 %collective-permute-done.52.refs_2_ = bf16[4,144,128]{2,1,0:T(8,128)(2,1)S(1)} collective-permute-done((bf16[4,144,128]{2,1,0:T(8,128)(2,1)S(1)}, bf16[4,144,128]{2,1,0:T(8,128)(2,1)S(1)}, u32[]{:S(2)}, u32[]{:S(2)}) %collective-permute-start.52) | collective-permute-done | bytes 147488 | tf_op jit(solution)/shard_map/ppermute | solution.py:456
  164.2 5.1 %collective-permute-done.53.refs_1_ = bf16[4,144,128]{2,1,0:T(8,128)(2,1)S(1)} collective-permute-done((bf16[4,144,128]{2,1,0:T(8,128)(2,1)S(1)}, bf16[4,144,128]{2,1,0:T(8,128)(2,1)S(1)}, u32[]{:S(2)}, u32[]{:S(2)}) %collective-permute-start.53) | collective-permute-done | bytes 147488 | tf_op jit(solution)/shard_map/ppermute | solution.py:456
  169.9 2.4 %flow_chunk.13 = (f32[1280,128]{1,0:T(8,128)S(1)}, f32[1,128]{1,0:T(1,128)S(1)}) custom-call(bf16[1280,2560]{1,0:T(8,128)(2,1)S(1)} %get-tuple-element.138.ptdf_ref, bf16[656,128]{1,0:T(8,128)(2,1)S(1)} %collective-permute-done.37.b0, bf16[656,128]{1,0:T(8,128)(2,1)S(1)} %collective-permute-done.49.b1, bf16[656,128]{1,0:T(8,128)(2,1)S(1)} %collective-permute-done.44.b2, ...), custom_call_target="tpu_custom_call" | custom-call | flops 104857600 | bytes 819200 | tf_op jit(solution)/shard_map/flow_chunk/pallas_call | solution.py:444
  173.0 2.4 %flow_chunk.14 = (f32[1280,128]{1,0:T(8,128)S(1)}, f32[1,128]{1,0:T(1,128)S(1)}) custom-call(bf16[1280,2560]{1,0:T(8,128)(2,1)S(1)} %get-tuple-element.144.ptdf_ref, bf16[656,128]{1,0:T(8,128)(2,1)S(1)} %collective-permute-done.38.b0, bf16[656,128]{1,0:T(8,128)(2,1)S(1)} %collective-permute-done.55.b1, bf16[656,128]{1,0:T(8,128)(2,1)S(1)} %collective-permute-done.56.b2, ...), custom_call_target="tpu_custom_call" | custom-call | flops 104857600 | bytes 819200 | tf_op jit(solution)/shard_map/flow_chunk/pallas_call | solution.py:444
  175.5 3.4 %flow_chunk.15 = (f32[1280,128]{1,0:T(8,128)}, bf16[128,1280]{1,0:T(8,128)(2,1)}, f32[1,128]{1,0:T(1,128)S(1)}) custom-call(bf16[1280,2560]{1,0:T(8,128)(2,1)S(1)} %get-tuple-element.131.ptdf_ref, bf16[656,128]{1,0:T(8,128)(2,1)S(1)} %collective-permute-done.43.b0, bf16[656,128]{1,0:T(8,128)(2,1)S(1)} %collective-permute-done.47.b1, ...), custom_call_target="tpu_custom_call" | custom-call | flops 104857600 | bytes 819200 | tf_op jit(solution)/shard_map/flow_chunk/pallas_call | solution.py:444
  179.4 2.2 %unpack_dispatch.1 = f32[768,128]{1,0:T(8,128)} custom-call(s32[1,768]{1,0:T(1,128)S(1)} %get-tuple-element.101.slot_ref, bf16[4,144,128]{2,1,0:T(8,128)(2,1)S(1)} %get-tuple-element.193.refs_0_, bf16[4,144,128]{2,1,0:T(8,128)(2,1)S(1)} %collective-permute-done.53.refs_1_, bf16[4,144,128]{2,1,0:T(8,128)(2,1)S(1)} %collective-permute-done.52.refs_2_, ...), custom_call_target="tpu_custom_call" | custom-call | flops 452984832 | bytes 1048576 | tf_op jit(solution)/shard_map/unpack_dispatch/pallas_call | solution.py:172
  (151 shorter events, 56.9 us)
Async XLA Ops:
  9.2 7.7 %collective-permute-start.1 = (bf16[128,640]{1,0:T(8,128)(2,1)}, bf16[128,640]{1,0:T(8,128)(2,1)}, u32[]{:S(2)}, u32[]{:S(2)}) collective-permute-start(bf16[128,640]{1,0:T(8,128)(2,1)} %fusion.8), channel_id=1, source_target_pairs={{0,2},{1,3},{2,0},{3,1},{4,6},{5,7},{6,4},{7,5},{8,10},{9,11},{10,... | collective-permute-start | bytes 491528 | tf_op jit(solution)/shard_map/ppermute | solution.py:456
  11.8 44.5 %all-to-all-start = ((bf16[16,160,256]{2,1,0:T(8,128)(2,1)}), bf16[16,160,256]{2,1,0:T(8,128)(2,1)S(1)}, u32[]{:S(2)}, u32[]{:S(2)}) async-start(bf16[16,160,256]{2,1,0:T(8,128)(2,1)} %get-tuple-element.121), calls=%async_computation | async-start | bytes 2621440 | tf_op jit(solution)/shard_map/all_to_all | solution.py:535
  25.1 7.3 %collective-permute-start.5 = (bf16[2,128,640]{2,1,0:T(8,128)(2,1)S(1)}, bf16[2,128,640]{2,1,0:T(8,128)(2,1)S(1)}, u32[]{:S(2)}, u32[]{:S(2)}) collective-permute-start(bf16[2,128,640]{2,1,0:T(8,128)(2,1)S(1)} %get-tuple-element.115), channel_id=1, source_target_pairs={{0,1},{1,0},{2,3},{3,2},{4,5},{5,4},{6,7},{7,6},{8,9},{9,8},{10,11... | collective-permute-start | bytes 983048 | tf_op jit(solution)/shard_map/ppermute | solution.py:456
  25.5 9.4 %collective-permute-start.6 = (bf16[128,640]{1,0:T(8,128)(2,1)S(1)}, bf16[128,640]{1,0:T(8,128)(2,1)S(1)}, u32[]{:S(2)}, u32[]{:S(2)}) collective-permute-start(bf16[128,640]{1,0:T(8,128)(2,1)S(1)} %fusion.9), channel_id=1, source_target_pairs={{0,2},{1,3},{2,0},{3,1},{4,6},{5,7},{6,4},{7,5},{8,10},{9,11},{10,... | collective-permute-start | bytes 491528 | tf_op jit(solution)/shard_map/ppermute | solution.py:456
  30.9 11.8 %collective-permute-start.8 = (bf16[128,640]{1,0:T(8,128)(2,1)S(1)}, bf16[128,640]{1,0:T(8,128)(2,1)S(1)}, u32[]{:S(2)}, u32[]{:S(2)}) collective-permute-start(bf16[128,640]{1,0:T(8,128)(2,1)S(1)} %fusion.7), channel_id=1, source_target_pairs={{0,4},{1,5},{2,6},{3,7},{4,0},{5,1},{6,2},{7,3},{8,12},{9,13},{10,... | collective-permute-start | bytes 491528 | tf_op jit(solution)/shard_map/ppermute | solution.py:456
  34.9 12.2 %collective-permute-start.7 = (bf16[128,640]{1,0:T(8,128)(2,1)S(1)}, bf16[128,640]{1,0:T(8,128)(2,1)S(1)}, u32[]{:S(2)}, u32[]{:S(2)}) collective-permute-start(bf16[128,640]{1,0:T(8,128)(2,1)S(1)} %fusion.11), channel_id=1, source_target_pairs={{0,2},{1,3},{2,0},{3,1},{4,6},{5,7},{6,4},{7,5},{8,10},{9,11},{10,... | collective-permute-start | bytes 491528 | tf_op jit(solution)/shard_map/ppermute | solution.py:456
  36.3 11.6 %collective-permute-start.4 = (bf16[128,640]{1,0:T(8,128)(2,1)S(1)}, bf16[128,640]{1,0:T(8,128)(2,1)S(1)}, u32[]{:S(2)}, u32[]{:S(2)}) collective-permute-start(bf16[128,640]{1,0:T(8,128)(2,1)S(1)} %fusion.10), channel_id=1, source_target_pairs={{0,2},{1,3},{2,0},{3,1},{4,6},{5,7},{6,4},{7,5},{8,10},{9,11},{10,... | collective-permute-start | bytes 491528 | tf_op jit(solution)/shard_map/ppermute | solution.py:456
  42.7 13.5 %collective-permute-start.10 = (bf16[128,640]{1,0:T(8,128)(2,1)S(1)}, bf16[128,640]{1,0:T(8,128)(2,1)S(1)}, u32[]{:S(2)}, u32[]{:S(2)}) collective-permute-start(bf16[128,640]{1,0:T(8,128)(2,1)S(1)} %fusion.5), channel_id=1, source_target_pairs={{0,8},{1,9},{2,10},{3,11},{4,12},{5,13},{6,14},{7,15},{8,0},{9,1},... | collective-permute-start | bytes 491528 | tf_op jit(solution)/shard_map/ppermute | solution.py:456
  47.2 9.0 %collective-permute-start.9 = (bf16[128,640]{1,0:T(8,128)(2,1)S(1)}, bf16[128,640]{1,0:T(8,128)(2,1)S(1)}, u32[]{:S(2)}, u32[]{:S(2)}) collective-permute-start(bf16[128,640]{1,0:T(8,128)(2,1)S(1)} %fusion.6), channel_id=1, source_target_pairs={{0,4},{1,5},{2,6},{3,7},{4,0},{5,1},{6,2},{7,3},{8,12},{9,13},{10,... | collective-permute-start | bytes 491528 | tf_op jit(solution)/shard_map/ppermute | solution.py:456
  62.9 8.9 %collective-permute-start.12 = (bf16[656,128]{1,0:T(8,128)(2,1)S(1)}, bf16[656,128]{1,0:T(8,128)(2,1)S(1)}, u32[]{:S(2)}, u32[]{:S(2)}) collective-permute-start(bf16[656,128]{1,0:T(8,128)(2,1)S(1)} %get-tuple-element.123.b0), channel_id=1, source_target_pairs={{0,4},{1,5},{2,6},{3,7},{4,0},{5,1},{6,2},{7,3},{8,12},{9,13},{10,... | collective-permute-start | bytes 503816 | tf_op jit(solution)/shard_map/ppermute | solution.py:456
  63.1 11.0 %collective-permute-start.13 = (bf16[656,128]{1,0:T(8,128)(2,1)S(1)}, bf16[656,128]{1,0:T(8,128)(2,1)S(1)}, u32[]{:S(2)}, u32[]{:S(2)}) collective-permute-start(bf16[656,128]{1,0:T(8,128)(2,1)S(1)} %get-tuple-element.123.b0), channel_id=1, source_target_pairs={{0,8},{1,9},{2,10},{3,11},{4,12},{5,13},{6,14},{7,15},{8,0},{9,1},... | collective-permute-start | bytes 503816 | tf_op jit(solution)/shard_map/ppermute | solution.py:456
  64.7 9.4 %collective-permute-start.14 = (bf16[656,128]{1,0:T(8,128)(2,1)S(1)}, bf16[656,128]{1,0:T(8,128)(2,1)S(1)}, u32[]{:S(2)}, u32[]{:S(2)}) collective-permute-start(bf16[656,128]{1,0:T(8,128)(2,1)S(1)} %get-tuple-element.123.b0), channel_id=1, source_target_pairs={{0,2},{1,3},{2,0},{3,1},{4,6},{5,7},{6,4},{7,5},{8,10},{9,11},{10,... | collective-permute-start | bytes 503816 | tf_op jit(solution)/shard_map/ppermute | solution.py:456
  74.1 8.9 %collective-permute-start.17 = (bf16[656,128]{1,0:T(8,128)(2,1)S(1)}, bf16[656,128]{1,0:T(8,128)(2,1)S(1)}, u32[]{:S(2)}, u32[]{:S(2)}) collective-permute-start(bf16[656,128]{1,0:T(8,128)(2,1)S(1)} %collective-permute-done.12.b0), channel_id=1, source_target_pairs={{0,2},{1,3},{2,0},{3,1},{4,6},{5,7},{6,4},{7,5},{8,10},{9,11},{10,... | collective-permute-start | bytes 503816 | tf_op jit(solution)/shard_map/ppermute | solution.py:456
  75.6 8.3 %collective-permute-start.20 = (bf16[656,128]{1,0:T(8,128)(2,1)S(1)}, bf16[656,128]{1,0:T(8,128)(2,1)S(1)}, u32[]{:S(2)}, u32[]{:S(2)}) collective-permute-start(bf16[656,128]{1,0:T(8,128)(2,1)S(1)} %collective-permute-done.12.b0), channel_id=1, source_target_pairs={{0,1},{1,0},{2,3},{3,2},{4,5},{5,4},{6,7},{7,6},{8,9},{9,8},{10,11... | collective-permute-start | bytes 503816 | tf_op jit(solution)/shard_map/ppermute | solution.py:456
  75.8 9.6 %collective-permute-start.24 = (bf16[656,128]{1,0:T(8,128)(2,1)S(1)}, bf16[656,128]{1,0:T(8,128)(2,1)S(1)}, u32[]{:S(2)}, u32[]{:S(2)}) collective-permute-start(bf16[656,128]{1,0:T(8,128)(2,1)S(1)} %collective-permute-done.13.b0), channel_id=1, source_target_pairs={{0,2},{1,3},{2,0},{3,1},{4,6},{5,7},{6,4},{7,5},{8,10},{9,11},{10,... | collective-permute-start | bytes 503816 | tf_op jit(solution)/shard_map/ppermute | solution.py:456
  83.3 7.3 %collective-permute-start.23 = (bf16[656,128]{1,0:T(8,128)(2,1)S(1)}, bf16[656,128]{1,0:T(8,128)(2,1)S(1)}, u32[]{:S(2)}, u32[]{:S(2)}) collective-permute-start(bf16[656,128]{1,0:T(8,128)(2,1)S(1)} %collective-permute-done.13.b0), channel_id=1, source_target_pairs={{0,1},{1,0},{2,3},{3,2},{4,5},{5,4},{6,7},{7,6},{8,9},{9,8},{10,11... | collective-permute-start | bytes 503816 | tf_op jit(solution)/shard_map/ppermute | solution.py:456
  83.8 9.2 %collective-permute-start.18 = (bf16[656,128]{1,0:T(8,128)(2,1)S(1)}, bf16[656,128]{1,0:T(8,128)(2,1)S(1)}, u32[]{:S(2)}, u32[]{:S(2)}) collective-permute-start(bf16[656,128]{1,0:T(8,128)(2,1)S(1)} %collective-permute-done.16.b0), channel_id=1, source_target_pairs={{0,1},{1,0},{2,3},{3,2},{4,5},{5,4},{6,7},{7,6},{8,9},{9,8},{10,11... | collective-permute-start | bytes 503816 | tf_op jit(solution)/shard_map/ppermute | solution.py:456
  101.9 9.5 %collective-permute-start.32 = (bf16[128,640]{1,0:T(8,128)(2,1)S(1)}, bf16[128,640]{1,0:T(8,128)(2,1)S(1)}, u32[]{:S(2)}, u32[]{:S(2)}) collective-permute-start(bf16[128,640]{1,0:T(8,128)(2,1)S(1)} %fusion.13), channel_id=1, source_target_pairs={{0,2},{1,3},{2,0},{3,1},{4,6},{5,7},{6,4},{7,5},{8,10},{9,11},{10,... | collective-permute-start | bytes 491528 | tf_op jit(solution)/shard_map/ppermute | solution.py:456
  113.1 8.2 %collective-permute-start.30 = (bf16[128,640]{1,0:T(8,128)(2,1)S(1)}, bf16[128,640]{1,0:T(8,128)(2,1)S(1)}, u32[]{:S(2)}, u32[]{:S(2)}) collective-permute-start(bf16[128,640]{1,0:T(8,128)(2,1)S(1)} %fusion.14), channel_id=1, source_target_pairs={{0,2},{1,3},{2,0},{3,1},{4,6},{5,7},{6,4},{7,5},{8,10},{9,11},{10,... | collective-permute-start | bytes 491528 | tf_op jit(solution)/shard_map/ppermute | solution.py:456
  116.3 10.4 %collective-permute-start.36 = (bf16[128,640]{1,0:T(8,128)(2,1)S(1)}, bf16[128,640]{1,0:T(8,128)(2,1)S(1)}, u32[]{:S(2)}, u32[]{:S(2)}) collective-permute-start(bf16[128,640]{1,0:T(8,128)(2,1)S(1)} %fusion.1), channel_id=1, source_target_pairs={{0,8},{1,9},{2,10},{3,11},{4,12},{5,13},{6,14},{7,15},{8,0},{9,1},... | collective-permute-start | bytes 491528 | tf_op jit(solution)/shard_map/ppermute | solution.py:456
  131.6 13.7 %collective-permute-start.37 = (bf16[656,128]{1,0:T(8,128)(2,1)S(1)}, bf16[656,128]{1,0:T(8,128)(2,1)S(1)}, u32[]{:S(2)}, u32[]{:S(2)}) collective-permute-start(bf16[656,128]{1,0:T(8,128)(2,1)S(1)} %get-tuple-element.167.b0), channel_id=1, source_target_pairs={{0,4},{1,5},{2,6},{3,7},{4,0},{5,1},{6,2},{7,3},{8,12},{9,13},{10,... | collective-permute-start | bytes 503816 | tf_op jit(solution)/shard_map/ppermute | solution.py:456
  132.4 12.9 %collective-permute-start.38 = (bf16[656,128]{1,0:T(8,128)(2,1)S(1)}, bf16[656,128]{1,0:T(8,128)(2,1)S(1)}, u32[]{:S(2)}, u32[]{:S(2)}) collective-permute-start(bf16[656,128]{1,0:T(8,128)(2,1)S(1)} %get-tuple-element.167.b0), channel_id=1, source_target_pairs={{0,8},{1,9},{2,10},{3,11},{4,12},{5,13},{6,14},{7,15},{8,0},{9,1},... | collective-permute-start | bytes 503816 | tf_op jit(solution)/shard_map/ppermute | solution.py:456
  133.9 11.4 %collective-permute-start.39 = (bf16[656,128]{1,0:T(8,128)(2,1)S(1)}, bf16[656,128]{1,0:T(8,128)(2,1)S(1)}, u32[]{:S(2)}, u32[]{:S(2)}) collective-permute-start(bf16[656,128]{1,0:T(8,128)(2,1)S(1)} %get-tuple-element.167.b0), channel_id=1, source_target_pairs={{0,2},{1,3},{2,0},{3,1},{4,6},{5,7},{6,4},{7,5},{8,10},{9,11},{10,... | collective-permute-start | bytes 503816 | tf_op jit(solution)/shard_map/ppermute | solution.py:456
  135.4 8.8 %collective-permute-start.41 = (bf16[4,144,128]{2,1,0:T(8,128)(2,1)S(1)}, bf16[4,144,128]{2,1,0:T(8,128)(2,1)S(1)}, u32[]{:S(2)}, u32[]{:S(2)}) collective-permute-start(bf16[4,144,128]{2,1,0:T(8,128)(2,1)S(1)} %get-tuple-element.204), channel_id=1, source_target_pairs={{0,2},{1,3},{2,0},{3,1},{4,6},{5,7},{6,4},{7,5},{8,10},{9,11},{10,... | collective-permute-start | bytes 442376 | tf_op jit(solution)/shard_map/ppermute | solution.py:456
  135.9 9.4 %collective-permute-start.42 = (bf16[4,144,128]{2,1,0:T(8,128)(2,1)S(1)}, bf16[4,144,128]{2,1,0:T(8,128)(2,1)S(1)}, u32[]{:S(2)}, u32[]{:S(2)}) collective-permute-start(bf16[4,144,128]{2,1,0:T(8,128)(2,1)S(1)} %get-tuple-element.206), channel_id=1, source_target_pairs={{0,3},{1,2},{2,1},{3,0},{4,7},{5,6},{6,5},{7,4},{8,11},{9,10},{10,... | collective-permute-start | bytes 442376 | tf_op jit(solution)/shard_map/ppermute | solution.py:456
  145.3 7.9 %collective-permute-start.43 = (bf16[656,128]{1,0:T(8,128)(2,1)S(1)}, bf16[656,128]{1,0:T(8,128)(2,1)S(1)}, u32[]{:S(2)}, u32[]{:S(2)}) collective-permute-start(bf16[656,128]{1,0:T(8,128)(2,1)S(1)} %collective-permute-done.38.b0), channel_id=1, source_target_pairs={{0,4},{1,5},{2,6},{3,7},{4,0},{5,1},{6,2},{7,3},{8,12},{9,13},{10,... | collective-permute-start | bytes 503816 | tf_op jit(solution)/shard_map/ppermute | solution.py:456
  148.7 8.7 %collective-permute-start.51 = (bf16[4,144,128]{2,1,0:T(8,128)(2,1)S(1)}, bf16[4,144,128]{2,1,0:T(8,128)(2,1)S(1)}, u32[]{:S(2)}, u32[]{:S(2)}) collective-permute-start(bf16[4,144,128]{2,1,0:T(8,128)(2,1)S(1)} %get-tuple-element.202), channel_id=1, source_target_pairs={{0,12},{1,13},{2,14},{3,15},{4,8},{5,9},{6,10},{7,11},{8,4},{9,5},... | collective-permute-start | bytes 442376 | tf_op jit(solution)/shard_map/ppermute | solution.py:456
  150.3 13.9 %collective-permute-start.52 = (bf16[4,144,128]{2,1,0:T(8,128)(2,1)S(1)}, bf16[4,144,128]{2,1,0:T(8,128)(2,1)S(1)}, u32[]{:S(2)}, u32[]{:S(2)}) collective-permute-start(bf16[4,144,128]{2,1,0:T(8,128)(2,1)S(1)} %get-tuple-element.201), channel_id=1, source_target_pairs={{0,8},{1,9},{2,10},{3,11},{4,12},{5,13},{6,14},{7,15},{8,0},{9,1},... | collective-permute-start | bytes 442376 | tf_op jit(solution)/shard_map/ppermute | solution.py:456
  150.8 18.5 %collective-permute-start.49 = (bf16[656,128]{1,0:T(8,128)(2,1)S(1)}, bf16[656,128]{1,0:T(8,128)(2,1)S(1)}, u32[]{:S(2)}, u32[]{:S(2)}) collective-permute-start(bf16[656,128]{1,0:T(8,128)(2,1)S(1)} %collective-permute-done.37.b0), channel_id=1, source_target_pairs={{0,1},{1,0},{2,3},{3,2},{4,5},{5,4},{6,7},{7,6},{8,9},{9,8},{10,11... | collective-permute-start | bytes 503816 | tf_op jit(solution)/shard_map/ppermute | solution.py:456
  153.3 16.6 %collective-permute-start.56 = (bf16[656,128]{1,0:T(8,128)(2,1)S(1)}, bf16[656,128]{1,0:T(8,128)(2,1)S(1)}, u32[]{:S(2)}, u32[]{:S(2)}) collective-permute-start(bf16[656,128]{1,0:T(8,128)(2,1)S(1)} %collective-permute-done.38.b0), channel_id=1, source_target_pairs={{0,2},{1,3},{2,0},{3,1},{4,6},{5,7},{6,4},{7,5},{8,10},{9,11},{10,... | collective-permute-start | bytes 503816 | tf_op jit(solution)/shard_map/ppermute | solution.py:456
  153.9 16.0 %collective-permute-start.50 = (bf16[656,128]{1,0:T(8,128)(2,1)S(1)}, bf16[656,128]{1,0:T(8,128)(2,1)S(1)}, u32[]{:S(2)}, u32[]{:S(2)}) collective-permute-start(bf16[656,128]{1,0:T(8,128)(2,1)S(1)} %collective-permute-done.44.b2), channel_id=1, source_target_pairs={{0,1},{1,0},{2,3},{3,2},{4,5},{5,4},{6,7},{7,6},{8,9},{9,8},{10,11... | collective-permute-start | bytes 503816 | tf_op jit(solution)/shard_map/ppermute | solution.py:456
  157.4 15.0 %collective-permute-start.48 = (bf16[656,128]{1,0:T(8,128)(2,1)S(1)}, bf16[656,128]{1,0:T(8,128)(2,1)S(1)}, u32[]{:S(2)}, u32[]{:S(2)}) collective-permute-start(bf16[656,128]{1,0:T(8,128)(2,1)S(1)} %collective-permute-done.43.b0), channel_id=1, source_target_pairs={{0,2},{1,3},{2,0},{3,1},{4,6},{5,7},{6,4},{7,5},{8,10},{9,11},{10,... | collective-permute-start | bytes 503816 | tf_op jit(solution)/shard_map/ppermute | solution.py:456
  (37 other events, 223.1 us)
